TPU v7x, 32 devices: a whole 2x2x4 slice. The times are simulated.
32 devices in a mesh: gx: 2 (over y), gz: 4 (over x, core), gy: 4 (over z).
Axes of the slice: x: 2, y: 2, z: 4, core: 2. Of those that a mesh axis runs over, the one named last changes fastest.
Arguments:
- gas_field: float32 [3, 32, 64, 512], P(None, 'gx', 'gy', 'gz'), may hold values from -6 to 6
- velocity: float32 [2048, 3, 128], P(('gx', 'gz', 'gy')), may hold values from -6 to 6
- fraction: float32 [2048, 3, 128], P(('gx', 'gz', 'gy')), may hold values from 0 to 1
- response: float32 [2048, 128], P(('gx', 'gz', 'gy')), may hold values from 0.25 to 2
- cell_index: int32 [2048, 128], P(('gx', 'gz', 'gy')), may hold values from 0 to 127
- brick_index: int32 [2048], P(('gx', 'gz', 'gy')), may hold values from 0 to 255
- crossing: int32 [192, 8], P(('gx', 'gz', 'gy')), may hold values from -1 to 63, as said below
Outputs:
- gas_next: float32 [3, 32, 64, 512], P(None, 'gx', 'gy', 'gz')
- velocity_next: float32 [2048, 3, 128], P(('gx', 'gz', 'gy'))
- arrivals: float32 [192, 8, 7, 128], P(('gx', 'gz', 'gy'))
Inputs may be any that keep to these rules, and one draw needn't show every extreme that they name: `crossing`: row 6 d + f lists the blocks of tile d (numbers 0 to 63 within the tile) that leave through face f (+x, -x, +y, -y, +z, -z): listed blocks first, then -1. No block is listed twice in one tile. Some face of some tile lists 8 blocks.
All inputs are finite; a program needn't handle non-finite values.
Results may differ from a plain program's by a relative error of at most 0.0003.
Values sent between devices are 32-bit elements; how exact they have to be, the bound alone decides.
No kernel may reach another device: no remote copies, remote signals or barrier semaphores. Data moves between devices by JAX's collectives and lax.ppermute only.
A program may use at most 128 MiB of HBM per device.

v0:
```python
import functools

import jax
import jax.numpy as jnp
from jax import lax
from jax.experimental import pallas as pl
from jax.experimental.pallas import tpu as pltpu
from jax.sharding import PartitionSpec as P

BX = 4
BY = 4
BZ = 8

TIME_STEP = 0.25
VISCOSITY = 0.4

LANES = 128
PACK = 32
ROWS_Y = 24
REACH_X = BX + 1
REACH_Y = 8
SPREAD = REACH_X * REACH_Y
REACH_Z = 2 * BZ
UNROLL = 8

WEIGHT, ALONG_Y, IN_Y, ALONG_Z, IN_Z, RATE, MOVING, OFFSET = 0, 5, 6, 7, 8, 9, 10, 13
TABLE_ROWS = 16
STATE = 8

VMEM = pl.BlockSpec(memory_space=pltpu.VMEM)
SMEM = pl.BlockSpec(memory_space=pltpu.SMEM)
HBM = pl.BlockSpec(memory_space=pltpu.HBM)


def moved_along(block, axis, distance):
    count = lax.axis_size(axis)
    return lax.ppermute(block, axis, [(i, (i + distance) % count) for i in range(count)])


def swapped_z(blocks):
    count = lax.axis_size("gz")
    first = [(i, i ^ 1) for i in range(count)]
    second = [(i, (((i + 1) ^ 1) - 1) % count) for i in range(count)]
    return lax.ppermute(blocks[0], "gz", first), lax.ppermute(blocks[1], "gz", second)


def swapped_y(blocks):
    nz, ny = lax.axis_size("gz"), lax.axis_size("gy")
    first = [(j, j ^ 1) for j in range(ny)]
    second = []
    for k in range(nz):
        second.append((k * ny, (k ^ 1) * ny))
        second.append((k * ny + ny - 1, (k ^ 1) * ny + ny - 1))
        second.extend((k * ny + j, k * ny + ((j + 1) ^ 1) - 1) for j in range(1, ny - 1))
    return lax.ppermute(blocks[0], "gy", first), lax.ppermute(blocks[1], ("gz", "gy"), second)


def moved_diagonally(block, distance):
    nx, nz = lax.axis_size("gx"), lax.axis_size("gz")
    route = [(i * nz + k, (i + distance) % nx * nz + (k + distance) % nz) for i in range(nx) for k in range(nz)]
    return lax.ppermute(block, ("gx", "gz"), route)


def call(body, outs, *operands, smem=(), hbm=(), smem_outs=(), scratch=(), aliases=None, cycles=0, limit=40):
    return pl.pallas_call(
        body,
        out_shape=[o if isinstance(o, jax.ShapeDtypeStruct) else jax.ShapeDtypeStruct(o, jnp.float32) for o in outs],
        in_specs=[SMEM if i in smem else HBM if i in hbm else VMEM for i in range(len(operands))],
        out_specs=[SMEM if i in smem_outs else VMEM for i in range(len(outs))],
        scratch_shapes=list(scratch),
        input_output_aliases=aliases or {},
        compiler_params=pltpu.CompilerParams(vmem_limit_bytes=limit * 1024 * 1024),
        cost_estimate=pl.CostEstimate(flops=cycles * 4096, bytes_accessed=cycles * 1024, transcendentals=0),
    )(*operands)


def lane_ids(rows):
    return lax.broadcasted_iota(jnp.int32, (rows, LANES), 1)


def row_ids(rows):
    return lax.broadcasted_iota(jnp.int32, (rows, LANES), 0)


def turned(value, shift):
    shift = shift % LANES
    return pltpu.roll(value, shift, 1) if shift else value


def odd(axis):
    return lax.axis_index(axis) % 2


def begin_kernel(
    gas_ref, velocity_in, fraction_in, response_in, cell_in, brick_in, crossing_in,
    grid_ref, face_ref, plane_ref, velocity_ref, fraction_ref, response_ref, cell_ref, brick_ref, crossing_ref, sems,
):
    comps, size_x, size_y, _ = gas_ref.shape
    pairs = [
        (gas_ref, grid_ref.at[:, 1 : size_x + 1, 0:size_y]),
        (velocity_in, velocity_ref), (fraction_in, fraction_ref), (response_in, response_ref),
        (cell_in, cell_ref), (brick_in, brick_ref), (crossing_in, crossing_ref),
    ]
    copies = [pltpu.make_async_copy(source, target, sems.at[i]) for i, (source, target) in enumerate(pairs)]
    for copy in copies:
        copy.start()
    zeros = jnp.zeros((ROWS_Y, LANES), jnp.float32)
    for c in range(comps):
        grid_ref[c, 0] = zeros
        grid_ref[c, size_x + 1] = zeros
        for x in range(size_x):
            grid_ref[c, x + 1, size_y:] = zeros[size_y:]
    copies[0].wait()
    lane = lane_ids(size_y)
    face = jnp.zeros((size_y, LANES), jnp.float32)
    for c in range(comps):
        plane_ref[c * size_y : (c + 1) * size_y] = grid_ref[c, 1, 0:size_y]
        for x in range(size_x):
            place = PACK * c + x
            face = jnp.where(lane == place, turned(grid_ref[c, x + 1, 0:size_y], place), face)
    face_ref[...] = face
    for copy in copies[1:]:
        copy.wait()


def parts_of(value):
    main = value.astype(jnp.bfloat16).astype(jnp.float32)
    return main, value - main


def lay_out(grid_ref, lines_ref, p, q, size_y, size_z):
    comps = grid_ref.shape[0]
    rows_z = size_z + 8
    count_y = size_y // BY
    for c in range(comps):
        planes = [grid_ref[c, p * BX + a + 1, q * BY : q * BY + REACH_Y] for a in range(REACH_X)]
        main, rest = parts_of(jnp.concatenate(planes, axis=0))
        stack = jnp.concatenate([main, rest, main, jnp.zeros((LANES - 3 * SPREAD, LANES), jnp.float32)], axis=0)
        at = ((p * count_y + q) * comps + c) * rows_z
        lines_ref[at : at + size_z] = jnp.transpose(stack)


def lay_out_top(turned_ref, lines_ref, q, comps, count_x, count_y, size_z):
    lane = lane_ids(count_x)
    rows_z = size_z + 8
    for c in range(comps):
        total = jnp.zeros((count_x, LANES), jnp.float32)
        for a in range(REACH_X):
            rows = turned_ref[pl.ds(PACK * c + a, count_x, stride=BX)]
            total = jnp.where(lane // REACH_Y == a, turned(rows, a * REACH_Y - q * BY), total)
        main, rest = parts_of(total)
        line = main + turned(rest, SPREAD) + turned(main, 2 * SPREAD)
        for p in range(count_x):
            at = ((p * count_y + q) * comps + c) * rows_z + size_z
            lines_ref[at : at + 1] = line[p : p + 1]


def prepare_kernel(
    grid_ref, velocity_ref, fraction_ref, response_ref, cell_ref, brick_ref,
    lines_ref, deposit_ref, table_ref, state_ref, ready_ref, list_ref,
):
    comps, size_x, size_y, size_z = grid_ref.shape[0], grid_ref.shape[1] - 2, grid_ref.shape[2] - 8, grid_ref.shape[3]
    nblocks = velocity_ref.shape[1]
    count_x, count_y, count_z = size_x // BX, size_y // BY, size_z // BZ
    rows_z = size_z + 8
    spare = table_ref.shape[1] - nblocks

    room = nblocks + UNROLL

    def visit(k, counts):
        late = jnp.where(lax.rem(lax.div(brick_ref[k], count_z), count_y) == count_y - 1, 1, 0)
        list_ref[jnp.where(late == 1, room + counts[1], counts[0])] = k
        return counts[0] + 1 - late, counts[1] + late

    early, late = lax.fori_loop(0, nblocks, visit, (jnp.int32(0), jnp.int32(0)), unroll=8)
    for base, count in ((0, early), (room, late)):
        for u in range(UNROLL):
            list_ref[base + count + u] = nblocks
    list_ref[2 * room] = early
    list_ref[2 * room + 1] = late
    ready_ref[...] = jnp.zeros_like(ready_ref)

    deposit_ref[...] = jnp.zeros_like(deposit_ref)
    for p in range(count_x):
        for q in range(count_y):
            for c in range(comps):
                at = ((p * count_y + q) * comps + c) * rows_z + size_z
                lines_ref[at : at + 8] = jnp.zeros((8, LANES), jnp.float32)
    for p in range(count_x - 1):
        for q in range(count_y - 1):
            lay_out(grid_ref, lines_ref, p, q, size_y, size_z)

    cells = cell_ref[...]
    cell_x, cell_y, cell_z = cells // (BY * BZ), cells // BZ % BY, cells % BZ
    along_x = fraction_ref[0]

    def put(row, value):
        table_ref[row, 0:nblocks] = value
        table_ref[row, nblocks : nblocks + spare] = jnp.zeros((spare, LANES), jnp.float32)

    for a in range(REACH_X):
        put(WEIGHT + a, jnp.where(cell_x == a, 1.0 - along_x, 0.0) + jnp.where(cell_x == a - 1, along_x, 0.0))
    put(ALONG_Y, fraction_ref[1])
    put(IN_Y, cell_y.astype(jnp.float32))
    put(ALONG_Z, fraction_ref[2])
    put(IN_Z, cell_z.astype(jnp.float32))
    put(RATE, 1.0 / response_ref[...])
    for c in range(comps):
        put(MOVING + c, velocity_ref[c])
        put(OFFSET + c, fraction_ref[c])
    state_ref[...] = jnp.zeros_like(state_ref)
    state_ref[pl.ds(2 * comps, nblocks, stride=STATE)] = response_ref[...]


def y_lines_kernel(grid_ref, face_ref, from_x_ref, edge_ref, ready_ref, out_ref):
    comps, size_x = grid_ref.shape[0], grid_ref.shape[1] - 2
    size_y = face_ref.shape[0]
    for c in range(comps):
        out_ref[c * size_x : (c + 1) * size_x] = grid_ref[c, 1 : size_x + 1, 0]
        out_ref[comps * size_x + c : comps * size_x + c + 1] = from_x_ref[c * size_y : c * size_y + 1]
    line = jnp.where(lane_ids(8) % PACK == size_x, turned(edge_ref[0:8], size_x), face_ref[0:8])
    out_ref[comps * size_x + comps : comps * size_x + comps + 1] = line[0:1]


def halo_xz_kernel(grid_in_ref, lines_in_ref, face_ref, from_x_ref, edge_ref, grid_ref, lines_ref, top_ref, turned_ref):
    comps, size_x = grid_ref.shape[0], grid_ref.shape[1] - 2
    size_y, size_z = face_ref.shape[0], grid_ref.shape[3]
    count_x, count_y = size_x // BX, size_y // BY
    for c in range(comps):
        grid_ref[c, size_x + 1, 0:size_y] = from_x_ref[c * size_y : (c + 1) * size_y]
    for q in range(count_y - 1):
        lay_out(grid_ref, lines_ref, count_x - 1, q, size_y, size_z)
    top = jnp.where(lane_ids(size_y) % PACK == size_x, turned(edge_ref[...], size_x), face_ref[...])
    top_ref[0:size_y] = top
    top_ref[size_y:] = jnp.zeros((LANES - size_y, LANES), jnp.float32)
    turned_ref[...] = jnp.transpose(top_ref[...])
    for q in range(count_y - 1):
        lay_out_top(turned_ref, lines_ref, q, comps, count_x, count_y, size_z)


def halo_y_kernel(size_y, grid_in_ref, lines_in_ref, top_in_ref, first_ref, second_ref, grid_ref, lines_ref, turned_ref):
    comps, size_x, size_z = grid_ref.shape[0], grid_ref.shape[1] - 2, grid_ref.shape[3]
    count_x, count_y = size_x // BX, size_y // BY
    inside = lax.axis_index("gy") != lax.axis_size("gy") - 1
    even = odd("gy") == 0
    kept = (row_ids(8) == 0) & inside

    def line_at(row):
        line = jnp.where(even, first_ref[row : row + 1], second_ref[row : row + 1])
        return jnp.where(kept, jnp.broadcast_to(line, (8, LANES)), 0.0)

    for c in range(comps):
        for x in range(size_x + 1):
            grid_ref[c, x + 1, size_y:] = line_at(c * size_x + x if x < size_x else comps * size_x + c)
    for p in range(count_x):
        lay_out(grid_ref, lines_ref, p, count_y - 1, size_y, size_z)
    corner = line_at(comps * size_x + comps)
    rest = jnp.zeros((LANES - size_y - 8, LANES), jnp.float32)
    turned_ref[...] = jnp.transpose(jnp.concatenate([top_in_ref[0:size_y], corner, rest], axis=0))
    lay_out_top(turned_ref, lines_ref, count_y - 1, comps, count_x, count_y, size_z)


def blocks_kernel(
    late, comps, size_x, count_y, count_z, rows_z,
    list_ref, brick_ref, lines_ref, table_ref, state_in_ref, deposit_in_ref, state_ref, deposit_ref,
):
    nblocks = brick_ref.shape[0]
    room = (list_ref.shape[0] - 2) // 2
    row_y = row_ids(REACH_Y).astype(jnp.float32)
    row_z = row_ids(REACH_Z).astype(jnp.float32)
    lane = lane_ids(REACH_Y)

    def hat(rows, inside, along):
        return jnp.where(rows == inside, 1.0 - along, 0.0) + jnp.where(rows == inside + 1.0, along, 0.0)

    def loaded(at):
        k = list_ref[at]
        brick = brick_ref[jnp.minimum(k, nblocks - 1)]
        brick_x = lax.div(brick, count_y * count_z)
        brick_y = lax.rem(lax.div(brick, count_z), count_y)
        brick_z = lax.rem(brick, count_z)
        sel = jnp.where(brick_z == count_z - 1, 1, 0)
        start = (sel * comps * (size_x + 1) + brick_x * BX) * ROWS_Y + brick_y * BY
        first = pl.multiple_of((brick_x * count_y + brick_y) * comps * rows_z + brick_z * BZ, 8)
        window = jnp.concatenate([lines_ref[pl.ds(first + c * rows_z, REACH_Z)] for c in range(comps)], axis=0)
        rows = [table_ref[i, pl.ds(k, 1)] for i in range(OFFSET + comps)]
        return k, start, brick_z * BZ, window, rows

    def moved_of(window, rows):
        weight_y = hat(row_y, rows[IN_Y], rows[ALONG_Y])
        weight_z = hat(row_z, rows[IN_Z], rows[ALONG_Z])
        main, rest = parts_of(jnp.concatenate([rows[WEIGHT + a] * weight_y for a in range(REACH_X)], axis=0))
        unused = jnp.zeros((LANES - 3 * SPREAD, LANES), jnp.float32)
        table = jnp.concatenate([main, main, rest, unused], axis=0).astype(jnp.bfloat16)
        seen = lax.dot_general(
            window.astype(jnp.bfloat16), table, (((1,), (0,)), ((), ())), preferred_element_type=jnp.float32
        )
        state, moved, pushed = [], [], []
        for c in range(comps):
            gas_sample = jnp.sum(seen[c * REACH_Z : (c + 1) * REACH_Z] * weight_z, axis=0, keepdims=True)
            drag = (gas_sample - rows[MOVING + c]) * rows[RATE]
            state.append(rows[MOVING + c] + TIME_STEP * drag)
            moved.append(rows[OFFSET + c] + TIME_STEP * state[c])
            pushed.append(drag * weight_z)
        pushed.append(jnp.zeros((LANES - comps * REACH_Z, LANES), jnp.float32))
        push_main, push_rest = parts_of(jnp.concatenate(pushed, axis=0))
        push = jnp.concatenate([push_main, push_rest, push_main], axis=1).astype(jnp.bfloat16)
        spread = jnp.concatenate([main, main, rest], axis=1).astype(jnp.bfloat16)
        shares = lax.dot_general(spread, push, (((1,), (1,)), ((), ())), preferred_element_type=jnp.float32)
        return state + moved, shares

    count = list_ref[2 * room + late]

    @pl.loop(0, (count + UNROLL - 1) // UNROLL)
    def _(group):
        at = late * room + group * UNROLL
        taken = [loaded(at + u) for u in range(UNROLL)]
        results = [moved_of(window, rows) for _, _, _, window, rows in taken]
        parts = []
        for (_, _, first_z, _, _), (_, shares) in zip(taken, results):
            within = ((lane - first_z) & (LANES - 1)) < REACH_Z
            parts.append([])
            for c in range(comps):
                shift = (first_z - c * REACH_Z + LANES) & (LANES - 1)
                for a in range(REACH_X):
                    part = pltpu.roll(shares[a * REACH_Y : (a + 1) * REACH_Y], shift, 1)
                    parts[-1].append(jnp.where(within, part, 0.0))
        for (k, _, _, _, _), (state, _) in zip(taken, results):
            for i, value in enumerate(state):
                state_ref[pl.ds(STATE * k + i, 1)] = value
        for (_, start, _, _, _), mine in zip(taken, parts):
            spots = [
                pl.ds(start + (c * (size_x + 1) + a) * ROWS_Y, REACH_Y) for c in range(comps) for a in range(REACH_X)
            ]
            sums = [deposit_ref[spot] + part for spot, part in zip(spots, mine)]
            for spot, total in zip(spots, sums):
                deposit_ref[spot] = total


def send_kernel(push, diffuse, crossing_ref, state_ref, grid_ref, deposit_ref, leaving_ref, velocity_ref, y_ref, x_ref, z_ref):
    comps, size_x = grid_ref.shape[0], grid_ref.shape[1] - 2
    size_y = z_ref.shape[0]
    nblocks = velocity_ref.shape[1]
    slots = crossing_ref.shape[1]
    rows = STATE * slots
    first = odd("gy") == 0
    velocity = [state_ref[pl.ds(c, nblocks, stride=STATE)] for c in range(comps)]
    for face in range(6):
        tiles = []
        for slot in range(slots):
            block = crossing_ref[face, slot]
            spot = pl.ds(pl.multiple_of(jnp.maximum(block, 0) * STATE, STATE), STATE)
            tiles.append(jnp.where(block >= 0, state_ref[spot], 0.0))
        leaving_ref[face] = jnp.concatenate(tiles, axis=0)
    y_ref[0, 0:rows] = jnp.where(first, leaving_ref[2], leaving_ref[3])
    y_ref[1, 0:rows] = jnp.where(first, leaving_ref[3], leaving_ref[2])
    for c in range(comps):
        velocity_ref[c] = velocity[c]
    lane = lane_ids(ROWS_Y)
    face = jnp.zeros((ROWS_Y, LANES), jnp.float32)
    for c in range(comps):
        for x in range(size_x + 1):
            beyond = push * deposit_ref[1, c, x]
            if x < size_x:
                behind = diffuse * turned(grid_ref[c, x + 1, 0:size_y], 1)
                beyond = jnp.concatenate([beyond[:size_y] + behind, beyond[size_y:]], axis=0)
            place = PACK * c + x
            face = jnp.where(lane == place, turned(beyond, place), face)
        wrapped = jnp.where(lane_ids(size_x) == 0, 0.0, deposit_ref[1, c, 0:size_x, size_y])
        line = diffuse * grid_ref[c, 1 : size_x + 1, size_y - 1] + push * (deposit_ref[0, c, 0:size_x, size_y] + wrapped)
        y_ref[0, rows + c * ROWS_Y : rows + c * ROWS_Y + size_x] = line
        wrapped = jnp.where(lane_ids(ROWS_Y) == 0, 0.0, deposit_ref[1, c, size_x])
        total = push * (deposit_ref[0, c, size_x] + wrapped)
        x_ref[c * size_y : (c + 1) * size_y] = diffuse * grid_ref[c, size_x, 0:size_y] + total[:size_y]
        at = rows + c * ROWS_Y + size_x
        y_ref[0, at : at + 8] = total[size_y:]
    z_ref[...] = face[:size_y]
    y_ref[0, rows + size_x + 1 : rows + size_x + 2] = face[size_y : size_y + 1]
    y_ref[1, rows:] = y_ref[0, rows:]


def base_kernel(push, diffuse, grid_ref, deposit_ref, top_ref, base_ref):
    comps, size_x, size_y, size_z = base_ref.shape
    lane = lane_ids(size_y)
    top = top_ref[0:size_y]
    for c in range(comps):
        for x in range(size_x):
            here = grid_ref[c, x + 1, 0:size_y]
            laplace = grid_ref[c, x + 2, 0:size_y]
            if x:
                laplace = laplace + grid_ref[c, x, 0:size_y]
            before = jnp.where(row_ids(size_y) == 0, 0.0, pltpu.roll(here, 1, 0))
            laplace = laplace + grid_ref[c, x + 1, 1 : size_y + 1] + before
            ahead = jnp.where(lane == size_z - 1, turned(top, size_z - 1 - (PACK * c + x)), turned(here, -1))
            laplace = laplace + ahead + jnp.where(lane == 0, 0.0, turned(here, 1)) - 6.0 * here
            total = deposit_ref[0, c, x, 0:size_y] + jnp.where(lane == 0, 0.0, deposit_ref[1, c, x, 0:size_y])
            base_ref[c, x] = here + diffuse * laplace + push * total


def below(first_ref, second_ref, rows):
    got = jnp.where(odd("gy") == 1, first_ref[rows], second_ref[rows])
    return jnp.where(lax.axis_index("gy") != 0, got, 0.0)


def relay_kernel(size_x, size_y, comps, count, first_ref, second_ref, x_in_ref, z_in_ref, leaving_ref, x_ref, z_ref, edge_ref):
    edge = comps * size_y
    x_ref[0:edge] = x_in_ref[...]
    for c in range(comps):
        at = count + c * ROWS_Y + size_x
        spot = slice(c * size_y, c * size_y + 1)
        x_ref[spot] = x_in_ref[spot] + below(first_ref, second_ref, slice(at, at + 1))
    x_ref[edge : edge + count] = leaving_ref[0]
    if x_ref.shape[0] > edge + count:
        x_ref[edge + count : edge + 2 * count] = leaving_ref[1]
    at = count + size_x + 1
    edge_ref[...] = z_in_ref[...]
    edge_ref[0:1] = z_in_ref[0:1] + below(first_ref, second_ref, slice(at, at + 1))
    up = odd("gz")
    z_ref[up, 0:count] = leaving_ref[4]
    z_ref[up, count : count + size_y] = edge_ref[...]
    z_ref[1 - up, 0:count] = leaving_ref[5]
    z_ref[1 - up, count : count + size_y] = jnp.zeros((size_y, LANES), jnp.float32)


def finish_kernel(
    count, base_ref, y1_ref, y2_ref, x_ref, minus_x_ref, z1_ref, z2_ref, edge_ref, gas_ref, arrivals_ref
):
    comps, size_x, size_y, _ = base_ref.shape
    first_row, first_lane = row_ids(size_y) == 0, lane_ids(size_y) == 0
    rows = slice(count, count + size_y)
    from_first = odd("gz") == 1
    face = jnp.where(from_first, z1_ref[rows], z2_ref[rows])
    corner = edge_ref[...]
    for c in range(comps):
        for x in range(size_x):
            at = count + c * ROWS_Y + x
            line = jnp.broadcast_to(below(y1_ref, y2_ref, slice(at, at + 1)), (size_y, LANES))
            total = base_ref[c, x] + jnp.where(first_row, line, 0.0)
            far = turned(face, -(PACK * c + x))
            if x == 0:
                total = total + x_ref[c * size_y : (c + 1) * size_y]
                far = far + turned(corner, -(PACK * c + size_x))
            gas_ref[c, x] = total + jnp.where(first_lane, far, 0.0)

    slots = arrivals_ref.shape[2]
    lower, upper = lax.axis_index("gy") != 0, lax.axis_index("gy") != lax.axis_size("gy") - 1
    odd_y = odd("gy") == 1
    for i in range(arrivals_ref.shape[1]):

        def rows_of(ref, at=0):
            return ref[pl.ds(at + i, slots, stride=STATE)]

        arrivals_ref[0, i] = rows_of(x_ref, comps * size_y)
        arrivals_ref[1, i] = rows_of(minus_x_ref, minus_x_ref.shape[0] - count)
        y1, y2 = rows_of(y1_ref), rows_of(y2_ref)
        arrivals_ref[2, i] = jnp.where(lower, jnp.where(odd_y, y1, y2), 0.0)
        arrivals_ref[3, i] = jnp.where(upper, jnp.where(odd_y, y2, y1), 0.0)
        z1, z2 = rows_of(z1_ref), rows_of(z2_ref)
        arrivals_ref[4, i] = jnp.where(from_first, z1, z2)
        arrivals_ref[5, i] = jnp.where(from_first, z2, z1)


def per_device(gas_field, velocity, fraction, response, cell_index, brick_index, crossing):
    comps, size_x, size_y, size_z = gas_field.shape
    nblocks = velocity.shape[0]
    loading = 0.5 * size_x * size_y * size_z / (nblocks * 128)
    push, diffuse = -TIME_STEP * loading, TIME_STEP * VISCOSITY
    velocity = jnp.transpose(velocity, (1, 0, 2))
    fraction = jnp.transpose(fraction, (1, 0, 2))
    spare = nblocks + 8
    rows_z = size_z + 8
    grid_shape = (comps, size_x + 2, ROWS_Y, LANES)
    lines_shape = ((size_x // BX) * (size_y // BY) * comps * rows_z, LANES)
    deposit_shape = (2 * comps * (size_x + 1) * ROWS_Y, LANES)

    inputs = (gas_field, velocity, fraction, response, cell_index, brick_index, crossing)
    inputs = [pltpu.with_memory_space_constraint(array, pltpu.HBM) for array in inputs]
    grid, face, plane, velocity, fraction, response, cell_index, brick_index, crossing = call(
        begin_kernel,
        [grid_shape, (size_y, LANES), (comps * size_y, LANES)]
        + [jax.ShapeDtypeStruct(array.shape, array.dtype) for array in inputs[1:]],
        *inputs, hbm=range(7), scratch=(pltpu.SemaphoreType.DMA((7,)),), limit=40,
    )
    from_z = moved_along(face, "gz", -1)
    from_x = moved_along(plane, "gx", -1)
    from_xz = moved_diagonally(face, -1)
    lines, deposit, table, state, ready, blocks = call(
        prepare_kernel,
        [
            lines_shape,
            deposit_shape,
            (TABLE_ROWS, spare, LANES),
            (STATE * spare, LANES),
            (8, LANES),
            jax.ShapeDtypeStruct((2 * (nblocks + UNROLL) + 2,), jnp.int32),
        ],
        grid, velocity, fraction, response, cell_index, brick_index,
        smem=(5,), smem_outs=(5,), cycles=3000,
    )
    line_rows = -(-(comps * size_x + comps + 1) // 8) * 8
    (y_lines,) = call(y_lines_kernel, [(line_rows, LANES)], grid, from_z, from_x, from_xz, ready)
    y1, y2 = swapped_y((y_lines, y_lines))
    square = pltpu.VMEM((LANES, LANES), jnp.float32)
    grid, lines, top = call(
        halo_xz_kernel, [grid_shape, lines_shape, (LANES, LANES)], grid, lines, from_z, from_x, from_xz,
        aliases={0: 0, 1: 1}, scratch=(square,), cycles=1000,
    )

    def advance(late, lines, state, deposit):
        return call(
            functools.partial(blocks_kernel, late, comps, size_x, size_y // BY, size_z // BZ, rows_z),
            [(STATE * spare, LANES), deposit_shape], blocks, brick_index, lines, table, state, deposit,
            smem=(0, 1), aliases={4: 0, 5: 1}, cycles=6000 - 4000 * late,
        )

    state, deposit = advance(0, lines, state, deposit)
    grid, lines = call(
        functools.partial(halo_y_kernel, size_y), [grid_shape, lines_shape], grid, lines, top, y1, y2,
        aliases={0: 0, 1: 1}, scratch=(square,), cycles=1000,
    )
    state, deposit = advance(1, lines, state, deposit)

    deposit = deposit.reshape(2, comps, size_x + 1, ROWS_Y, LANES)
    count = STATE * crossing.shape[1]
    leaving, velocity_next, to_y, to_x, to_z = call(
        functools.partial(send_kernel, push, diffuse),
        [
            (6, count, LANES),
            (comps, nblocks, LANES),
            (2, count + comps * ROWS_Y, LANES),
            (comps * size_y, LANES),
            (size_y, LANES),
        ],
        crossing, state, grid, deposit, smem=(0,), cycles=1000,
    )
    y1, y2 = swapped_y((to_y[0], to_y[1]))
    (base,) = call(
        functools.partial(base_kernel, push, diffuse), [gas_field.shape], grid, deposit, top, cycles=1000,
    )
    edge = comps * size_y
    both = lax.axis_size("gx") == 2
    to_x, to_z, to_xz = call(
        functools.partial(relay_kernel, size_x, size_y, comps, count),
        [(edge + (2 if both else 1) * count, LANES), (2, count + size_y, LANES), (size_y, LANES)],
        y1, y2, to_x, to_z, leaving,
    )
    got_x = moved_along(to_x, "gx", 1)
    z1, z2 = swapped_z((to_z[0], to_z[1]))
    got_xz = moved_diagonally(to_xz, 1)
    got_mx = got_x if both else moved_along(leaving[1], "gx", -1)
    gas_next, arrivals = call(
        functools.partial(finish_kernel, count), [gas_field.shape, (6, 7, crossing.shape[1], LANES)],
        base, y1, y2, got_x, got_mx, z1, z2, got_xz,
    )
    return gas_next, jnp.transpose(velocity_next, (1, 0, 2)), jnp.transpose(arrivals, (0, 2, 1, 3))


def solution(mesh):
    owner = ("gx", "gz", "gy")
    in_specs = (
        P(None, "gx", "gy", "gz"),
        P(owner, None, None),
        P(owner, None, None),
        P(owner, None),
        P(owner, None),
        P(owner),
        P(owner, None),
    )
    out_specs = (
        P(None, "gx", "gy", "gz"),
        P(owner, None, None),
        P(owner, None, None, None),
    )
    return jax.shard_map(
        per_device, mesh=mesh, in_specs=in_specs, out_specs=out_specs, check_vma=False
    )
```

profile of v0, /device:TPU:0, one launch (start us, length us, event | category | flops | bytes accessed | tf_op | source)
XLA Modules:
  0.0 38.8 jit_solution(4136954263463575759)
XLA Ops:
  0.6 1.2 %shard_map.94 = (f32[3,18,24,128]{3,2,1,0:T(8,128)S(1)}, f32[16,128]{1,0:T(8,128)S(1)}, f32[48,128]{1,0:T(8,128)S(1)}, f32[3,64,128]{2,1,0:T(8,128)S(1)}, f32[3,...) custom-call(f32[3,16,16,128]{3,2,1,0:T(8,128)} %gas_ref.1, ...), custom_call_target="tpu_custom_call" | custom-call | tf_op jit(solution)/shard_map/pallas_call | solution.py:65
  1.9 3.0 %collective-permute-start.1 = (f32[48,128]{1,0:T(8,128)S(1)}, f32[48,128]{1,0:T(8,128)S(1)}, u32[]{:S(2)}, u32[]{:S(2)}) collective-permute-start(f32[48,128]{1,0:T(8,128)S(1)} %get-tuple-element.45), channel_id=1, source_target_pairs={{0,16},{16,0},{1,17},{17,1},{2,18},{18,2},{3,19},{19,3},{4,20},{20... | collective-permute-start | bytes 73736 | tf_op jit(solution)/shard_map/ppermute | solution.py:37
  4.9 0.6 %collective-permute-start.2 = (f32[16,128]{1,0:T(8,128)S(1)}, f32[16,128]{1,0:T(8,128)S(1)}, u32[]{:S(2)}, u32[]{:S(2)}) collective-permute-start(f32[16,128]{1,0:T(8,128)S(1)} %get-tuple-element.44), channel_id=1, source_target_pairs={{0,28},{4,16},{8,20},{12,24},{16,12},{20,0},{24,4},{28,8},{1,29},{... | collective-permute-start | bytes 24584 | tf_op jit(solution)/shard_map/ppermute | solution.py:61
  5.5 1.1 %collective-permute-start = (f32[16,128]{1,0:T(8,128)S(1)}, f32[16,128]{1,0:T(8,128)S(1)}, u32[]{:S(2)}, u32[]{:S(2)}) collective-permute-start(f32[16,128]{1,0:T(8,128)S(1)} %get-tuple-element.44), channel_id=1, source_target_pairs={{0,12},{4,0},{8,4},{12,8},{1,13},{5,1},{9,5},{13,9},{2,14},{6,2},{... | collective-permute-start | bytes 24584 | tf_op jit(solution)/shard_map/ppermute | solution.py:37
  6.6 2.2 %shard_map.95 = (f32[6528,128]{1,0:T(8,128)S(1)}, f32[2448,128]{1,0:T(8,128)S(1)}, f32[16,72,128]{2,1,0:T(8,128)S(1)}, f32[576,128]{1,0:T(8,128)S(1)}, f32[8,128]{1,0:T(8,128)S(1)}, /*index=5*/s32[146]{0:T(256)S(1)}) custom-call(f32[3,18,24,128]{3,2,1,0:T(8,128)S(1)} %get-tuple-element.37.grid_ref.grid_in_ref, ...), custom_call_target="tpu_custom_call" | custom-call | flops 12288000 | bytes 3072000 | tf_op jit(solution)/shard_map/pallas_call | solution.py:65
  8.8 0.0 collective-permute-done.2.edge_ref
  8.9 0.0 collective-permute-done.face_ref
  8.9 0.0 collective-permute-done.1.from_x_ref
  8.9 0.1 shard_map.97
  8.9 0.0 collective-permute-start.4
  9.0 3.1 %collective-permute-start.3 = (f32[56,128]{1,0:T(8,128)S(1)}, f32[56,128]{1,0:T(8,128)S(1)}, u32[]{:S(2)}, u32[]{:S(2)}) collective-permute-start(f32[56,128]{1,0:T(8,128)S(1)} %shard_map.97), channel_id=1, source_target_pairs={{0,1},{1,0},{2,3},{3,2},{4,5},{5,4},{6,7},{7,6},{8,9},{9,8},{10,11... | collective-permute-start | bytes 86024 | tf_op jit(solution)/shard_map/ppermute | solution.py:55
  12.1 0.4 %shard_map.96 = (f32[3,18,24,128]{3,2,1,0:T(8,128)S(1)}, f32[6528,128]{1,0:T(8,128)S(1)}, f32[128,128]{1,0:T(8,128)S(1)}) custom-call(f32[3,18,24,128]{3,2,1,0:T(8,128)S(1)} %get-tuple-element.37.grid_ref.grid_in_ref, f32[6528,128]{1,0:T(8,128)S(1)} %get-tuple-element.43.lines_in_ref, ...), custom_call_target="tpu_custom_call", output_to_operand_aliasing={{0}: (0, {}), {1}: (1, {})} | custom-call | flops 4096000 | bytes 1024000 | tf_op jit(solution)/shard_map/pallas_call | solution.py:65
  12.6 8.0 %shard_map.99 = (f32[576,128]{1,0:T(8,128)S(1)}, f32[2448,128]{1,0:T(8,128)S(1)}) custom-call(s32[146]{0:T(256)S(1)} %get-tuple-element.51.list_ref, s32[64]{0:T(128)S(1)} %get-tuple-element.42.brick_ref, f32[6528,128]{1,0:T(8,128)S(1)} %get-tuple-element.47.lines_in_ref.lines_ref, ...), custom_call_target="tpu_custom_call", output_to_operand_aliasing={{0}: (4, {}), {1}: (5, {})} | custom-call | flops 24576000 | bytes 6144000 | tf_op jit(solution)/shard_map/pallas_call | solution.py:65
  20.6 0.0 collective-permute-done.4.second_ref
  20.6 0.0 collective-permute-done.3.first_ref
  20.6 0.6 %shard_map.98 = (f32[3,18,24,128]{3,2,1,0:T(8,128)S(1)}, f32[6528,128]{1,0:T(8,128)S(1)}) custom-call(f32[3,18,24,128]{3,2,1,0:T(8,128)S(1)} %get-tuple-element.46.grid_in_ref, f32[6528,128]{1,0:T(8,128)S(1)} %get-tuple-element.47.lines_in_ref.lines_ref, ...), custom_call_target="tpu_custom_call", output_to_operand_aliasing={{0}: (0, {}), {1}: (1, {})} | custom-call | flops 4096000 | bytes 1024000 | tf_op jit(solution)/shard_map/pallas_call | solution.py:65
  21.2 2.7 %shard_map.100 = (f32[576,128]{1,0:T(8,128)S(1)}, f32[2448,128]{1,0:T(8,128)S(1)}) custom-call(s32[146]{0:T(256)S(1)} %get-tuple-element.51.list_ref, s32[64]{0:T(128)S(1)} %get-tuple-element.42.brick_ref, f32[6528,128]{1,0:T(8,128)S(1)} %get-tuple-element.52.lines_ref, ...), custom_call_target="tpu_custom_call", output_to_operand_aliasing={{0}: (4, {}), {1}: (5, {})} | custom-call | flops 8192000 | bytes 2048000 | tf_op jit(solution)/shard_map/pallas_call | solution.py:65
  23.9 3.1 %shard_map.102 = (f32[6,64,128]{2,1,0:T(8,128)S(1)}, f32[3,64,128]{2,1,0:T(8,128)}, f32[2,136,128]{2,1,0:T(8,128)S(1)}, f32[48,128]{1,0:T(8,128)S(1)}, f32[16,128]{1,0:T(8,128)S(1)}) custom-call(s32[6,8]{1,0:T(8,128)S(1)} %get-tuple-element.59.crossing_ref, f32[576,128]{1,0:T(8,128)S(1)} %get-tuple-element.60.state_ref, ...), custom_call_target="tpu_custom_call" | custom-call | flops 4096000 | bytes 1024000 | tf_op jit(solution)/shard_map/pallas_call | solution.py:65
  26.9 0.1 collective-permute-start.6
  27.0 1.6 %collective-permute-start.5 = (f32[136,128]{1,0:T(8,128)S(1)}, f32[136,128]{1,0:T(8,128)S(1)}, u32[]{:S(2)}, u32[]{:S(2)}) collective-permute-start(f32[136,128]{1,0:T(8,128)S(1)} %get-tuple-element.72), channel_id=1, source_target_pairs={{0,1},{1,0},{2,3},{3,2},{4,5},{5,4},{6,7},{7,6},{8,9},{9,8},{10,11... | collective-permute-start | bytes 208904 | tf_op jit(solution)/shard_map/ppermute | solution.py:55
  28.7 0.0 collective-permute-done.6.second_ref.y2_ref
  28.7 3.0 %collective-permute-done.5.first_ref.y1_ref = f32[136,128]{1,0:T(8,128)S(1)} collective-permute-done((f32[136,128]{1,0:T(8,128)S(1)}, f32[136,128]{1,0:T(8,128)S(1)}, u32[]{:S(2)}, u32[]{:S(2)}) %collective-permute-start.5) | collective-permute-done | bytes 69664 | tf_op jit(solution)/shard_map/ppermute | solution.py:55
  31.7 1.6 %collective-permute-start.7 = (f32[176,128]{1,0:T(8,128)S(1)}, f32[176,128]{1,0:T(8,128)S(1)}, u32[]{:S(2)}, u32[]{:S(2)}) collective-permute-start(f32[176,128]{1,0:T(8,128)S(1)} %get-tuple-element.65), channel_id=1, source_target_pairs={{0,16},{16,0},{1,17},{17,1},{2,18},{18,2},{3,19},{19,3},{4,20},{20... | collective-permute-start | bytes 270344 | tf_op jit(solution)/shard_map/ppermute | solution.py:37
  33.2 0.0 collective-permute-start.9
  33.3 0.6 %collective-permute-start.8 = (f32[80,128]{1,0:T(8,128)S(1)}, f32[80,128]{1,0:T(8,128)S(1)}, u32[]{:S(2)}, u32[]{:S(2)}) collective-permute-start(f32[80,128]{1,0:T(8,128)S(1)} %get-tuple-element.74), channel_id=1, source_target_pairs={{0,4},{4,0},{8,12},{12,8},{1,5},{5,1},{9,13},{13,9},{2,6},{6,2},{1... | collective-permute-start | bytes 122888 | tf_op jit(solution)/shard_map/ppermute | solution.py:44
  33.9 0.2 collective-permute-start.10
  34.1 0.4 shard_map.101.base_ref
  34.5 3.4 %collective-permute-done.10.edge_ref = f32[16,128]{1,0:T(8,128)S(1)} collective-permute-done((f32[16,128]{1,0:T(8,128)S(1)}, f32[16,128]{1,0:T(8,128)S(1)}, u32[]{:S(2)}, u32[]{:S(2)}) %collective-permute-start.10) | collective-permute-done | bytes 8224 | tf_op jit(solution)/shard_map/ppermute | solution.py:61
  37.9 0.0 collective-permute-done.9.z2_ref
  37.9 0.0 collective-permute-done.8.z1_ref
  37.9 0.0 collective-permute-done.7.x_ref.minus_x_ref
  37.9 1.0 %shard_map.104 = (f32[3,16,16,128]{3,2,1,0:T(8,128)}, f32[6,7,8,128]{3,2,1,0:T(8,128)}) custom-call(f32[3,16,16,128]{3,2,1,0:T(8,128)S(1)} %shard_map.101.base_ref, f32[136,128]{1,0:T(8,128)S(1)} %collective-permute-done.5.first_ref.y1_ref, f32[136,128]{1,0:T(8,128)S(1)} %collective-permute-done.6.second_ref.y2_ref, ...), custom_call_target="tpu_custom_call" | custom-call | tf_op jit(solution)/shard_map/pallas_call | solution.py:65
  (3 shorter events, 0.0 us)
Async XLA Ops:
  1.9 7.0 %collective-permute-start.1 = (f32[48,128]{1,0:T(8,128)S(1)}, f32[48,128]{1,0:T(8,128)S(1)}, u32[]{:S(2)}, u32[]{:S(2)}) collective-permute-start(f32[48,128]{1,0:T(8,128)S(1)} %get-tuple-element.45), channel_id=1, source_target_pairs={{0,16},{16,0},{1,17},{17,1},{2,18},{18,2},{3,19},{19,3},{4,20},{20... | collective-permute-start | bytes 73736 | tf_op jit(solution)/shard_map/ppermute | solution.py:37
  4.9 3.9 %collective-permute-start.2 = (f32[16,128]{1,0:T(8,128)S(1)}, f32[16,128]{1,0:T(8,128)S(1)}, u32[]{:S(2)}, u32[]{:S(2)}) collective-permute-start(f32[16,128]{1,0:T(8,128)S(1)} %get-tuple-element.44), channel_id=1, source_target_pairs={{0,28},{4,16},{8,20},{12,24},{16,12},{20,0},{24,4},{28,8},{1,29},{... | collective-permute-start | bytes 24584 | tf_op jit(solution)/shard_map/ppermute | solution.py:61
  5.5 3.3 %collective-permute-start = (f32[16,128]{1,0:T(8,128)S(1)}, f32[16,128]{1,0:T(8,128)S(1)}, u32[]{:S(2)}, u32[]{:S(2)}) collective-permute-start(f32[16,128]{1,0:T(8,128)S(1)} %get-tuple-element.44), channel_id=1, source_target_pairs={{0,12},{4,0},{8,4},{12,8},{1,13},{5,1},{9,5},{13,9},{2,14},{6,2},{... | collective-permute-start | bytes 24584 | tf_op jit(solution)/shard_map/ppermute | solution.py:37
  8.9 11.6 %collective-permute-start.4 = (f32[56,128]{1,0:T(8,128)S(1)}, f32[56,128]{1,0:T(8,128)S(1)}, u32[]{:S(2)}, u32[]{:S(2)}) collective-permute-start(f32[56,128]{1,0:T(8,128)S(1)} %shard_map.97), channel_id=1, source_target_pairs={{0,4},{3,7},{1,2},{2,1},{4,0},{7,3},{5,6},{6,5},{8,12},{11,15},{9,... | collective-permute-start | bytes 86024 | tf_op jit(solution)/shard_map/ppermute | solution.py:55
  9.0 11.6 %collective-permute-start.3 = (f32[56,128]{1,0:T(8,128)S(1)}, f32[56,128]{1,0:T(8,128)S(1)}, u32[]{:S(2)}, u32[]{:S(2)}) collective-permute-start(f32[56,128]{1,0:T(8,128)S(1)} %shard_map.97), channel_id=1, source_target_pairs={{0,1},{1,0},{2,3},{3,2},{4,5},{5,4},{6,7},{7,6},{8,9},{9,8},{10,11... | collective-permute-start | bytes 86024 | tf_op jit(solution)/shard_map/ppermute | solution.py:55
  26.9 1.7 %collective-permute-start.6 = (f32[136,128]{1,0:T(8,128)S(1)}, f32[136,128]{1,0:T(8,128)S(1)}, u32[]{:S(2)}, u32[]{:S(2)}) collective-permute-start(f32[136,128]{1,0:T(8,128)S(1)} %get-tuple-element.71), channel_id=1, source_target_pairs={{0,4},{3,7},{1,2},{2,1},{4,0},{7,3},{5,6},{6,5},{8,12},{11,15},{9,... | collective-permute-start | bytes 208904 | tf_op jit(solution)/shard_map/ppermute | solution.py:55
  27.0 4.6 %collective-permute-start.5 = (f32[136,128]{1,0:T(8,128)S(1)}, f32[136,128]{1,0:T(8,128)S(1)}, u32[]{:S(2)}, u32[]{:S(2)}) collective-permute-start(f32[136,128]{1,0:T(8,128)S(1)} %get-tuple-element.72), channel_id=1, source_target_pairs={{0,1},{1,0},{2,3},{3,2},{4,5},{5,4},{6,7},{7,6},{8,9},{9,8},{10,11... | collective-permute-start | bytes 208904 | tf_op jit(solution)/shard_map/ppermute | solution.py:55
  31.7 6.2 %collective-permute-start.7 = (f32[176,128]{1,0:T(8,128)S(1)}, f32[176,128]{1,0:T(8,128)S(1)}, u32[]{:S(2)}, u32[]{:S(2)}) collective-permute-start(f32[176,128]{1,0:T(8,128)S(1)} %get-tuple-element.65), channel_id=1, source_target_pairs={{0,16},{16,0},{1,17},{17,1},{2,18},{18,2},{3,19},{19,3},{4,20},{20... | collective-permute-start | bytes 270344 | tf_op jit(solution)/shard_map/ppermute | solution.py:37
  33.2 4.6 %collective-permute-start.9 = (f32[80,128]{1,0:T(8,128)S(1)}, f32[80,128]{1,0:T(8,128)S(1)}, u32[]{:S(2)}, u32[]{:S(2)}) collective-permute-start(f32[80,128]{1,0:T(8,128)S(1)} %get-tuple-element.73), channel_id=1, source_target_pairs={{0,12},{4,8},{8,4},{12,0},{1,13},{5,9},{9,5},{13,1},{2,14},{6,10},... | collective-permute-start | bytes 122888 | tf_op jit(solution)/shard_map/ppermute | solution.py:44
  33.3 4.6 %collective-permute-start.8 = (f32[80,128]{1,0:T(8,128)S(1)}, f32[80,128]{1,0:T(8,128)S(1)}, u32[]{:S(2)}, u32[]{:S(2)}) collective-permute-start(f32[80,128]{1,0:T(8,128)S(1)} %get-tuple-element.74), channel_id=1, source_target_pairs={{0,4},{4,0},{8,12},{12,8},{1,5},{5,1},{9,13},{13,9},{2,6},{6,2},{1... | collective-permute-start | bytes 122888 | tf_op jit(solution)/shard_map/ppermute | solution.py:44
  33.9 4.0 %collective-permute-start.10 = (f32[16,128]{1,0:T(8,128)S(1)}, f32[16,128]{1,0:T(8,128)S(1)}, u32[]{:S(2)}, u32[]{:S(2)}) collective-permute-start(f32[16,128]{1,0:T(8,128)S(1)} %get-tuple-element.67), channel_id=1, source_target_pairs={{0,20},{4,24},{8,28},{12,16},{16,4},{20,8},{24,12},{28,0},{1,21},{... | collective-permute-start | bytes 24584 | tf_op jit(solution)/shard_map/ppermute | solution.py:61
where the time goes:
time: 39 us; the launch traced here: 38.8 us
  Pallas kernels  19.6 us (50%)
  starting transfers between devices  12.1 us (31%)
  waiting for transfers between devices  6.35 us (16%)
  between operations  0.77 us (2%)
    pallas_call x11, Pallas kernels, call(): pl.pallas_call(body, out_shape=[o if isinstance(o, jax.ShapeDtypeStruct)...  19.6 us
    ppermute x3, starting transfers between devices, moved_along(): lax.ppermute(block, axis, [(i, (i + distance) % count) for i in range(cou...  5.74 us
    ppermute x2, starting transfers between devices, swapped_y(): lax.ppermute(blocks[0], 'gy', first)  4.78 us
    ppermute x2, waiting for transfers between devices, moved_diagonally(): return lax.ppermute(block, ('gx', 'gz'), route)  3.38 us
    ppermute x2, waiting for transfers between devices, swapped_y(): lax.ppermute(blocks[0], 'gy', first)  2.95 us
    ppermute x2, starting transfers between devices, moved_diagonally(): return lax.ppermute(block, ('gx', 'gz'), route)  0.81 us
  transfers between devices with their start and end apart: 11, of which 2 were waited for; matrix products, arithmetic and copies ran while one was open for 0% of the time, Pallas kernels for 28%

commit v1 on v0

--- a/solution.py
+++ b/solution.py
@@ -23,7 +23,7 @@
 REACH_Z = 2 * BZ
 UNROLL = 8
 
-WEIGHT, ALONG_Y, IN_Y, ALONG_Z, IN_Z, RATE, MOVING, OFFSET = 0, 5, 6, 7, 8, 9, 10, 13
+WEIGHT, ALONG_Y, IN_Y, ALONG_Z, IN_Z, RESPONSE, MOVING, OFFSET = 0, 5, 6, 7, 8, 9, 10, 13
 TABLE_ROWS = 16
 STATE = 8
 
@@ -157,13 +157,12 @@
 
 def prepare_kernel(
     grid_ref, velocity_ref, fraction_ref, response_ref, cell_ref, brick_ref,
-    lines_ref, deposit_ref, table_ref, state_ref, ready_ref, list_ref,
+    lines_ref, deposit_ref, table_ref, ready_ref, list_ref,
 ):
     comps, size_x, size_y, size_z = grid_ref.shape[0], grid_ref.shape[1] - 2, grid_ref.shape[2] - 8, grid_ref.shape[3]
     nblocks = velocity_ref.shape[1]
     count_x, count_y, count_z = size_x // BX, size_y // BY, size_z // BZ
     rows_z = size_z + 8
-    spare = table_ref.shape[1] - nblocks
 
     room = nblocks + UNROLL
 
@@ -195,8 +194,7 @@
     along_x = fraction_ref[0]
 
     def put(row, value):
-        table_ref[row, 0:nblocks] = value
-        table_ref[row, nblocks : nblocks + spare] = jnp.zeros((spare, LANES), jnp.float32)
+        table_ref[pl.ds(row, nblocks, stride=TABLE_ROWS)] = value
 
     for a in range(REACH_X):
         put(WEIGHT + a, jnp.where(cell_x == a, 1.0 - along_x, 0.0) + jnp.where(cell_x == a - 1, along_x, 0.0))
@@ -204,12 +202,13 @@
     put(IN_Y, cell_y.astype(jnp.float32))
     put(ALONG_Z, fraction_ref[2])
     put(IN_Z, cell_z.astype(jnp.float32))
-    put(RATE, 1.0 / response_ref[...])
+    put(RESPONSE, response_ref[...])
     for c in range(comps):
         put(MOVING + c, velocity_ref[c])
         put(OFFSET + c, fraction_ref[c])
-    state_ref[...] = jnp.zeros_like(state_ref)
-    state_ref[pl.ds(2 * comps, nblocks, stride=STATE)] = response_ref[...]
+    spare = table_ref.shape[0] - nblocks * TABLE_ROWS
+    row = row_ids(spare)
+    table_ref[nblocks * TABLE_ROWS :] = jnp.where(row % TABLE_ROWS == RESPONSE, 1.0, 0.0)
 
 
 def y_lines_kernel(grid_ref, face_ref, from_x_ref, edge_ref, ready_ref, out_ref):
@@ -261,11 +260,13 @@
 
 
 def blocks_kernel(
-    late, comps, size_x, count_y, count_z, rows_z,
-    list_ref, brick_ref, lines_ref, table_ref, state_in_ref, deposit_in_ref, state_ref, deposit_ref,
+    late, comps, count_x, count_y, count_z, rows_z,
+    list_ref, brick_ref, lines_ref, table_ref, *refs,
 ):
+    state_ref, deposit_ref = refs[-2:]
     nblocks = brick_ref.shape[0]
     room = (list_ref.shape[0] - 2) // 2
+    sub = row_ids(8)
     row_y = row_ids(REACH_Y).astype(jnp.float32)
     row_z = row_ids(REACH_Z).astype(jnp.float32)
     lane = lane_ids(REACH_Y)
@@ -275,15 +276,17 @@
 
     def loaded(at):
         k = list_ref[at]
-        brick = brick_ref[jnp.minimum(k, nblocks - 1)]
+        brick = jnp.where(k < nblocks, brick_ref[jnp.minimum(k, nblocks - 1)], 0)
         brick_x = lax.div(brick, count_y * count_z)
         brick_y = lax.rem(lax.div(brick, count_z), count_y)
         brick_z = lax.rem(brick, count_z)
         sel = jnp.where(brick_z == count_z - 1, 1, 0)
-        start = (sel * comps * (size_x + 1) + brick_x * BX) * ROWS_Y + brick_y * BY
-        first = pl.multiple_of((brick_x * count_y + brick_y) * comps * rows_z + brick_z * BZ, 8)
+        pair = brick_x * count_y + brick_y
+        start = pl.multiple_of((sel * count_x * count_y + pair) * comps * SPREAD, 8)
+        first = pl.multiple_of(pair * comps * rows_z + brick_z * BZ, 8)
         window = jnp.concatenate([lines_ref[pl.ds(first + c * rows_z, REACH_Z)] for c in range(comps)], axis=0)
-        rows = [table_ref[i, pl.ds(k, 1)] for i in range(OFFSET + comps)]
+        table = table_ref[pl.ds(pl.multiple_of(k * TABLE_ROWS, TABLE_ROWS), TABLE_ROWS)]
+        rows = [table[i : i + 1] for i in range(TABLE_ROWS)]
         return k, start, brick_z * BZ, window, rows
 
     def moved_of(window, rows):
@@ -295,10 +298,11 @@
         seen = lax.dot_general(
             window.astype(jnp.bfloat16), table, (((1,), (0,)), ((), ())), preferred_element_type=jnp.float32
         )
+        rate = 1.0 / rows[RESPONSE]
         state, moved, pushed = [], [], []
         for c in range(comps):
             gas_sample = jnp.sum(seen[c * REACH_Z : (c + 1) * REACH_Z] * weight_z, axis=0, keepdims=True)
-            drag = (gas_sample - rows[MOVING + c]) * rows[RATE]
+            drag = (gas_sample - rows[MOVING + c]) * rate
             state.append(rows[MOVING + c] + TIME_STEP * drag)
             moved.append(rows[OFFSET + c] + TIME_STEP * state[c])
             pushed.append(drag * weight_z)
@@ -307,7 +311,10 @@
         push = jnp.concatenate([push_main, push_rest, push_main], axis=1).astype(jnp.bfloat16)
         spread = jnp.concatenate([main, main, rest], axis=1).astype(jnp.bfloat16)
         shares = lax.dot_general(spread, push, (((1,), (1,)), ((), ())), preferred_element_type=jnp.float32)
-        return state + moved, shares
+        tile = jnp.broadcast_to(rows[RESPONSE], (STATE, LANES))
+        for i, value in enumerate(state + moved):
+            tile = jnp.where(sub == i, value, tile)
+        return tile, shares
 
     count = list_ref[2 * room + late]
 
@@ -325,16 +332,45 @@
                 for a in range(REACH_X):
                     part = pltpu.roll(shares[a * REACH_Y : (a + 1) * REACH_Y], shift, 1)
                     parts[-1].append(jnp.where(within, part, 0.0))
-        for (k, _, _, _, _), (state, _) in zip(taken, results):
-            for i, value in enumerate(state):
-                state_ref[pl.ds(STATE * k + i, 1)] = value
+        for (k, _, _, _, _), (tile, _) in zip(taken, results):
+            state_ref[pl.ds(pl.multiple_of(STATE * k, STATE), STATE)] = tile
         for (_, start, _, _, _), mine in zip(taken, parts):
-            spots = [
-                pl.ds(start + (c * (size_x + 1) + a) * ROWS_Y, REACH_Y) for c in range(comps) for a in range(REACH_X)
-            ]
+            spots = [pl.ds(start + i * REACH_Y, REACH_Y) for i in range(comps * REACH_X)]
             sums = [deposit_ref[spot] + part for spot, part in zip(spots, mine)]
             for spot, total in zip(spots, sums):
                 deposit_ref[spot] = total
+
+
+def merge_kernel(tiles_ref, plane_ref):
+    _, comps, planes, _, _ = plane_ref.shape
+    count_x, count_y = (planes - 1) // BX, tiles_ref.shape[0] // (2 * ((planes - 1) // BX) * comps * SPREAD)
+    top = row_ids(REACH_Y) >= BY
+
+    for sel in (0, 1):
+        for c in range(comps):
+            for x in range(planes):
+                bricks = [(x // BX, x % BX)] if x < planes - 1 else []
+                if x and x % BX == 0:
+                    bricks.append((x // BX - 1, BX))
+
+                def tile(q):
+                    total = None
+                    for p, a in bricks:
+                        at = (((sel * count_x + p) * count_y + q) * comps + c) * SPREAD + a * REACH_Y
+                        value = tiles_ref[at : at + REACH_Y]
+                        total = value if total is None else total + value
+                    return total
+
+                carried = None
+                for q in range(0, count_y, 2):
+                    here = tile(q)
+                    if carried is not None:
+                        here = here + carried
+                    between = pltpu.roll(tile(q + 1), BY, 0)
+                    here = here + jnp.where(top, between, 0.0)
+                    carried = jnp.where(top, 0.0, between)
+                    plane_ref[sel, c, x, q * BY : q * BY + REACH_Y] = here
+                plane_ref[sel, c, x, count_y * BY :] = carried
 
 
 def send_kernel(push, diffuse, crossing_ref, state_ref, grid_ref, deposit_ref, leaving_ref, velocity_ref, y_ref, x_ref, z_ref):
@@ -350,7 +386,8 @@
         for slot in range(slots):
             block = crossing_ref[face, slot]
             spot = pl.ds(pl.multiple_of(jnp.maximum(block, 0) * STATE, STATE), STATE)
-            tiles.append(jnp.where(block >= 0, state_ref[spot], 0.0))
+            live = jnp.full((STATE, LANES), block, jnp.int32) >= 0
+            tiles.append(jnp.where(live, state_ref[spot], 0.0))
         leaving_ref[face] = jnp.concatenate(tiles, axis=0)
     y_ref[0, 0:rows] = jnp.where(first, leaving_ref[2], leaving_ref[3])
     y_ref[1, 0:rows] = jnp.where(first, leaving_ref[3], leaving_ref[2])
@@ -471,7 +508,7 @@
     rows_z = size_z + 8
     grid_shape = (comps, size_x + 2, ROWS_Y, LANES)
     lines_shape = ((size_x // BX) * (size_y // BY) * comps * rows_z, LANES)
-    deposit_shape = (2 * comps * (size_x + 1) * ROWS_Y, LANES)
+    deposit_shape = (2 * (size_x // BX) * (size_y // BY) * comps * SPREAD, LANES)
 
     inputs = (gas_field, velocity, fraction, response, cell_index, brick_index, crossing)
     inputs = [pltpu.with_memory_space_constraint(array, pltpu.HBM) for array in inputs]
@@ -484,18 +521,17 @@
     from_z = moved_along(face, "gz", -1)
     from_x = moved_along(plane, "gx", -1)
     from_xz = moved_diagonally(face, -1)
-    lines, deposit, table, state, ready, blocks = call(
+    lines, deposit, table, ready, blocks = call(
         prepare_kernel,
         [
             lines_shape,
             deposit_shape,
-            (TABLE_ROWS, spare, LANES),
-            (STATE * spare, LANES),
+            (TABLE_ROWS * spare, LANES),
             (8, LANES),
             jax.ShapeDtypeStruct((2 * (nblocks + UNROLL) + 2,), jnp.int32),
         ],
         grid, velocity, fraction, response, cell_index, brick_index,
-        smem=(5,), smem_outs=(5,), cycles=3000,
+        smem=(5,), smem_outs=(4,), cycles=3000,
     )
     line_rows = -(-(comps * size_x + comps + 1) // 8) * 8
     (y_lines,) = call(y_lines_kernel, [(line_rows, LANES)], grid, from_z, from_x, from_xz, ready)
@@ -506,21 +542,21 @@
         aliases={0: 0, 1: 1}, scratch=(square,), cycles=1000,
     )
 
-    def advance(late, lines, state, deposit):
+    def advance(late, lines, deposit, *state):
         return call(
-            functools.partial(blocks_kernel, late, comps, size_x, size_y // BY, size_z // BZ, rows_z),
-            [(STATE * spare, LANES), deposit_shape], blocks, brick_index, lines, table, state, deposit,
-            smem=(0, 1), aliases={4: 0, 5: 1}, cycles=6000 - 4000 * late,
+            functools.partial(blocks_kernel, late, comps, size_x // BX, size_y // BY, size_z // BZ, rows_z),
+            [(STATE * spare, LANES), deposit_shape], blocks, brick_index, lines, table, deposit, *state,
+            smem=(0, 1), aliases={4: 1, 5: 0} if state else {4: 1}, cycles=6000 - 4000 * late,
         )
 
-    state, deposit = advance(0, lines, state, deposit)
+    state, deposit = advance(0, lines, deposit)
     grid, lines = call(
         functools.partial(halo_y_kernel, size_y), [grid_shape, lines_shape], grid, lines, top, y1, y2,
         aliases={0: 0, 1: 1}, scratch=(square,), cycles=1000,
     )
-    state, deposit = advance(1, lines, state, deposit)
-
-    deposit = deposit.reshape(2, comps, size_x + 1, ROWS_Y, LANES)
+    state, deposit = advance(1, lines, deposit, state)
+
+    (deposit,) = call(merge_kernel, [(2, comps, size_x + 1, ROWS_Y, LANES)], deposit, cycles=500)
     count = STATE * crossing.shape[1]
     leaving, velocity_next, to_y, to_x, to_z = call(
         functools.partial(send_kernel, push, diffuse),

time: 39 us -> 39.1 us (level)
    ppermute x1, starting transfers between devices: 0.64 us -> 1.31 us  [swapped_z(): lax.ppermute(blocks[0], 'gz', first)]
    ppermute x3, starting transfers between devices: 5.74 us -> 5.07 us  [moved_along(): lax.ppermute(block, axis, [(i, (i + distance) % count) for i in range(cou...]
    pallas_call x11 -> x12, Pallas kernels: 19.6 us -> 19.7 us  [call(): pl.pallas_call(body, out_shape=[o if isinstance(o, jax.ShapeDtypeStruct)...]
  transfers between devices with their start and end apart: 11 -> 11, of which waited for: 2 -> 2; matrix products, arithmetic and copies ran while one was open for 0% -> 0% of each run, Pallas kernels for 28% -> 25%
where the time goes in v1:
time: 39.1 us; the launch traced here: 38.9 us
  Pallas kernels  19.7 us (50%)
  starting transfers between devices  12.2 us (31%)
  waiting for transfers between devices  6.18 us (16%)
  between operations  0.78 us (2%)
    pallas_call x12, Pallas kernels, call(): pl.pallas_call(body, out_shape=[o if isinstance(o, jax.ShapeDtypeStruct)...  19.7 us
    ppermute x3, starting transfers between devices, moved_along(): lax.ppermute(block, axis, [(i, (i + distance) % count) for i in range(cou...  5.07 us
    ppermute x2, starting transfers between devices, swapped_y(): lax.ppermute(blocks[0], 'gy', first)  4.78 us
    ppermute x2, waiting for transfers between devices, moved_diagonally(): return lax.ppermute(block, ('gx', 'gz'), route)  3.2 us
    ppermute x2, waiting for transfers between devices, swapped_y(): lax.ppermute(blocks[0], 'gy', first)  2.96 us
    ppermute x1, starting transfers between devices, swapped_z(): lax.ppermute(blocks[0], 'gz', first)  1.31 us
    ppermute x2, starting transfers between devices, moved_diagonally(): return lax.ppermute(block, ('gx', 'gz'), route)  0.97 us
  transfers between devices with their start and end apart: 11, of which 2 were waited for; matrix products, arithmetic and copies ran while one was open for 0% of the time, Pallas kernels for 25%

profile of v1, /device:TPU:0, one launch (start us, length us, event | category | flops | bytes accessed | tf_op | source)
XLA Modules:
  0.0 38.9 jit_solution(14533034214003444496)
XLA Ops:
  0.6 1.2 %shard_map.94 = (f32[3,18,24,128]{3,2,1,0:T(8,128)S(1)}, f32[16,128]{1,0:T(8,128)S(1)}, f32[48,128]{1,0:T(8,128)S(1)}, f32[3,64,128]{2,1,0:T(8,128)S(1)}, f32[3,...) custom-call(f32[3,16,16,128]{3,2,1,0:T(8,128)} %gas_ref.1, ...), custom_call_target="tpu_custom_call" | custom-call | tf_op jit(solution)/shard_map/pallas_call | solution.py:65
  1.9 3.0 %collective-permute-start.1 = (f32[48,128]{1,0:T(8,128)S(1)}, f32[48,128]{1,0:T(8,128)S(1)}, u32[]{:S(2)}, u32[]{:S(2)}) collective-permute-start(f32[48,128]{1,0:T(8,128)S(1)} %get-tuple-element.44), channel_id=1, source_target_pairs={{0,16},{16,0},{1,17},{17,1},{2,18},{18,2},{3,19},{19,3},{4,20},{20... | collective-permute-start | bytes 73736 | tf_op jit(solution)/shard_map/ppermute | solution.py:37
  4.9 0.6 %collective-permute-start.2 = (f32[16,128]{1,0:T(8,128)S(1)}, f32[16,128]{1,0:T(8,128)S(1)}, u32[]{:S(2)}, u32[]{:S(2)}) collective-permute-start(f32[16,128]{1,0:T(8,128)S(1)} %get-tuple-element.43), channel_id=1, source_target_pairs={{0,28},{4,16},{8,20},{12,24},{16,12},{20,0},{24,4},{28,8},{1,29},{... | collective-permute-start | bytes 24584 | tf_op jit(solution)/shard_map/ppermute | solution.py:61
  5.5 1.1 %collective-permute-start = (f32[16,128]{1,0:T(8,128)S(1)}, f32[16,128]{1,0:T(8,128)S(1)}, u32[]{:S(2)}, u32[]{:S(2)}) collective-permute-start(f32[16,128]{1,0:T(8,128)S(1)} %get-tuple-element.43), channel_id=1, source_target_pairs={{0,12},{4,0},{8,4},{12,8},{1,13},{5,1},{9,5},{13,9},{2,14},{6,2},{... | collective-permute-start | bytes 24584 | tf_op jit(solution)/shard_map/ppermute | solution.py:37
  6.6 2.0 %shard_map.95 = (f32[6528,128]{1,0:T(8,128)S(1)}, f32[3840,128]{1,0:T(8,128)S(1)}, f32[1152,128]{1,0:T(8,128)S(1)}, f32[8,128]{1,0:T(8,128)S(1)}, s32[146]{0:T(256)S(1)}) custom-call(f32[3,18,24,128]{3,2,1,0:T(8,128)S(1)} %get-tuple-element.36.grid_ref.grid_in_ref, f32[3,64,128]{2,1,0:T(8,128)S(1)} %get-tuple-element.37.velocity_ref, ...), custom_call_target="tpu_custom_call" | custom-call | flops 12288000 | bytes 3072000 | tf_op jit(solution)/shard_map/pallas_call | solution.py:65
  8.7 0.0 collective-permute-done.2.edge_ref
  8.7 0.0 collective-permute-done.face_ref
  8.7 0.0 collective-permute-done.1.from_x_ref
  8.7 0.1 shard_map.97
  8.8 0.0 collective-permute-start.4
  8.8 3.1 %collective-permute-start.3 = (f32[56,128]{1,0:T(8,128)S(1)}, f32[56,128]{1,0:T(8,128)S(1)}, u32[]{:S(2)}, u32[]{:S(2)}) collective-permute-start(f32[56,128]{1,0:T(8,128)S(1)} %shard_map.97), channel_id=1, source_target_pairs={{0,1},{1,0},{2,3},{3,2},{4,5},{5,4},{6,7},{7,6},{8,9},{9,8},{10,11... | collective-permute-start | bytes 86024 | tf_op jit(solution)/shard_map/ppermute | solution.py:55
  11.9 0.4 %shard_map.96 = (f32[3,18,24,128]{3,2,1,0:T(8,128)S(1)}, f32[6528,128]{1,0:T(8,128)S(1)}, f32[128,128]{1,0:T(8,128)S(1)}) custom-call(f32[3,18,24,128]{3,2,1,0:T(8,128)S(1)} %get-tuple-element.36.grid_ref.grid_in_ref, f32[6528,128]{1,0:T(8,128)S(1)} %get-tuple-element.42.lines_in_ref, ...), custom_call_target="tpu_custom_call", output_to_operand_aliasing={{0}: (0, {}), {1}: (1, {})} | custom-call | flops 4096000 | bytes 1024000 | tf_op jit(solution)/shard_map/pallas_call | solution.py:65
  12.4 7.0 %shard_map.99 = (f32[576,128]{1,0:T(8,128)S(1)}, f32[3840,128]{1,0:T(8,128)S(1)}) custom-call(s32[146]{0:T(256)S(1)} %get-tuple-element.50.list_ref, s32[64]{0:T(128)S(1)} %get-tuple-element.41.brick_ref, f32[6528,128]{1,0:T(8,128)S(1)} %get-tuple-element.46.lines_in_ref.lines_ref, ...), custom_call_target="tpu_custom_call", output_to_operand_aliasing={{1}: (4, {})} | custom-call | flops 24576000 | bytes 6144000 | tf_op jit(solution)/shard_map/pallas_call | solution.py:65
  19.4 0.0 collective-permute-done.4.second_ref
  19.4 0.0 collective-permute-done.3.first_ref
  19.4 0.6 %shard_map.98 = (f32[3,18,24,128]{3,2,1,0:T(8,128)S(1)}, f32[6528,128]{1,0:T(8,128)S(1)}) custom-call(f32[3,18,24,128]{3,2,1,0:T(8,128)S(1)} %get-tuple-element.45.grid_in_ref, f32[6528,128]{1,0:T(8,128)S(1)} %get-tuple-element.46.lines_in_ref.lines_ref, ...), custom_call_target="tpu_custom_call", output_to_operand_aliasing={{0}: (0, {}), {1}: (1, {})} | custom-call | flops 4096000 | bytes 1024000 | tf_op jit(solution)/shard_map/pallas_call | solution.py:65
  20.0 3.8 %shard_map.100 = (f32[576,128]{1,0:T(8,128)S(1)}, f32[3840,128]{1,0:T(8,128)S(1)}) custom-call(s32[146]{0:T(256)S(1)} %get-tuple-element.50.list_ref, s32[64]{0:T(128)S(1)} %get-tuple-element.41.brick_ref, f32[6528,128]{1,0:T(8,128)S(1)} %get-tuple-element.51.lines_ref, ...), custom_call_target="tpu_custom_call", output_to_operand_aliasing={{1}: (4, {}), {0}: (5, {})} | custom-call | flops 8192000 | bytes 2048000 | tf_op jit(solution)/shard_map/pallas_call | solution.py:65
  23.8 0.1 shard_map.101.deposit_ref
  23.9 3.1 %shard_map.103 = (f32[6,64,128]{2,1,0:T(8,128)S(1)}, f32[3,64,128]{2,1,0:T(8,128)}, f32[2,136,128]{2,1,0:T(8,128)S(1)}, f32[48,128]{1,0:T(8,128)S(1)}, f32[16,128]{1,0:T(8,128)S(1)}) custom-call(s32[6,8]{1,0:T(8,128)S(1)} %get-tuple-element.57.crossing_ref, f32[576,128]{1,0:T(8,128)S(1)} %get-tuple-element.58.state_ref, ...), custom_call_target="tpu_custom_call" | custom-call | flops 4096000 | bytes 1024000 | tf_op jit(solution)/shard_map/pallas_call | solution.py:65
  27.0 0.1 collective-permute-start.6
  27.1 1.6 %collective-permute-start.5 = (f32[136,128]{1,0:T(8,128)S(1)}, f32[136,128]{1,0:T(8,128)S(1)}, u32[]{:S(2)}, u32[]{:S(2)}) collective-permute-start(f32[136,128]{1,0:T(8,128)S(1)} %get-tuple-element.70), channel_id=1, source_target_pairs={{0,1},{1,0},{2,3},{3,2},{4,5},{5,4},{6,7},{7,6},{8,9},{9,8},{10,11... | collective-permute-start | bytes 208904 | tf_op jit(solution)/shard_map/ppermute | solution.py:55
  28.7 0.0 collective-permute-done.6.second_ref.y2_ref
  28.7 3.0 %collective-permute-done.5.first_ref.y1_ref = f32[136,128]{1,0:T(8,128)S(1)} collective-permute-done((f32[136,128]{1,0:T(8,128)S(1)}, f32[136,128]{1,0:T(8,128)S(1)}, u32[]{:S(2)}, u32[]{:S(2)}) %collective-permute-start.5) | collective-permute-done | bytes 69664 | tf_op jit(solution)/shard_map/ppermute | solution.py:55
  31.7 0.9 %collective-permute-start.7 = (f32[176,128]{1,0:T(8,128)S(1)}, f32[176,128]{1,0:T(8,128)S(1)}, u32[]{:S(2)}, u32[]{:S(2)}) collective-permute-start(f32[176,128]{1,0:T(8,128)S(1)} %get-tuple-element.63), channel_id=1, source_target_pairs={{0,16},{16,0},{1,17},{17,1},{2,18},{18,2},{3,19},{19,3},{4,20},{20... | collective-permute-start | bytes 270344 | tf_op jit(solution)/shard_map/ppermute | solution.py:37
  32.6 0.0 collective-permute-start.9
  32.6 1.3 %collective-permute-start.8 = (f32[80,128]{1,0:T(8,128)S(1)}, f32[80,128]{1,0:T(8,128)S(1)}, u32[]{:S(2)}, u32[]{:S(2)}) collective-permute-start(f32[80,128]{1,0:T(8,128)S(1)} %get-tuple-element.72), channel_id=1, source_target_pairs={{0,4},{4,0},{8,12},{12,8},{1,5},{5,1},{9,13},{13,9},{2,6},{6,2},{1... | collective-permute-start | bytes 122888 | tf_op jit(solution)/shard_map/ppermute | solution.py:44
  33.9 0.4 collective-permute-start.10
  34.3 0.4 %shard_map.102.base_ref = f32[3,16,16,128]{3,2,1,0:T(8,128)S(1)} custom-call(f32[3,18,24,128]{3,2,1,0:T(8,128)S(1)} %get-tuple-element.49.grid_ref, f32[2,3,17,24,128]{4,3,2,1,0:T(8,128)S(1)} %shard_map.101.deposit_ref, f32[128,128]{1,0:T(8,128)S(1)} %get-tuple-element.47.top_in_ref.top_ref), custom_call_target="tpu_custom_call" | custom-call | flops 4096000 | bytes 1024000 | tf_op jit(solution)/shard_map/pallas_call | solution.py:65
  34.7 3.2 %collective-permute-done.10.edge_ref = f32[16,128]{1,0:T(8,128)S(1)} collective-permute-done((f32[16,128]{1,0:T(8,128)S(1)}, f32[16,128]{1,0:T(8,128)S(1)}, u32[]{:S(2)}, u32[]{:S(2)}) %collective-permute-start.10) | collective-permute-done | bytes 8224 | tf_op jit(solution)/shard_map/ppermute | solution.py:61
  37.9 0.0 collective-permute-done.9.z2_ref
  37.9 0.0 collective-permute-done.8.z1_ref
  37.9 0.0 collective-permute-done.7.x_ref.minus_x_ref
  37.9 1.0 %shard_map.105 = (f32[3,16,16,128]{3,2,1,0:T(8,128)}, f32[6,7,8,128]{3,2,1,0:T(8,128)}) custom-call(f32[3,16,16,128]{3,2,1,0:T(8,128)S(1)} %shard_map.102.base_ref, f32[136,128]{1,0:T(8,128)S(1)} %collective-permute-done.5.first_ref.y1_ref, f32[136,128]{1,0:T(8,128)S(1)} %collective-permute-done.6.second_ref.y2_ref, ...), custom_call_target="tpu_custom_call" | custom-call | tf_op jit(solution)/shard_map/pallas_call | solution.py:65
  (3 shorter events, 0.0 us)
Async XLA Ops:
  1.9 6.8 %collective-permute-start.1 = (f32[48,128]{1,0:T(8,128)S(1)}, f32[48,128]{1,0:T(8,128)S(1)}, u32[]{:S(2)}, u32[]{:S(2)}) collective-permute-start(f32[48,128]{1,0:T(8,128)S(1)} %get-tuple-element.44), channel_id=1, source_target_pairs={{0,16},{16,0},{1,17},{17,1},{2,18},{18,2},{3,19},{19,3},{4,20},{20... | collective-permute-start | bytes 73736 | tf_op jit(solution)/shard_map/ppermute | solution.py:37
  4.9 3.7 %collective-permute-start.2 = (f32[16,128]{1,0:T(8,128)S(1)}, f32[16,128]{1,0:T(8,128)S(1)}, u32[]{:S(2)}, u32[]{:S(2)}) collective-permute-start(f32[16,128]{1,0:T(8,128)S(1)} %get-tuple-element.43), channel_id=1, source_target_pairs={{0,28},{4,16},{8,20},{12,24},{16,12},{20,0},{24,4},{28,8},{1,29},{... | collective-permute-start | bytes 24584 | tf_op jit(solution)/shard_map/ppermute | solution.py:61
  5.5 3.2 %collective-permute-start = (f32[16,128]{1,0:T(8,128)S(1)}, f32[16,128]{1,0:T(8,128)S(1)}, u32[]{:S(2)}, u32[]{:S(2)}) collective-permute-start(f32[16,128]{1,0:T(8,128)S(1)} %get-tuple-element.43), channel_id=1, source_target_pairs={{0,12},{4,0},{8,4},{12,8},{1,13},{5,1},{9,5},{13,9},{2,14},{6,2},{... | collective-permute-start | bytes 24584 | tf_op jit(solution)/shard_map/ppermute | solution.py:37
  8.8 10.6 %collective-permute-start.4 = (f32[56,128]{1,0:T(8,128)S(1)}, f32[56,128]{1,0:T(8,128)S(1)}, u32[]{:S(2)}, u32[]{:S(2)}) collective-permute-start(f32[56,128]{1,0:T(8,128)S(1)} %shard_map.97), channel_id=1, source_target_pairs={{0,4},{3,7},{1,2},{2,1},{4,0},{7,3},{5,6},{6,5},{8,12},{11,15},{9,... | collective-permute-start | bytes 86024 | tf_op jit(solution)/shard_map/ppermute | solution.py:55
  8.8 10.6 %collective-permute-start.3 = (f32[56,128]{1,0:T(8,128)S(1)}, f32[56,128]{1,0:T(8,128)S(1)}, u32[]{:S(2)}, u32[]{:S(2)}) collective-permute-start(f32[56,128]{1,0:T(8,128)S(1)} %shard_map.97), channel_id=1, source_target_pairs={{0,1},{1,0},{2,3},{3,2},{4,5},{5,4},{6,7},{7,6},{8,9},{9,8},{10,11... | collective-permute-start | bytes 86024 | tf_op jit(solution)/shard_map/ppermute | solution.py:55
  27.0 1.7 %collective-permute-start.6 = (f32[136,128]{1,0:T(8,128)S(1)}, f32[136,128]{1,0:T(8,128)S(1)}, u32[]{:S(2)}, u32[]{:S(2)}) collective-permute-start(f32[136,128]{1,0:T(8,128)S(1)} %get-tuple-element.69), channel_id=1, source_target_pairs={{0,4},{3,7},{1,2},{2,1},{4,0},{7,3},{5,6},{6,5},{8,12},{11,15},{9,... | collective-permute-start | bytes 208904 | tf_op jit(solution)/shard_map/ppermute | solution.py:55
  27.1 4.6 %collective-permute-start.5 = (f32[136,128]{1,0:T(8,128)S(1)}, f32[136,128]{1,0:T(8,128)S(1)}, u32[]{:S(2)}, u32[]{:S(2)}) collective-permute-start(f32[136,128]{1,0:T(8,128)S(1)} %get-tuple-element.70), channel_id=1, source_target_pairs={{0,1},{1,0},{2,3},{3,2},{4,5},{5,4},{6,7},{7,6},{8,9},{9,8},{10,11... | collective-permute-start | bytes 208904 | tf_op jit(solution)/shard_map/ppermute | solution.py:55
  31.7 6.2 %collective-permute-start.7 = (f32[176,128]{1,0:T(8,128)S(1)}, f32[176,128]{1,0:T(8,128)S(1)}, u32[]{:S(2)}, u32[]{:S(2)}) collective-permute-start(f32[176,128]{1,0:T(8,128)S(1)} %get-tuple-element.63), channel_id=1, source_target_pairs={{0,16},{16,0},{1,17},{17,1},{2,18},{18,2},{3,19},{19,3},{4,20},{20... | collective-permute-start | bytes 270344 | tf_op jit(solution)/shard_map/ppermute | solution.py:37
  32.6 5.3 %collective-permute-start.9 = (f32[80,128]{1,0:T(8,128)S(1)}, f32[80,128]{1,0:T(8,128)S(1)}, u32[]{:S(2)}, u32[]{:S(2)}) collective-permute-start(f32[80,128]{1,0:T(8,128)S(1)} %get-tuple-element.71), channel_id=1, source_target_pairs={{0,12},{4,8},{8,4},{12,0},{1,13},{5,9},{9,5},{13,1},{2,14},{6,10},... | collective-permute-start | bytes 122888 | tf_op jit(solution)/shard_map/ppermute | solution.py:44
  32.6 5.3 %collective-permute-start.8 = (f32[80,128]{1,0:T(8,128)S(1)}, f32[80,128]{1,0:T(8,128)S(1)}, u32[]{:S(2)}, u32[]{:S(2)}) collective-permute-start(f32[80,128]{1,0:T(8,128)S(1)} %get-tuple-element.72), channel_id=1, source_target_pairs={{0,4},{4,0},{8,12},{12,8},{1,5},{5,1},{9,13},{13,9},{2,6},{6,2},{1... | collective-permute-start | bytes 122888 | tf_op jit(solution)/shard_map/ppermute | solution.py:44
  33.9 4.0 %collective-permute-start.10 = (f32[16,128]{1,0:T(8,128)S(1)}, f32[16,128]{1,0:T(8,128)S(1)}, u32[]{:S(2)}, u32[]{:S(2)}) collective-permute-start(f32[16,128]{1,0:T(8,128)S(1)} %get-tuple-element.65), channel_id=1, source_target_pairs={{0,20},{4,24},{8,28},{12,16},{16,4},{20,8},{24,12},{28,0},{1,21},{... | collective-permute-start | bytes 24584 | tf_op jit(solution)/shard_map/ppermute | solution.py:61

commit v2 on v1

--- a/solution.py
+++ b/solution.py
@@ -289,15 +289,13 @@
         rows = [table[i : i + 1] for i in range(TABLE_ROWS)]
         return k, start, brick_z * BZ, window, rows
 
-    def moved_of(window, rows):
+    def weighted(rows):
         weight_y = hat(row_y, rows[IN_Y], rows[ALONG_Y])
         weight_z = hat(row_z, rows[IN_Z], rows[ALONG_Z])
-        main, rest = parts_of(jnp.concatenate([rows[WEIGHT + a] * weight_y for a in range(REACH_X)], axis=0))
-        unused = jnp.zeros((LANES - 3 * SPREAD, LANES), jnp.float32)
-        table = jnp.concatenate([main, main, rest, unused], axis=0).astype(jnp.bfloat16)
-        seen = lax.dot_general(
-            window.astype(jnp.bfloat16), table, (((1,), (0,)), ((), ())), preferred_element_type=jnp.float32
-        )
+        weight = jnp.concatenate([rows[WEIGHT + a] * weight_y for a in range(REACH_X)], axis=0)
+        return weight_z, *parts_of(weight)
+
+    def stepped(seen, weight_z, rows):
         rate = 1.0 / rows[RESPONSE]
         state, moved, pushed = [], [], []
         for c in range(comps):
@@ -306,15 +304,43 @@
             state.append(rows[MOVING + c] + TIME_STEP * drag)
             moved.append(rows[OFFSET + c] + TIME_STEP * state[c])
             pushed.append(drag * weight_z)
-        pushed.append(jnp.zeros((LANES - comps * REACH_Z, LANES), jnp.float32))
-        push_main, push_rest = parts_of(jnp.concatenate(pushed, axis=0))
-        push = jnp.concatenate([push_main, push_rest, push_main], axis=1).astype(jnp.bfloat16)
-        spread = jnp.concatenate([main, main, rest], axis=1).astype(jnp.bfloat16)
-        shares = lax.dot_general(spread, push, (((1,), (1,)), ((), ())), preferred_element_type=jnp.float32)
         tile = jnp.broadcast_to(rows[RESPONSE], (STATE, LANES))
         for i, value in enumerate(state + moved):
             tile = jnp.where(sub == i, value, tile)
-        return tile, shares
+        gap = jnp.zeros((LANES // 2 - comps * REACH_Z, LANES), jnp.float32)
+        main, rest = parts_of(jnp.concatenate(pushed, axis=0))
+        return tile, jnp.concatenate([main, gap, rest, gap], axis=0)
+
+    def pair_of(one, two):
+        tables, windows, weights = [], [], []
+        for _, _, _, window, rows in (one, two):
+            weight_z, main, rest = weighted(rows)
+            weights.append((weight_z, main, rest))
+            unused = jnp.zeros((LANES - 3 * SPREAD, LANES), jnp.float32)
+            tables.append(jnp.concatenate([main, main, rest, unused], axis=0).astype(jnp.bfloat16))
+            windows.append(window)
+        seen = lax.dot_general(
+            jnp.concatenate(windows, axis=0).astype(jnp.bfloat16), jnp.concatenate(tables, axis=1),
+            (((1,), (0,)), ((), ())), preferred_element_type=jnp.float32,
+        )
+        height = comps * REACH_Z
+        tiles, pushes, spreads = [], [], []
+        for i, (_, _, _, _, rows) in enumerate((one, two)):
+            mine = seen[i * height : (i + 1) * height, i * LANES : (i + 1) * LANES]
+            tile, push = stepped(mine, weights[i][0], rows)
+            tiles.append(tile)
+            pushes.append(push)
+            spreads.extend(weights[i][1:])
+        shares = lax.dot_general(
+            jnp.concatenate(spreads, axis=0).astype(jnp.bfloat16), jnp.concatenate(pushes, axis=0).astype(jnp.bfloat16),
+            (((1,), (1,)), ((), ())), preferred_element_type=jnp.float32,
+        )
+        results = []
+        for i, tile in enumerate(tiles):
+            mine = shares[2 * i * SPREAD : 2 * (i + 1) * SPREAD, i * LANES : (i + 1) * LANES]
+            mine = mine[:SPREAD] + mine[SPREAD:]
+            results.append((tile, mine + pltpu.roll(mine, LANES // 2, 1)))
+        return results
 
     count = list_ref[2 * room + late]
 
@@ -322,7 +348,9 @@
     def _(group):
         at = late * room + group * UNROLL
         taken = [loaded(at + u) for u in range(UNROLL)]
-        results = [moved_of(window, rows) for _, _, _, window, rows in taken]
+        results = []
+        for u in range(0, UNROLL, 2):
+            results.extend(pair_of(taken[u], taken[u + 1]))
         parts = []
         for (_, _, first_z, _, _), (_, shares) in zip(taken, results):
             within = ((lane - first_z) & (LANES - 1)) < REACH_Z
@@ -373,13 +401,9 @@
                 plane_ref[sel, c, x, count_y * BY :] = carried
 
 
-def send_kernel(push, diffuse, crossing_ref, state_ref, grid_ref, deposit_ref, leaving_ref, velocity_ref, y_ref, x_ref, z_ref):
-    comps, size_x = grid_ref.shape[0], grid_ref.shape[1] - 2
-    size_y = z_ref.shape[0]
-    nblocks = velocity_ref.shape[1]
+def leave_kernel(crossing_ref, state_ref, leaving_ref, velocity_ref):
+    comps, nblocks = velocity_ref.shape[:2]
     slots = crossing_ref.shape[1]
-    rows = STATE * slots
-    first = odd("gy") == 0
     velocity = [state_ref[pl.ds(c, nblocks, stride=STATE)] for c in range(comps)]
     for face in range(6):
         tiles = []
@@ -389,10 +413,17 @@
             live = jnp.full((STATE, LANES), block, jnp.int32) >= 0
             tiles.append(jnp.where(live, state_ref[spot], 0.0))
         leaving_ref[face] = jnp.concatenate(tiles, axis=0)
+    for c in range(comps):
+        velocity_ref[c] = velocity[c]
+
+
+def send_kernel(push, diffuse, leaving_ref, grid_ref, deposit_ref, y_ref, x_ref, z_ref):
+    comps, size_x = grid_ref.shape[0], grid_ref.shape[1] - 2
+    size_y = z_ref.shape[0]
+    rows = leaving_ref.shape[1]
+    first = odd("gy") == 0
     y_ref[0, 0:rows] = jnp.where(first, leaving_ref[2], leaving_ref[3])
     y_ref[1, 0:rows] = jnp.where(first, leaving_ref[3], leaving_ref[2])
-    for c in range(comps):
-        velocity_ref[c] = velocity[c]
     lane = lane_ids(ROWS_Y)
     face = jnp.zeros((ROWS_Y, LANES), jnp.float32)
     for c in range(comps):
@@ -558,16 +589,13 @@
 
     (deposit,) = call(merge_kernel, [(2, comps, size_x + 1, ROWS_Y, LANES)], deposit, cycles=500)
     count = STATE * crossing.shape[1]
-    leaving, velocity_next, to_y, to_x, to_z = call(
+    leaving, velocity_next = call(
+        leave_kernel, [(6, count, LANES), (comps, nblocks, LANES)], crossing, state, smem=(0,), cycles=500,
+    )
+    to_y, to_x, to_z = call(
         functools.partial(send_kernel, push, diffuse),
-        [
-            (6, count, LANES),
-            (comps, nblocks, LANES),
-            (2, count + comps * ROWS_Y, LANES),
-            (comps * size_y, LANES),
-            (size_y, LANES),
-        ],
-        crossing, state, grid, deposit, smem=(0,), cycles=1000,
+        [(2, count + comps * ROWS_Y, LANES), (comps * size_y, LANES), (size_y, LANES)],
+        leaving, grid, deposit, cycles=500,
     )
     y1, y2 = swapped_y((to_y[0], to_y[1]))
     (base,) = call(

time: 39.1 us -> 36.8 us (0.941)
  Pallas kernels: 19.7 us -> 17.3 us
    pallas_call x12 -> x13, Pallas kernels: 19.7 us -> 17.3 us  [call(): pl.pallas_call(body, out_shape=[o if isinstance(o, jax.ShapeDtypeStruct)...]
    ppermute x3, starting transfers between devices: 5.07 us -> 5.75 us  [moved_along(): lax.ppermute(block, axis, [(i, (i + distance) % count) for i in range(cou...]
    ppermute x1, starting transfers between devices: 1.31 us -> 0.66 us  [swapped_z(): lax.ppermute(blocks[0], 'gz', first)]
  transfers between devices with their start and end apart: 11 -> 11, of which waited for: 2 -> 2; matrix products, arithmetic and copies ran while one was open for 0% -> 0% of each run, Pallas kernels for 25% -> 22%
where the time goes in v2:
time: 36.8 us; the launch traced here: 36.6 us
  Pallas kernels  17.3 us (47%)
  starting transfers between devices  12.2 us (33%)
  waiting for transfers between devices  6.18 us (17%)
  between operations  0.78 us (2%)
    pallas_call x13, Pallas kernels, call(): pl.pallas_call(body, out_shape=[o if isinstance(o, jax.ShapeDtypeStruct)...  17.3 us
    ppermute x3, starting transfers between devices, moved_along(): lax.ppermute(block, axis, [(i, (i + distance) % count) for i in range(cou...  5.75 us
    ppermute x2, starting transfers between devices, swapped_y(): lax.ppermute(blocks[0], 'gy', first)  4.79 us
    ppermute x2, waiting for transfers between devices, moved_diagonally(): return lax.ppermute(block, ('gx', 'gz'), route)  3.22 us
    ppermute x2, waiting for transfers between devices, swapped_y(): lax.ppermute(blocks[0], 'gy', first)  2.95 us
    ppermute x2, starting transfers between devices, moved_diagonally(): return lax.ppermute(block, ('gx', 'gz'), route)  0.95 us
  transfers between devices with their start and end apart: 11, of which 2 were waited for; matrix products, arithmetic and copies ran while one was open for 0% of the time, Pallas kernels for 22%

profile of v2, /device:TPU:0, one launch (start us, length us, event | category | flops | bytes accessed | tf_op | source)
XLA Modules:
  0.0 36.6 jit_solution(10625005425500411922)
XLA Ops:
  0.6 1.2 %shard_map.94 = (f32[3,18,24,128]{3,2,1,0:T(8,128)S(1)}, f32[16,128]{1,0:T(8,128)S(1)}, f32[48,128]{1,0:T(8,128)S(1)}, f32[3,64,128]{2,1,0:T(8,128)S(1)}, f32[3,...) custom-call(f32[3,16,16,128]{3,2,1,0:T(8,128)} %gas_ref.1, ...), custom_call_target="tpu_custom_call" | custom-call | tf_op jit(solution)/shard_map/pallas_call | solution.py:65
  1.9 3.0 %collective-permute-start.1 = (f32[48,128]{1,0:T(8,128)S(1)}, f32[48,128]{1,0:T(8,128)S(1)}, u32[]{:S(2)}, u32[]{:S(2)}) collective-permute-start(f32[48,128]{1,0:T(8,128)S(1)} %get-tuple-element.44), channel_id=1, source_target_pairs={{0,16},{16,0},{1,17},{17,1},{2,18},{18,2},{3,19},{19,3},{4,20},{20... | collective-permute-start | bytes 73736 | tf_op jit(solution)/shard_map/ppermute | solution.py:37
  4.9 0.6 %collective-permute-start.2 = (f32[16,128]{1,0:T(8,128)S(1)}, f32[16,128]{1,0:T(8,128)S(1)}, u32[]{:S(2)}, u32[]{:S(2)}) collective-permute-start(f32[16,128]{1,0:T(8,128)S(1)} %get-tuple-element.43), channel_id=1, source_target_pairs={{0,28},{4,16},{8,20},{12,24},{16,12},{20,0},{24,4},{28,8},{1,29},{... | collective-permute-start | bytes 24584 | tf_op jit(solution)/shard_map/ppermute | solution.py:61
  5.5 1.1 %collective-permute-start = (f32[16,128]{1,0:T(8,128)S(1)}, f32[16,128]{1,0:T(8,128)S(1)}, u32[]{:S(2)}, u32[]{:S(2)}) collective-permute-start(f32[16,128]{1,0:T(8,128)S(1)} %get-tuple-element.43), channel_id=1, source_target_pairs={{0,12},{4,0},{8,4},{12,8},{1,13},{5,1},{9,5},{13,9},{2,14},{6,2},{... | collective-permute-start | bytes 24584 | tf_op jit(solution)/shard_map/ppermute | solution.py:37
  6.6 2.0 %shard_map.95 = (f32[6528,128]{1,0:T(8,128)S(1)}, f32[3840,128]{1,0:T(8,128)S(1)}, f32[1152,128]{1,0:T(8,128)S(1)}, f32[8,128]{1,0:T(8,128)S(1)}, s32[146]{0:T(256)S(1)}) custom-call(f32[3,18,24,128]{3,2,1,0:T(8,128)S(1)} %get-tuple-element.36.grid_ref.grid_in_ref, f32[3,64,128]{2,1,0:T(8,128)S(1)} %get-tuple-element.37.velocity_ref, ...), custom_call_target="tpu_custom_call" | custom-call | flops 12288000 | bytes 3072000 | tf_op jit(solution)/shard_map/pallas_call | solution.py:65
  8.7 0.0 collective-permute-done.2.edge_ref
  8.7 0.0 collective-permute-done.face_ref
  8.7 0.0 collective-permute-done.1.from_x_ref
  8.7 0.1 shard_map.97
  8.8 0.0 collective-permute-start.4
  8.8 3.1 %collective-permute-start.3 = (f32[56,128]{1,0:T(8,128)S(1)}, f32[56,128]{1,0:T(8,128)S(1)}, u32[]{:S(2)}, u32[]{:S(2)}) collective-permute-start(f32[56,128]{1,0:T(8,128)S(1)} %shard_map.97), channel_id=1, source_target_pairs={{0,1},{1,0},{2,3},{3,2},{4,5},{5,4},{6,7},{7,6},{8,9},{9,8},{10,11... | collective-permute-start | bytes 86024 | tf_op jit(solution)/shard_map/ppermute | solution.py:55
  11.9 0.4 %shard_map.96 = (f32[3,18,24,128]{3,2,1,0:T(8,128)S(1)}, f32[6528,128]{1,0:T(8,128)S(1)}, f32[128,128]{1,0:T(8,128)S(1)}) custom-call(f32[3,18,24,128]{3,2,1,0:T(8,128)S(1)} %get-tuple-element.36.grid_ref.grid_in_ref, f32[6528,128]{1,0:T(8,128)S(1)} %get-tuple-element.42.lines_in_ref, ...), custom_call_target="tpu_custom_call", output_to_operand_aliasing={{0}: (0, {}), {1}: (1, {})} | custom-call | flops 4096000 | bytes 1024000 | tf_op jit(solution)/shard_map/pallas_call | solution.py:65
  12.4 5.4 %shard_map.99 = (f32[576,128]{1,0:T(8,128)S(1)}, f32[3840,128]{1,0:T(8,128)S(1)}) custom-call(s32[146]{0:T(256)S(1)} %get-tuple-element.50.list_ref, s32[64]{0:T(128)S(1)} %get-tuple-element.41.brick_ref, f32[6528,128]{1,0:T(8,128)S(1)} %get-tuple-element.46.lines_in_ref.lines_ref, ...), custom_call_target="tpu_custom_call", output_to_operand_aliasing={{1}: (4, {})} | custom-call | flops 24576000 | bytes 6144000 | tf_op jit(solution)/shard_map/pallas_call | solution.py:65
  17.8 0.0 collective-permute-done.4.second_ref
  17.8 0.0 collective-permute-done.3.first_ref
  17.8 0.6 %shard_map.98 = (f32[3,18,24,128]{3,2,1,0:T(8,128)S(1)}, f32[6528,128]{1,0:T(8,128)S(1)}) custom-call(f32[3,18,24,128]{3,2,1,0:T(8,128)S(1)} %get-tuple-element.45.grid_in_ref, f32[6528,128]{1,0:T(8,128)S(1)} %get-tuple-element.46.lines_in_ref.lines_ref, ...), custom_call_target="tpu_custom_call", output_to_operand_aliasing={{0}: (0, {}), {1}: (1, {})} | custom-call | flops 4096000 | bytes 1024000 | tf_op jit(solution)/shard_map/pallas_call | solution.py:65
  18.4 3.0 %shard_map.100 = (f32[576,128]{1,0:T(8,128)S(1)}, f32[3840,128]{1,0:T(8,128)S(1)}) custom-call(s32[146]{0:T(256)S(1)} %get-tuple-element.50.list_ref, s32[64]{0:T(128)S(1)} %get-tuple-element.41.brick_ref, f32[6528,128]{1,0:T(8,128)S(1)} %get-tuple-element.51.lines_ref, ...), custom_call_target="tpu_custom_call", output_to_operand_aliasing={{1}: (4, {}), {0}: (5, {})} | custom-call | flops 8192000 | bytes 2048000 | tf_op jit(solution)/shard_map/pallas_call | solution.py:65
  21.4 0.1 shard_map.101.deposit_ref
  21.5 1.4 %shard_map.103 = (f32[6,64,128]{2,1,0:T(8,128)S(1)}, f32[3,64,128]{2,1,0:T(8,128)}) custom-call(s32[6,8]{1,0:T(8,128)S(1)} %get-tuple-element.57.crossing_ref, f32[576,128]{1,0:T(8,128)S(1)} %get-tuple-element.58.state_ref), custom_call_target="tpu_custom_call" | custom-call | flops 2048000 | bytes 512000 | tf_op jit(solution)/shard_map/pallas_call | solution.py:65
  22.9 1.8 %shard_map.104 = (f32[2,136,128]{2,1,0:T(8,128)S(1)}, f32[48,128]{1,0:T(8,128)S(1)}, f32[16,128]{1,0:T(8,128)S(1)}) custom-call(f32[6,64,128]{2,1,0:T(8,128)S(1)} %get-tuple-element.59.leaving_ref, f32[3,18,24,128]{3,2,1,0:T(8,128)S(1)} %get-tuple-element.49.grid_ref, f32[2,3,17,24,128]{4,3,2,1,0:T(8,128)S(1)} %shard_map.101.deposit_ref), custom_call_target="tpu_custom_call" | custom-call | flops 2048000 | bytes 512000 | tf_op jit(solution)/shard_map/pallas_call | solution.py:65
  24.6 0.1 collective-permute-start.6
  24.7 1.6 %collective-permute-start.5 = (f32[136,128]{1,0:T(8,128)S(1)}, f32[136,128]{1,0:T(8,128)S(1)}, u32[]{:S(2)}, u32[]{:S(2)}) collective-permute-start(f32[136,128]{1,0:T(8,128)S(1)} %get-tuple-element.70), channel_id=1, source_target_pairs={{0,1},{1,0},{2,3},{3,2},{4,5},{5,4},{6,7},{7,6},{8,9},{9,8},{10,11... | collective-permute-start | bytes 208904 | tf_op jit(solution)/shard_map/ppermute | solution.py:55
  26.4 0.0 collective-permute-done.6.second_ref.y2_ref
  26.4 2.9 %collective-permute-done.5.first_ref.y1_ref = f32[136,128]{1,0:T(8,128)S(1)} collective-permute-done((f32[136,128]{1,0:T(8,128)S(1)}, f32[136,128]{1,0:T(8,128)S(1)}, u32[]{:S(2)}, u32[]{:S(2)}) %collective-permute-start.5) | collective-permute-done | bytes 69664 | tf_op jit(solution)/shard_map/ppermute | solution.py:55
  29.3 1.6 %collective-permute-start.7 = (f32[176,128]{1,0:T(8,128)S(1)}, f32[176,128]{1,0:T(8,128)S(1)}, u32[]{:S(2)}, u32[]{:S(2)}) collective-permute-start(f32[176,128]{1,0:T(8,128)S(1)} %get-tuple-element.63), channel_id=1, source_target_pairs={{0,16},{16,0},{1,17},{17,1},{2,18},{18,2},{3,19},{19,3},{4,20},{20... | collective-permute-start | bytes 270344 | tf_op jit(solution)/shard_map/ppermute | solution.py:37
  30.9 0.0 collective-permute-start.9
  31.0 0.7 %collective-permute-start.8 = (f32[80,128]{1,0:T(8,128)S(1)}, f32[80,128]{1,0:T(8,128)S(1)}, u32[]{:S(2)}, u32[]{:S(2)}) collective-permute-start(f32[80,128]{1,0:T(8,128)S(1)} %get-tuple-element.72), channel_id=1, source_target_pairs={{0,4},{4,0},{8,12},{12,8},{1,5},{5,1},{9,13},{13,9},{2,6},{6,2},{1... | collective-permute-start | bytes 122888 | tf_op jit(solution)/shard_map/ppermute | solution.py:44
  31.6 0.4 collective-permute-start.10
  32.0 0.4 %shard_map.102.base_ref = f32[3,16,16,128]{3,2,1,0:T(8,128)S(1)} custom-call(f32[3,18,24,128]{3,2,1,0:T(8,128)S(1)} %get-tuple-element.49.grid_ref, f32[2,3,17,24,128]{4,3,2,1,0:T(8,128)S(1)} %shard_map.101.deposit_ref, f32[128,128]{1,0:T(8,128)S(1)} %get-tuple-element.47.top_in_ref.top_ref), custom_call_target="tpu_custom_call" | custom-call | flops 4096000 | bytes 1024000 | tf_op jit(solution)/shard_map/pallas_call | solution.py:65
  32.4 3.2 %collective-permute-done.10.edge_ref = f32[16,128]{1,0:T(8,128)S(1)} collective-permute-done((f32[16,128]{1,0:T(8,128)S(1)}, f32[16,128]{1,0:T(8,128)S(1)}, u32[]{:S(2)}, u32[]{:S(2)}) %collective-permute-start.10) | collective-permute-done | bytes 8224 | tf_op jit(solution)/shard_map/ppermute | solution.py:61
  35.6 0.0 collective-permute-done.9.z2_ref
  35.6 0.0 collective-permute-done.8.z1_ref
  35.6 0.0 collective-permute-done.7.x_ref.minus_x_ref
  35.6 1.0 %shard_map.106 = (f32[3,16,16,128]{3,2,1,0:T(8,128)}, f32[6,7,8,128]{3,2,1,0:T(8,128)}) custom-call(f32[3,16,16,128]{3,2,1,0:T(8,128)S(1)} %shard_map.102.base_ref, f32[136,128]{1,0:T(8,128)S(1)} %collective-permute-done.5.first_ref.y1_ref, f32[136,128]{1,0:T(8,128)S(1)} %collective-permute-done.6.second_ref.y2_ref, ...), custom_call_target="tpu_custom_call" | custom-call | tf_op jit(solution)/shard_map/pallas_call | solution.py:65
  (3 shorter events, 0.0 us)
Async XLA Ops:
  1.9 6.8 %collective-permute-start.1 = (f32[48,128]{1,0:T(8,128)S(1)}, f32[48,128]{1,0:T(8,128)S(1)}, u32[]{:S(2)}, u32[]{:S(2)}) collective-permute-start(f32[48,128]{1,0:T(8,128)S(1)} %get-tuple-element.44), channel_id=1, source_target_pairs={{0,16},{16,0},{1,17},{17,1},{2,18},{18,2},{3,19},{19,3},{4,20},{20... | collective-permute-start | bytes 73736 | tf_op jit(solution)/shard_map/ppermute | solution.py:37
  4.9 3.7 %collective-permute-start.2 = (f32[16,128]{1,0:T(8,128)S(1)}, f32[16,128]{1,0:T(8,128)S(1)}, u32[]{:S(2)}, u32[]{:S(2)}) collective-permute-start(f32[16,128]{1,0:T(8,128)S(1)} %get-tuple-element.43), channel_id=1, source_target_pairs={{0,28},{4,16},{8,20},{12,24},{16,12},{20,0},{24,4},{28,8},{1,29},{... | collective-permute-start | bytes 24584 | tf_op jit(solution)/shard_map/ppermute | solution.py:61
  5.5 3.2 %collective-permute-start = (f32[16,128]{1,0:T(8,128)S(1)}, f32[16,128]{1,0:T(8,128)S(1)}, u32[]{:S(2)}, u32[]{:S(2)}) collective-permute-start(f32[16,128]{1,0:T(8,128)S(1)} %get-tuple-element.43), channel_id=1, source_target_pairs={{0,12},{4,0},{8,4},{12,8},{1,13},{5,1},{9,5},{13,9},{2,14},{6,2},{... | collective-permute-start | bytes 24584 | tf_op jit(solution)/shard_map/ppermute | solution.py:37
  8.8 9.0 %collective-permute-start.4 = (f32[56,128]{1,0:T(8,128)S(1)}, f32[56,128]{1,0:T(8,128)S(1)}, u32[]{:S(2)}, u32[]{:S(2)}) collective-permute-start(f32[56,128]{1,0:T(8,128)S(1)} %shard_map.97), channel_id=1, source_target_pairs={{0,4},{3,7},{1,2},{2,1},{4,0},{7,3},{5,6},{6,5},{8,12},{11,15},{9,... | collective-permute-start | bytes 86024 | tf_op jit(solution)/shard_map/ppermute | solution.py:55
  8.8 9.0 %collective-permute-start.3 = (f32[56,128]{1,0:T(8,128)S(1)}, f32[56,128]{1,0:T(8,128)S(1)}, u32[]{:S(2)}, u32[]{:S(2)}) collective-permute-start(f32[56,128]{1,0:T(8,128)S(1)} %shard_map.97), channel_id=1, source_target_pairs={{0,1},{1,0},{2,3},{3,2},{4,5},{5,4},{6,7},{7,6},{8,9},{9,8},{10,11... | collective-permute-start | bytes 86024 | tf_op jit(solution)/shard_map/ppermute | solution.py:55
  24.6 1.7 %collective-permute-start.6 = (f32[136,128]{1,0:T(8,128)S(1)}, f32[136,128]{1,0:T(8,128)S(1)}, u32[]{:S(2)}, u32[]{:S(2)}) collective-permute-start(f32[136,128]{1,0:T(8,128)S(1)} %get-tuple-element.69), channel_id=1, source_target_pairs={{0,4},{3,7},{1,2},{2,1},{4,0},{7,3},{5,6},{6,5},{8,12},{11,15},{9,... | collective-permute-start | bytes 208904 | tf_op jit(solution)/shard_map/ppermute | solution.py:55
  24.7 4.6 %collective-permute-start.5 = (f32[136,128]{1,0:T(8,128)S(1)}, f32[136,128]{1,0:T(8,128)S(1)}, u32[]{:S(2)}, u32[]{:S(2)}) collective-permute-start(f32[136,128]{1,0:T(8,128)S(1)} %get-tuple-element.70), channel_id=1, source_target_pairs={{0,1},{1,0},{2,3},{3,2},{4,5},{5,4},{6,7},{7,6},{8,9},{9,8},{10,11... | collective-permute-start | bytes 208904 | tf_op jit(solution)/shard_map/ppermute | solution.py:55
  29.3 6.3 %collective-permute-start.7 = (f32[176,128]{1,0:T(8,128)S(1)}, f32[176,128]{1,0:T(8,128)S(1)}, u32[]{:S(2)}, u32[]{:S(2)}) collective-permute-start(f32[176,128]{1,0:T(8,128)S(1)} %get-tuple-element.63), channel_id=1, source_target_pairs={{0,16},{16,0},{1,17},{17,1},{2,18},{18,2},{3,19},{19,3},{4,20},{20... | collective-permute-start | bytes 270344 | tf_op jit(solution)/shard_map/ppermute | solution.py:37
  30.9 4.6 %collective-permute-start.9 = (f32[80,128]{1,0:T(8,128)S(1)}, f32[80,128]{1,0:T(8,128)S(1)}, u32[]{:S(2)}, u32[]{:S(2)}) collective-permute-start(f32[80,128]{1,0:T(8,128)S(1)} %get-tuple-element.71), channel_id=1, source_target_pairs={{0,12},{4,8},{8,4},{12,0},{1,13},{5,9},{9,5},{13,1},{2,14},{6,10},... | collective-permute-start | bytes 122888 | tf_op jit(solution)/shard_map/ppermute | solution.py:44
  31.0 4.6 %collective-permute-start.8 = (f32[80,128]{1,0:T(8,128)S(1)}, f32[80,128]{1,0:T(8,128)S(1)}, u32[]{:S(2)}, u32[]{:S(2)}) collective-permute-start(f32[80,128]{1,0:T(8,128)S(1)} %get-tuple-element.72), channel_id=1, source_target_pairs={{0,4},{4,0},{8,12},{12,8},{1,5},{5,1},{9,13},{13,9},{2,6},{6,2},{1... | collective-permute-start | bytes 122888 | tf_op jit(solution)/shard_map/ppermute | solution.py:44
  31.6 4.0 %collective-permute-start.10 = (f32[16,128]{1,0:T(8,128)S(1)}, f32[16,128]{1,0:T(8,128)S(1)}, u32[]{:S(2)}, u32[]{:S(2)}) collective-permute-start(f32[16,128]{1,0:T(8,128)S(1)} %get-tuple-element.65), channel_id=1, source_target_pairs={{0,20},{4,24},{8,28},{12,16},{16,4},{20,8},{24,12},{28,0},{1,21},{... | collective-permute-start | bytes 24584 | tf_op jit(solution)/shard_map/ppermute | solution.py:61

commit v3 on v2

--- a/solution.py
+++ b/solution.py
@@ -21,7 +21,7 @@
 REACH_Y = 8
 SPREAD = REACH_X * REACH_Y
 REACH_Z = 2 * BZ
-UNROLL = 8
+UNROLL = 4
 
 WEIGHT, ALONG_Y, IN_Y, ALONG_Z, IN_Z, RESPONSE, MOVING, OFFSET = 0, 5, 6, 7, 8, 9, 10, 13
 TABLE_ROWS = 16
@@ -105,20 +105,26 @@
     for copy in copies:
         copy.start()
     zeros = jnp.zeros((ROWS_Y, LANES), jnp.float32)
-    for c in range(comps):
+
+    @pl.loop(0, comps)
+    def _(c):
         grid_ref[c, 0] = zeros
         grid_ref[c, size_x + 1] = zeros
         for x in range(size_x):
             grid_ref[c, x + 1, size_y:] = zeros[size_y:]
+
     copies[0].wait()
     lane = lane_ids(size_y)
-    face = jnp.zeros((size_y, LANES), jnp.float32)
-    for c in range(comps):
-        plane_ref[c * size_y : (c + 1) * size_y] = grid_ref[c, 1, 0:size_y]
+    face_ref[...] = jnp.zeros_like(face_ref)
+
+    @pl.loop(0, comps)
+    def _(c):
+        plane_ref[pl.ds(pl.multiple_of(c * size_y, 8), size_y)] = grid_ref[c, 1, 0:size_y]
+        face = jnp.zeros((size_y, LANES), jnp.float32)
         for x in range(size_x):
-            place = PACK * c + x
-            face = jnp.where(lane == place, turned(grid_ref[c, x + 1, 0:size_y], place), face)
-    face_ref[...] = face
+            face = jnp.where(lane == x, turned(grid_ref[c, x + 1, 0:size_y], x), face)
+        face_ref[...] = face_ref[...] + pltpu.roll(face, PACK * c, 1)
+
     for copy in copies[1:]:
         copy.wait()
 
@@ -128,16 +134,22 @@
     return main, value - main
 
 
-def lay_out(grid_ref, lines_ref, p, q, size_y, size_z):
+def lay_out(grid_ref, lines_ref, first, last, size_y, size_z, columns):
     comps = grid_ref.shape[0]
     rows_z = size_z + 8
     count_y = size_y // BY
-    for c in range(comps):
-        planes = [grid_ref[c, p * BX + a + 1, q * BY : q * BY + REACH_Y] for a in range(REACH_X)]
-        main, rest = parts_of(jnp.concatenate(planes, axis=0))
-        stack = jnp.concatenate([main, rest, main, jnp.zeros((LANES - 3 * SPREAD, LANES), jnp.float32)], axis=0)
-        at = ((p * count_y + q) * comps + c) * rows_z
-        lines_ref[at : at + size_z] = jnp.transpose(stack)
+
+    @pl.loop(first, last)
+    def _(p):
+        @pl.loop(0, comps)
+        def _(c):
+            for q in columns:
+                planes = [grid_ref[c, p * BX + a + 1, q * BY : q * BY + REACH_Y] for a in range(REACH_X)]
+                main, rest = parts_of(jnp.concatenate(planes, axis=0))
+                unused = jnp.zeros((LANES - 3 * SPREAD, LANES), jnp.float32)
+                stack = jnp.concatenate([main, rest, main, unused], axis=0)
+                at = pl.multiple_of(((p * count_y + q) * comps + c) * rows_z, 8)
+                lines_ref[pl.ds(at, size_z)] = jnp.transpose(stack)
 
 
 def lay_out_top(turned_ref, lines_ref, q, comps, count_x, count_y, size_z):
@@ -179,16 +191,15 @@
     list_ref[2 * room + 1] = late
     ready_ref[...] = jnp.zeros_like(ready_ref)
 
-    deposit_ref[...] = jnp.zeros_like(deposit_ref)
-    for p in range(count_x):
-        for q in range(count_y):
-            for c in range(comps):
-                at = ((p * count_y + q) * comps + c) * rows_z + size_z
-                lines_ref[at : at + 8] = jnp.zeros((8, LANES), jnp.float32)
-    for p in range(count_x - 1):
-        for q in range(count_y - 1):
-            lay_out(grid_ref, lines_ref, p, q, size_y, size_z)
-
+    @pl.loop(0, deposit_ref.shape[0] // SPREAD)
+    def _(i):
+        deposit_ref[pl.ds(pl.multiple_of(i * SPREAD, 8), SPREAD)] = jnp.zeros((SPREAD, LANES), jnp.float32)
+
+    @pl.loop(0, lines_ref.shape[0] // rows_z)
+    def _(i):
+        lines_ref[pl.ds(pl.multiple_of(i * rows_z + size_z, 8), 8)] = jnp.zeros((8, LANES), jnp.float32)
+
+    lay_out(grid_ref, lines_ref, 0, count_x - 1, size_y, size_z, range(count_y - 1))
     cells = cell_ref[...]
     cell_x, cell_y, cell_z = cells // (BY * BZ), cells // BZ % BY, cells % BZ
     along_x = fraction_ref[0]
@@ -227,8 +238,7 @@
     count_x, count_y = size_x // BX, size_y // BY
     for c in range(comps):
         grid_ref[c, size_x + 1, 0:size_y] = from_x_ref[c * size_y : (c + 1) * size_y]
-    for q in range(count_y - 1):
-        lay_out(grid_ref, lines_ref, count_x - 1, q, size_y, size_z)
+    lay_out(grid_ref, lines_ref, count_x - 1, count_x, size_y, size_z, range(count_y - 1))
     top = jnp.where(lane_ids(size_y) % PACK == size_x, turned(edge_ref[...], size_x), face_ref[...])
     top_ref[0:size_y] = top
     top_ref[size_y:] = jnp.zeros((LANES - size_y, LANES), jnp.float32)
@@ -241,19 +251,26 @@
     comps, size_x, size_z = grid_ref.shape[0], grid_ref.shape[1] - 2, grid_ref.shape[3]
     count_x, count_y = size_x // BX, size_y // BY
     inside = lax.axis_index("gy") != lax.axis_size("gy") - 1
-    even = odd("gy") == 0
     kept = (row_ids(8) == 0) & inside
 
-    def line_at(row):
-        line = jnp.where(even, first_ref[row : row + 1], second_ref[row : row + 1])
+    def top_of(line):
         return jnp.where(kept, jnp.broadcast_to(line, (8, LANES)), 0.0)
 
+    def rows_at(rows):
+        return jnp.where(jnp.full((1, LANES), odd("gy")) == 0, first_ref[rows], second_ref[rows])
+
+    @pl.loop(0, comps)
+    def _(c):
+        lines = rows_at(pl.ds(pl.multiple_of(c * size_x, 8), size_x))
+        for x in range(size_x):
+            grid_ref[c, x + 1, size_y:] = top_of(lines[x : x + 1])
+
     for c in range(comps):
-        for x in range(size_x + 1):
-            grid_ref[c, x + 1, size_y:] = line_at(c * size_x + x if x < size_x else comps * size_x + c)
-    for p in range(count_x):
-        lay_out(grid_ref, lines_ref, p, count_y - 1, size_y, size_z)
-    corner = line_at(comps * size_x + comps)
+        row = comps * size_x + c
+        grid_ref[c, size_x + 1, size_y:] = top_of(rows_at(slice(row, row + 1)))
+    lay_out(grid_ref, lines_ref, 0, count_x, size_y, size_z, [count_y - 1])
+    row = comps * size_x + comps
+    corner = top_of(rows_at(slice(row, row + 1)))
     rest = jnp.zeros((LANES - size_y - 8, LANES), jnp.float32)
     turned_ref[...] = jnp.transpose(jnp.concatenate([top_in_ref[0:size_y], corner, rest], axis=0))
     lay_out_top(turned_ref, lines_ref, count_y - 1, comps, count_x, count_y, size_z)
@@ -374,38 +391,40 @@
     count_x, count_y = (planes - 1) // BX, tiles_ref.shape[0] // (2 * ((planes - 1) // BX) * comps * SPREAD)
     top = row_ids(REACH_Y) >= BY
 
-    for sel in (0, 1):
-        for c in range(comps):
-            for x in range(planes):
-                bricks = [(x // BX, x % BX)] if x < planes - 1 else []
-                if x and x % BX == 0:
-                    bricks.append((x // BX - 1, BX))
-
-                def tile(q):
-                    total = None
-                    for p, a in bricks:
-                        at = (((sel * count_x + p) * count_y + q) * comps + c) * SPREAD + a * REACH_Y
-                        value = tiles_ref[at : at + REACH_Y]
-                        total = value if total is None else total + value
-                    return total
-
-                carried = None
-                for q in range(0, count_y, 2):
-                    here = tile(q)
-                    if carried is not None:
-                        here = here + carried
-                    between = pltpu.roll(tile(q + 1), BY, 0)
-                    here = here + jnp.where(top, between, 0.0)
-                    carried = jnp.where(top, 0.0, between)
-                    plane_ref[sel, c, x, q * BY : q * BY + REACH_Y] = here
-                plane_ref[sel, c, x, count_y * BY :] = carried
-
-
-def leave_kernel(crossing_ref, state_ref, leaving_ref, velocity_ref):
-    comps, nblocks = velocity_ref.shape[:2]
+    @pl.loop(0, 2 * comps)
+    def _(i):
+        sel, c = lax.div(i, comps), lax.rem(i, comps)
+        base = (sel * count_x * count_y * comps + c) * SPREAD
+        for x in range(planes):
+            bricks = [(x // BX, x % BX)] if x < planes - 1 else []
+            if x and x % BX == 0:
+                bricks.append((x // BX - 1, BX))
+
+            def tile(q):
+                total = None
+                for p, a in bricks:
+                    at = pl.multiple_of(base + (p * count_y + q) * comps * SPREAD + a * REACH_Y, 8)
+                    value = tiles_ref[pl.ds(at, REACH_Y)]
+                    total = value if total is None else total + value
+                return total
+
+            carried = None
+            for q in range(0, count_y, 2):
+                here = tile(q)
+                if carried is not None:
+                    here = here + carried
+                between = pltpu.roll(tile(q + 1), BY, 0)
+                here = here + jnp.where(top, between, 0.0)
+                carried = jnp.where(top, 0.0, between)
+                plane_ref[sel, c, x, q * BY : q * BY + REACH_Y] = here
+            plane_ref[sel, c, x, count_y * BY :] = carried
+
+
+def leave_kernel(crossing_ref, state_ref, leaving_ref):
     slots = crossing_ref.shape[1]
-    velocity = [state_ref[pl.ds(c, nblocks, stride=STATE)] for c in range(comps)]
-    for face in range(6):
+
+    @pl.loop(0, 6)
+    def _(face):
         tiles = []
         for slot in range(slots):
             block = crossing_ref[face, slot]
@@ -413,53 +432,58 @@
             live = jnp.full((STATE, LANES), block, jnp.int32) >= 0
             tiles.append(jnp.where(live, state_ref[spot], 0.0))
         leaving_ref[face] = jnp.concatenate(tiles, axis=0)
-    for c in range(comps):
-        velocity_ref[c] = velocity[c]
-
-
-def send_kernel(push, diffuse, leaving_ref, grid_ref, deposit_ref, y_ref, x_ref, z_ref):
+
+
+def send_kernel(push, diffuse, leaving_ref, grid_ref, deposit_ref, y_ref, x_ref, z_ref, face_ref):
     comps, size_x = grid_ref.shape[0], grid_ref.shape[1] - 2
     size_y = z_ref.shape[0]
     rows = leaving_ref.shape[1]
-    first = odd("gy") == 0
+    first = jnp.full((rows, LANES), odd("gy")) == 0
     y_ref[0, 0:rows] = jnp.where(first, leaving_ref[2], leaving_ref[3])
     y_ref[1, 0:rows] = jnp.where(first, leaving_ref[3], leaving_ref[2])
     lane = lane_ids(ROWS_Y)
-    face = jnp.zeros((ROWS_Y, LANES), jnp.float32)
-    for c in range(comps):
+    sub = row_ids(ROWS_Y)
+    face_ref[...] = jnp.zeros_like(face_ref)
+
+    @pl.loop(0, comps)
+    def _(c):
+        face = jnp.zeros((ROWS_Y, LANES), jnp.float32)
+        lines = jnp.zeros((ROWS_Y, LANES), jnp.float32)
         for x in range(size_x + 1):
             beyond = push * deposit_ref[1, c, x]
+            top = push * deposit_ref[0, c, x, size_y:] + jnp.where(lane[:8] == 0, 0.0, beyond[size_y:])
             if x < size_x:
-                behind = diffuse * turned(grid_ref[c, x + 1, 0:size_y], 1)
-                beyond = jnp.concatenate([beyond[:size_y] + behind, beyond[size_y:]], axis=0)
-            place = PACK * c + x
-            face = jnp.where(lane == place, turned(beyond, place), face)
-        wrapped = jnp.where(lane_ids(size_x) == 0, 0.0, deposit_ref[1, c, 0:size_x, size_y])
-        line = diffuse * grid_ref[c, 1 : size_x + 1, size_y - 1] + push * (deposit_ref[0, c, 0:size_x, size_y] + wrapped)
-        y_ref[0, rows + c * ROWS_Y : rows + c * ROWS_Y + size_x] = line
-        wrapped = jnp.where(lane_ids(ROWS_Y) == 0, 0.0, deposit_ref[1, c, size_x])
-        total = push * (deposit_ref[0, c, size_x] + wrapped)
-        x_ref[c * size_y : (c + 1) * size_y] = diffuse * grid_ref[c, size_x, 0:size_y] + total[:size_y]
-        at = rows + c * ROWS_Y + size_x
-        y_ref[0, at : at + 8] = total[size_y:]
-    z_ref[...] = face[:size_y]
-    y_ref[0, rows + size_x + 1 : rows + size_x + 2] = face[size_y : size_y + 1]
+                here = grid_ref[c, x + 1, 0:size_y]
+                beyond = jnp.concatenate([beyond[:size_y] + diffuse * turned(here, 1), beyond[size_y:]], axis=0)
+                top = top[0:1] + diffuse * here[size_y - 1 :]
+            else:
+                here = grid_ref[c, size_x, 0:size_y]
+                total = push * deposit_ref[0, c, x, 0:size_y] + jnp.where(lane[:size_y] == 0, 0.0, beyond[:size_y])
+                x_ref[pl.ds(pl.multiple_of(c * size_y, 8), size_y)] = diffuse * here + total
+                top = top[0:1]
+            lines = jnp.where(sub == x, top, lines)
+            face = jnp.where(lane == x, turned(beyond, x), face)
+        y_ref[0, pl.ds(pl.multiple_of(rows + c * ROWS_Y, 8), ROWS_Y)] = lines
+        face_ref[...] = face_ref[...] + pltpu.roll(face, PACK * c, 1)
+
+    z_ref[...] = face_ref[0:size_y]
+    y_ref[0, rows + size_x + 1 : rows + size_x + 2] = face_ref[size_y : size_y + 1]
     y_ref[1, rows:] = y_ref[0, rows:]
 
 
 def base_kernel(push, diffuse, grid_ref, deposit_ref, top_ref, base_ref):
     comps, size_x, size_y, size_z = base_ref.shape
     lane = lane_ids(size_y)
-    top = top_ref[0:size_y]
-    for c in range(comps):
+
+    @pl.loop(0, comps)
+    def _(c):
+        top = pltpu.roll(top_ref[0:size_y], (LANES - PACK * c) % LANES, 1)
         for x in range(size_x):
             here = grid_ref[c, x + 1, 0:size_y]
-            laplace = grid_ref[c, x + 2, 0:size_y]
-            if x:
-                laplace = laplace + grid_ref[c, x, 0:size_y]
             before = jnp.where(row_ids(size_y) == 0, 0.0, pltpu.roll(here, 1, 0))
+            laplace = grid_ref[c, x, 0:size_y] + grid_ref[c, x + 2, 0:size_y]
             laplace = laplace + grid_ref[c, x + 1, 1 : size_y + 1] + before
-            ahead = jnp.where(lane == size_z - 1, turned(top, size_z - 1 - (PACK * c + x)), turned(here, -1))
+            ahead = jnp.where(lane == size_z - 1, turned(top, size_z - 1 - x), turned(here, -1))
             laplace = laplace + ahead + jnp.where(lane == 0, 0.0, turned(here, 1)) - 6.0 * here
             total = deposit_ref[0, c, x, 0:size_y] + jnp.where(lane == 0, 0.0, deposit_ref[1, c, x, 0:size_y])
             base_ref[c, x] = here + diffuse * laplace + push * total
@@ -491,28 +515,32 @@
 
 
 def finish_kernel(
-    count, base_ref, y1_ref, y2_ref, x_ref, minus_x_ref, z1_ref, z2_ref, edge_ref, gas_ref, arrivals_ref
+    count, base_ref, y1_ref, y2_ref, x_ref, minus_x_ref, z1_ref, z2_ref, edge_ref, state_ref,
+    gas_ref, arrivals_ref, velocity_ref,
 ):
     comps, size_x, size_y, _ = base_ref.shape
     first_row, first_lane = row_ids(size_y) == 0, lane_ids(size_y) == 0
     rows = slice(count, count + size_y)
-    from_first = odd("gz") == 1
-    face = jnp.where(from_first, z1_ref[rows], z2_ref[rows])
-    corner = edge_ref[...]
-    for c in range(comps):
+    odd_y, odd_z = jnp.full((1, LANES), odd("gy")) == 1, jnp.full((1, LANES), odd("gz")) == 1
+    place = jnp.full((1, LANES), lax.axis_index("gy"))
+    lower, upper = place != 0, place != lax.axis_size("gy") - 1
+    face = jnp.where(odd_z, z1_ref[rows], z2_ref[rows])
+
+    @pl.loop(0, comps)
+    def _(c):
+        spot = pl.ds(pl.multiple_of(count + c * ROWS_Y, 8), ROWS_Y)
+        lines = jnp.where(lower, jnp.where(odd_y, y1_ref[spot], y2_ref[spot]), 0.0)
+        mine = pltpu.roll(face, (LANES - PACK * c) % LANES, 1)
         for x in range(size_x):
-            at = count + c * ROWS_Y + x
-            line = jnp.broadcast_to(below(y1_ref, y2_ref, slice(at, at + 1)), (size_y, LANES))
+            line = jnp.broadcast_to(lines[x : x + 1], (size_y, LANES))
             total = base_ref[c, x] + jnp.where(first_row, line, 0.0)
-            far = turned(face, -(PACK * c + x))
+            far = turned(mine, -x)
             if x == 0:
-                total = total + x_ref[c * size_y : (c + 1) * size_y]
-                far = far + turned(corner, -(PACK * c + size_x))
+                total = total + x_ref[pl.ds(pl.multiple_of(c * size_y, 8), size_y)]
+                far = far + pltpu.roll(edge_ref[...], (2 * LANES - PACK * c - size_x) % LANES, 1)
             gas_ref[c, x] = total + jnp.where(first_lane, far, 0.0)
 
     slots = arrivals_ref.shape[2]
-    lower, upper = lax.axis_index("gy") != 0, lax.axis_index("gy") != lax.axis_size("gy") - 1
-    odd_y = odd("gy") == 1
     for i in range(arrivals_ref.shape[1]):
 
         def rows_of(ref, at=0):
@@ -524,8 +552,10 @@
         arrivals_ref[2, i] = jnp.where(lower, jnp.where(odd_y, y1, y2), 0.0)
         arrivals_ref[3, i] = jnp.where(upper, jnp.where(odd_y, y2, y1), 0.0)
         z1, z2 = rows_of(z1_ref), rows_of(z2_ref)
-        arrivals_ref[4, i] = jnp.where(from_first, z1, z2)
-        arrivals_ref[5, i] = jnp.where(from_first, z2, z1)
+        arrivals_ref[4, i] = jnp.where(odd_z, z1, z2)
+        arrivals_ref[5, i] = jnp.where(odd_z, z2, z1)
+    for c in range(comps):
+        velocity_ref[c] = state_ref[pl.ds(c, velocity_ref.shape[1], stride=STATE)]
 
 
 def per_device(gas_field, velocity, fraction, response, cell_index, brick_index, crossing):
@@ -589,13 +619,11 @@
 
     (deposit,) = call(merge_kernel, [(2, comps, size_x + 1, ROWS_Y, LANES)], deposit, cycles=500)
     count = STATE * crossing.shape[1]
-    leaving, velocity_next = call(
-        leave_kernel, [(6, count, LANES), (comps, nblocks, LANES)], crossing, state, smem=(0,), cycles=500,
-    )
+    (leaving,) = call(leave_kernel, [(6, count, LANES)], crossing, state, smem=(0,), cycles=500)
     to_y, to_x, to_z = call(
         functools.partial(send_kernel, push, diffuse),
         [(2, count + comps * ROWS_Y, LANES), (comps * size_y, LANES), (size_y, LANES)],
-        leaving, grid, deposit, cycles=500,
+        leaving, grid, deposit, cycles=500, scratch=(pltpu.VMEM((ROWS_Y, LANES), jnp.float32),),
     )
     y1, y2 = swapped_y((to_y[0], to_y[1]))
     (base,) = call(
@@ -612,9 +640,10 @@
     z1, z2 = swapped_z((to_z[0], to_z[1]))
     got_xz = moved_diagonally(to_xz, 1)
     got_mx = got_x if both else moved_along(leaving[1], "gx", -1)
-    gas_next, arrivals = call(
-        functools.partial(finish_kernel, count), [gas_field.shape, (6, 7, crossing.shape[1], LANES)],
-        base, y1, y2, got_x, got_mx, z1, z2, got_xz,
+    gas_next, arrivals, velocity_next = call(
+        functools.partial(finish_kernel, count),
+        [gas_field.shape, (6, 7, crossing.shape[1], LANES), (comps, nblocks, LANES)],
+        base, y1, y2, got_x, got_mx, z1, z2, got_xz, state,
     )
     return gas_next, jnp.transpose(velocity_next, (1, 0, 2)), jnp.transpose(arrivals, (0, 2, 1, 3))
 

time: 36.8 us -> 41.4 us (1.12)
  Pallas kernels: 17.3 us -> 22.3 us
    pallas_call x13, Pallas kernels: 17.3 us -> 22.3 us  [call(): pl.pallas_call(body, out_shape=[o if isinstance(o, jax.ShapeDtypeStruct)...]
  transfers between devices with their start and end apart: 11 -> 11, of which waited for: 2 -> 2; matrix products, arithmetic and copies ran while one was open for 0% -> 0% of each run, Pallas kernels for 22% -> 32%
where the time goes in v3:
time: 41.4 us; the launch traced here: 41.3 us
  Pallas kernels  22.3 us (54%)
  starting transfers between devices  12 us (29%)
  waiting for transfers between devices  6.21 us (15%)
  between operations  0.78 us (2%)
    pallas_call x13, Pallas kernels, call(): pl.pallas_call(body, out_shape=[o if isinstance(o, jax.ShapeDtypeStruct)...  22.3 us
    ppermute x3, starting transfers between devices, moved_along(): lax.ppermute(block, axis, [(i, (i + distance) % count) for i in range(cou...  5.74 us
    ppermute x2, starting transfers between devices, swapped_y(): lax.ppermute(blocks[0], 'gy', first)  4.78 us
    ppermute x2, waiting for transfers between devices, moved_diagonally(): return lax.ppermute(block, ('gx', 'gz'), route)  3.24 us
    ppermute x2, waiting for transfers between devices, swapped_y(): lax.ppermute(blocks[0], 'gy', first)  2.95 us
  transfers between devices with their start and end apart: 11, of which 2 were waited for; matrix products, arithmetic and copies ran while one was open for 0% of the time, Pallas kernels for 32%

profile of v3, /device:TPU:0, one launch (start us, length us, event | category | flops | bytes accessed | tf_op | source)
XLA Modules:
  0.0 41.3 jit_solution(16714795412413008889)
XLA Ops:
  0.6 1.6 %shard_map.94 = (f32[3,18,24,128]{3,2,1,0:T(8,128)S(1)}, f32[16,128]{1,0:T(8,128)S(1)}, f32[48,128]{1,0:T(8,128)S(1)}, f32[3,64,128]{2,1,0:T(8,128)S(1)}, f32[3,...) custom-call(f32[3,16,16,128]{3,2,1,0:T(8,128)} %gas_ref.1, ...), custom_call_target="tpu_custom_call" | custom-call | tf_op jit(solution)/shard_map/pallas_call | solution.py:65
  2.2 3.0 %collective-permute-start.1 = (f32[48,128]{1,0:T(8,128)S(1)}, f32[48,128]{1,0:T(8,128)S(1)}, u32[]{:S(2)}, u32[]{:S(2)}) collective-permute-start(f32[48,128]{1,0:T(8,128)S(1)} %get-tuple-element.43), channel_id=1, source_target_pairs={{0,16},{16,0},{1,17},{17,1},{2,18},{18,2},{3,19},{19,3},{4,20},{20... | collective-permute-start | bytes 73736 | tf_op jit(solution)/shard_map/ppermute | solution.py:37
  5.3 0.6 %collective-permute-start.2 = (f32[16,128]{1,0:T(8,128)S(1)}, f32[16,128]{1,0:T(8,128)S(1)}, u32[]{:S(2)}, u32[]{:S(2)}) collective-permute-start(f32[16,128]{1,0:T(8,128)S(1)} %get-tuple-element.42), channel_id=1, source_target_pairs={{0,28},{4,16},{8,20},{12,24},{16,12},{20,0},{24,4},{28,8},{1,29},{... | collective-permute-start | bytes 24584 | tf_op jit(solution)/shard_map/ppermute | solution.py:61
  5.8 1.1 %collective-permute-start = (f32[16,128]{1,0:T(8,128)S(1)}, f32[16,128]{1,0:T(8,128)S(1)}, u32[]{:S(2)}, u32[]{:S(2)}) collective-permute-start(f32[16,128]{1,0:T(8,128)S(1)} %get-tuple-element.42), channel_id=1, source_target_pairs={{0,12},{4,0},{8,4},{12,8},{1,13},{5,1},{9,5},{13,9},{2,14},{6,2},{... | collective-permute-start | bytes 24584 | tf_op jit(solution)/shard_map/ppermute | solution.py:37
  7.0 3.8 %shard_map.95 = (f32[6528,128]{1,0:T(8,128)S(1)}, f32[3840,128]{1,0:T(8,128)S(1)}, f32[1152,128]{1,0:T(8,128)S(1)}, f32[8,128]{1,0:T(8,128)S(1)}, s32[138]{0:T(256)S(1)}) custom-call(f32[3,18,24,128]{3,2,1,0:T(8,128)S(1)} %get-tuple-element.35.grid_ref.grid_in_ref, f32[3,64,128]{2,1,0:T(8,128)S(1)} %get-tuple-element.36.velocity_ref, ...), custom_call_target="tpu_custom_call" | custom-call | flops 12288000 | bytes 3072000 | tf_op jit(solution)/shard_map/pallas_call | solution.py:65
  10.8 0.0 collective-permute-done.2.edge_ref
  10.8 0.0 collective-permute-done.face_ref
  10.8 0.0 collective-permute-done.1.from_x_ref
  10.8 0.1 shard_map.97
  10.9 0.0 collective-permute-start.4
  10.9 3.1 %collective-permute-start.3 = (f32[56,128]{1,0:T(8,128)S(1)}, f32[56,128]{1,0:T(8,128)S(1)}, u32[]{:S(2)}, u32[]{:S(2)}) collective-permute-start(f32[56,128]{1,0:T(8,128)S(1)} %shard_map.97), channel_id=1, source_target_pairs={{0,1},{1,0},{2,3},{3,2},{4,5},{5,4},{6,7},{7,6},{8,9},{9,8},{10,11... | collective-permute-start | bytes 86024 | tf_op jit(solution)/shard_map/ppermute | solution.py:55
  14.1 0.7 %shard_map.96 = (f32[3,18,24,128]{3,2,1,0:T(8,128)S(1)}, f32[6528,128]{1,0:T(8,128)S(1)}, f32[128,128]{1,0:T(8,128)S(1)}) custom-call(f32[3,18,24,128]{3,2,1,0:T(8,128)S(1)} %get-tuple-element.35.grid_ref.grid_in_ref, f32[6528,128]{1,0:T(8,128)S(1)} %get-tuple-element.41.lines_in_ref, ...), custom_call_target="tpu_custom_call", output_to_operand_aliasing={{0}: (0, {}), {1}: (1, {})} | custom-call | flops 4096000 | bytes 1024000 | tf_op jit(solution)/shard_map/pallas_call | solution.py:65
  14.8 8.0 %shard_map.99 = (f32[576,128]{1,0:T(8,128)S(1)}, f32[3840,128]{1,0:T(8,128)S(1)}) custom-call(s32[138]{0:T(256)S(1)} %get-tuple-element.49.list_ref, s32[64]{0:T(128)S(1)} %get-tuple-element.40.brick_ref, f32[6528,128]{1,0:T(8,128)S(1)} %get-tuple-element.45.lines_in_ref.lines_ref, ...), custom_call_target="tpu_custom_call", output_to_operand_aliasing={{1}: (4, {})} | custom-call | flops 24576000 | bytes 6144000 | tf_op jit(solution)/shard_map/pallas_call | solution.py:65
  22.8 0.0 collective-permute-done.4.second_ref
  22.8 0.0 collective-permute-done.3.first_ref
  22.8 1.5 %shard_map.98 = (f32[3,18,24,128]{3,2,1,0:T(8,128)S(1)}, f32[6528,128]{1,0:T(8,128)S(1)}) custom-call(f32[3,18,24,128]{3,2,1,0:T(8,128)S(1)} %get-tuple-element.44.grid_in_ref, f32[6528,128]{1,0:T(8,128)S(1)} %get-tuple-element.45.lines_in_ref.lines_ref, ...), custom_call_target="tpu_custom_call", output_to_operand_aliasing={{0}: (0, {}), {1}: (1, {})} | custom-call | flops 4096000 | bytes 1024000 | tf_op jit(solution)/shard_map/pallas_call | solution.py:65
  24.3 2.9 %shard_map.100 = (f32[576,128]{1,0:T(8,128)S(1)}, f32[3840,128]{1,0:T(8,128)S(1)}) custom-call(s32[138]{0:T(256)S(1)} %get-tuple-element.49.list_ref, s32[64]{0:T(128)S(1)} %get-tuple-element.40.brick_ref, f32[6528,128]{1,0:T(8,128)S(1)} %get-tuple-element.50.lines_ref, ...), custom_call_target="tpu_custom_call", output_to_operand_aliasing={{1}: (4, {}), {0}: (5, {})} | custom-call | flops 8192000 | bytes 2048000 | tf_op jit(solution)/shard_map/pallas_call | solution.py:65
  27.2 0.2 shard_map.101.deposit_ref
  27.4 0.7 %shard_map.103.leaving_ref = f32[6,64,128]{2,1,0:T(8,128)S(1)} custom-call(s32[6,8]{1,0:T(8,128)S(1)} %get-tuple-element.56.crossing_ref, f32[576,128]{1,0:T(8,128)S(1)} %get-tuple-element.57.state_ref), custom_call_target="tpu_custom_call" | custom-call | flops 2048000 | bytes 512000 | tf_op jit(solution)/shard_map/pallas_call | solution.py:65
  28.2 0.8 %shard_map.104 = (f32[2,136,128]{2,1,0:T(8,128)S(1)}, f32[48,128]{1,0:T(8,128)S(1)}, f32[16,128]{1,0:T(8,128)S(1)}) custom-call(f32[6,64,128]{2,1,0:T(8,128)S(1)} %shard_map.103.leaving_ref, f32[3,18,24,128]{3,2,1,0:T(8,128)S(1)} %get-tuple-element.48.grid_ref, f32[2,3,17,24,128]{4,3,2,1,0:T(8,128)S(1)} %shard_map.101.deposit_ref), custom_call_target="tpu_custom_call" | custom-call | flops 2048000 | bytes 512000 | tf_op jit(solution)/shard_map/pallas_call | solution.py:65
  29.0 0.1 collective-permute-start.6
  29.1 1.6 %collective-permute-start.5 = (f32[136,128]{1,0:T(8,128)S(1)}, f32[136,128]{1,0:T(8,128)S(1)}, u32[]{:S(2)}, u32[]{:S(2)}) collective-permute-start(f32[136,128]{1,0:T(8,128)S(1)} %get-tuple-element.68), channel_id=1, source_target_pairs={{0,1},{1,0},{2,3},{3,2},{4,5},{5,4},{6,7},{7,6},{8,9},{9,8},{10,11... | collective-permute-start | bytes 208904 | tf_op jit(solution)/shard_map/ppermute | solution.py:55
  30.7 0.0 collective-permute-done.6.second_ref.y2_ref
  30.7 3.0 %collective-permute-done.5.first_ref.y1_ref = f32[136,128]{1,0:T(8,128)S(1)} collective-permute-done((f32[136,128]{1,0:T(8,128)S(1)}, f32[136,128]{1,0:T(8,128)S(1)}, u32[]{:S(2)}, u32[]{:S(2)}) %collective-permute-start.5) | collective-permute-done | bytes 69664 | tf_op jit(solution)/shard_map/ppermute | solution.py:55
  33.7 1.6 %collective-permute-start.7 = (f32[176,128]{1,0:T(8,128)S(1)}, f32[176,128]{1,0:T(8,128)S(1)}, u32[]{:S(2)}, u32[]{:S(2)}) collective-permute-start(f32[176,128]{1,0:T(8,128)S(1)} %get-tuple-element.61), channel_id=1, source_target_pairs={{0,16},{16,0},{1,17},{17,1},{2,18},{18,2},{3,19},{19,3},{4,20},{20... | collective-permute-start | bytes 270344 | tf_op jit(solution)/shard_map/ppermute | solution.py:37
  35.3 0.0 collective-permute-start.9
  35.3 0.6 %collective-permute-start.8 = (f32[80,128]{1,0:T(8,128)S(1)}, f32[80,128]{1,0:T(8,128)S(1)}, u32[]{:S(2)}, u32[]{:S(2)}) collective-permute-start(f32[80,128]{1,0:T(8,128)S(1)} %get-tuple-element.70), channel_id=1, source_target_pairs={{0,4},{4,0},{8,12},{12,8},{1,5},{5,1},{9,13},{13,9},{2,6},{6,2},{1... | collective-permute-start | bytes 122888 | tf_op jit(solution)/shard_map/ppermute | solution.py:44
  35.9 0.1 collective-permute-start.10
  36.0 0.6 %shard_map.102.base_ref = f32[3,16,16,128]{3,2,1,0:T(8,128)S(1)} custom-call(f32[3,18,24,128]{3,2,1,0:T(8,128)S(1)} %get-tuple-element.48.grid_ref, f32[2,3,17,24,128]{4,3,2,1,0:T(8,128)S(1)} %shard_map.101.deposit_ref, f32[128,128]{1,0:T(8,128)S(1)} %get-tuple-element.46.top_in_ref.top_ref), custom_call_target="tpu_custom_call" | custom-call | flops 4096000 | bytes 1024000 | tf_op jit(solution)/shard_map/pallas_call | solution.py:65
  36.7 3.2 %collective-permute-done.10.edge_ref = f32[16,128]{1,0:T(8,128)S(1)} collective-permute-done((f32[16,128]{1,0:T(8,128)S(1)}, f32[16,128]{1,0:T(8,128)S(1)}, u32[]{:S(2)}, u32[]{:S(2)}) %collective-permute-start.10) | collective-permute-done | bytes 8224 | tf_op jit(solution)/shard_map/ppermute | solution.py:61
  39.9 0.0 collective-permute-done.9.z2_ref
  39.9 0.0 collective-permute-done.8.z1_ref
  39.9 0.0 collective-permute-done.7.x_ref.minus_x_ref
  39.9 1.4 %shard_map.106 = (f32[3,16,16,128]{3,2,1,0:T(8,128)}, f32[6,7,8,128]{3,2,1,0:T(8,128)}, f32[3,64,128]{2,1,0:T(8,128)}) custom-call(f32[3,16,16,128]{3,2,1,0:T(8,128)S(1)} %shard_map.102.base_ref, f32[136,128]{1,0:T(8,128)S(1)} %collective-permute-done.5.first_ref.y1_ref, f32[136,128]{1,0:T(8,128)S(1)} %collective-permute-done.6.second_ref.y2_ref, ...), custom_call_target="tpu_custom_call" | custom-call | tf_op jit(solution)/shard_map/pallas_call | solution.py:65
  (3 shorter events, 0.0 us)
Async XLA Ops:
  2.2 8.6 %collective-permute-start.1 = (f32[48,128]{1,0:T(8,128)S(1)}, f32[48,128]{1,0:T(8,128)S(1)}, u32[]{:S(2)}, u32[]{:S(2)}) collective-permute-start(f32[48,128]{1,0:T(8,128)S(1)} %get-tuple-element.43), channel_id=1, source_target_pairs={{0,16},{16,0},{1,17},{17,1},{2,18},{18,2},{3,19},{19,3},{4,20},{20... | collective-permute-start | bytes 73736 | tf_op jit(solution)/shard_map/ppermute | solution.py:37
  5.3 5.5 %collective-permute-start.2 = (f32[16,128]{1,0:T(8,128)S(1)}, f32[16,128]{1,0:T(8,128)S(1)}, u32[]{:S(2)}, u32[]{:S(2)}) collective-permute-start(f32[16,128]{1,0:T(8,128)S(1)} %get-tuple-element.42), channel_id=1, source_target_pairs={{0,28},{4,16},{8,20},{12,24},{16,12},{20,0},{24,4},{28,8},{1,29},{... | collective-permute-start | bytes 24584 | tf_op jit(solution)/shard_map/ppermute | solution.py:61
  5.8 4.9 %collective-permute-start = (f32[16,128]{1,0:T(8,128)S(1)}, f32[16,128]{1,0:T(8,128)S(1)}, u32[]{:S(2)}, u32[]{:S(2)}) collective-permute-start(f32[16,128]{1,0:T(8,128)S(1)} %get-tuple-element.42), channel_id=1, source_target_pairs={{0,12},{4,0},{8,4},{12,8},{1,13},{5,1},{9,5},{13,9},{2,14},{6,2},{... | collective-permute-start | bytes 24584 | tf_op jit(solution)/shard_map/ppermute | solution.py:37
  10.9 11.9 %collective-permute-start.4 = (f32[56,128]{1,0:T(8,128)S(1)}, f32[56,128]{1,0:T(8,128)S(1)}, u32[]{:S(2)}, u32[]{:S(2)}) collective-permute-start(f32[56,128]{1,0:T(8,128)S(1)} %shard_map.97), channel_id=1, source_target_pairs={{0,4},{3,7},{1,2},{2,1},{4,0},{7,3},{5,6},{6,5},{8,12},{11,15},{9,... | collective-permute-start | bytes 86024 | tf_op jit(solution)/shard_map/ppermute | solution.py:55
  10.9 11.9 %collective-permute-start.3 = (f32[56,128]{1,0:T(8,128)S(1)}, f32[56,128]{1,0:T(8,128)S(1)}, u32[]{:S(2)}, u32[]{:S(2)}) collective-permute-start(f32[56,128]{1,0:T(8,128)S(1)} %shard_map.97), channel_id=1, source_target_pairs={{0,1},{1,0},{2,3},{3,2},{4,5},{5,4},{6,7},{7,6},{8,9},{9,8},{10,11... | collective-permute-start | bytes 86024 | tf_op jit(solution)/shard_map/ppermute | solution.py:55
  29.0 1.7 %collective-permute-start.6 = (f32[136,128]{1,0:T(8,128)S(1)}, f32[136,128]{1,0:T(8,128)S(1)}, u32[]{:S(2)}, u32[]{:S(2)}) collective-permute-start(f32[136,128]{1,0:T(8,128)S(1)} %get-tuple-element.67), channel_id=1, source_target_pairs={{0,4},{3,7},{1,2},{2,1},{4,0},{7,3},{5,6},{6,5},{8,12},{11,15},{9,... | collective-permute-start | bytes 208904 | tf_op jit(solution)/shard_map/ppermute | solution.py:55
  29.1 4.6 %collective-permute-start.5 = (f32[136,128]{1,0:T(8,128)S(1)}, f32[136,128]{1,0:T(8,128)S(1)}, u32[]{:S(2)}, u32[]{:S(2)}) collective-permute-start(f32[136,128]{1,0:T(8,128)S(1)} %get-tuple-element.68), channel_id=1, source_target_pairs={{0,1},{1,0},{2,3},{3,2},{4,5},{5,4},{6,7},{7,6},{8,9},{9,8},{10,11... | collective-permute-start | bytes 208904 | tf_op jit(solution)/shard_map/ppermute | solution.py:55
  33.7 6.2 %collective-permute-start.7 = (f32[176,128]{1,0:T(8,128)S(1)}, f32[176,128]{1,0:T(8,128)S(1)}, u32[]{:S(2)}, u32[]{:S(2)}) collective-permute-start(f32[176,128]{1,0:T(8,128)S(1)} %get-tuple-element.61), channel_id=1, source_target_pairs={{0,16},{16,0},{1,17},{17,1},{2,18},{18,2},{3,19},{19,3},{4,20},{20... | collective-permute-start | bytes 270344 | tf_op jit(solution)/shard_map/ppermute | solution.py:37
  35.3 4.6 %collective-permute-start.9 = (f32[80,128]{1,0:T(8,128)S(1)}, f32[80,128]{1,0:T(8,128)S(1)}, u32[]{:S(2)}, u32[]{:S(2)}) collective-permute-start(f32[80,128]{1,0:T(8,128)S(1)} %get-tuple-element.69), channel_id=1, source_target_pairs={{0,12},{4,8},{8,4},{12,0},{1,13},{5,9},{9,5},{13,1},{2,14},{6,10},... | collective-permute-start | bytes 122888 | tf_op jit(solution)/shard_map/ppermute | solution.py:44
  35.3 4.6 %collective-permute-start.8 = (f32[80,128]{1,0:T(8,128)S(1)}, f32[80,128]{1,0:T(8,128)S(1)}, u32[]{:S(2)}, u32[]{:S(2)}) collective-permute-start(f32[80,128]{1,0:T(8,128)S(1)} %get-tuple-element.70), channel_id=1, source_target_pairs={{0,4},{4,0},{8,12},{12,8},{1,5},{5,1},{9,13},{13,9},{2,6},{6,2},{1... | collective-permute-start | bytes 122888 | tf_op jit(solution)/shard_map/ppermute | solution.py:44
  35.9 4.0 %collective-permute-start.10 = (f32[16,128]{1,0:T(8,128)S(1)}, f32[16,128]{1,0:T(8,128)S(1)}, u32[]{:S(2)}, u32[]{:S(2)}) collective-permute-start(f32[16,128]{1,0:T(8,128)S(1)} %get-tuple-element.63), channel_id=1, source_target_pairs={{0,20},{4,24},{8,28},{12,16},{16,4},{20,8},{24,12},{28,0},{1,21},{... | collective-permute-start | bytes 24584 | tf_op jit(solution)/shard_map/ppermute | solution.py:61

commit v4 on v2

--- a/solution.py
+++ b/solution.py
@@ -237,16 +237,14 @@
         lay_out_top(turned_ref, lines_ref, q, comps, count_x, count_y, size_z)
 
 
-def halo_y_kernel(size_y, grid_in_ref, lines_in_ref, top_in_ref, first_ref, second_ref, grid_ref, lines_ref, turned_ref):
+def halo_y_kernel(size_y, grid_in_ref, lines_in_ref, top_in_ref, from_y_ref, grid_ref, lines_ref, turned_ref):
     comps, size_x, size_z = grid_ref.shape[0], grid_ref.shape[1] - 2, grid_ref.shape[3]
     count_x, count_y = size_x // BX, size_y // BY
     inside = lax.axis_index("gy") != lax.axis_size("gy") - 1
-    even = odd("gy") == 0
     kept = (row_ids(8) == 0) & inside
 
     def line_at(row):
-        line = jnp.where(even, first_ref[row : row + 1], second_ref[row : row + 1])
-        return jnp.where(kept, jnp.broadcast_to(line, (8, LANES)), 0.0)
+        return jnp.where(kept, jnp.broadcast_to(from_y_ref[row : row + 1], (8, LANES)), 0.0)
 
     for c in range(comps):
         for x in range(size_x + 1):
@@ -263,7 +261,7 @@
     late, comps, count_x, count_y, count_z, rows_z,
     list_ref, brick_ref, lines_ref, table_ref, *refs,
 ):
-    state_ref, deposit_ref = refs[-2:]
+    state_ref, deposit_ref, push_ref, spread_ref = refs[-4:]
     nblocks = brick_ref.shape[0]
     room = (list_ref.shape[0] - 2) // 2
     sub = row_ids(8)
@@ -274,20 +272,19 @@
     def hat(rows, inside, along):
         return jnp.where(rows == inside, 1.0 - along, 0.0) + jnp.where(rows == inside + 1.0, along, 0.0)
 
-    def loaded(at):
+    def place_of(at):
         k = list_ref[at]
         brick = jnp.where(k < nblocks, brick_ref[jnp.minimum(k, nblocks - 1)], 0)
         brick_x = lax.div(brick, count_y * count_z)
         brick_y = lax.rem(lax.div(brick, count_z), count_y)
-        brick_z = lax.rem(brick, count_z)
-        sel = jnp.where(brick_z == count_z - 1, 1, 0)
-        pair = brick_x * count_y + brick_y
-        start = pl.multiple_of((sel * count_x * count_y + pair) * comps * SPREAD, 8)
+        return k, brick_x * count_y + brick_y, lax.rem(brick, count_z)
+
+    def loaded(at):
+        k, pair, brick_z = place_of(at)
         first = pl.multiple_of(pair * comps * rows_z + brick_z * BZ, 8)
         window = jnp.concatenate([lines_ref[pl.ds(first + c * rows_z, REACH_Z)] for c in range(comps)], axis=0)
         table = table_ref[pl.ds(pl.multiple_of(k * TABLE_ROWS, TABLE_ROWS), TABLE_ROWS)]
-        rows = [table[i : i + 1] for i in range(TABLE_ROWS)]
-        return k, start, brick_z * BZ, window, rows
+        return k, window, [table[i : i + 1] for i in range(TABLE_ROWS)]
 
     def weighted(rows):
         weight_y = hat(row_y, rows[IN_Y], rows[ALONG_Y])
@@ -311,9 +308,9 @@
         main, rest = parts_of(jnp.concatenate(pushed, axis=0))
         return tile, jnp.concatenate([main, gap, rest, gap], axis=0)
 
-    def pair_of(one, two):
+    def gathered(one, two):
         tables, windows, weights = [], [], []
-        for _, _, _, window, rows in (one, two):
+        for _, window, rows in (one, two):
             weight_z, main, rest = weighted(rows)
             weights.append((weight_z, main, rest))
             unused = jnp.zeros((LANES - 3 * SPREAD, LANES), jnp.float32)
@@ -325,48 +322,66 @@
         )
         height = comps * REACH_Z
         tiles, pushes, spreads = [], [], []
-        for i, (_, _, _, _, rows) in enumerate((one, two)):
+        for i, (_, _, rows) in enumerate((one, two)):
             mine = seen[i * height : (i + 1) * height, i * LANES : (i + 1) * LANES]
             tile, push = stepped(mine, weights[i][0], rows)
             tiles.append(tile)
             pushes.append(push)
             spreads.extend(weights[i][1:])
-        shares = lax.dot_general(
-            jnp.concatenate(spreads, axis=0).astype(jnp.bfloat16), jnp.concatenate(pushes, axis=0).astype(jnp.bfloat16),
-            (((1,), (1,)), ((), ())), preferred_element_type=jnp.float32,
-        )
+        return tiles, jnp.concatenate(pushes, axis=0).astype(jnp.bfloat16), jnp.concatenate(spreads, axis=0).astype(jnp.bfloat16)
+
+    def shared(push, spread):
+        shares = lax.dot_general(spread, push, (((1,), (1,)), ((), ())), preferred_element_type=jnp.float32)
         results = []
-        for i, tile in enumerate(tiles):
+        for i in (0, 1):
             mine = shares[2 * i * SPREAD : 2 * (i + 1) * SPREAD, i * LANES : (i + 1) * LANES]
             mine = mine[:SPREAD] + mine[SPREAD:]
-            results.append((tile, mine + pltpu.roll(mine, LANES // 2, 1)))
+            results.append(mine + pltpu.roll(mine, LANES // 2, 1))
         return results
 
     count = list_ref[2 * room + late]
-
-    @pl.loop(0, (count + UNROLL - 1) // UNROLL)
+    groups = (count + UNROLL - 1) // UNROLL
+    push_ref[...] = jnp.zeros_like(push_ref)
+    spread_ref[...] = jnp.zeros_like(spread_ref)
+
+    @pl.loop(0, groups + 1)
     def _(group):
-        at = late * room + group * UNROLL
-        taken = [loaded(at + u) for u in range(UNROLL)]
-        results = []
+        now = late * room + jnp.maximum(jnp.minimum(group, groups - 1), 0) * UNROLL
+        before = late * room + jnp.maximum(group - 1, 0) * UNROLL
+        taken = [loaded(now + u) for u in range(UNROLL)]
+        old = [(push_ref[i], spread_ref[i]) for i in range(UNROLL // 2)]
+        shares = []
+        for push, spread in old:
+            shares.extend(shared(push, spread))
+        tiles, fresh = [], []
         for u in range(0, UNROLL, 2):
-            results.extend(pair_of(taken[u], taken[u + 1]))
-        parts = []
-        for (_, _, first_z, _, _), (_, shares) in zip(taken, results):
+            both, push, spread = gathered(taken[u], taken[u + 1])
+            tiles.extend(both)
+            fresh.append((push, spread))
+        sums = []
+        for u in range(UNROLL):
+            _, pair, brick_z = place_of(before + u)
+            first_z = brick_z * BZ
             within = ((lane - first_z) & (LANES - 1)) < REACH_Z
-            parts.append([])
+            parts = []
             for c in range(comps):
                 shift = (first_z - c * REACH_Z + LANES) & (LANES - 1)
                 for a in range(REACH_X):
-                    part = pltpu.roll(shares[a * REACH_Y : (a + 1) * REACH_Y], shift, 1)
-                    parts[-1].append(jnp.where(within, part, 0.0))
-        for (k, _, _, _, _), (tile, _) in zip(taken, results):
+                    part = pltpu.roll(shares[u][a * REACH_Y : (a + 1) * REACH_Y], shift, 1)
+                    parts.append(jnp.where(within, part, 0.0))
+            sel = jnp.where(brick_z == count_z - 1, 1, 0)
+            start = pl.multiple_of((sel * count_x * count_y + pair) * comps * SPREAD, 8)
+            sums.append((start, parts))
+        for start, parts in sums:
+            spots = [pl.ds(start + i * REACH_Y, REACH_Y) for i in range(comps * REACH_X)]
+            totals = [deposit_ref[spot] + part for spot, part in zip(spots, parts)]
+            for spot, total in zip(spots, totals):
+                deposit_ref[spot] = total
+        for (k, _, _), tile in zip(taken, tiles):
             state_ref[pl.ds(pl.multiple_of(STATE * k, STATE), STATE)] = tile
-        for (_, start, _, _, _), mine in zip(taken, parts):
-            spots = [pl.ds(start + i * REACH_Y, REACH_Y) for i in range(comps * REACH_X)]
-            sums = [deposit_ref[spot] + part for spot, part in zip(spots, mine)]
-            for spot, total in zip(spots, sums):
-                deposit_ref[spot] = total
+        for i, (push, spread) in enumerate(fresh):
+            push_ref[i] = push
+            spread_ref[i] = spread
 
 
 def merge_kernel(tiles_ref, plane_ref):
@@ -401,10 +416,9 @@
                 plane_ref[sel, c, x, count_y * BY :] = carried
 
 
-def leave_kernel(crossing_ref, state_ref, leaving_ref, velocity_ref):
-    comps, nblocks = velocity_ref.shape[:2]
+def leave_kernel(crossing_ref, state_ref, leaving_ref):
     slots = crossing_ref.shape[1]
-    velocity = [state_ref[pl.ds(c, nblocks, stride=STATE)] for c in range(comps)]
+
     for face in range(6):
         tiles = []
         for slot in range(slots):
@@ -413,37 +427,42 @@
             live = jnp.full((STATE, LANES), block, jnp.int32) >= 0
             tiles.append(jnp.where(live, state_ref[spot], 0.0))
         leaving_ref[face] = jnp.concatenate(tiles, axis=0)
-    for c in range(comps):
-        velocity_ref[c] = velocity[c]
-
-
-def send_kernel(push, diffuse, leaving_ref, grid_ref, deposit_ref, y_ref, x_ref, z_ref):
+
+
+def send_kernel(push, diffuse, leaving_ref, grid_ref, deposit_ref, y_ref, x_ref, z_ref, face_ref):
     comps, size_x = grid_ref.shape[0], grid_ref.shape[1] - 2
     size_y = z_ref.shape[0]
     rows = leaving_ref.shape[1]
-    first = odd("gy") == 0
+    first = jnp.full((rows, LANES), odd("gy")) == 0
     y_ref[0, 0:rows] = jnp.where(first, leaving_ref[2], leaving_ref[3])
     y_ref[1, 0:rows] = jnp.where(first, leaving_ref[3], leaving_ref[2])
     lane = lane_ids(ROWS_Y)
-    face = jnp.zeros((ROWS_Y, LANES), jnp.float32)
-    for c in range(comps):
+    sub = row_ids(ROWS_Y)
+    face_ref[...] = jnp.zeros_like(face_ref)
+
+    @pl.loop(0, comps)
+    def _(c):
+        face = jnp.zeros((ROWS_Y, LANES), jnp.float32)
+        lines = jnp.zeros((ROWS_Y, LANES), jnp.float32)
         for x in range(size_x + 1):
             beyond = push * deposit_ref[1, c, x]
+            top = push * deposit_ref[0, c, x, size_y:] + jnp.where(lane[:8] == 0, 0.0, beyond[size_y:])
             if x < size_x:
-                behind = diffuse * turned(grid_ref[c, x + 1, 0:size_y], 1)
-                beyond = jnp.concatenate([beyond[:size_y] + behind, beyond[size_y:]], axis=0)
-            place = PACK * c + x
-            face = jnp.where(lane == place, turned(beyond, place), face)
-        wrapped = jnp.where(lane_ids(size_x) == 0, 0.0, deposit_ref[1, c, 0:size_x, size_y])
-        line = diffuse * grid_ref[c, 1 : size_x + 1, size_y - 1] + push * (deposit_ref[0, c, 0:size_x, size_y] + wrapped)
-        y_ref[0, rows + c * ROWS_Y : rows + c * ROWS_Y + size_x] = line
-        wrapped = jnp.where(lane_ids(ROWS_Y) == 0, 0.0, deposit_ref[1, c, size_x])
-        total = push * (deposit_ref[0, c, size_x] + wrapped)
-        x_ref[c * size_y : (c + 1) * size_y] = diffuse * grid_ref[c, size_x, 0:size_y] + total[:size_y]
-        at = rows + c * ROWS_Y + size_x
-        y_ref[0, at : at + 8] = total[size_y:]
-    z_ref[...] = face[:size_y]
-    y_ref[0, rows + size_x + 1 : rows + size_x + 2] = face[size_y : size_y + 1]
+                here = grid_ref[c, x + 1, 0:size_y]
+                beyond = jnp.concatenate([beyond[:size_y] + diffuse * turned(here, 1), beyond[size_y:]], axis=0)
+                top = top[0:1] + diffuse * here[size_y - 1 :]
+            else:
+                here = grid_ref[c, size_x, 0:size_y]
+                total = push * deposit_ref[0, c, x, 0:size_y] + jnp.where(lane[:size_y] == 0, 0.0, beyond[:size_y])
+                x_ref[pl.ds(pl.multiple_of(c * size_y, 8), size_y)] = diffuse * here + total
+                top = top[0:1]
+            lines = jnp.where(sub == x, top, lines)
+            face = jnp.where(lane == x, turned(beyond, x), face)
+        y_ref[0, pl.ds(pl.multiple_of(rows + c * ROWS_Y, 8), ROWS_Y)] = lines
+        face_ref[...] = face_ref[...] + pltpu.roll(face, PACK * c, 1)
+
+    z_ref[...] = face_ref[0:size_y]
+    y_ref[0, rows + size_x + 1 : rows + size_x + 2] = face_ref[size_y : size_y + 1]
     y_ref[1, rows:] = y_ref[0, rows:]
 
 
@@ -491,7 +510,8 @@
 
 
 def finish_kernel(
-    count, base_ref, y1_ref, y2_ref, x_ref, minus_x_ref, z1_ref, z2_ref, edge_ref, gas_ref, arrivals_ref
+    count, base_ref, y1_ref, y2_ref, x_ref, minus_x_ref, z1_ref, z2_ref, edge_ref, state_ref,
+    gas_ref, arrivals_ref, velocity_ref,
 ):
     comps, size_x, size_y, _ = base_ref.shape
     first_row, first_lane = row_ids(size_y) == 0, lane_ids(size_y) == 0
@@ -526,6 +546,8 @@
         z1, z2 = rows_of(z1_ref), rows_of(z2_ref)
         arrivals_ref[4, i] = jnp.where(from_first, z1, z2)
         arrivals_ref[5, i] = jnp.where(from_first, z2, z1)
+    for c in range(comps):
+        velocity_ref[c] = state_ref[pl.ds(c, velocity_ref.shape[1], stride=STATE)]
 
 
 def per_device(gas_field, velocity, fraction, response, cell_index, brick_index, crossing):
@@ -566,7 +588,7 @@
     )
     line_rows = -(-(comps * size_x + comps + 1) // 8) * 8
     (y_lines,) = call(y_lines_kernel, [(line_rows, LANES)], grid, from_z, from_x, from_xz, ready)
-    y1, y2 = swapped_y((y_lines, y_lines))
+    from_y = moved_along(y_lines, "gy", -1)
     square = pltpu.VMEM((LANES, LANES), jnp.float32)
     grid, lines, top = call(
         halo_xz_kernel, [grid_shape, lines_shape, (LANES, LANES)], grid, lines, from_z, from_x, from_xz,
@@ -578,24 +600,26 @@
             functools.partial(blocks_kernel, late, comps, size_x // BX, size_y // BY, size_z // BZ, rows_z),
             [(STATE * spare, LANES), deposit_shape], blocks, brick_index, lines, table, deposit, *state,
             smem=(0, 1), aliases={4: 1, 5: 0} if state else {4: 1}, cycles=6000 - 4000 * late,
+            scratch=(
+                pltpu.VMEM((UNROLL // 2, 2 * LANES, LANES), jnp.bfloat16),
+                pltpu.VMEM((UNROLL // 2, 4 * SPREAD, LANES), jnp.bfloat16),
+            ),
         )
 
     state, deposit = advance(0, lines, deposit)
     grid, lines = call(
-        functools.partial(halo_y_kernel, size_y), [grid_shape, lines_shape], grid, lines, top, y1, y2,
+        functools.partial(halo_y_kernel, size_y), [grid_shape, lines_shape], grid, lines, top, from_y,
         aliases={0: 0, 1: 1}, scratch=(square,), cycles=1000,
     )
     state, deposit = advance(1, lines, deposit, state)
 
     (deposit,) = call(merge_kernel, [(2, comps, size_x + 1, ROWS_Y, LANES)], deposit, cycles=500)
     count = STATE * crossing.shape[1]
-    leaving, velocity_next = call(
-        leave_kernel, [(6, count, LANES), (comps, nblocks, LANES)], crossing, state, smem=(0,), cycles=500,
-    )
+    (leaving,) = call(leave_kernel, [(6, count, LANES)], crossing, state, smem=(0,), cycles=500)
     to_y, to_x, to_z = call(
         functools.partial(send_kernel, push, diffuse),
         [(2, count + comps * ROWS_Y, LANES), (comps * size_y, LANES), (size_y, LANES)],
-        leaving, grid, deposit, cycles=500,
+        leaving, grid, deposit, cycles=500, scratch=(pltpu.VMEM((ROWS_Y, LANES), jnp.float32),),
     )
     y1, y2 = swapped_y((to_y[0], to_y[1]))
     (base,) = call(
@@ -612,9 +636,10 @@
     z1, z2 = swapped_z((to_z[0], to_z[1]))
     got_xz = moved_diagonally(to_xz, 1)
     got_mx = got_x if both else moved_along(leaving[1], "gx", -1)
-    gas_next, arrivals = call(
-        functools.partial(finish_kernel, count), [gas_field.shape, (6, 7, crossing.shape[1], LANES)],
-        base, y1, y2, got_x, got_mx, z1, z2, got_xz,
+    gas_next, arrivals, velocity_next = call(
+        functools.partial(finish_kernel, count),
+        [gas_field.shape, (6, 7, crossing.shape[1], LANES), (comps, nblocks, LANES)],
+        base, y1, y2, got_x, got_mx, z1, z2, got_xz, state,
     )
     return gas_next, jnp.transpose(velocity_next, (1, 0, 2)), jnp.transpose(arrivals, (0, 2, 1, 3))
 

time: 36.8 us -> 33.9 us (0.921)
  Pallas kernels: 17.3 us -> 13.9 us
  waiting for transfers between devices: 6.18 us -> 8.01 us
  starting transfers between devices: 12.2 us -> 11.2 us
    ppermute x2 -> x1, starting transfers between devices: 4.79 us -> 0.07 us  [swapped_y(): lax.ppermute(blocks[0], 'gy', first)]
    ppermute x3 -> x4, starting transfers between devices: 5.75 us -> 9.38 us  [moved_along(): lax.ppermute(block, axis, [(i, (i + distance) % count) for i in range(cou...]
    pallas_call x13, Pallas kernels: 17.3 us -> 13.9 us  [call(): pl.pallas_call(body, out_shape=[o if isinstance(o, jax.ShapeDtypeStruct)...]
    ppermute x2 -> x1, waiting for transfers between devices: 0.01 us -> 1.17 us  [swapped_y(): lax.ppermute(blocks[1], ('gz', 'gy'), second)]
    ppermute x2 -> x1, waiting for transfers between devices: 2.95 us -> 3.35 us  [swapped_y(): lax.ppermute(blocks[0], 'gy', first)]
  transfers between devices with their start and end apart: 11 -> 10, of which waited for: 2 -> 3; matrix products, arithmetic and copies ran while one was open for 0% -> 0% of each run, Pallas kernels for 22% -> 22%
where the time goes in v4:
time: 33.9 us
  Pallas kernels  13.9 us (41%)
  starting transfers between devices  11.2 us (33%)
  waiting for transfers between devices  8.01 us (24%)
  between operations  0.77 us (2%)
    pallas_call x13, Pallas kernels, call(): pl.pallas_call(body, out_shape=[o if isinstance(o, jax.ShapeDtypeStruct)...  13.9 us
    ppermute x4, starting transfers between devices, moved_along(): lax.ppermute(block, axis, [(i, (i + distance) % count) for i in range(cou...  9.38 us
    ppermute x2, waiting for transfers between devices, moved_diagonally(): return lax.ppermute(block, ('gx', 'gz'), route)  3.48 us
    ppermute x1, waiting for transfers between devices, swapped_y(): lax.ppermute(blocks[0], 'gy', first)  3.35 us
    ppermute x1, waiting for transfers between devices, swapped_y(): lax.ppermute(blocks[1], ('gz', 'gy'), second)  1.17 us
    ppermute x1, starting transfers between devices, swapped_z(): lax.ppermute(blocks[0], 'gz', first)  0.95 us
    ppermute x2, starting transfers between devices, moved_diagonally(): return lax.ppermute(block, ('gx', 'gz'), route)  0.69 us
  transfers between devices with their start and end apart: 10, of which 3 were waited for; matrix products, arithmetic and copies ran while one was open for 0% of the time, Pallas kernels for 22%

profile of v4, /device:TPU:0, one launch (start us, length us, event | category | flops | bytes accessed | tf_op | source)
XLA Modules:
  0.0 33.9 jit_solution(8337275817398489657)
XLA Ops:
  0.6 1.2 %shard_map.94 = (f32[3,18,24,128]{3,2,1,0:T(8,128)S(1)}, f32[16,128]{1,0:T(8,128)S(1)}, f32[48,128]{1,0:T(8,128)S(1)}, f32[3,64,128]{2,1,0:T(8,128)S(1)}, f32[3,...) custom-call(f32[3,16,16,128]{3,2,1,0:T(8,128)} %gas_ref.1, ...), custom_call_target="tpu_custom_call" | custom-call | tf_op jit(solution)/shard_map/pallas_call | solution.py:65
  1.9 3.0 %collective-permute-start.1 = (f32[48,128]{1,0:T(8,128)S(1)}, f32[48,128]{1,0:T(8,128)S(1)}, u32[]{:S(2)}, u32[]{:S(2)}) collective-permute-start(f32[48,128]{1,0:T(8,128)S(1)} %get-tuple-element.43), channel_id=1, source_target_pairs={{0,16},{16,0},{1,17},{17,1},{2,18},{18,2},{3,19},{19,3},{4,20},{20... | collective-permute-start | bytes 73736 | tf_op jit(solution)/shard_map/ppermute | solution.py:37
  4.9 0.6 %collective-permute-start.2 = (f32[16,128]{1,0:T(8,128)S(1)}, f32[16,128]{1,0:T(8,128)S(1)}, u32[]{:S(2)}, u32[]{:S(2)}) collective-permute-start(f32[16,128]{1,0:T(8,128)S(1)} %get-tuple-element.42), channel_id=1, source_target_pairs={{0,28},{4,16},{8,20},{12,24},{16,12},{20,0},{24,4},{28,8},{1,29},{... | collective-permute-start | bytes 24584 | tf_op jit(solution)/shard_map/ppermute | solution.py:61
  5.5 1.1 %collective-permute-start = (f32[16,128]{1,0:T(8,128)S(1)}, f32[16,128]{1,0:T(8,128)S(1)}, u32[]{:S(2)}, u32[]{:S(2)}) collective-permute-start(f32[16,128]{1,0:T(8,128)S(1)} %get-tuple-element.42), channel_id=1, source_target_pairs={{0,12},{4,0},{8,4},{12,8},{1,13},{5,1},{9,5},{13,9},{2,14},{6,2},{... | collective-permute-start | bytes 24584 | tf_op jit(solution)/shard_map/ppermute | solution.py:37
  6.6 2.0 %shard_map.95 = (f32[6528,128]{1,0:T(8,128)S(1)}, f32[3840,128]{1,0:T(8,128)S(1)}, f32[1152,128]{1,0:T(8,128)S(1)}, f32[8,128]{1,0:T(8,128)S(1)}, s32[146]{0:T(256)S(1)}) custom-call(f32[3,18,24,128]{3,2,1,0:T(8,128)S(1)} %get-tuple-element.35.grid_ref.grid_in_ref, f32[3,64,128]{2,1,0:T(8,128)S(1)} %get-tuple-element.36.velocity_ref, ...), custom_call_target="tpu_custom_call" | custom-call | flops 12288000 | bytes 3072000 | tf_op jit(solution)/shard_map/pallas_call | solution.py:65
  8.7 0.0 collective-permute-done.2.edge_ref
  8.7 0.0 collective-permute-done.face_ref
  8.7 0.0 collective-permute-done.1.from_x_ref
  8.7 0.1 shard_map.97
  8.8 3.6 %collective-permute-start.3 = (f32[56,128]{1,0:T(8,128)S(1)}, f32[56,128]{1,0:T(8,128)S(1)}, u32[]{:S(2)}, u32[]{:S(2)}) collective-permute-start(f32[56,128]{1,0:T(8,128)S(1)} %shard_map.97), channel_id=1, source_target_pairs={{0,3},{1,0},{2,1},{3,2},{4,7},{5,4},{6,5},{7,6},{8,11},{9,8},{10,9... | collective-permute-start | bytes 86024 | tf_op jit(solution)/shard_map/ppermute | solution.py:37
  12.4 0.4 %shard_map.96 = (f32[3,18,24,128]{3,2,1,0:T(8,128)S(1)}, f32[6528,128]{1,0:T(8,128)S(1)}, f32[128,128]{1,0:T(8,128)S(1)}) custom-call(f32[3,18,24,128]{3,2,1,0:T(8,128)S(1)} %get-tuple-element.35.grid_ref.grid_in_ref, f32[6528,128]{1,0:T(8,128)S(1)} %get-tuple-element.41.lines_in_ref, ...), custom_call_target="tpu_custom_call", output_to_operand_aliasing={{0}: (0, {}), {1}: (1, {})} | custom-call | flops 4096000 | bytes 1024000 | tf_op jit(solution)/shard_map/pallas_call | solution.py:65
  12.8 4.5 %shard_map.99 = (f32[576,128]{1,0:T(8,128)S(1)}, f32[3840,128]{1,0:T(8,128)S(1)}) custom-call(s32[146]{0:T(256)S(1)} %get-tuple-element.49.list_ref, s32[64]{0:T(128)S(1)} %get-tuple-element.40.brick_ref, f32[6528,128]{1,0:T(8,128)S(1)} %get-tuple-element.45.lines_in_ref.lines_ref, ...), custom_call_target="tpu_custom_call", output_to_operand_aliasing={{1}: (4, {})} | custom-call | flops 24576000 | bytes 6144000 | tf_op jit(solution)/shard_map/pallas_call | solution.py:65
  17.3 0.0 collective-permute-done.3.from_y_ref
  17.3 0.6 %shard_map.98 = (f32[3,18,24,128]{3,2,1,0:T(8,128)S(1)}, f32[6528,128]{1,0:T(8,128)S(1)}) custom-call(f32[3,18,24,128]{3,2,1,0:T(8,128)S(1)} %get-tuple-element.44.grid_in_ref, f32[6528,128]{1,0:T(8,128)S(1)} %get-tuple-element.45.lines_in_ref.lines_ref, ...), custom_call_target="tpu_custom_call", output_to_operand_aliasing={{0}: (0, {}), {1}: (1, {})} | custom-call | flops 4096000 | bytes 1024000 | tf_op jit(solution)/shard_map/pallas_call | solution.py:65
  17.9 2.1 %shard_map.100 = (f32[576,128]{1,0:T(8,128)S(1)}, f32[3840,128]{1,0:T(8,128)S(1)}) custom-call(s32[146]{0:T(256)S(1)} %get-tuple-element.49.list_ref, s32[64]{0:T(128)S(1)} %get-tuple-element.40.brick_ref, f32[6528,128]{1,0:T(8,128)S(1)} %get-tuple-element.50.lines_ref, ...), custom_call_target="tpu_custom_call", output_to_operand_aliasing={{1}: (4, {}), {0}: (5, {})} | custom-call | flops 8192000 | bytes 2048000 | tf_op jit(solution)/shard_map/pallas_call | solution.py:65
  20.0 0.1 shard_map.101.deposit_ref
  20.1 0.7 %shard_map.103.leaving_ref = f32[6,64,128]{2,1,0:T(8,128)S(1)} custom-call(s32[6,8]{1,0:T(8,128)S(1)} %get-tuple-element.56.crossing_ref, f32[576,128]{1,0:T(8,128)S(1)} %get-tuple-element.57.state_ref), custom_call_target="tpu_custom_call" | custom-call | flops 2048000 | bytes 512000 | tf_op jit(solution)/shard_map/pallas_call | solution.py:65
  20.8 0.8 %shard_map.104 = (f32[2,136,128]{2,1,0:T(8,128)S(1)}, f32[48,128]{1,0:T(8,128)S(1)}, f32[16,128]{1,0:T(8,128)S(1)}) custom-call(f32[6,64,128]{2,1,0:T(8,128)S(1)} %shard_map.103.leaving_ref, f32[3,18,24,128]{3,2,1,0:T(8,128)S(1)} %get-tuple-element.48.grid_ref, f32[2,3,17,24,128]{4,3,2,1,0:T(8,128)S(1)} %shard_map.101.deposit_ref), custom_call_target="tpu_custom_call" | custom-call | flops 2048000 | bytes 512000 | tf_op jit(solution)/shard_map/pallas_call | solution.py:65
  21.6 0.1 collective-permute-start.5
  21.7 0.1 collective-permute-start.4
  21.8 1.2 %collective-permute-done.5.second_ref.y2_ref = f32[136,128]{1,0:T(8,128)S(1)} collective-permute-done((f32[136,128]{1,0:T(8,128)S(1)}, f32[136,128]{1,0:T(8,128)S(1)}, u32[]{:S(2)}, u32[]{:S(2)}) %collective-permute-start.5) | collective-permute-done | bytes 69664 | tf_op jit(solution)/shard_map/ppermute | solution.py:55
  22.9 3.3 %collective-permute-done.4.first_ref.y1_ref = f32[136,128]{1,0:T(8,128)S(1)} collective-permute-done((f32[136,128]{1,0:T(8,128)S(1)}, f32[136,128]{1,0:T(8,128)S(1)}, u32[]{:S(2)}, u32[]{:S(2)}) %collective-permute-start.4) | collective-permute-done | bytes 69664 | tf_op jit(solution)/shard_map/ppermute | solution.py:55
  26.3 1.6 %collective-permute-start.6 = (f32[176,128]{1,0:T(8,128)S(1)}, f32[176,128]{1,0:T(8,128)S(1)}, u32[]{:S(2)}, u32[]{:S(2)}) collective-permute-start(f32[176,128]{1,0:T(8,128)S(1)} %get-tuple-element.61), channel_id=1, source_target_pairs={{0,16},{16,0},{1,17},{17,1},{2,18},{18,2},{3,19},{19,3},{4,20},{20... | collective-permute-start | bytes 270344 | tf_op jit(solution)/shard_map/ppermute | solution.py:37
  27.9 0.0 collective-permute-start.8
  28.0 1.0 %collective-permute-start.7 = (f32[80,128]{1,0:T(8,128)S(1)}, f32[80,128]{1,0:T(8,128)S(1)}, u32[]{:S(2)}, u32[]{:S(2)}) collective-permute-start(f32[80,128]{1,0:T(8,128)S(1)} %get-tuple-element.70), channel_id=1, source_target_pairs={{0,4},{4,0},{8,12},{12,8},{1,5},{5,1},{9,13},{13,9},{2,6},{6,2},{1... | collective-permute-start | bytes 122888 | tf_op jit(solution)/shard_map/ppermute | solution.py:44
  28.9 0.1 collective-permute-start.9
  29.0 0.4 %shard_map.102.base_ref = f32[3,16,16,128]{3,2,1,0:T(8,128)S(1)} custom-call(f32[3,18,24,128]{3,2,1,0:T(8,128)S(1)} %get-tuple-element.48.grid_ref, f32[2,3,17,24,128]{4,3,2,1,0:T(8,128)S(1)} %shard_map.101.deposit_ref, f32[128,128]{1,0:T(8,128)S(1)} %get-tuple-element.46.top_in_ref.top_ref), custom_call_target="tpu_custom_call" | custom-call | flops 4096000 | bytes 1024000 | tf_op jit(solution)/shard_map/pallas_call | solution.py:65
  29.4 3.5 %collective-permute-done.9.edge_ref = f32[16,128]{1,0:T(8,128)S(1)} collective-permute-done((f32[16,128]{1,0:T(8,128)S(1)}, f32[16,128]{1,0:T(8,128)S(1)}, u32[]{:S(2)}, u32[]{:S(2)}) %collective-permute-start.9) | collective-permute-done | bytes 8224 | tf_op jit(solution)/shard_map/ppermute | solution.py:61
  32.9 0.0 collective-permute-done.8.z2_ref
  32.9 0.0 collective-permute-done.7.z1_ref
  32.9 0.0 collective-permute-done.6.x_ref.minus_x_ref
  32.9 1.0 %shard_map.106 = (f32[3,16,16,128]{3,2,1,0:T(8,128)}, f32[6,7,8,128]{3,2,1,0:T(8,128)}, f32[3,64,128]{2,1,0:T(8,128)}) custom-call(f32[3,16,16,128]{3,2,1,0:T(8,128)S(1)} %shard_map.102.base_ref, f32[136,128]{1,0:T(8,128)S(1)} %collective-permute-done.4.first_ref.y1_ref, f32[136,128]{1,0:T(8,128)S(1)} %collective-permute-done.5.second_ref.y2_ref, ...), custom_call_target="tpu_custom_call" | custom-call | tf_op jit(solution)/shard_map/pallas_call | solution.py:65
  (3 shorter events, 0.0 us)
Async XLA Ops:
  1.9 6.8 %collective-permute-start.1 = (f32[48,128]{1,0:T(8,128)S(1)}, f32[48,128]{1,0:T(8,128)S(1)}, u32[]{:S(2)}, u32[]{:S(2)}) collective-permute-start(f32[48,128]{1,0:T(8,128)S(1)} %get-tuple-element.43), channel_id=1, source_target_pairs={{0,16},{16,0},{1,17},{17,1},{2,18},{18,2},{3,19},{19,3},{4,20},{20... | collective-permute-start | bytes 73736 | tf_op jit(solution)/shard_map/ppermute | solution.py:37
  4.9 3.7 %collective-permute-start.2 = (f32[16,128]{1,0:T(8,128)S(1)}, f32[16,128]{1,0:T(8,128)S(1)}, u32[]{:S(2)}, u32[]{:S(2)}) collective-permute-start(f32[16,128]{1,0:T(8,128)S(1)} %get-tuple-element.42), channel_id=1, source_target_pairs={{0,28},{4,16},{8,20},{12,24},{16,12},{20,0},{24,4},{28,8},{1,29},{... | collective-permute-start | bytes 24584 | tf_op jit(solution)/shard_map/ppermute | solution.py:61
  5.5 3.2 %collective-permute-start = (f32[16,128]{1,0:T(8,128)S(1)}, f32[16,128]{1,0:T(8,128)S(1)}, u32[]{:S(2)}, u32[]{:S(2)}) collective-permute-start(f32[16,128]{1,0:T(8,128)S(1)} %get-tuple-element.42), channel_id=1, source_target_pairs={{0,12},{4,0},{8,4},{12,8},{1,13},{5,1},{9,5},{13,9},{2,14},{6,2},{... | collective-permute-start | bytes 24584 | tf_op jit(solution)/shard_map/ppermute | solution.py:37
  8.8 8.6 %collective-permute-start.3 = (f32[56,128]{1,0:T(8,128)S(1)}, f32[56,128]{1,0:T(8,128)S(1)}, u32[]{:S(2)}, u32[]{:S(2)}) collective-permute-start(f32[56,128]{1,0:T(8,128)S(1)} %shard_map.97), channel_id=1, source_target_pairs={{0,3},{1,0},{2,1},{3,2},{4,7},{5,4},{6,5},{7,6},{8,11},{9,8},{10,9... | collective-permute-start | bytes 86024 | tf_op jit(solution)/shard_map/ppermute | solution.py:37
  21.6 1.3 %collective-permute-start.5 = (f32[136,128]{1,0:T(8,128)S(1)}, f32[136,128]{1,0:T(8,128)S(1)}, u32[]{:S(2)}, u32[]{:S(2)}) collective-permute-start(f32[136,128]{1,0:T(8,128)S(1)} %get-tuple-element.67), channel_id=1, source_target_pairs={{0,4},{3,7},{1,2},{2,1},{4,0},{7,3},{5,6},{6,5},{8,12},{11,15},{9,... | collective-permute-start | bytes 208904 | tf_op jit(solution)/shard_map/ppermute | solution.py:55
  21.7 4.6 %collective-permute-start.4 = (f32[136,128]{1,0:T(8,128)S(1)}, f32[136,128]{1,0:T(8,128)S(1)}, u32[]{:S(2)}, u32[]{:S(2)}) collective-permute-start(f32[136,128]{1,0:T(8,128)S(1)} %get-tuple-element.68), channel_id=1, source_target_pairs={{0,1},{1,0},{2,3},{3,2},{4,5},{5,4},{6,7},{7,6},{8,9},{9,8},{10,11... | collective-permute-start | bytes 208904 | tf_op jit(solution)/shard_map/ppermute | solution.py:55
  26.3 6.6 %collective-permute-start.6 = (f32[176,128]{1,0:T(8,128)S(1)}, f32[176,128]{1,0:T(8,128)S(1)}, u32[]{:S(2)}, u32[]{:S(2)}) collective-permute-start(f32[176,128]{1,0:T(8,128)S(1)} %get-tuple-element.61), channel_id=1, source_target_pairs={{0,16},{16,0},{1,17},{17,1},{2,18},{18,2},{3,19},{19,3},{4,20},{20... | collective-permute-start | bytes 270344 | tf_op jit(solution)/shard_map/ppermute | solution.py:37
  27.9 4.9 %collective-permute-start.8 = (f32[80,128]{1,0:T(8,128)S(1)}, f32[80,128]{1,0:T(8,128)S(1)}, u32[]{:S(2)}, u32[]{:S(2)}) collective-permute-start(f32[80,128]{1,0:T(8,128)S(1)} %get-tuple-element.69), channel_id=1, source_target_pairs={{0,12},{4,8},{8,4},{12,0},{1,13},{5,9},{9,5},{13,1},{2,14},{6,10},... | collective-permute-start | bytes 122888 | tf_op jit(solution)/shard_map/ppermute | solution.py:44
  28.0 4.9 %collective-permute-start.7 = (f32[80,128]{1,0:T(8,128)S(1)}, f32[80,128]{1,0:T(8,128)S(1)}, u32[]{:S(2)}, u32[]{:S(2)}) collective-permute-start(f32[80,128]{1,0:T(8,128)S(1)} %get-tuple-element.70), channel_id=1, source_target_pairs={{0,4},{4,0},{8,12},{12,8},{1,5},{5,1},{9,13},{13,9},{2,6},{6,2},{1... | collective-permute-start | bytes 122888 | tf_op jit(solution)/shard_map/ppermute | solution.py:44
  28.9 4.0 %collective-permute-start.9 = (f32[16,128]{1,0:T(8,128)S(1)}, f32[16,128]{1,0:T(8,128)S(1)}, u32[]{:S(2)}, u32[]{:S(2)}) collective-permute-start(f32[16,128]{1,0:T(8,128)S(1)} %get-tuple-element.63), channel_id=1, source_target_pairs={{0,20},{4,24},{8,28},{12,16},{16,4},{20,8},{24,12},{28,0},{1,21},{... | collective-permute-start | bytes 24584 | tf_op jit(solution)/shard_map/ppermute | solution.py:61

commit v5 on v4

--- a/solution.py
+++ b/solution.py
@@ -257,13 +257,9 @@
     lay_out_top(turned_ref, lines_ref, count_y - 1, comps, count_x, count_y, size_z)
 
 
-def blocks_kernel(
-    late, comps, count_x, count_y, count_z, rows_z,
-    list_ref, brick_ref, lines_ref, table_ref, *refs,
-):
-    state_ref, deposit_ref, push_ref, spread_ref = refs[-4:]
+def block_steps(dims, list_ref, brick_ref):
+    comps, count_x, count_y, count_z, rows_z = dims
     nblocks = brick_ref.shape[0]
-    room = (list_ref.shape[0] - 2) // 2
     sub = row_ids(8)
     row_y = row_ids(REACH_Y).astype(jnp.float32)
     row_z = row_ids(REACH_Z).astype(jnp.float32)
@@ -279,7 +275,7 @@
         brick_y = lax.rem(lax.div(brick, count_z), count_y)
         return k, brick_x * count_y + brick_y, lax.rem(brick, count_z)
 
-    def loaded(at):
+    def loaded(at, lines_ref, table_ref):
         k, pair, brick_z = place_of(at)
         first = pl.multiple_of(pair * comps * rows_z + brick_z * BZ, 8)
         window = jnp.concatenate([lines_ref[pl.ds(first + c * rows_z, REACH_Z)] for c in range(comps)], axis=0)
@@ -339,35 +335,17 @@
             results.append(mine + pltpu.roll(mine, LANES // 2, 1))
         return results
 
-    count = list_ref[2 * room + late]
-    groups = (count + UNROLL - 1) // UNROLL
-    push_ref[...] = jnp.zeros_like(push_ref)
-    spread_ref[...] = jnp.zeros_like(spread_ref)
-
-    @pl.loop(0, groups + 1)
-    def _(group):
-        now = late * room + jnp.maximum(jnp.minimum(group, groups - 1), 0) * UNROLL
-        before = late * room + jnp.maximum(group - 1, 0) * UNROLL
-        taken = [loaded(now + u) for u in range(UNROLL)]
-        old = [(push_ref[i], spread_ref[i]) for i in range(UNROLL // 2)]
-        shares = []
-        for push, spread in old:
-            shares.extend(shared(push, spread))
-        tiles, fresh = [], []
-        for u in range(0, UNROLL, 2):
-            both, push, spread = gathered(taken[u], taken[u + 1])
-            tiles.extend(both)
-            fresh.append((push, spread))
+    def add(deposit_ref, at, shares):
         sums = []
-        for u in range(UNROLL):
-            _, pair, brick_z = place_of(before + u)
+        for u, share in enumerate(shares):
+            _, pair, brick_z = place_of(at + u)
             first_z = brick_z * BZ
             within = ((lane - first_z) & (LANES - 1)) < REACH_Z
             parts = []
             for c in range(comps):
                 shift = (first_z - c * REACH_Z + LANES) & (LANES - 1)
                 for a in range(REACH_X):
-                    part = pltpu.roll(shares[u][a * REACH_Y : (a + 1) * REACH_Y], shift, 1)
+                    part = pltpu.roll(share[a * REACH_Y : (a + 1) * REACH_Y], shift, 1)
                     parts.append(jnp.where(within, part, 0.0))
             sel = jnp.where(brick_z == count_z - 1, 1, 0)
             start = pl.multiple_of((sel * count_x * count_y + pair) * comps * SPREAD, 8)
@@ -377,11 +355,89 @@
             totals = [deposit_ref[spot] + part for spot, part in zip(spots, parts)]
             for spot, total in zip(spots, totals):
                 deposit_ref[spot] = total
+
+    def group_of(taken):
+        tiles, fresh = [], []
+        for u in range(0, UNROLL, 2):
+            both, push, spread = gathered(taken[u], taken[u + 1])
+            tiles.extend(both)
+            fresh.append((push, spread))
+        return tiles, fresh
+
+    def keep(state_ref, taken, tiles):
         for (k, _, _), tile in zip(taken, tiles):
             state_ref[pl.ds(pl.multiple_of(STATE * k, STATE), STATE)] = tile
+
+    def deposits_of(kept):
+        shares = []
+        for push, spread in kept:
+            shares.extend(shared(push, spread))
+        return shares
+
+    return loaded, group_of, keep, deposits_of, add
+
+
+def groups_in(list_ref, late):
+    room = (list_ref.shape[0] - 2) // 2
+    return late * room, (list_ref[2 * room + late] + UNROLL - 1) // UNROLL
+
+
+def gather_kernel(dims, list_ref, brick_ref, lines_ref, table_ref, state_ref, push_ref, spread_ref):
+    loaded, group_of, keep, _, _ = block_steps(dims, list_ref, brick_ref)
+    base, groups = groups_in(list_ref, 0)
+
+    @pl.loop(0, groups)
+    def _(group):
+        taken = [loaded(base + group * UNROLL + u, lines_ref, table_ref) for u in range(UNROLL)]
+        tiles, fresh = group_of(taken)
+        keep(state_ref, taken, tiles)
+        for i, (push, spread) in enumerate(fresh):
+            push_ref[group * (UNROLL // 2) + i] = push
+            spread_ref[group * (UNROLL // 2) + i] = spread
+
+
+def deposit_kernel(dims, list_ref, brick_ref, push_ref, spread_ref, deposit_in_ref, deposit_ref):
+    _, _, _, deposits_of, add = block_steps(dims, list_ref, brick_ref)
+    base, groups = groups_in(list_ref, 0)
+
+    @pl.loop(0, groups)
+    def _(group):
+        pairs = [group * (UNROLL // 2) + i for i in range(UNROLL // 2)]
+        add(deposit_ref, base + group * UNROLL, deposits_of([(push_ref[i], spread_ref[i]) for i in pairs]))
+
+
+def late_kernel(
+    dims, slots, list_ref, brick_ref, crossing_ref, lines_ref, table_ref, state_in_ref, deposit_in_ref,
+    state_ref, deposit_ref, leaving_ref, push_ref, spread_ref,
+):
+    loaded, group_of, keep, deposits_of, add = block_steps(dims, list_ref, brick_ref)
+    base, groups = groups_in(list_ref, 1)
+    push_ref[...] = jnp.zeros_like(push_ref)
+    spread_ref[...] = jnp.zeros_like(spread_ref)
+
+    @pl.loop(0, groups + 1)
+    def _(group):
+        now = base + jnp.maximum(jnp.minimum(group, groups - 1), 0) * UNROLL
+        before = base + jnp.maximum(group - 1, 0) * UNROLL
+        taken = [loaded(now + u, lines_ref, table_ref) for u in range(UNROLL)]
+        shares = deposits_of([(push_ref[i], spread_ref[i]) for i in range(UNROLL // 2)])
+        tiles, fresh = group_of(taken)
+        add(deposit_ref, before, shares)
+        keep(state_ref, taken, tiles)
         for i, (push, spread) in enumerate(fresh):
             push_ref[i] = push
             spread_ref[i] = spread
+
+    rows = leaving_ref.shape[0] // (6 * slots)
+    for face in range(6):
+        tiles = []
+        for slot in range(slots):
+            block = crossing_ref[face, slot]
+            spot = pl.ds(pl.multiple_of(jnp.maximum(block, 0) * STATE, STATE), STATE)
+            live = jnp.full((STATE, LANES), block, jnp.int32) >= 0
+            tiles.append(jnp.where(live, state_ref[spot], 0.0))
+        for slot, tile in enumerate(tiles):
+            leaving_ref[pl.ds(face * rows * slots + slot, rows, stride=slots)] = tile[:rows]
 
 
 def merge_kernel(tiles_ref, plane_ref):
@@ -416,54 +472,54 @@
                 plane_ref[sel, c, x, count_y * BY :] = carried
 
 
-def leave_kernel(crossing_ref, state_ref, leaving_ref):
-    slots = crossing_ref.shape[1]
-
-    for face in range(6):
-        tiles = []
-        for slot in range(slots):
-            block = crossing_ref[face, slot]
-            spot = pl.ds(pl.multiple_of(jnp.maximum(block, 0) * STATE, STATE), STATE)
-            live = jnp.full((STATE, LANES), block, jnp.int32) >= 0
-            tiles.append(jnp.where(live, state_ref[spot], 0.0))
-        leaving_ref[face] = jnp.concatenate(tiles, axis=0)
-
-
-def send_kernel(push, diffuse, leaving_ref, grid_ref, deposit_ref, y_ref, x_ref, z_ref, face_ref):
-    comps, size_x = grid_ref.shape[0], grid_ref.shape[1] - 2
-    size_y = z_ref.shape[0]
+def send_y_kernel(push, diffuse, leaving_ref, grid_ref, tiles_ref, y_ref, lines_ref):
+    comps, size_x, size_y = grid_ref.shape[0], grid_ref.shape[1] - 2, grid_ref.shape[2] - 8
+    count_x, count_y = size_x // BX, size_y // BY
     rows = leaving_ref.shape[1]
     first = jnp.full((rows, LANES), odd("gy")) == 0
     y_ref[0, 0:rows] = jnp.where(first, leaving_ref[2], leaving_ref[3])
     y_ref[1, 0:rows] = jnp.where(first, leaving_ref[3], leaving_ref[2])
-    lane = lane_ids(ROWS_Y)
-    sub = row_ids(ROWS_Y)
-    face_ref[...] = jnp.zeros_like(face_ref)
-
-    @pl.loop(0, comps)
-    def _(c):
-        face = jnp.zeros((ROWS_Y, LANES), jnp.float32)
-        lines = jnp.zeros((ROWS_Y, LANES), jnp.float32)
+    lines_ref[...] = jnp.zeros_like(lines_ref)
+    for sel in (0, 1):
+        for c in range(comps):
+            for p in range(count_x):
+                at = (((sel * count_x + p) * count_y + count_y - 1) * comps + c) * SPREAD + BY
+                spot = slice(c * ROWS_Y + p * BX, c * ROWS_Y + p * BX + REACH_X)
+                lines_ref[sel, spot] = lines_ref[sel, spot] + tiles_ref[pl.ds(at, REACH_X, stride=REACH_Y)]
+    lane, sub = lane_ids(ROWS_Y), row_ids(ROWS_Y)
+    corner = jnp.zeros((1, LANES), jnp.float32)
+    for c in range(comps):
+        spot = slice(c * ROWS_Y, (c + 1) * ROWS_Y)
+        wrapped = lines_ref[1, spot]
+        line = push * (lines_ref[0, spot] + jnp.where(lane == 0, 0.0, wrapped))
+        beside = jnp.concatenate([grid_ref[c, 1 : size_x + 1, size_y - 1], jnp.zeros((8, LANES), jnp.float32)], axis=0)
+        line = line + diffuse * beside
+        y_ref[0, rows + c * ROWS_Y : rows + (c + 1) * ROWS_Y] = line
+        y_ref[1, rows + c * ROWS_Y : rows + (c + 1) * ROWS_Y] = line
+        far = jnp.broadcast_to(push * wrapped[:, 0:1], (ROWS_Y, LANES))
+        corner = corner + jnp.sum(jnp.where(lane == sub + PACK * c, far, 0.0), axis=0, keepdims=True)
+    at = rows + size_x + 1
+    y_ref[0, at : at + 1] = corner
+    y_ref[1, at : at + 1] = corner
+
+
+def send_xz_kernel(push, diffuse, grid_ref, deposit_ref, x_ref, z_ref):
+    comps, size_x = grid_ref.shape[0], grid_ref.shape[1] - 2
+    size_y = z_ref.shape[0]
+    lane = lane_ids(size_y)
+    packed = jnp.zeros((size_y, LANES), jnp.float32)
+    for c in range(comps):
+        face = jnp.zeros((size_y, LANES), jnp.float32)
         for x in range(size_x + 1):
-            beyond = push * deposit_ref[1, c, x]
-            top = push * deposit_ref[0, c, x, size_y:] + jnp.where(lane[:8] == 0, 0.0, beyond[size_y:])
+            beyond = push * deposit_ref[1, c, x, 0:size_y]
             if x < size_x:
-                here = grid_ref[c, x + 1, 0:size_y]
-                beyond = jnp.concatenate([beyond[:size_y] + diffuse * turned(here, 1), beyond[size_y:]], axis=0)
-                top = top[0:1] + diffuse * here[size_y - 1 :]
+                beyond = beyond + diffuse * turned(grid_ref[c, x + 1, 0:size_y], 1)
             else:
-                here = grid_ref[c, size_x, 0:size_y]
-                total = push * deposit_ref[0, c, x, 0:size_y] + jnp.where(lane[:size_y] == 0, 0.0, beyond[:size_y])
-                x_ref[pl.ds(pl.multiple_of(c * size_y, 8), size_y)] = diffuse * here + total
-                top = top[0:1]
-            lines = jnp.where(sub == x, top, lines)
+                total = push * deposit_ref[0, c, x, 0:size_y] + jnp.where(lane == 0, 0.0, beyond)
+                x_ref[c * size_y : (c + 1) * size_y] = diffuse * grid_ref[c, size_x, 0:size_y] + total
             face = jnp.where(lane == x, turned(beyond, x), face)
-        y_ref[0, pl.ds(pl.multiple_of(rows + c * ROWS_Y, 8), ROWS_Y)] = lines
-        face_ref[...] = face_ref[...] + pltpu.roll(face, PACK * c, 1)
-
-    z_ref[...] = face_ref[0:size_y]
-    y_ref[0, rows + size_x + 1 : rows + size_x + 2] = face_ref[size_y : size_y + 1]
-    y_ref[1, rows:] = y_ref[0, rows:]
+        packed = packed + turned(face, PACK * c)
+    z_ref[...] = packed
 
 
 def base_kernel(push, diffuse, grid_ref, deposit_ref, top_ref, base_ref):
@@ -536,7 +592,7 @@
     for i in range(arrivals_ref.shape[1]):
 
         def rows_of(ref, at=0):
-            return ref[pl.ds(at + i, slots, stride=STATE)]
+            return ref[at + i * slots : at + (i + 1) * slots]
 
         arrivals_ref[0, i] = rows_of(x_ref, comps * size_y)
         arrivals_ref[1, i] = rows_of(minus_x_ref, minus_x_ref.shape[0] - count)
@@ -595,33 +651,45 @@
         aliases={0: 0, 1: 1}, scratch=(square,), cycles=1000,
     )
 
-    def advance(late, lines, deposit, *state):
-        return call(
-            functools.partial(blocks_kernel, late, comps, size_x // BX, size_y // BY, size_z // BZ, rows_z),
-            [(STATE * spare, LANES), deposit_shape], blocks, brick_index, lines, table, deposit, *state,
-            smem=(0, 1), aliases={4: 1, 5: 0} if state else {4: 1}, cycles=6000 - 4000 * late,
-            scratch=(
-                pltpu.VMEM((UNROLL // 2, 2 * LANES, LANES), jnp.bfloat16),
-                pltpu.VMEM((UNROLL // 2, 4 * SPREAD, LANES), jnp.bfloat16),
-            ),
-        )
-
-    state, deposit = advance(0, lines, deposit)
+    dims = (comps, size_x // BX, size_y // BY, size_z // BZ, rows_z)
+    slots = crossing.shape[1]
+    count = 7 * slots
+
+    def parts(pairs):
+        return [(pairs, 2 * LANES, LANES), (pairs, 4 * SPREAD, LANES)]
+
+    state, push_parts, spread_parts = call(
+        functools.partial(gather_kernel, dims),
+        [(STATE * spare, LANES)]
+        + [jax.ShapeDtypeStruct(shape, jnp.bfloat16) for shape in parts((nblocks + UNROLL) // 2)],
+        blocks, brick_index, lines, table, smem=(0, 1), cycles=4000,
+    )
     grid, lines = call(
         functools.partial(halo_y_kernel, size_y), [grid_shape, lines_shape], grid, lines, top, from_y,
         aliases={0: 0, 1: 1}, scratch=(square,), cycles=1000,
     )
-    state, deposit = advance(1, lines, deposit, state)
-
+    state, deposit, leaving = call(
+        functools.partial(late_kernel, dims, slots),
+        [(STATE * spare, LANES), deposit_shape, (6 * count, LANES)],
+        blocks, brick_index, crossing, lines, table, state, deposit,
+        smem=(0, 1, 2), aliases={5: 0, 6: 1}, cycles=2000,
+        scratch=[pltpu.VMEM(shape, jnp.bfloat16) for shape in parts(UNROLL // 2)],
+    )
+    leaving = leaving.reshape(6, count, LANES)
+    (to_y,) = call(
+        functools.partial(send_y_kernel, push, diffuse), [(2, count + comps * ROWS_Y, LANES)],
+        leaving, grid, deposit, cycles=300, scratch=(pltpu.VMEM((2, comps * ROWS_Y, LANES), jnp.float32),),
+    )
+    y1, y2 = swapped_y((to_y[0], to_y[1]))
+    (deposit,) = call(
+        functools.partial(deposit_kernel, dims), [deposit_shape], blocks, brick_index, push_parts, spread_parts, deposit,
+        smem=(0, 1), aliases={4: 0}, cycles=4000,
+    )
     (deposit,) = call(merge_kernel, [(2, comps, size_x + 1, ROWS_Y, LANES)], deposit, cycles=500)
-    count = STATE * crossing.shape[1]
-    (leaving,) = call(leave_kernel, [(6, count, LANES)], crossing, state, smem=(0,), cycles=500)
-    to_y, to_x, to_z = call(
-        functools.partial(send_kernel, push, diffuse),
-        [(2, count + comps * ROWS_Y, LANES), (comps * size_y, LANES), (size_y, LANES)],
-        leaving, grid, deposit, cycles=500, scratch=(pltpu.VMEM((ROWS_Y, LANES), jnp.float32),),
-    )
-    y1, y2 = swapped_y((to_y[0], to_y[1]))
+    to_x, to_z = call(
+        functools.partial(send_xz_kernel, push, diffuse), [(comps * size_y, LANES), (size_y, LANES)],
+        grid, deposit, cycles=500,
+    )
     (base,) = call(
         functools.partial(base_kernel, push, diffuse), [gas_field.shape], grid, deposit, top, cycles=1000,
     )

time: 33.9 us -> 30.9 us (0.912)
  waiting for transfers between devices: 8.01 us -> 3.46 us
  starting transfers between devices: 11.2 us -> 12.2 us
  Pallas kernels: 13.9 us -> 14.4 us
    ppermute x1, waiting for transfers between devices: 3.35 us -> 0.01 us  [swapped_y(): lax.ppermute(blocks[0], 'gy', first)]
    ppermute x1, waiting for transfers between devices: 1.17 us -> 0.01 us  [swapped_y(): lax.ppermute(blocks[1], ('gz', 'gy'), second)]
    ppermute x1, starting transfers between devices: 0.07 us -> 0.74 us  [swapped_y(): lax.ppermute(blocks[0], 'gy', first)]
    pallas_call x13 -> x14, Pallas kernels: 13.9 us -> 14.4 us  [call(): pl.pallas_call(body, out_shape=[o if isinstance(o, jax.ShapeDtypeStruct)...]
    ppermute x4, starting transfers between devices: 9.38 us -> 9.83 us  [moved_along(): lax.ppermute(block, axis, [(i, (i + distance) % count) for i in range(cou...]
  transfers between devices with their start and end apart: 10 -> 10, of which waited for: 3 -> 1; matrix products, arithmetic and copies ran while one was open for 0% -> 0% of each run, Pallas kernels for 22% -> 30%
where the time goes in v5:
time: 30.9 us
  Pallas kernels  14.4 us (47%)
  starting transfers between devices  12.2 us (39%)
  waiting for transfers between devices  3.46 us (11%)
  between operations  0.77 us (2%)
    pallas_call x14, Pallas kernels, call(): pl.pallas_call(body, out_shape=[o if isinstance(o, jax.ShapeDtypeStruct)...  14.4 us
    ppermute x4, starting transfers between devices, moved_along(): lax.ppermute(block, axis, [(i, (i + distance) % count) for i in range(cou...  9.83 us
    ppermute x2, waiting for transfers between devices, moved_diagonally(): return lax.ppermute(block, ('gx', 'gz'), route)  3.44 us
    ppermute x1, starting transfers between devices, swapped_z(): lax.ppermute(blocks[0], 'gz', first)  0.81 us
    ppermute x1, starting transfers between devices, swapped_y(): lax.ppermute(blocks[0], 'gy', first)  0.74 us
    ppermute x2, starting transfers between devices, moved_diagonally(): return lax.ppermute(block, ('gx', 'gz'), route)  0.73 us
  transfers between devices with their start and end apart: 10, of which 1 were waited for; matrix products, arithmetic and copies ran while one was open for 0% of the time, Pallas kernels for 30%

profile of v5, /device:TPU:0, one launch (start us, length us, event | category | flops | bytes accessed | tf_op | source)
XLA Modules:
  0.0 30.9 jit_solution(11113643508635920536)
XLA Ops:
  0.6 1.2 %shard_map.94 = (f32[3,18,24,128]{3,2,1,0:T(8,128)S(1)}, f32[16,128]{1,0:T(8,128)S(1)}, f32[48,128]{1,0:T(8,128)S(1)}, f32[3,64,128]{2,1,0:T(8,128)S(1)}, f32[3,...) custom-call(f32[3,16,16,128]{3,2,1,0:T(8,128)} %gas_ref.1, ...), custom_call_target="tpu_custom_call" | custom-call | tf_op jit(solution)/shard_map/pallas_call | solution.py:65
  1.9 3.0 %collective-permute-start.1 = (f32[48,128]{1,0:T(8,128)S(1)}, f32[48,128]{1,0:T(8,128)S(1)}, u32[]{:S(2)}, u32[]{:S(2)}) collective-permute-start(f32[48,128]{1,0:T(8,128)S(1)} %get-tuple-element.44), channel_id=1, source_target_pairs={{0,16},{16,0},{1,17},{17,1},{2,18},{18,2},{3,19},{19,3},{4,20},{20... | collective-permute-start | bytes 73736 | tf_op jit(solution)/shard_map/ppermute | solution.py:37
  4.9 0.6 %collective-permute-start.2 = (f32[16,128]{1,0:T(8,128)S(1)}, f32[16,128]{1,0:T(8,128)S(1)}, u32[]{:S(2)}, u32[]{:S(2)}) collective-permute-start(f32[16,128]{1,0:T(8,128)S(1)} %get-tuple-element.43), channel_id=1, source_target_pairs={{0,28},{4,16},{8,20},{12,24},{16,12},{20,0},{24,4},{28,8},{1,29},{... | collective-permute-start | bytes 24584 | tf_op jit(solution)/shard_map/ppermute | solution.py:61
  5.5 1.1 %collective-permute-start = (f32[16,128]{1,0:T(8,128)S(1)}, f32[16,128]{1,0:T(8,128)S(1)}, u32[]{:S(2)}, u32[]{:S(2)}) collective-permute-start(f32[16,128]{1,0:T(8,128)S(1)} %get-tuple-element.43), channel_id=1, source_target_pairs={{0,12},{4,0},{8,4},{12,8},{1,13},{5,1},{9,5},{13,9},{2,14},{6,2},{... | collective-permute-start | bytes 24584 | tf_op jit(solution)/shard_map/ppermute | solution.py:37
  6.6 2.0 %shard_map.95 = (f32[6528,128]{1,0:T(8,128)S(1)}, f32[3840,128]{1,0:T(8,128)S(1)}, f32[1152,128]{1,0:T(8,128)S(1)}, f32[8,128]{1,0:T(8,128)S(1)}, s32[146]{0:T(256)S(1)}) custom-call(f32[3,18,24,128]{3,2,1,0:T(8,128)S(1)} %get-tuple-element.36.grid_ref.grid_in_ref, f32[3,64,128]{2,1,0:T(8,128)S(1)} %get-tuple-element.37.velocity_ref, ...), custom_call_target="tpu_custom_call" | custom-call | flops 12288000 | bytes 3072000 | tf_op jit(solution)/shard_map/pallas_call | solution.py:65
  8.7 0.0 collective-permute-done.2.edge_ref
  8.7 0.0 collective-permute-done.face_ref
  8.7 0.0 collective-permute-done.1.from_x_ref
  8.7 0.1 shard_map.97
  8.8 3.6 %collective-permute-start.3 = (f32[56,128]{1,0:T(8,128)S(1)}, f32[56,128]{1,0:T(8,128)S(1)}, u32[]{:S(2)}, u32[]{:S(2)}) collective-permute-start(f32[56,128]{1,0:T(8,128)S(1)} %shard_map.97), channel_id=1, source_target_pairs={{0,3},{1,0},{2,1},{3,2},{4,7},{5,4},{6,5},{7,6},{8,11},{9,8},{10,9... | collective-permute-start | bytes 86024 | tf_op jit(solution)/shard_map/ppermute | solution.py:37
  12.4 0.4 %shard_map.96 = (f32[3,18,24,128]{3,2,1,0:T(8,128)S(1)}, f32[6528,128]{1,0:T(8,128)S(1)}, f32[128,128]{1,0:T(8,128)S(1)}) custom-call(f32[3,18,24,128]{3,2,1,0:T(8,128)S(1)} %get-tuple-element.36.grid_ref.grid_in_ref, f32[6528,128]{1,0:T(8,128)S(1)} %get-tuple-element.42.lines_in_ref, ...), custom_call_target="tpu_custom_call", output_to_operand_aliasing={{0}: (0, {}), {1}: (1, {})} | custom-call | flops 4096000 | bytes 1024000 | tf_op jit(solution)/shard_map/pallas_call | solution.py:65
  12.8 2.2 %shard_map.99 = (f32[576,128]{1,0:T(8,128)S(1)}, bf16[36,256,128]{2,1,0:T(8,128)(2,1)S(1)}, bf16[36,160,128]{2,1,0:T(8,128)(2,1)S(1)}) custom-call(s32[146]{0:T(256)S(1)} %get-tuple-element.50.list_ref, s32[64]{0:T(128)S(1)} %get-tuple-element.41.brick_ref, f32[6528,128]{1,0:T(8,128)S(1)} %get-tuple-element.46.lines_in_ref.lines_ref, ...), custom_call_target="tpu_custom_call" | custom-call | flops 16384000 | bytes 4096000 | tf_op jit(solution)/shard_map/pallas_call | solution.py:65
  15.0 0.0 collective-permute-done.3.from_y_ref
  15.0 0.6 %shard_map.98 = (f32[3,18,24,128]{3,2,1,0:T(8,128)S(1)}, f32[6528,128]{1,0:T(8,128)S(1)}) custom-call(f32[3,18,24,128]{3,2,1,0:T(8,128)S(1)} %get-tuple-element.45.grid_in_ref, f32[6528,128]{1,0:T(8,128)S(1)} %get-tuple-element.46.lines_in_ref.lines_ref, ...), custom_call_target="tpu_custom_call", output_to_operand_aliasing={{0}: (0, {}), {1}: (1, {})} | custom-call | flops 4096000 | bytes 1024000 | tf_op jit(solution)/shard_map/pallas_call | solution.py:65
  15.6 2.2 %shard_map.100 = (f32[576,128]{1,0:T(8,128)S(1)}, f32[3840,128]{1,0:T(8,128)S(1)}, f32[336,128]{1,0:T(8,128)S(1)}) custom-call(s32[146]{0:T(256)S(1)} %get-tuple-element.50.list_ref, s32[64]{0:T(128)S(1)} %get-tuple-element.41.brick_ref, s32[6,8]{1,0:T(8,128)S(1)} %get-tuple-element.54.crossing_ref, ...), custom_call_target="tpu_custom_call", output_to_operand_aliasing={{0}: (5, {}), {1}: (6, {})} | custom-call | flops 8192000 | bytes 2048000 | tf_op jit(solution)/shard_map/pallas_call | solution.py:65
  17.9 0.1 shard_map.104
  18.0 0.1 collective-permute-start.5
  18.1 0.7 %collective-permute-start.4 = (f32[128,128]{1,0:T(8,128)S(1)}, f32[128,128]{1,0:T(8,128)S(1)}, u32[]{:S(2)}, u32[]{:S(2)}) collective-permute-start(f32[128,128]{1,0:T(8,128)S(1)} %get-tuple-element.70), channel_id=1, source_target_pairs={{0,1},{1,0},{2,3},{3,2},{4,5},{5,4},{6,7},{7,6},{8,9},{9,8},{10,11... | collective-permute-start | bytes 196616 | tf_op jit(solution)/shard_map/ppermute | solution.py:55
  18.9 3.3 %shard_map.101.tiles_ref = f32[3840,128]{1,0:T(8,128)S(1)} custom-call(s32[146]{0:T(256)S(1)} %get-tuple-element.50.list_ref, s32[64]{0:T(128)S(1)} %get-tuple-element.41.brick_ref, bf16[36,256,128]{2,1,0:T(8,128)(2,1)S(1)} %get-tuple-element.52.push_ref, bf16[36,160,128]{2,1,0:T(8,128)(2,1)S(1)} %get-tuple-element.53.spread_ref, ...), custom_call_target="tpu_custom_call", output_to_operand_aliasing={{}: (4, {})} | custom-call | flops 16384000 | bytes 4096000 | tf_op jit(solution)/shard_map/pallas_call | solution.py:65
  22.2 0.1 shard_map.102.deposit_ref
  22.3 0.7 %shard_map.105 = (f32[48,128]{1,0:T(8,128)S(1)}, f32[16,128]{1,0:T(8,128)S(1)}) custom-call(f32[3,18,24,128]{3,2,1,0:T(8,128)S(1)} %get-tuple-element.49.grid_ref, f32[2,3,17,24,128]{4,3,2,1,0:T(8,128)S(1)} %shard_map.102.deposit_ref), custom_call_target="tpu_custom_call" | custom-call | flops 2048000 | bytes 512000 | tf_op jit(solution)/shard_map/pallas_call | solution.py:65
  23.0 0.0 collective-permute-done.5.second_ref.y2_ref
  23.0 0.0 collective-permute-done.4.first_ref.y1_ref
  23.0 2.1 %collective-permute-start.6 = (f32[160,128]{1,0:T(8,128)S(1)}, f32[160,128]{1,0:T(8,128)S(1)}, u32[]{:S(2)}, u32[]{:S(2)}) collective-permute-start(f32[160,128]{1,0:T(8,128)S(1)} %get-tuple-element.62), channel_id=1, source_target_pairs={{0,16},{16,0},{1,17},{17,1},{2,18},{18,2},{3,19},{19,3},{4,20},{20... | collective-permute-start | bytes 245768 | tf_op jit(solution)/shard_map/ppermute | solution.py:37
  25.1 0.1 collective-permute-start.8
  25.1 0.8 %collective-permute-start.7 = (f32[72,128]{1,0:T(8,128)S(1)}, f32[72,128]{1,0:T(8,128)S(1)}, u32[]{:S(2)}, u32[]{:S(2)}) collective-permute-start(f32[72,128]{1,0:T(8,128)S(1)} %get-tuple-element.72), channel_id=1, source_target_pairs={{0,4},{4,0},{8,12},{12,8},{1,5},{5,1},{9,13},{13,9},{2,6},{6,2},{1... | collective-permute-start | bytes 110600 | tf_op jit(solution)/shard_map/ppermute | solution.py:44
  25.9 0.1 collective-permute-start.9
  26.1 0.4 %shard_map.103.base_ref = f32[3,16,16,128]{3,2,1,0:T(8,128)S(1)} custom-call(f32[3,18,24,128]{3,2,1,0:T(8,128)S(1)} %get-tuple-element.49.grid_ref, f32[2,3,17,24,128]{4,3,2,1,0:T(8,128)S(1)} %shard_map.102.deposit_ref, f32[128,128]{1,0:T(8,128)S(1)} %get-tuple-element.47.top_in_ref.top_ref), custom_call_target="tpu_custom_call" | custom-call | flops 4096000 | bytes 1024000 | tf_op jit(solution)/shard_map/pallas_call | solution.py:65
  26.5 3.4 %collective-permute-done.9.edge_ref = f32[16,128]{1,0:T(8,128)S(1)} collective-permute-done((f32[16,128]{1,0:T(8,128)S(1)}, f32[16,128]{1,0:T(8,128)S(1)}, u32[]{:S(2)}, u32[]{:S(2)}) %collective-permute-start.9) | collective-permute-done | bytes 8224 | tf_op jit(solution)/shard_map/ppermute | solution.py:61
  29.9 0.0 collective-permute-done.8.z2_ref
  29.9 0.0 collective-permute-done.7.z1_ref
  29.9 0.0 collective-permute-done.6.x_ref.minus_x_ref
  29.9 1.0 %shard_map.107 = (f32[3,16,16,128]{3,2,1,0:T(8,128)}, f32[6,7,8,128]{3,2,1,0:T(8,128)}, f32[3,64,128]{2,1,0:T(8,128)}) custom-call(f32[3,16,16,128]{3,2,1,0:T(8,128)S(1)} %shard_map.103.base_ref, f32[128,128]{1,0:T(8,128)S(1)} %collective-permute-done.4.first_ref.y1_ref, f32[128,128]{1,0:T(8,128)S(1)} %collective-permute-done.5.second_ref.y2_ref, ...), custom_call_target="tpu_custom_call" | custom-call | tf_op jit(solution)/shard_map/pallas_call | solution.py:65
  (3 shorter events, 0.0 us)
Async XLA Ops:
  1.9 6.8 %collective-permute-start.1 = (f32[48,128]{1,0:T(8,128)S(1)}, f32[48,128]{1,0:T(8,128)S(1)}, u32[]{:S(2)}, u32[]{:S(2)}) collective-permute-start(f32[48,128]{1,0:T(8,128)S(1)} %get-tuple-element.44), channel_id=1, source_target_pairs={{0,16},{16,0},{1,17},{17,1},{2,18},{18,2},{3,19},{19,3},{4,20},{20... | collective-permute-start | bytes 73736 | tf_op jit(solution)/shard_map/ppermute | solution.py:37
  4.9 3.7 %collective-permute-start.2 = (f32[16,128]{1,0:T(8,128)S(1)}, f32[16,128]{1,0:T(8,128)S(1)}, u32[]{:S(2)}, u32[]{:S(2)}) collective-permute-start(f32[16,128]{1,0:T(8,128)S(1)} %get-tuple-element.43), channel_id=1, source_target_pairs={{0,28},{4,16},{8,20},{12,24},{16,12},{20,0},{24,4},{28,8},{1,29},{... | collective-permute-start | bytes 24584 | tf_op jit(solution)/shard_map/ppermute | solution.py:61
  5.5 3.2 %collective-permute-start = (f32[16,128]{1,0:T(8,128)S(1)}, f32[16,128]{1,0:T(8,128)S(1)}, u32[]{:S(2)}, u32[]{:S(2)}) collective-permute-start(f32[16,128]{1,0:T(8,128)S(1)} %get-tuple-element.43), channel_id=1, source_target_pairs={{0,12},{4,0},{8,4},{12,8},{1,13},{5,1},{9,5},{13,9},{2,14},{6,2},{... | collective-permute-start | bytes 24584 | tf_op jit(solution)/shard_map/ppermute | solution.py:37
  8.8 6.3 %collective-permute-start.3 = (f32[56,128]{1,0:T(8,128)S(1)}, f32[56,128]{1,0:T(8,128)S(1)}, u32[]{:S(2)}, u32[]{:S(2)}) collective-permute-start(f32[56,128]{1,0:T(8,128)S(1)} %shard_map.97), channel_id=1, source_target_pairs={{0,3},{1,0},{2,1},{3,2},{4,7},{5,4},{6,5},{7,6},{8,11},{9,8},{10,9... | collective-permute-start | bytes 86024 | tf_op jit(solution)/shard_map/ppermute | solution.py:37
  18.0 4.9 %collective-permute-start.5 = (f32[128,128]{1,0:T(8,128)S(1)}, f32[128,128]{1,0:T(8,128)S(1)}, u32[]{:S(2)}, u32[]{:S(2)}) collective-permute-start(f32[128,128]{1,0:T(8,128)S(1)} %get-tuple-element.69), channel_id=1, source_target_pairs={{0,4},{3,7},{1,2},{2,1},{4,0},{7,3},{5,6},{6,5},{8,12},{11,15},{9,... | collective-permute-start | bytes 196616 | tf_op jit(solution)/shard_map/ppermute | solution.py:55
  18.1 4.8 %collective-permute-start.4 = (f32[128,128]{1,0:T(8,128)S(1)}, f32[128,128]{1,0:T(8,128)S(1)}, u32[]{:S(2)}, u32[]{:S(2)}) collective-permute-start(f32[128,128]{1,0:T(8,128)S(1)} %get-tuple-element.70), channel_id=1, source_target_pairs={{0,1},{1,0},{2,3},{3,2},{4,5},{5,4},{6,7},{7,6},{8,9},{9,8},{10,11... | collective-permute-start | bytes 196616 | tf_op jit(solution)/shard_map/ppermute | solution.py:55
  23.0 6.9 %collective-permute-start.6 = (f32[160,128]{1,0:T(8,128)S(1)}, f32[160,128]{1,0:T(8,128)S(1)}, u32[]{:S(2)}, u32[]{:S(2)}) collective-permute-start(f32[160,128]{1,0:T(8,128)S(1)} %get-tuple-element.62), channel_id=1, source_target_pairs={{0,16},{16,0},{1,17},{17,1},{2,18},{18,2},{3,19},{19,3},{4,20},{20... | collective-permute-start | bytes 245768 | tf_op jit(solution)/shard_map/ppermute | solution.py:37
  25.1 4.8 %collective-permute-start.8 = (f32[72,128]{1,0:T(8,128)S(1)}, f32[72,128]{1,0:T(8,128)S(1)}, u32[]{:S(2)}, u32[]{:S(2)}) collective-permute-start(f32[72,128]{1,0:T(8,128)S(1)} %get-tuple-element.71), channel_id=1, source_target_pairs={{0,12},{4,8},{8,4},{12,0},{1,13},{5,9},{9,5},{13,1},{2,14},{6,10},... | collective-permute-start | bytes 110600 | tf_op jit(solution)/shard_map/ppermute | solution.py:44
  25.1 4.8 %collective-permute-start.7 = (f32[72,128]{1,0:T(8,128)S(1)}, f32[72,128]{1,0:T(8,128)S(1)}, u32[]{:S(2)}, u32[]{:S(2)}) collective-permute-start(f32[72,128]{1,0:T(8,128)S(1)} %get-tuple-element.72), channel_id=1, source_target_pairs={{0,4},{4,0},{8,12},{12,8},{1,5},{5,1},{9,13},{13,9},{2,6},{6,2},{1... | collective-permute-start | bytes 110600 | tf_op jit(solution)/shard_map/ppermute | solution.py:44
  25.9 4.0 %collective-permute-start.9 = (f32[16,128]{1,0:T(8,128)S(1)}, f32[16,128]{1,0:T(8,128)S(1)}, u32[]{:S(2)}, u32[]{:S(2)}) collective-permute-start(f32[16,128]{1,0:T(8,128)S(1)} %get-tuple-element.64), channel_id=1, source_target_pairs={{0,20},{4,24},{8,28},{12,16},{16,4},{20,8},{24,12},{28,0},{1,21},{... | collective-permute-start | bytes 24584 | tf_op jit(solution)/shard_map/ppermute | solution.py:61

commit v6 on v5

--- a/solution.py
+++ b/solution.py
@@ -237,14 +237,16 @@
         lay_out_top(turned_ref, lines_ref, q, comps, count_x, count_y, size_z)
 
 
-def halo_y_kernel(size_y, grid_in_ref, lines_in_ref, top_in_ref, from_y_ref, grid_ref, lines_ref, turned_ref):
+def halo_y_kernel(size_y, grid_in_ref, lines_in_ref, top_in_ref, first_ref, second_ref, grid_ref, lines_ref, turned_ref):
     comps, size_x, size_z = grid_ref.shape[0], grid_ref.shape[1] - 2, grid_ref.shape[3]
     count_x, count_y = size_x // BX, size_y // BY
     inside = lax.axis_index("gy") != lax.axis_size("gy") - 1
     kept = (row_ids(8) == 0) & inside
+    even = jnp.full((1, LANES), odd("gy")) == 0
 
     def line_at(row):
-        return jnp.where(kept, jnp.broadcast_to(from_y_ref[row : row + 1], (8, LANES)), 0.0)
+        line = jnp.where(even, first_ref[row : row + 1], second_ref[row : row + 1])
+        return jnp.where(kept, jnp.broadcast_to(line, (8, LANES)), 0.0)
 
     for c in range(comps):
         for x in range(size_x + 1):
@@ -258,12 +260,12 @@
 
 
 def block_steps(dims, list_ref, brick_ref):
-    comps, count_x, count_y, count_z, rows_z = dims
+    comps, _, count_y, count_z, rows_z = dims
     nblocks = brick_ref.shape[0]
     sub = row_ids(8)
     row_y = row_ids(REACH_Y).astype(jnp.float32)
     row_z = row_ids(REACH_Z).astype(jnp.float32)
-    lane = lane_ids(REACH_Y)
+    lanes = lane_ids(REACH_Z)
 
     def hat(rows, inside, along):
         return jnp.where(rows == inside, 1.0 - along, 0.0) + jnp.where(rows == inside + 1.0, along, 0.0)
@@ -300,9 +302,7 @@
         tile = jnp.broadcast_to(rows[RESPONSE], (STATE, LANES))
         for i, value in enumerate(state + moved):
             tile = jnp.where(sub == i, value, tile)
-        gap = jnp.zeros((LANES // 2 - comps * REACH_Z, LANES), jnp.float32)
-        main, rest = parts_of(jnp.concatenate(pushed, axis=0))
-        return tile, jnp.concatenate([main, gap, rest, gap], axis=0)
+        return tile, jnp.concatenate(parts_of(jnp.concatenate(pushed, axis=0)), axis=0)
 
     def gathered(one, two):
         tables, windows, weights = [], [], []
@@ -317,51 +317,41 @@
             (((1,), (0,)), ((), ())), preferred_element_type=jnp.float32,
         )
         height = comps * REACH_Z
-        tiles, pushes, spreads = [], [], []
+        tiles, fresh = [], []
         for i, (_, _, rows) in enumerate((one, two)):
+            weight_z, main, rest = weights[i]
             mine = seen[i * height : (i + 1) * height, i * LANES : (i + 1) * LANES]
-            tile, push = stepped(mine, weights[i][0], rows)
+            tile, push = stepped(mine, weight_z, rows)
             tiles.append(tile)
-            pushes.append(push)
-            spreads.extend(weights[i][1:])
-        return tiles, jnp.concatenate(pushes, axis=0).astype(jnp.bfloat16), jnp.concatenate(spreads, axis=0).astype(jnp.bfloat16)
+            unused = jnp.zeros((LANES - comps * SPREAD, LANES), jnp.float32)
+            spread = jnp.concatenate([main] * comps + [unused] + [rest] * comps + [unused], axis=0)
+            fresh.append((push.astype(jnp.bfloat16), spread.astype(jnp.bfloat16)))
+        return tiles, fresh
 
     def shared(push, spread):
-        shares = lax.dot_general(spread, push, (((1,), (1,)), ((), ())), preferred_element_type=jnp.float32)
-        results = []
-        for i in (0, 1):
-            mine = shares[2 * i * SPREAD : 2 * (i + 1) * SPREAD, i * LANES : (i + 1) * LANES]
-            mine = mine[:SPREAD] + mine[SPREAD:]
-            results.append(mine + pltpu.roll(mine, LANES // 2, 1))
-        return results
+        shares = lax.dot_general(push, spread, (((1,), (1,)), ((), ())), preferred_element_type=jnp.float32)
+        height = comps * REACH_Z
+        total = shares[:height, :LANES] + shares[:height, LANES:] + shares[height:, :LANES]
+        result = jnp.zeros((REACH_Z, LANES), jnp.float32)
+        for c in range(comps):
+            inside = (lanes >= c * SPREAD) & (lanes < (c + 1) * SPREAD)
+            result = jnp.where(inside, total[c * REACH_Z : (c + 1) * REACH_Z], result)
+        return result
 
     def add(deposit_ref, at, shares):
-        sums = []
-        for u, share in enumerate(shares):
+        spots = []
+        for u in range(len(shares)):
             _, pair, brick_z = place_of(at + u)
-            first_z = brick_z * BZ
-            within = ((lane - first_z) & (LANES - 1)) < REACH_Z
-            parts = []
-            for c in range(comps):
-                shift = (first_z - c * REACH_Z + LANES) & (LANES - 1)
-                for a in range(REACH_X):
-                    part = pltpu.roll(share[a * REACH_Y : (a + 1) * REACH_Y], shift, 1)
-                    parts.append(jnp.where(within, part, 0.0))
-            sel = jnp.where(brick_z == count_z - 1, 1, 0)
-            start = pl.multiple_of((sel * count_x * count_y + pair) * comps * SPREAD, 8)
-            sums.append((start, parts))
-        for start, parts in sums:
-            spots = [pl.ds(start + i * REACH_Y, REACH_Y) for i in range(comps * REACH_X)]
-            totals = [deposit_ref[spot] + part for spot, part in zip(spots, parts)]
-            for spot, total in zip(spots, totals):
-                deposit_ref[spot] = total
+            spots.append(pl.ds(pl.multiple_of(pair * rows_z + brick_z * BZ, 8), REACH_Z))
+        for spot, share in zip(spots, shares):
+            deposit_ref[spot] = deposit_ref[spot] + share
 
     def group_of(taken):
         tiles, fresh = [], []
         for u in range(0, UNROLL, 2):
-            both, push, spread = gathered(taken[u], taken[u + 1])
+            both, kept = gathered(taken[u], taken[u + 1])
             tiles.extend(both)
-            fresh.append((push, spread))
+            fresh.extend(kept)
         return tiles, fresh
 
     def keep(state_ref, taken, tiles):
@@ -369,10 +359,7 @@
             state_ref[pl.ds(pl.multiple_of(STATE * k, STATE), STATE)] = tile
 
     def deposits_of(kept):
-        shares = []
-        for push, spread in kept:
-            shares.extend(shared(push, spread))
-        return shares
+        return [shared(push, spread) for push, spread in kept]
 
     return loaded, group_of, keep, deposits_of, add
 
@@ -392,8 +379,8 @@
         tiles, fresh = group_of(taken)
         keep(state_ref, taken, tiles)
         for i, (push, spread) in enumerate(fresh):
-            push_ref[group * (UNROLL // 2) + i] = push
-            spread_ref[group * (UNROLL // 2) + i] = spread
+            push_ref[group * UNROLL + i] = push
+            spread_ref[group * UNROLL + i] = spread
 
 
 def deposit_kernel(dims, list_ref, brick_ref, push_ref, spread_ref, deposit_in_ref, deposit_ref):
@@ -402,8 +389,8 @@
 
     @pl.loop(0, groups)
     def _(group):
-        pairs = [group * (UNROLL // 2) + i for i in range(UNROLL // 2)]
-        add(deposit_ref, base + group * UNROLL, deposits_of([(push_ref[i], spread_ref[i]) for i in pairs]))
+        mine = [group * UNROLL + i for i in range(UNROLL)]
+        add(deposit_ref, base + group * UNROLL, deposits_of([(push_ref[i], spread_ref[i]) for i in mine]))
 
 
 def late_kernel(
@@ -420,7 +407,7 @@
         now = base + jnp.maximum(jnp.minimum(group, groups - 1), 0) * UNROLL
         before = base + jnp.maximum(group - 1, 0) * UNROLL
         taken = [loaded(now + u, lines_ref, table_ref) for u in range(UNROLL)]
-        shares = deposits_of([(push_ref[i], spread_ref[i]) for i in range(UNROLL // 2)])
+        shares = deposits_of([(push_ref[i], spread_ref[i]) for i in range(UNROLL)])
         tiles, fresh = group_of(taken)
         add(deposit_ref, before, shares)
         keep(state_ref, taken, tiles)
@@ -440,109 +427,144 @@
             leaving_ref[pl.ds(face * rows * slots + slot, rows, stride=slots)] = tile[:rows]
 
 
-def merge_kernel(tiles_ref, plane_ref):
-    _, comps, planes, _, _ = plane_ref.shape
-    count_x, count_y = (planes - 1) // BX, tiles_ref.shape[0] // (2 * ((planes - 1) // BX) * comps * SPREAD)
-    top = row_ids(REACH_Y) >= BY
-
-    for sel in (0, 1):
-        for c in range(comps):
-            for x in range(planes):
-                bricks = [(x // BX, x % BX)] if x < planes - 1 else []
-                if x and x % BX == 0:
-                    bricks.append((x // BX - 1, BX))
-
-                def tile(q):
-                    total = None
-                    for p, a in bricks:
-                        at = (((sel * count_x + p) * count_y + q) * comps + c) * SPREAD + a * REACH_Y
-                        value = tiles_ref[at : at + REACH_Y]
-                        total = value if total is None else total + value
-                    return total
-
-                carried = None
-                for q in range(0, count_y, 2):
-                    here = tile(q)
-                    if carried is not None:
-                        here = here + carried
-                    between = pltpu.roll(tile(q + 1), BY, 0)
-                    here = here + jnp.where(top, between, 0.0)
-                    carried = jnp.where(top, 0.0, between)
-                    plane_ref[sel, c, x, q * BY : q * BY + REACH_Y] = here
-                plane_ref[sel, c, x, count_y * BY :] = carried
-
-
-def send_y_kernel(push, diffuse, leaving_ref, grid_ref, tiles_ref, y_ref, lines_ref):
-    comps, size_x, size_y = grid_ref.shape[0], grid_ref.shape[1] - 2, grid_ref.shape[2] - 8
+def top_rows(deposit_ref, q, count_x, count_y, rows_z, size_z):
+    total = None
+    for p in range(count_x):
+        at = (p * count_y + q) * rows_z + size_z
+        value = pltpu.roll(deposit_ref[at : at + 8], p, 0) if p else deposit_ref[at : at + 8]
+        total = value if total is None else total + value
+    return total
+
+
+def send_y_kernel(push, diffuse, leaving_ref, grid_ref, deposit_ref, y_ref, tiles_ref, lines_ref):
+    comps, size_x, size_y, size_z = grid_ref.shape[0], grid_ref.shape[1] - 2, grid_ref.shape[2] - 8, grid_ref.shape[3]
     count_x, count_y = size_x // BX, size_y // BY
+    rows_z = size_z + 8
     rows = leaving_ref.shape[1]
+    height = comps * SPREAD
+    for p in range(count_x):
+        at = (p * count_y + count_y - 1) * rows_z
+        tiles_ref[p * height : (p + 1) * height] = jnp.transpose(deposit_ref[at : at + size_z])[:height]
     first = jnp.full((rows, LANES), odd("gy")) == 0
     y_ref[0, 0:rows] = jnp.where(first, leaving_ref[2], leaving_ref[3])
     y_ref[1, 0:rows] = jnp.where(first, leaving_ref[3], leaving_ref[2])
     lines_ref[...] = jnp.zeros_like(lines_ref)
-    for sel in (0, 1):
-        for c in range(comps):
-            for p in range(count_x):
-                at = (((sel * count_x + p) * count_y + count_y - 1) * comps + c) * SPREAD + BY
-                spot = slice(c * ROWS_Y + p * BX, c * ROWS_Y + p * BX + REACH_X)
-                lines_ref[sel, spot] = lines_ref[sel, spot] + tiles_ref[pl.ds(at, REACH_X, stride=REACH_Y)]
-    lane, sub = lane_ids(ROWS_Y), row_ids(ROWS_Y)
-    corner = jnp.zeros((1, LANES), jnp.float32)
+    for c in range(comps):
+        for p in range(count_x):
+            spot = slice(c * ROWS_Y + p * BX, c * ROWS_Y + p * BX + REACH_X)
+            line = tiles_ref[pl.ds(p * height + c * SPREAD + BY, REACH_X, stride=REACH_Y)]
+            lines_ref[spot] = lines_ref[spot] + line
+    wrapped = top_rows(deposit_ref, count_y - 1, count_x, count_y, rows_z, size_z)
+    lane = lane_ids(8)
+    packed = jnp.zeros((8, LANES), jnp.float32)
     for c in range(comps):
         spot = slice(c * ROWS_Y, (c + 1) * ROWS_Y)
-        wrapped = lines_ref[1, spot]
-        line = push * (lines_ref[0, spot] + jnp.where(lane == 0, 0.0, wrapped))
         beside = jnp.concatenate([grid_ref[c, 1 : size_x + 1, size_y - 1], jnp.zeros((8, LANES), jnp.float32)], axis=0)
-        line = line + diffuse * beside
+        line = push * lines_ref[spot] + diffuse * beside
         y_ref[0, rows + c * ROWS_Y : rows + (c + 1) * ROWS_Y] = line
         y_ref[1, rows + c * ROWS_Y : rows + (c + 1) * ROWS_Y] = line
-        far = jnp.broadcast_to(push * wrapped[:, 0:1], (ROWS_Y, LANES))
-        corner = corner + jnp.sum(jnp.where(lane == sub + PACK * c, far, 0.0), axis=0, keepdims=True)
+        for a in range(REACH_X):
+            place = PACK * c + a
+            value = turned(wrapped, place - c * SPREAD - a * REACH_Y - BY)
+            packed = packed + jnp.where(lane == place, value, 0.0)
+    corner = packed[0:1]
+    for p in range(1, count_x):
+        corner = corner + turned(packed[p : p + 1], p * BX)
     at = rows + size_x + 1
-    y_ref[0, at : at + 1] = corner
-    y_ref[1, at : at + 1] = corner
-
-
-def send_xz_kernel(push, diffuse, grid_ref, deposit_ref, x_ref, z_ref):
+    y_ref[0, at : at + 1] = push * corner
+    y_ref[1, at : at + 1] = push * corner
+
+
+def merge_kernel(deposit_ref, top_tiles_ref, plane_ref, face_ref, tiles_ref, turned_ref):
+    comps, planes = plane_ref.shape[:2]
+    count_x, size_z = (planes - 1) // BX, plane_ref.shape[3]
+    rows_z = size_z + 8
+    count_y = deposit_ref.shape[0] // (rows_z * count_x)
+    height = comps * SPREAD
+    for p in range(count_x):
+        for q in range(count_y - 1):
+            at = p * count_y + q
+            value = jnp.transpose(deposit_ref[at * rows_z : at * rows_z + size_z])
+            tiles_ref[at * height : (at + 1) * height] = value[:height]
+    top = row_ids(REACH_Y) >= BY
+    for c in range(comps):
+        for x in range(planes):
+            bricks = [(x // BX, x % BX)] if x < planes - 1 else []
+            if x and x % BX == 0:
+                bricks.append((x // BX - 1, BX))
+
+            def tile(q):
+                total = None
+                for p, a in bricks:
+                    at = c * SPREAD + a * REACH_Y
+                    if q < count_y - 1:
+                        value = tiles_ref[(p * count_y + q) * height + at : (p * count_y + q) * height + at + REACH_Y]
+                    else:
+                        value = top_tiles_ref[p * height + at : p * height + at + REACH_Y]
+                    total = value if total is None else total + value
+                return total
+
+            carried = None
+            for q in range(0, count_y, 2):
+                here = tile(q)
+                if carried is not None:
+                    here = here + carried
+                between = pltpu.roll(tile(q + 1), BY, 0)
+                here = here + jnp.where(top, between, 0.0)
+                carried = jnp.where(top, 0.0, between)
+                plane_ref[c, x, q * BY : q * BY + REACH_Y] = here
+            plane_ref[c, x, count_y * BY :] = carried
+
+    lane = lane_ids(count_x)
+    turned_ref[...] = jnp.zeros_like(turned_ref)
+    for q in range(count_y):
+        wrapped = top_rows(deposit_ref, q, count_x, count_y, rows_z, size_z)[:count_x]
+        within = (lane >= q * BY) & (lane <= (q + 1) * BY)
+        for c in range(comps):
+            for a in range(REACH_X):
+                value = turned(wrapped, q * BY - c * SPREAD - a * REACH_Y)
+                spot = pl.ds(PACK * c + a, count_x, stride=BX)
+                turned_ref[spot] = turned_ref[spot] + jnp.where(within, value, 0.0)
+    face_ref[...] = jnp.transpose(turned_ref[...])[: face_ref.shape[0]]
+
+
+def send_xz_kernel(push, diffuse, grid_ref, deposit_ref, face_ref, x_ref, z_ref):
     comps, size_x = grid_ref.shape[0], grid_ref.shape[1] - 2
     size_y = z_ref.shape[0]
     lane = lane_ids(size_y)
-    packed = jnp.zeros((size_y, LANES), jnp.float32)
-    for c in range(comps):
-        face = jnp.zeros((size_y, LANES), jnp.float32)
-        for x in range(size_x + 1):
-            beyond = push * deposit_ref[1, c, x, 0:size_y]
-            if x < size_x:
-                beyond = beyond + diffuse * turned(grid_ref[c, x + 1, 0:size_y], 1)
-            else:
-                total = push * deposit_ref[0, c, x, 0:size_y] + jnp.where(lane == 0, 0.0, beyond)
-                x_ref[c * size_y : (c + 1) * size_y] = diffuse * grid_ref[c, size_x, 0:size_y] + total
-            face = jnp.where(lane == x, turned(beyond, x), face)
-        packed = packed + turned(face, PACK * c)
+    packed = push * face_ref[0:size_y]
+    for c in range(comps):
+        for x in range(size_x):
+            place = PACK * c + x
+            packed = packed + jnp.where(lane == place, diffuse * turned(grid_ref[c, x + 1, 0:size_y], place + 1), 0.0)
+        total = push * deposit_ref[c, size_x, 0:size_y]
+        x_ref[c * size_y : (c + 1) * size_y] = diffuse * grid_ref[c, size_x, 0:size_y] + total
     z_ref[...] = packed
 
 
-def base_kernel(push, diffuse, grid_ref, deposit_ref, top_ref, base_ref):
+def base_kernel(push, diffuse, count, grid_ref, deposit_ref, top_ref, y1_ref, y2_ref, state_ref, base_ref, velocity_ref):
     comps, size_x, size_y, size_z = base_ref.shape
-    lane = lane_ids(size_y)
+    lane, sub = lane_ids(size_y), row_ids(size_y)
     top = top_ref[0:size_y]
     for c in range(comps):
+        at = count + c * ROWS_Y
+        lines = below(y1_ref, y2_ref, slice(at, at + size_x))
         for x in range(size_x):
             here = grid_ref[c, x + 1, 0:size_y]
-            laplace = grid_ref[c, x + 2, 0:size_y]
-            if x:
-                laplace = laplace + grid_ref[c, x, 0:size_y]
-            before = jnp.where(row_ids(size_y) == 0, 0.0, pltpu.roll(here, 1, 0))
+            before = jnp.where(sub == 0, 0.0, pltpu.roll(here, 1, 0))
+            laplace = grid_ref[c, x, 0:size_y] + grid_ref[c, x + 2, 0:size_y]
             laplace = laplace + grid_ref[c, x + 1, 1 : size_y + 1] + before
             ahead = jnp.where(lane == size_z - 1, turned(top, size_z - 1 - (PACK * c + x)), turned(here, -1))
             laplace = laplace + ahead + jnp.where(lane == 0, 0.0, turned(here, 1)) - 6.0 * here
-            total = deposit_ref[0, c, x, 0:size_y] + jnp.where(lane == 0, 0.0, deposit_ref[1, c, x, 0:size_y])
-            base_ref[c, x] = here + diffuse * laplace + push * total
+            total = here + diffuse * laplace + push * deposit_ref[c, x, 0:size_y]
+            line = jnp.broadcast_to(lines[x : x + 1], (size_y, LANES))
+            base_ref[c, x] = total + jnp.where(sub == 0, line, 0.0)
+        velocity_ref[c] = state_ref[pl.ds(c, velocity_ref.shape[1], stride=STATE)]
 
 
 def below(first_ref, second_ref, rows):
-    got = jnp.where(odd("gy") == 1, first_ref[rows], second_ref[rows])
-    return jnp.where(lax.axis_index("gy") != 0, got, 0.0)
+    got = jnp.where(jnp.full((1, LANES), odd("gy")) == 1, first_ref[rows], second_ref[rows])
+    return jnp.where(jnp.full((1, LANES), lax.axis_index("gy")) != 0, got, 0.0)
 
 
 def relay_kernel(size_x, size_y, comps, count, first_ref, second_ref, x_in_ref, z_in_ref, leaving_ref, x_ref, z_ref, edge_ref):
@@ -566,20 +588,19 @@
 
 
 def finish_kernel(
-    count, base_ref, y1_ref, y2_ref, x_ref, minus_x_ref, z1_ref, z2_ref, edge_ref, state_ref,
-    gas_ref, arrivals_ref, velocity_ref,
+    count, base_ref, y1_ref, y2_ref, x_ref, minus_x_ref, z1_ref, z2_ref, edge_ref, gas_ref, arrivals_ref,
 ):
     comps, size_x, size_y, _ = base_ref.shape
-    first_row, first_lane = row_ids(size_y) == 0, lane_ids(size_y) == 0
+    first_lane = lane_ids(size_y) == 0
+    odd_y, odd_z = jnp.full((1, LANES), odd("gy")) == 1, jnp.full((1, LANES), odd("gz")) == 1
+    place = jnp.full((1, LANES), lax.axis_index("gy"))
+    lower, upper = place != 0, place != lax.axis_size("gy") - 1
     rows = slice(count, count + size_y)
-    from_first = odd("gz") == 1
-    face = jnp.where(from_first, z1_ref[rows], z2_ref[rows])
+    face = jnp.where(odd_z, z1_ref[rows], z2_ref[rows])
     corner = edge_ref[...]
     for c in range(comps):
         for x in range(size_x):
-            at = count + c * ROWS_Y + x
-            line = jnp.broadcast_to(below(y1_ref, y2_ref, slice(at, at + 1)), (size_y, LANES))
-            total = base_ref[c, x] + jnp.where(first_row, line, 0.0)
+            total = base_ref[c, x]
             far = turned(face, -(PACK * c + x))
             if x == 0:
                 total = total + x_ref[c * size_y : (c + 1) * size_y]
@@ -587,8 +608,6 @@
             gas_ref[c, x] = total + jnp.where(first_lane, far, 0.0)
 
     slots = arrivals_ref.shape[2]
-    lower, upper = lax.axis_index("gy") != 0, lax.axis_index("gy") != lax.axis_size("gy") - 1
-    odd_y = odd("gy") == 1
     for i in range(arrivals_ref.shape[1]):
 
         def rows_of(ref, at=0):
@@ -600,10 +619,8 @@
         arrivals_ref[2, i] = jnp.where(lower, jnp.where(odd_y, y1, y2), 0.0)
         arrivals_ref[3, i] = jnp.where(upper, jnp.where(odd_y, y2, y1), 0.0)
         z1, z2 = rows_of(z1_ref), rows_of(z2_ref)
-        arrivals_ref[4, i] = jnp.where(from_first, z1, z2)
-        arrivals_ref[5, i] = jnp.where(from_first, z2, z1)
-    for c in range(comps):
-        velocity_ref[c] = state_ref[pl.ds(c, velocity_ref.shape[1], stride=STATE)]
+        arrivals_ref[4, i] = jnp.where(odd_z, z1, z2)
+        arrivals_ref[5, i] = jnp.where(odd_z, z2, z1)
 
 
 def per_device(gas_field, velocity, fraction, response, cell_index, brick_index, crossing):
@@ -617,7 +634,7 @@
     rows_z = size_z + 8
     grid_shape = (comps, size_x + 2, ROWS_Y, LANES)
     lines_shape = ((size_x // BX) * (size_y // BY) * comps * rows_z, LANES)
-    deposit_shape = (2 * (size_x // BX) * (size_y // BY) * comps * SPREAD, LANES)
+    deposit_shape = ((size_x // BX) * (size_y // BY) * rows_z, LANES)
 
     inputs = (gas_field, velocity, fraction, response, cell_index, brick_index, crossing)
     inputs = [pltpu.with_memory_space_constraint(array, pltpu.HBM) for array in inputs]
@@ -644,7 +661,7 @@
     )
     line_rows = -(-(comps * size_x + comps + 1) // 8) * 8
     (y_lines,) = call(y_lines_kernel, [(line_rows, LANES)], grid, from_z, from_x, from_xz, ready)
-    from_y = moved_along(y_lines, "gy", -1)
+    y1, y2 = swapped_y((y_lines, y_lines))
     square = pltpu.VMEM((LANES, LANES), jnp.float32)
     grid, lines, top = call(
         halo_xz_kernel, [grid_shape, lines_shape, (LANES, LANES)], grid, lines, from_z, from_x, from_xz,
@@ -655,17 +672,17 @@
     slots = crossing.shape[1]
     count = 7 * slots
 
-    def parts(pairs):
-        return [(pairs, 2 * LANES, LANES), (pairs, 4 * SPREAD, LANES)]
+    def parts(many):
+        return [(many, 2 * comps * REACH_Z, LANES), (many, 2 * LANES, LANES)]
 
     state, push_parts, spread_parts = call(
         functools.partial(gather_kernel, dims),
         [(STATE * spare, LANES)]
-        + [jax.ShapeDtypeStruct(shape, jnp.bfloat16) for shape in parts((nblocks + UNROLL) // 2)],
+        + [jax.ShapeDtypeStruct(shape, jnp.bfloat16) for shape in parts(nblocks + UNROLL)],
         blocks, brick_index, lines, table, smem=(0, 1), cycles=4000,
     )
     grid, lines = call(
-        functools.partial(halo_y_kernel, size_y), [grid_shape, lines_shape], grid, lines, top, from_y,
+        functools.partial(halo_y_kernel, size_y), [grid_shape, lines_shape], grid, lines, top, y1, y2,
         aliases={0: 0, 1: 1}, scratch=(square,), cycles=1000,
     )
     state, deposit, leaving = call(
@@ -673,25 +690,31 @@
         [(STATE * spare, LANES), deposit_shape, (6 * count, LANES)],
         blocks, brick_index, crossing, lines, table, state, deposit,
         smem=(0, 1, 2), aliases={5: 0, 6: 1}, cycles=2000,
-        scratch=[pltpu.VMEM(shape, jnp.bfloat16) for shape in parts(UNROLL // 2)],
+        scratch=[pltpu.VMEM(shape, jnp.bfloat16) for shape in parts(UNROLL)],
     )
     leaving = leaving.reshape(6, count, LANES)
-    (to_y,) = call(
-        functools.partial(send_y_kernel, push, diffuse), [(2, count + comps * ROWS_Y, LANES)],
-        leaving, grid, deposit, cycles=300, scratch=(pltpu.VMEM((2, comps * ROWS_Y, LANES), jnp.float32),),
+    height = comps * SPREAD
+    to_y, top_tiles = call(
+        functools.partial(send_y_kernel, push, diffuse),
+        [(2, count + comps * ROWS_Y, LANES), ((size_x // BX) * height, LANES)],
+        leaving, grid, deposit, cycles=300, scratch=(pltpu.VMEM((comps * ROWS_Y, LANES), jnp.float32),),
     )
     y1, y2 = swapped_y((to_y[0], to_y[1]))
     (deposit,) = call(
         functools.partial(deposit_kernel, dims), [deposit_shape], blocks, brick_index, push_parts, spread_parts, deposit,
         smem=(0, 1), aliases={4: 0}, cycles=4000,
     )
-    (deposit,) = call(merge_kernel, [(2, comps, size_x + 1, ROWS_Y, LANES)], deposit, cycles=500)
+    deposit, over = call(
+        merge_kernel, [(comps, size_x + 1, ROWS_Y, LANES), (ROWS_Y, LANES)], deposit, top_tiles,
+        cycles=1000, scratch=(pltpu.VMEM(((size_x // BX) * (size_y // BY) * height, LANES), jnp.float32), square),
+    )
     to_x, to_z = call(
         functools.partial(send_xz_kernel, push, diffuse), [(comps * size_y, LANES), (size_y, LANES)],
-        grid, deposit, cycles=500,
-    )
-    (base,) = call(
-        functools.partial(base_kernel, push, diffuse), [gas_field.shape], grid, deposit, top, cycles=1000,
+        grid, deposit, over, cycles=500,
+    )
+    base, velocity_next = call(
+        functools.partial(base_kernel, push, diffuse, count), [gas_field.shape, (comps, nblocks, LANES)],
+        grid, deposit, top, y1, y2, state, cycles=1000,
     )
     edge = comps * size_y
     both = lax.axis_size("gx") == 2
@@ -704,10 +727,9 @@
     z1, z2 = swapped_z((to_z[0], to_z[1]))
     got_xz = moved_diagonally(to_xz, 1)
     got_mx = got_x if both else moved_along(leaving[1], "gx", -1)
-    gas_next, arrivals, velocity_next = call(
-        functools.partial(finish_kernel, count),
-        [gas_field.shape, (6, 7, crossing.shape[1], LANES), (comps, nblocks, LANES)],
-        base, y1, y2, got_x, got_mx, z1, z2, got_xz, state,
+    gas_next, arrivals = call(
+        functools.partial(finish_kernel, count), [gas_field.shape, (6, 7, slots, LANES)],
+        base, y1, y2, got_x, got_mx, z1, z2, got_xz,
     )
     return gas_next, jnp.transpose(velocity_next, (1, 0, 2)), jnp.transpose(arrivals, (0, 2, 1, 3))
 

time: 30.9 us -> 30.9 us (level)
  waiting for transfers between devices: 3.46 us -> 3.02 us
    ppermute x4 -> x3, starting transfers between devices: 9.83 us -> 5.59 us  [moved_along(): lax.ppermute(block, axis, [(i, (i + distance) % count) for i in range(cou...]
    ppermute x1 -> x2, starting transfers between devices: 0.74 us -> 4.93 us  [swapped_y(): lax.ppermute(blocks[0], 'gy', first)]
    ppermute x2, waiting for transfers between devices: 3.44 us -> 3 us  [moved_diagonally(): return lax.ppermute(block, ('gx', 'gz'), route)]
    ppermute x1, starting transfers between devices: 0.81 us -> 1.21 us  [swapped_z(): lax.ppermute(blocks[0], 'gz', first)]
  transfers between devices with their start and end apart: 10 -> 11, of which waited for: 1 -> 1; matrix products, arithmetic and copies ran while one was open for 0% -> 0% of each run, Pallas kernels for 30% -> 30%
where the time goes in v6:
time: 30.9 us; the launch traced here: 30.8 us
  Pallas kernels  14.4 us (47%)
  starting transfers between devices  12.5 us (40%)
  waiting for transfers between devices  3.02 us (10%)
  between operations  0.79 us (3%)
    pallas_call x14, Pallas kernels, call(): pl.pallas_call(body, out_shape=[o if isinstance(o, jax.ShapeDtypeStruct)...  14.4 us
    ppermute x3, starting transfers between devices, moved_along(): lax.ppermute(block, axis, [(i, (i + distance) % count) for i in range(cou...  5.59 us
    ppermute x2, starting transfers between devices, swapped_y(): lax.ppermute(blocks[0], 'gy', first)  4.93 us
    ppermute x2, waiting for transfers between devices, moved_diagonally(): return lax.ppermute(block, ('gx', 'gz'), route)  3 us
    ppermute x1, starting transfers between devices, swapped_z(): lax.ppermute(blocks[0], 'gz', first)  1.21 us
  transfers between devices with their start and end apart: 11, of which 1 were waited for; matrix products, arithmetic and copies ran while one was open for 0% of the time, Pallas kernels for 30%

profile of v6, /device:TPU:0, one launch (start us, length us, event | category | flops | bytes accessed | tf_op | source)
XLA Modules:
  0.0 30.8 jit_solution(11784285475512211410)
XLA Ops:
  0.6 1.2 %shard_map.94 = (f32[3,18,24,128]{3,2,1,0:T(8,128)S(1)}, f32[16,128]{1,0:T(8,128)S(1)}, f32[48,128]{1,0:T(8,128)S(1)}, f32[3,64,128]{2,1,0:T(8,128)S(1)}, f32[3,...) custom-call(f32[3,16,16,128]{3,2,1,0:T(8,128)} %gas_ref.1, ...), custom_call_target="tpu_custom_call" | custom-call | tf_op jit(solution)/shard_map/pallas_call | solution.py:65
  1.9 3.0 %collective-permute-start.1 = (f32[48,128]{1,0:T(8,128)S(1)}, f32[48,128]{1,0:T(8,128)S(1)}, u32[]{:S(2)}, u32[]{:S(2)}) collective-permute-start(f32[48,128]{1,0:T(8,128)S(1)} %get-tuple-element.49), channel_id=1, source_target_pairs={{0,16},{16,0},{1,17},{17,1},{2,18},{18,2},{3,19},{19,3},{4,20},{20... | collective-permute-start | bytes 73736 | tf_op jit(solution)/shard_map/ppermute | solution.py:37
  4.9 0.6 %collective-permute-start.2 = (f32[16,128]{1,0:T(8,128)S(1)}, f32[16,128]{1,0:T(8,128)S(1)}, u32[]{:S(2)}, u32[]{:S(2)}) collective-permute-start(f32[16,128]{1,0:T(8,128)S(1)} %get-tuple-element.48), channel_id=1, source_target_pairs={{0,28},{4,16},{8,20},{12,24},{16,12},{20,0},{24,4},{28,8},{1,29},{... | collective-permute-start | bytes 24584 | tf_op jit(solution)/shard_map/ppermute | solution.py:61
  5.5 1.1 %collective-permute-start = (f32[16,128]{1,0:T(8,128)S(1)}, f32[16,128]{1,0:T(8,128)S(1)}, u32[]{:S(2)}, u32[]{:S(2)}) collective-permute-start(f32[16,128]{1,0:T(8,128)S(1)} %get-tuple-element.48), channel_id=1, source_target_pairs={{0,12},{4,0},{8,4},{12,8},{1,13},{5,1},{9,5},{13,9},{2,14},{6,2},{... | collective-permute-start | bytes 24584 | tf_op jit(solution)/shard_map/ppermute | solution.py:37
  6.6 2.0 %shard_map.95 = (f32[6528,128]{1,0:T(8,128)S(1)}, f32[2176,128]{1,0:T(8,128)S(1)}, f32[1152,128]{1,0:T(8,128)S(1)}, f32[8,128]{1,0:T(8,128)S(1)}, s32[146]{0:T(256)S(1)}) custom-call(f32[3,18,24,128]{3,2,1,0:T(8,128)S(1)} %get-tuple-element.41.grid_ref.grid_in_ref, f32[3,64,128]{2,1,0:T(8,128)S(1)} %get-tuple-element.42.velocity_ref, ...), custom_call_target="tpu_custom_call" | custom-call | flops 12288000 | bytes 3072000 | tf_op jit(solution)/shard_map/pallas_call | solution.py:65
  8.7 0.0 collective-permute-done.2.edge_ref
  8.7 0.0 collective-permute-done.face_ref
  8.7 0.0 collective-permute-done.1.from_x_ref
  8.7 0.1 shard_map.97
  8.8 0.0 collective-permute-start.4
  8.8 3.1 %collective-permute-start.3 = (f32[56,128]{1,0:T(8,128)S(1)}, f32[56,128]{1,0:T(8,128)S(1)}, u32[]{:S(2)}, u32[]{:S(2)}) collective-permute-start(f32[56,128]{1,0:T(8,128)S(1)} %shard_map.97), channel_id=1, source_target_pairs={{0,1},{1,0},{2,3},{3,2},{4,5},{5,4},{6,7},{7,6},{8,9},{9,8},{10,11... | collective-permute-start | bytes 86024 | tf_op jit(solution)/shard_map/ppermute | solution.py:55
  11.9 0.4 %shard_map.96 = (f32[3,18,24,128]{3,2,1,0:T(8,128)S(1)}, f32[6528,128]{1,0:T(8,128)S(1)}, f32[128,128]{1,0:T(8,128)S(1)}) custom-call(f32[3,18,24,128]{3,2,1,0:T(8,128)S(1)} %get-tuple-element.41.grid_ref.grid_in_ref, f32[6528,128]{1,0:T(8,128)S(1)} %get-tuple-element.47.lines_in_ref, ...), custom_call_target="tpu_custom_call", output_to_operand_aliasing={{0}: (0, {}), {1}: (1, {})} | custom-call | flops 4096000 | bytes 1024000 | tf_op jit(solution)/shard_map/pallas_call | solution.py:65
  12.4 2.5 %shard_map.99 = (f32[576,128]{1,0:T(8,128)S(1)}, bf16[72,96,128]{2,1,0:T(8,128)(2,1)S(1)}, bf16[72,256,128]{2,1,0:T(8,128)(2,1)S(1)}) custom-call(s32[146]{0:T(256)S(1)} %get-tuple-element.55.list_ref, s32[64]{0:T(128)S(1)} %get-tuple-element.46.brick_ref, f32[6528,128]{1,0:T(8,128)S(1)} %get-tuple-element.51.lines_in_ref.lines_ref, ...), custom_call_target="tpu_custom_call" | custom-call | flops 16384000 | bytes 4096000 | tf_op jit(solution)/shard_map/pallas_call | solution.py:65
  14.9 0.0 collective-permute-done.4.second_ref
  14.9 0.0 collective-permute-done.3.first_ref
  14.9 0.6 %shard_map.98 = (f32[3,18,24,128]{3,2,1,0:T(8,128)S(1)}, f32[6528,128]{1,0:T(8,128)S(1)}) custom-call(f32[3,18,24,128]{3,2,1,0:T(8,128)S(1)} %get-tuple-element.50.grid_in_ref, f32[6528,128]{1,0:T(8,128)S(1)} %get-tuple-element.51.lines_in_ref.lines_ref, ...), custom_call_target="tpu_custom_call", output_to_operand_aliasing={{0}: (0, {}), {1}: (1, {})} | custom-call | flops 4096000 | bytes 1024000 | tf_op jit(solution)/shard_map/pallas_call | solution.py:65
  15.5 2.1 %shard_map.100 = (f32[576,128]{1,0:T(8,128)S(1)}, f32[2176,128]{1,0:T(8,128)S(1)}, f32[336,128]{1,0:T(8,128)S(1)}) custom-call(s32[146]{0:T(256)S(1)} %get-tuple-element.55.list_ref, s32[64]{0:T(128)S(1)} %get-tuple-element.46.brick_ref, s32[6,8]{1,0:T(8,128)S(1)} %get-tuple-element.59.crossing_ref, ...), custom_call_target="tpu_custom_call", output_to_operand_aliasing={{0}: (5, {}), {1}: (6, {})} | custom-call | flops 8192000 | bytes 2048000 | tf_op jit(solution)/shard_map/pallas_call | solution.py:65
  17.6 0.2 shard_map.102
  17.8 0.1 collective-permute-start.6
  17.9 1.8 %collective-permute-start.5 = (f32[128,128]{1,0:T(8,128)S(1)}, f32[128,128]{1,0:T(8,128)S(1)}, u32[]{:S(2)}, u32[]{:S(2)}) collective-permute-start(f32[128,128]{1,0:T(8,128)S(1)} %get-tuple-element.80), channel_id=1, source_target_pairs={{0,1},{1,0},{2,3},{3,2},{4,5},{5,4},{6,7},{7,6},{8,9},{9,8},{10,11... | collective-permute-start | bytes 196616 | tf_op jit(solution)/shard_map/ppermute | solution.py:55
  19.7 2.8 %shard_map.101.deposit_ref = f32[2176,128]{1,0:T(8,128)S(1)} custom-call(s32[146]{0:T(256)S(1)} %get-tuple-element.55.list_ref, s32[64]{0:T(128)S(1)} %get-tuple-element.46.brick_ref, bf16[72,96,128]{2,1,0:T(8,128)(2,1)S(1)} %get-tuple-element.57.push_ref, bf16[72,256,128]{2,1,0:T(8,128)(2,1)S(1)} %get-tuple-element.58.spread_ref, ...), custom_call_target="tpu_custom_call", output_to_operand_aliasing={{}: (4, {})} | custom-call | flops 16384000 | bytes 4096000 | tf_op jit(solution)/shard_map/pallas_call | solution.py:65
  22.4 0.4 %shard_map.103 = (f32[3,17,24,128]{3,2,1,0:T(8,128)S(1)}, f32[24,128]{1,0:T(8,128)S(1)}) custom-call(f32[2176,128]{1,0:T(8,128)S(1)} %shard_map.101.deposit_ref, f32[480,128]{1,0:T(8,128)S(1)} %get-tuple-element.65.top_tiles_ref), custom_call_target="tpu_custom_call" | custom-call | flops 4096000 | bytes 1024000 | tf_op jit(solution)/shard_map/pallas_call | solution.py:65
  22.9 0.2 shard_map.105
  23.1 0.0 collective-permute-done.6.y2_ref.second_ref
  23.1 0.0 collective-permute-done.5.y1_ref.first_ref
  23.1 1.4 %collective-permute-start.7 = (f32[160,128]{1,0:T(8,128)S(1)}, f32[160,128]{1,0:T(8,128)S(1)}, u32[]{:S(2)}, u32[]{:S(2)}) collective-permute-start(f32[160,128]{1,0:T(8,128)S(1)} %get-tuple-element.73), channel_id=1, source_target_pairs={{0,16},{16,0},{1,17},{17,1},{2,18},{18,2},{3,19},{19,3},{4,20},{20... | collective-permute-start | bytes 245768 | tf_op jit(solution)/shard_map/ppermute | solution.py:37
  24.5 0.1 collective-permute-start.9
  24.6 1.2 %collective-permute-start.8 = (f32[72,128]{1,0:T(8,128)S(1)}, f32[72,128]{1,0:T(8,128)S(1)}, u32[]{:S(2)}, u32[]{:S(2)}) collective-permute-start(f32[72,128]{1,0:T(8,128)S(1)} %get-tuple-element.82), channel_id=1, source_target_pairs={{0,4},{4,0},{8,12},{12,8},{1,5},{5,1},{9,13},{13,9},{2,6},{6,2},{1... | collective-permute-start | bytes 110600 | tf_op jit(solution)/shard_map/ppermute | solution.py:44
  25.8 0.0 collective-permute-start.10
  25.8 1.0 %shard_map.104 = (f32[3,16,16,128]{3,2,1,0:T(8,128)S(1)}, f32[3,64,128]{2,1,0:T(8,128)}) custom-call(f32[3,18,24,128]{3,2,1,0:T(8,128)S(1)} %get-tuple-element.54.grid_ref, f32[3,17,24,128]{3,2,1,0:T(8,128)S(1)} %get-tuple-element.66.deposit_ref, f32[128,128]{1,0:T(8,128)S(1)} %get-tuple-element.52.top_in_ref.top_ref, ...), custom_call_target="tpu_custom_call" | custom-call | flops 4096000 | bytes 1024000 | tf_op jit(solution)/shard_map/pallas_call | solution.py:65
  26.8 3.0 %collective-permute-done.10.edge_ref = f32[16,128]{1,0:T(8,128)S(1)} collective-permute-done((f32[16,128]{1,0:T(8,128)S(1)}, f32[16,128]{1,0:T(8,128)S(1)}, u32[]{:S(2)}, u32[]{:S(2)}) %collective-permute-start.10) | collective-permute-done | bytes 8224 | tf_op jit(solution)/shard_map/ppermute | solution.py:61
  29.8 0.0 collective-permute-done.9.z2_ref
  29.8 0.0 collective-permute-done.8.z1_ref
  29.8 0.0 collective-permute-done.7.x_ref.minus_x_ref
  29.8 0.9 %shard_map.107 = (f32[3,16,16,128]{3,2,1,0:T(8,128)}, f32[6,7,8,128]{3,2,1,0:T(8,128)}) custom-call(f32[3,16,16,128]{3,2,1,0:T(8,128)S(1)} %get-tuple-element.69.base_ref, f32[128,128]{1,0:T(8,128)S(1)} %collective-permute-done.5.y1_ref.first_ref, f32[128,128]{1,0:T(8,128)S(1)} %collective-permute-done.6.y2_ref.second_ref, ...), custom_call_target="tpu_custom_call" | custom-call | tf_op jit(solution)/shard_map/pallas_call | solution.py:65
  (3 shorter events, 0.0 us)
Async XLA Ops:
  1.9 6.8 %collective-permute-start.1 = (f32[48,128]{1,0:T(8,128)S(1)}, f32[48,128]{1,0:T(8,128)S(1)}, u32[]{:S(2)}, u32[]{:S(2)}) collective-permute-start(f32[48,128]{1,0:T(8,128)S(1)} %get-tuple-element.49), channel_id=1, source_target_pairs={{0,16},{16,0},{1,17},{17,1},{2,18},{18,2},{3,19},{19,3},{4,20},{20... | collective-permute-start | bytes 73736 | tf_op jit(solution)/shard_map/ppermute | solution.py:37
  4.9 3.7 %collective-permute-start.2 = (f32[16,128]{1,0:T(8,128)S(1)}, f32[16,128]{1,0:T(8,128)S(1)}, u32[]{:S(2)}, u32[]{:S(2)}) collective-permute-start(f32[16,128]{1,0:T(8,128)S(1)} %get-tuple-element.48), channel_id=1, source_target_pairs={{0,28},{4,16},{8,20},{12,24},{16,12},{20,0},{24,4},{28,8},{1,29},{... | collective-permute-start | bytes 24584 | tf_op jit(solution)/shard_map/ppermute | solution.py:61
  5.5 3.2 %collective-permute-start = (f32[16,128]{1,0:T(8,128)S(1)}, f32[16,128]{1,0:T(8,128)S(1)}, u32[]{:S(2)}, u32[]{:S(2)}) collective-permute-start(f32[16,128]{1,0:T(8,128)S(1)} %get-tuple-element.48), channel_id=1, source_target_pairs={{0,12},{4,0},{8,4},{12,8},{1,13},{5,1},{9,5},{13,9},{2,14},{6,2},{... | collective-permute-start | bytes 24584 | tf_op jit(solution)/shard_map/ppermute | solution.py:37
  8.8 6.1 %collective-permute-start.4 = (f32[56,128]{1,0:T(8,128)S(1)}, f32[56,128]{1,0:T(8,128)S(1)}, u32[]{:S(2)}, u32[]{:S(2)}) collective-permute-start(f32[56,128]{1,0:T(8,128)S(1)} %shard_map.97), channel_id=1, source_target_pairs={{0,4},{3,7},{1,2},{2,1},{4,0},{7,3},{5,6},{6,5},{8,12},{11,15},{9,... | collective-permute-start | bytes 86024 | tf_op jit(solution)/shard_map/ppermute | solution.py:55
  8.8 6.1 %collective-permute-start.3 = (f32[56,128]{1,0:T(8,128)S(1)}, f32[56,128]{1,0:T(8,128)S(1)}, u32[]{:S(2)}, u32[]{:S(2)}) collective-permute-start(f32[56,128]{1,0:T(8,128)S(1)} %shard_map.97), channel_id=1, source_target_pairs={{0,1},{1,0},{2,3},{3,2},{4,5},{5,4},{6,7},{7,6},{8,9},{9,8},{10,11... | collective-permute-start | bytes 86024 | tf_op jit(solution)/shard_map/ppermute | solution.py:55
  17.8 5.3 %collective-permute-start.6 = (f32[128,128]{1,0:T(8,128)S(1)}, f32[128,128]{1,0:T(8,128)S(1)}, u32[]{:S(2)}, u32[]{:S(2)}) collective-permute-start(f32[128,128]{1,0:T(8,128)S(1)} %get-tuple-element.79), channel_id=1, source_target_pairs={{0,4},{3,7},{1,2},{2,1},{4,0},{7,3},{5,6},{6,5},{8,12},{11,15},{9,... | collective-permute-start | bytes 196616 | tf_op jit(solution)/shard_map/ppermute | solution.py:55
  17.9 5.2 %collective-permute-start.5 = (f32[128,128]{1,0:T(8,128)S(1)}, f32[128,128]{1,0:T(8,128)S(1)}, u32[]{:S(2)}, u32[]{:S(2)}) collective-permute-start(f32[128,128]{1,0:T(8,128)S(1)} %get-tuple-element.80), channel_id=1, source_target_pairs={{0,1},{1,0},{2,3},{3,2},{4,5},{5,4},{6,7},{7,6},{8,9},{9,8},{10,11... | collective-permute-start | bytes 196616 | tf_op jit(solution)/shard_map/ppermute | solution.py:55
  23.1 6.7 %collective-permute-start.7 = (f32[160,128]{1,0:T(8,128)S(1)}, f32[160,128]{1,0:T(8,128)S(1)}, u32[]{:S(2)}, u32[]{:S(2)}) collective-permute-start(f32[160,128]{1,0:T(8,128)S(1)} %get-tuple-element.73), channel_id=1, source_target_pairs={{0,16},{16,0},{1,17},{17,1},{2,18},{18,2},{3,19},{19,3},{4,20},{20... | collective-permute-start | bytes 245768 | tf_op jit(solution)/shard_map/ppermute | solution.py:37
  24.5 5.3 %collective-permute-start.9 = (f32[72,128]{1,0:T(8,128)S(1)}, f32[72,128]{1,0:T(8,128)S(1)}, u32[]{:S(2)}, u32[]{:S(2)}) collective-permute-start(f32[72,128]{1,0:T(8,128)S(1)} %get-tuple-element.81), channel_id=1, source_target_pairs={{0,12},{4,8},{8,4},{12,0},{1,13},{5,9},{9,5},{13,1},{2,14},{6,10},... | collective-permute-start | bytes 110600 | tf_op jit(solution)/shard_map/ppermute | solution.py:44
  24.6 5.2 %collective-permute-start.8 = (f32[72,128]{1,0:T(8,128)S(1)}, f32[72,128]{1,0:T(8,128)S(1)}, u32[]{:S(2)}, u32[]{:S(2)}) collective-permute-start(f32[72,128]{1,0:T(8,128)S(1)} %get-tuple-element.82), channel_id=1, source_target_pairs={{0,4},{4,0},{8,12},{12,8},{1,5},{5,1},{9,13},{13,9},{2,6},{6,2},{1... | collective-permute-start | bytes 110600 | tf_op jit(solution)/shard_map/ppermute | solution.py:44
  25.8 4.0 %collective-permute-start.10 = (f32[16,128]{1,0:T(8,128)S(1)}, f32[16,128]{1,0:T(8,128)S(1)}, u32[]{:S(2)}, u32[]{:S(2)}) collective-permute-start(f32[16,128]{1,0:T(8,128)S(1)} %get-tuple-element.75), channel_id=1, source_target_pairs={{0,20},{4,24},{8,28},{12,16},{16,4},{20,8},{24,12},{28,0},{1,21},{... | collective-permute-start | bytes 24584 | tf_op jit(solution)/shard_map/ppermute | solution.py:61

commit v7 on v6

--- a/solution.py
+++ b/solution.py
@@ -369,7 +369,21 @@
     return late * room, (list_ref[2 * room + late] + UNROLL - 1) // UNROLL
 
 
-def gather_kernel(dims, list_ref, brick_ref, lines_ref, table_ref, state_ref, push_ref, spread_ref):
+def fetched(sems, *pairs):
+    copies = [pltpu.make_async_copy(source, target, sems.at[i]) for i, (source, target) in enumerate(pairs)]
+    for copy in copies:
+        copy.start()
+    return copies
+
+
+def gather_kernel(
+    dims, list_in, brick_in, table_ref, grid_in_ref, lines_in_ref, face_ref, from_x_ref, edge_ref,
+    state_ref, push_ref, spread_ref, grid_ref, lines_ref, top_ref, list_ref, brick_ref, turned_ref, sems,
+):
+    copies = fetched(sems, (list_in, list_ref), (brick_in, brick_ref))
+    halo_xz_kernel(grid_in_ref, lines_in_ref, face_ref, from_x_ref, edge_ref, grid_ref, lines_ref, top_ref, turned_ref)
+    for copy in copies:
+        copy.wait()
     loaded, group_of, keep, _, _ = block_steps(dims, list_ref, brick_ref)
     base, groups = groups_in(list_ref, 0)
 
@@ -394,9 +408,17 @@
 
 
 def late_kernel(
-    dims, slots, list_ref, brick_ref, crossing_ref, lines_ref, table_ref, state_in_ref, deposit_in_ref,
-    state_ref, deposit_ref, leaving_ref, push_ref, spread_ref,
+    dims, slots, list_in, brick_in, crossing_in, table_ref, grid_in_ref, lines_in_ref, top_in_ref, first_ref, second_ref,
+    state_in_ref, deposit_in_ref,
+    grid_ref, lines_ref, state_ref, deposit_ref, leaving_ref,
+    push_ref, spread_ref, list_ref, brick_ref, crossing_ref, turned_ref, sems,
 ):
+    copies = fetched(sems, (list_in, list_ref), (brick_in, brick_ref), (crossing_in, crossing_ref))
+    halo_y_kernel(
+        dims[2] * BY, grid_in_ref, lines_in_ref, top_in_ref, first_ref, second_ref, grid_ref, lines_ref, turned_ref
+    )
+    for copy in copies:
+        copy.wait()
     loaded, group_of, keep, deposits_of, add = block_steps(dims, list_ref, brick_ref)
     base, groups = groups_in(list_ref, 1)
     push_ref[...] = jnp.zeros_like(push_ref)
@@ -578,11 +600,12 @@
     if x_ref.shape[0] > edge + count:
         x_ref[edge + count : edge + 2 * count] = leaving_ref[1]
     at = count + size_x + 1
-    edge_ref[...] = z_in_ref[...]
+    edge_ref[size_y:] = jnp.zeros((edge_ref.shape[0] - size_y, LANES), jnp.float32)
+    edge_ref[0:size_y] = z_in_ref[...]
     edge_ref[0:1] = z_in_ref[0:1] + below(first_ref, second_ref, slice(at, at + 1))
     up = odd("gz")
     z_ref[up, 0:count] = leaving_ref[4]
-    z_ref[up, count : count + size_y] = edge_ref[...]
+    z_ref[up, count : count + size_y] = edge_ref[0:size_y]
     z_ref[1 - up, 0:count] = leaving_ref[5]
     z_ref[1 - up, count : count + size_y] = jnp.zeros((size_y, LANES), jnp.float32)
 
@@ -597,7 +620,7 @@
     lower, upper = place != 0, place != lax.axis_size("gy") - 1
     rows = slice(count, count + size_y)
     face = jnp.where(odd_z, z1_ref[rows], z2_ref[rows])
-    corner = edge_ref[...]
+    corner = edge_ref[0:size_y]
     for c in range(comps):
         for x in range(size_x):
             total = base_ref[c, x]
@@ -663,11 +686,7 @@
     (y_lines,) = call(y_lines_kernel, [(line_rows, LANES)], grid, from_z, from_x, from_xz, ready)
     y1, y2 = swapped_y((y_lines, y_lines))
     square = pltpu.VMEM((LANES, LANES), jnp.float32)
-    grid, lines, top = call(
-        halo_xz_kernel, [grid_shape, lines_shape, (LANES, LANES)], grid, lines, from_z, from_x, from_xz,
-        aliases={0: 0, 1: 1}, scratch=(square,), cycles=1000,
-    )
-
+    scalars = (pltpu.SMEM(blocks.shape, jnp.int32), pltpu.SMEM(brick_index.shape, jnp.int32))
     dims = (comps, size_x // BX, size_y // BY, size_z // BZ, rows_z)
     slots = crossing.shape[1]
     count = 7 * slots
@@ -675,22 +694,26 @@
     def parts(many):
         return [(many, 2 * comps * REACH_Z, LANES), (many, 2 * LANES, LANES)]
 
-    state, push_parts, spread_parts = call(
+    state, push_parts, spread_parts, grid, lines, top = call(
         functools.partial(gather_kernel, dims),
         [(STATE * spare, LANES)]
-        + [jax.ShapeDtypeStruct(shape, jnp.bfloat16) for shape in parts(nblocks + UNROLL)],
-        blocks, brick_index, lines, table, smem=(0, 1), cycles=4000,
-    )
-    grid, lines = call(
-        functools.partial(halo_y_kernel, size_y), [grid_shape, lines_shape], grid, lines, top, y1, y2,
-        aliases={0: 0, 1: 1}, scratch=(square,), cycles=1000,
-    )
-    state, deposit, leaving = call(
+        + [jax.ShapeDtypeStruct(shape, jnp.bfloat16) for shape in parts(nblocks + UNROLL)]
+        + [grid_shape, lines_shape, (LANES, LANES)],
+        blocks, brick_index, table, grid, lines, from_z, from_x, from_xz,
+        aliases={3: 3, 4: 4}, cycles=4000, scratch=(*scalars, square, pltpu.SemaphoreType.DMA((2,))),
+    )
+    grid, lines, state, deposit, leaving = call(
         functools.partial(late_kernel, dims, slots),
-        [(STATE * spare, LANES), deposit_shape, (6 * count, LANES)],
-        blocks, brick_index, crossing, lines, table, state, deposit,
-        smem=(0, 1, 2), aliases={5: 0, 6: 1}, cycles=2000,
-        scratch=[pltpu.VMEM(shape, jnp.bfloat16) for shape in parts(UNROLL)],
+        [grid_shape, lines_shape, (STATE * spare, LANES), deposit_shape, (6 * count, LANES)],
+        blocks, brick_index, crossing, table, grid, lines, top, y1, y2, state, deposit,
+        aliases={4: 0, 5: 1, 9: 2, 10: 3}, cycles=2000,
+        scratch=[
+            *(pltpu.VMEM(shape, jnp.bfloat16) for shape in parts(UNROLL)),
+            *scalars,
+            pltpu.SMEM(crossing.shape, jnp.int32),
+            square,
+            pltpu.SemaphoreType.DMA((3,)),
+        ],
     )
     leaving = leaving.reshape(6, count, LANES)
     height = comps * SPREAD
@@ -720,7 +743,7 @@
     both = lax.axis_size("gx") == 2
     to_x, to_z, to_xz = call(
         functools.partial(relay_kernel, size_x, size_y, comps, count),
-        [(edge + (2 if both else 1) * count, LANES), (2, count + size_y, LANES), (size_y, LANES)],
+        [(edge + (2 if both else 1) * count, LANES), (2, count + size_y, LANES), (count + size_y + 8, LANES)],
         y1, y2, to_x, to_z, leaving,
     )
     got_x = moved_along(to_x, "gx", 1)

time: 30.9 us -> 29.8 us (0.964); the launches traced: 30.8 us -> 29.3 us
  waiting for transfers between devices: 3.02 us -> 1.82 us
  Pallas kernels: 14.4 us -> 13.9 us
    ppermute x2, waiting for transfers between devices: 3 us -> 0.01 us  [moved_diagonally(): return lax.ppermute(block, ('gx', 'gz'), route)]
    ppermute x1, starting transfers between devices: 0.06 us -> 1.34 us  [swapped_z(): lax.ppermute(blocks[1], 'gz', second)]
    ppermute x1, starting transfers between devices: 1.21 us -> 0.01 us  [swapped_z(): lax.ppermute(blocks[0], 'gz', first)]
    ppermute x1, waiting for transfers between devices: 0.01 us -> 1.07 us  [swapped_z(): lax.ppermute(blocks[1], 'gz', second)]
    ppermute x3, waiting for transfers between devices: 0.01 us -> 0.74 us  [moved_along(): lax.ppermute(block, axis, [(i, (i + distance) % count) for i in range(cou...]
    pallas_call x14 -> x12, Pallas kernels: 14.4 us -> 13.9 us  [call(): pl.pallas_call(body, out_shape=[o if isinstance(o, jax.ShapeDtypeStruct)...]
  transfers between devices with their start and end apart: 11 -> 11, of which waited for: 1 -> 2; matrix products, arithmetic and copies ran while one was open for 0% -> 0% of each run, Pallas kernels for 30% -> 30%
where the time goes in v7:
time: 29.8 us; the launch traced here: 29.3 us
  Pallas kernels  13.9 us (47%)
  starting transfers between devices  12.8 us (43%)
  waiting for transfers between devices  1.82 us (6%)
  between operations  0.77 us (3%)
    pallas_call x12, Pallas kernels, call(): pl.pallas_call(body, out_shape=[o if isinstance(o, jax.ShapeDtypeStruct)...  13.9 us
    ppermute x3, starting transfers between devices, moved_along(): lax.ppermute(block, axis, [(i, (i + distance) % count) for i in range(cou...  5.52 us
    ppermute x2, starting transfers between devices, swapped_y(): lax.ppermute(blocks[0], 'gy', first)  4.95 us
    ppermute x1, starting transfers between devices, swapped_z(): lax.ppermute(blocks[1], 'gz', second)  1.34 us
    ppermute x1, waiting for transfers between devices, swapped_z(): lax.ppermute(blocks[1], 'gz', second)  1.07 us
    ppermute x2, starting transfers between devices, moved_diagonally(): return lax.ppermute(block, ('gx', 'gz'), route)  0.88 us
    ppermute x3, waiting for transfers between devices, moved_along(): lax.ppermute(block, axis, [(i, (i + distance) % count) for i in range(cou...  0.74 us
  transfers between devices with their start and end apart: 11, of which 2 were waited for; matrix products, arithmetic and copies ran while one was open for 0% of the time, Pallas kernels for 30%

profile of v7, /device:TPU:0, one launch (start us, length us, event | category | flops | bytes accessed | tf_op | source)
XLA Modules:
  0.0 29.3 jit_solution(16490075870121670049)
XLA Ops:
  0.6 1.2 %shard_map.94 = (f32[3,18,24,128]{3,2,1,0:T(8,128)S(1)}, f32[16,128]{1,0:T(8,128)S(1)}, f32[48,128]{1,0:T(8,128)S(1)}, f32[3,64,128]{2,1,0:T(8,128)S(1)}, f32[3,...) custom-call(f32[3,16,16,128]{3,2,1,0:T(8,128)} %gas_ref.1, ...), custom_call_target="tpu_custom_call" | custom-call | tf_op jit(solution)/shard_map/pallas_call | solution.py:65
  1.9 3.0 %collective-permute-start.1 = (f32[48,128]{1,0:T(8,128)S(1)}, f32[48,128]{1,0:T(8,128)S(1)}, u32[]{:S(2)}, u32[]{:S(2)}) collective-permute-start(f32[48,128]{1,0:T(8,128)S(1)} %get-tuple-element.51), channel_id=1, source_target_pairs={{0,16},{16,0},{1,17},{17,1},{2,18},{18,2},{3,19},{19,3},{4,20},{20... | collective-permute-start | bytes 73736 | tf_op jit(solution)/shard_map/ppermute | solution.py:37
  4.9 0.6 %collective-permute-start.2 = (f32[16,128]{1,0:T(8,128)S(1)}, f32[16,128]{1,0:T(8,128)S(1)}, u32[]{:S(2)}, u32[]{:S(2)}) collective-permute-start(f32[16,128]{1,0:T(8,128)S(1)} %get-tuple-element.50), channel_id=1, source_target_pairs={{0,28},{4,16},{8,20},{12,24},{16,12},{20,0},{24,4},{28,8},{1,29},{... | collective-permute-start | bytes 24584 | tf_op jit(solution)/shard_map/ppermute | solution.py:61
  5.5 1.1 %collective-permute-start = (f32[16,128]{1,0:T(8,128)S(1)}, f32[16,128]{1,0:T(8,128)S(1)}, u32[]{:S(2)}, u32[]{:S(2)}) collective-permute-start(f32[16,128]{1,0:T(8,128)S(1)} %get-tuple-element.50), channel_id=1, source_target_pairs={{0,12},{4,0},{8,4},{12,8},{1,13},{5,1},{9,5},{13,9},{2,14},{6,2},{... | collective-permute-start | bytes 24584 | tf_op jit(solution)/shard_map/ppermute | solution.py:37
  6.6 2.0 %shard_map.95 = (f32[6528,128]{1,0:T(8,128)S(1)}, f32[2176,128]{1,0:T(8,128)S(1)}, f32[1152,128]{1,0:T(8,128)S(1)}, f32[8,128]{1,0:T(8,128)S(1)}, s32[146]{0:T(256)S(1)}) custom-call(f32[3,18,24,128]{3,2,1,0:T(8,128)S(1)} %get-tuple-element.40.grid_ref.grid_in_ref, f32[3,64,128]{2,1,0:T(8,128)S(1)} %get-tuple-element.41.velocity_ref, ...), custom_call_target="tpu_custom_call" | custom-call | flops 12288000 | bytes 3072000 | tf_op jit(solution)/shard_map/pallas_call | solution.py:65
  8.7 0.0 collective-permute-done.2.edge_ref
  8.7 0.0 collective-permute-done.face_ref
  8.7 0.0 collective-permute-done.1.from_x_ref
  8.7 0.1 shard_map.97
  8.8 0.0 collective-permute-start.4
  8.8 3.1 %collective-permute-start.3 = (f32[56,128]{1,0:T(8,128)S(1)}, f32[56,128]{1,0:T(8,128)S(1)}, u32[]{:S(2)}, u32[]{:S(2)}) collective-permute-start(f32[56,128]{1,0:T(8,128)S(1)} %shard_map.97), channel_id=1, source_target_pairs={{0,1},{1,0},{2,3},{3,2},{4,5},{5,4},{6,7},{7,6},{8,9},{9,8},{10,11... | collective-permute-start | bytes 86024 | tf_op jit(solution)/shard_map/ppermute | solution.py:55
  11.9 2.5 %shard_map.96 = (f32[576,128]{1,0:T(8,128)S(1)}, bf16[72,96,128]{2,1,0:T(8,128)(2,1)S(1)}, bf16[72,256,128]{2,1,0:T(8,128)(2,1)S(1)}, f32[3,18,24,128]{3,2,1,0:T...) custom-call(s32[146]{0:T(256)S(1)} %get-tuple-element.46.list_in.list_, ...), custom_call_target="tpu_custom_call", output_to_operand_aliasing={{3}: (3, {}), {4}: (4, {})} | custom-call | flops 16384000 | bytes 4096000 | tf_op jit(solution)/shard_map/pallas_call | solution.py:65
  14.4 0.0 collective-permute-done.4.second_ref
  14.5 0.0 collective-permute-done.3.first_ref
  14.5 2.5 %shard_map.98 = (f32[3,18,24,128]{3,2,1,0:T(8,128)S(1)}, f32[6528,128]{1,0:T(8,128)S(1)}, f32[576,128]{1,0:T(8,128)S(1)}, f32[2176,128]{1,0:T(8,128)S(1)}, f32[336,128]{1,0:T(8,128)S(1)}) custom-call(s32[146]{0:T(256)S(1)} %get-tuple-element.46.list_in.list_ref, ...), custom_call_target="tpu_custom_call", output_to_operand_aliasing={{0}: (4, {}), {1}: (5, {}), {2}: (9, {}), {3}: (10, {})} | custom-call | flops 8192000 | bytes 2048000 | tf_op jit(solution)/shard_map/pallas_call | solution.py:65
  17.0 0.2 shard_map.100
  17.2 0.1 collective-permute-start.6
  17.3 1.8 %collective-permute-start.5 = (f32[128,128]{1,0:T(8,128)S(1)}, f32[128,128]{1,0:T(8,128)S(1)}, u32[]{:S(2)}, u32[]{:S(2)}) collective-permute-start(f32[128,128]{1,0:T(8,128)S(1)} %get-tuple-element.78), channel_id=1, source_target_pairs={{0,1},{1,0},{2,3},{3,2},{4,5},{5,4},{6,7},{7,6},{8,9},{9,8},{10,11... | collective-permute-start | bytes 196616 | tf_op jit(solution)/shard_map/ppermute | solution.py:55
  19.1 2.8 %shard_map.99.deposit_ref = f32[2176,128]{1,0:T(8,128)S(1)} custom-call(s32[146]{0:T(256)S(1)} %get-tuple-element.46.list_in.list_ref, s32[64]{0:T(128)S(1)} %get-tuple-element.45.brick_ref.brick_in, bf16[72,96,128]{2,1,0:T(8,128)(2,1)S(1)} %get-tuple-element.59.push_ref, ...), custom_call_target="tpu_custom_call", output_to_operand_aliasing={{}: (4, {})} | custom-call | flops 16384000 | bytes 4096000 | tf_op jit(solution)/shard_map/pallas_call | solution.py:65
  21.9 0.4 %shard_map.101 = (f32[3,17,24,128]{3,2,1,0:T(8,128)S(1)}, f32[24,128]{1,0:T(8,128)S(1)}) custom-call(f32[2176,128]{1,0:T(8,128)S(1)} %shard_map.99.deposit_ref, f32[480,128]{1,0:T(8,128)S(1)} %get-tuple-element.63.top_tiles_ref), custom_call_target="tpu_custom_call" | custom-call | flops 4096000 | bytes 1024000 | tf_op jit(solution)/shard_map/pallas_call | solution.py:65
  22.3 0.2 shard_map.103
  22.5 0.0 collective-permute-done.6.y2_ref.second_ref
  22.5 0.0 collective-permute-done.5.y1_ref.first_ref
  22.6 0.3 collective-permute-start.10
  22.9 1.4 %collective-permute-start.7 = (f32[160,128]{1,0:T(8,128)S(1)}, f32[160,128]{1,0:T(8,128)S(1)}, u32[]{:S(2)}, u32[]{:S(2)}) collective-permute-start(f32[160,128]{1,0:T(8,128)S(1)} %get-tuple-element.71), channel_id=1, source_target_pairs={{0,16},{16,0},{1,17},{17,1},{2,18},{18,2},{3,19},{19,3},{4,20},{20... | collective-permute-start | bytes 245768 | tf_op jit(solution)/shard_map/ppermute | solution.py:37
  24.2 1.3 %collective-permute-start.9 = (f32[72,128]{1,0:T(8,128)S(1)}, f32[72,128]{1,0:T(8,128)S(1)}, u32[]{:S(2)}, u32[]{:S(2)}) collective-permute-start(f32[72,128]{1,0:T(8,128)S(1)} %get-tuple-element.79), channel_id=1, source_target_pairs={{0,12},{4,8},{8,4},{12,0},{1,13},{5,9},{9,5},{13,1},{2,14},{6,10},... | collective-permute-start | bytes 110600 | tf_op jit(solution)/shard_map/ppermute | solution.py:44
  25.6 0.0 collective-permute-start.8
  25.6 1.0 %shard_map.102 = (f32[3,16,16,128]{3,2,1,0:T(8,128)S(1)}, f32[3,64,128]{2,1,0:T(8,128)}) custom-call(f32[3,18,24,128]{3,2,1,0:T(8,128)S(1)} %get-tuple-element.58.grid_ref, f32[3,17,24,128]{3,2,1,0:T(8,128)S(1)} %get-tuple-element.64.deposit_ref, f32[128,128]{1,0:T(8,128)S(1)} %get-tuple-element.54.top_in_ref.top_ref, ...), custom_call_target="tpu_custom_call" | custom-call | flops 4096000 | bytes 1024000 | tf_op jit(solution)/shard_map/pallas_call | solution.py:65
  26.5 1.1 %collective-permute-done.9.z2_ref = f32[72,128]{1,0:T(8,128)S(1)} collective-permute-done((f32[72,128]{1,0:T(8,128)S(1)}, f32[72,128]{1,0:T(8,128)S(1)}, u32[]{:S(2)}, u32[]{:S(2)}) %collective-permute-start.9) | collective-permute-done | bytes 36896 | tf_op jit(solution)/shard_map/ppermute | solution.py:44
  27.6 0.0 collective-permute-done.8.z1_ref
  27.6 0.0 collective-permute-done.10.edge_ref
  27.6 0.7 %collective-permute-done.7.x_ref.minus_x_ref = f32[160,128]{1,0:T(8,128)S(1)} collective-permute-done((f32[160,128]{1,0:T(8,128)S(1)}, f32[160,128]{1,0:T(8,128)S(1)}, u32[]{:S(2)}, u32[]{:S(2)}) %collective-permute-start.7) | collective-permute-done | bytes 81952 | tf_op jit(solution)/shard_map/ppermute | solution.py:37
  28.3 0.9 %shard_map.105 = (f32[3,16,16,128]{3,2,1,0:T(8,128)}, f32[6,7,8,128]{3,2,1,0:T(8,128)}) custom-call(f32[3,16,16,128]{3,2,1,0:T(8,128)S(1)} %get-tuple-element.67.base_ref, f32[128,128]{1,0:T(8,128)S(1)} %collective-permute-done.5.y1_ref.first_ref, f32[128,128]{1,0:T(8,128)S(1)} %collective-permute-done.6.y2_ref.second_ref, ...), custom_call_target="tpu_custom_call" | custom-call | tf_op jit(solution)/shard_map/pallas_call | solution.py:65
  (3 shorter events, 0.0 us)
Async XLA Ops:
  1.9 6.8 %collective-permute-start.1 = (f32[48,128]{1,0:T(8,128)S(1)}, f32[48,128]{1,0:T(8,128)S(1)}, u32[]{:S(2)}, u32[]{:S(2)}) collective-permute-start(f32[48,128]{1,0:T(8,128)S(1)} %get-tuple-element.51), channel_id=1, source_target_pairs={{0,16},{16,0},{1,17},{17,1},{2,18},{18,2},{3,19},{19,3},{4,20},{20... | collective-permute-start | bytes 73736 | tf_op jit(solution)/shard_map/ppermute | solution.py:37
  4.9 3.7 %collective-permute-start.2 = (f32[16,128]{1,0:T(8,128)S(1)}, f32[16,128]{1,0:T(8,128)S(1)}, u32[]{:S(2)}, u32[]{:S(2)}) collective-permute-start(f32[16,128]{1,0:T(8,128)S(1)} %get-tuple-element.50), channel_id=1, source_target_pairs={{0,28},{4,16},{8,20},{12,24},{16,12},{20,0},{24,4},{28,8},{1,29},{... | collective-permute-start | bytes 24584 | tf_op jit(solution)/shard_map/ppermute | solution.py:61
  5.5 3.2 %collective-permute-start = (f32[16,128]{1,0:T(8,128)S(1)}, f32[16,128]{1,0:T(8,128)S(1)}, u32[]{:S(2)}, u32[]{:S(2)}) collective-permute-start(f32[16,128]{1,0:T(8,128)S(1)} %get-tuple-element.50), channel_id=1, source_target_pairs={{0,12},{4,0},{8,4},{12,8},{1,13},{5,1},{9,5},{13,9},{2,14},{6,2},{... | collective-permute-start | bytes 24584 | tf_op jit(solution)/shard_map/ppermute | solution.py:37
  8.8 5.7 %collective-permute-start.4 = (f32[56,128]{1,0:T(8,128)S(1)}, f32[56,128]{1,0:T(8,128)S(1)}, u32[]{:S(2)}, u32[]{:S(2)}) collective-permute-start(f32[56,128]{1,0:T(8,128)S(1)} %shard_map.97), channel_id=1, source_target_pairs={{0,4},{3,7},{1,2},{2,1},{4,0},{7,3},{5,6},{6,5},{8,12},{11,15},{9,... | collective-permute-start | bytes 86024 | tf_op jit(solution)/shard_map/ppermute | solution.py:55
  8.8 5.7 %collective-permute-start.3 = (f32[56,128]{1,0:T(8,128)S(1)}, f32[56,128]{1,0:T(8,128)S(1)}, u32[]{:S(2)}, u32[]{:S(2)}) collective-permute-start(f32[56,128]{1,0:T(8,128)S(1)} %shard_map.97), channel_id=1, source_target_pairs={{0,1},{1,0},{2,3},{3,2},{4,5},{5,4},{6,7},{7,6},{8,9},{9,8},{10,11... | collective-permute-start | bytes 86024 | tf_op jit(solution)/shard_map/ppermute | solution.py:55
  17.2 5.3 %collective-permute-start.6 = (f32[128,128]{1,0:T(8,128)S(1)}, f32[128,128]{1,0:T(8,128)S(1)}, u32[]{:S(2)}, u32[]{:S(2)}) collective-permute-start(f32[128,128]{1,0:T(8,128)S(1)} %get-tuple-element.77), channel_id=1, source_target_pairs={{0,4},{3,7},{1,2},{2,1},{4,0},{7,3},{5,6},{6,5},{8,12},{11,15},{9,... | collective-permute-start | bytes 196616 | tf_op jit(solution)/shard_map/ppermute | solution.py:55
  17.3 5.2 %collective-permute-start.5 = (f32[128,128]{1,0:T(8,128)S(1)}, f32[128,128]{1,0:T(8,128)S(1)}, u32[]{:S(2)}, u32[]{:S(2)}) collective-permute-start(f32[128,128]{1,0:T(8,128)S(1)} %get-tuple-element.78), channel_id=1, source_target_pairs={{0,1},{1,0},{2,3},{3,2},{4,5},{5,4},{6,7},{7,6},{8,9},{9,8},{10,11... | collective-permute-start | bytes 196616 | tf_op jit(solution)/shard_map/ppermute | solution.py:55
  22.6 5.0 %collective-permute-start.10 = (f32[80,128]{1,0:T(8,128)S(1)}, f32[80,128]{1,0:T(8,128)S(1)}, u32[]{:S(2)}, u32[]{:S(2)}) collective-permute-start(f32[80,128]{1,0:T(8,128)S(1)} %get-tuple-element.73), channel_id=1, source_target_pairs={{0,20},{4,24},{8,28},{12,16},{16,4},{20,8},{24,12},{28,0},{1,21},{... | collective-permute-start | bytes 122888 | tf_op jit(solution)/shard_map/ppermute | solution.py:61
  22.9 5.5 %collective-permute-start.7 = (f32[160,128]{1,0:T(8,128)S(1)}, f32[160,128]{1,0:T(8,128)S(1)}, u32[]{:S(2)}, u32[]{:S(2)}) collective-permute-start(f32[160,128]{1,0:T(8,128)S(1)} %get-tuple-element.71), channel_id=1, source_target_pairs={{0,16},{16,0},{1,17},{17,1},{2,18},{18,2},{3,19},{19,3},{4,20},{20... | collective-permute-start | bytes 245768 | tf_op jit(solution)/shard_map/ppermute | solution.py:37
  24.2 3.4 %collective-permute-start.9 = (f32[72,128]{1,0:T(8,128)S(1)}, f32[72,128]{1,0:T(8,128)S(1)}, u32[]{:S(2)}, u32[]{:S(2)}) collective-permute-start(f32[72,128]{1,0:T(8,128)S(1)} %get-tuple-element.79), channel_id=1, source_target_pairs={{0,12},{4,8},{8,4},{12,0},{1,13},{5,9},{9,5},{13,1},{2,14},{6,10},... | collective-permute-start | bytes 110600 | tf_op jit(solution)/shard_map/ppermute | solution.py:44
  25.6 2.0 %collective-permute-start.8 = (f32[72,128]{1,0:T(8,128)S(1)}, f32[72,128]{1,0:T(8,128)S(1)}, u32[]{:S(2)}, u32[]{:S(2)}) collective-permute-start(f32[72,128]{1,0:T(8,128)S(1)} %get-tuple-element.80), channel_id=1, source_target_pairs={{0,4},{4,0},{8,12},{12,8},{1,5},{5,1},{9,13},{13,9},{2,6},{6,2},{1... | collective-permute-start | bytes 110600 | tf_op jit(solution)/shard_map/ppermute | solution.py:44

commit v8 on v7

--- a/solution.py
+++ b/solution.py
@@ -52,7 +52,8 @@
         second.append((k * ny, (k ^ 1) * ny))
         second.append((k * ny + ny - 1, (k ^ 1) * ny + ny - 1))
         second.extend((k * ny + j, k * ny + ((j + 1) ^ 1) - 1) for j in range(1, ny - 1))
-    return lax.ppermute(blocks[0], "gy", first), lax.ppermute(blocks[1], ("gz", "gy"), second)
+    middle = lax.ppermute(blocks[1], ("gz", "gy"), second)
+    return lax.ppermute(blocks[0], "gy", first), middle
 
 
 def moved_diagonally(block, distance):
@@ -61,12 +62,14 @@
     return lax.ppermute(block, ("gx", "gz"), route)
 
 
-def call(body, outs, *operands, smem=(), hbm=(), smem_outs=(), scratch=(), aliases=None, cycles=0, limit=40):
+def call(
+    body, outs, *operands, smem=(), hbm=(), smem_outs=(), hbm_outs=(), scratch=(), aliases=None, cycles=0, limit=40
+):
     return pl.pallas_call(
         body,
         out_shape=[o if isinstance(o, jax.ShapeDtypeStruct) else jax.ShapeDtypeStruct(o, jnp.float32) for o in outs],
         in_specs=[SMEM if i in smem else HBM if i in hbm else VMEM for i in range(len(operands))],
-        out_specs=[SMEM if i in smem_outs else VMEM for i in range(len(outs))],
+        out_specs=[SMEM if i in smem_outs else HBM if i in hbm_outs else VMEM for i in range(len(outs))],
         scratch_shapes=list(scratch),
         input_output_aliases=aliases or {},
         compiler_params=pltpu.CompilerParams(vmem_limit_bytes=limit * 1024 * 1024),
@@ -611,7 +614,8 @@
 
 
 def finish_kernel(
-    count, base_ref, y1_ref, y2_ref, x_ref, minus_x_ref, z1_ref, z2_ref, edge_ref, gas_ref, arrivals_ref,
+    count, base_ref, y1_ref, y2_ref, x_ref, minus_x_ref, z1_ref, z2_ref, edge_ref, gas_out, arrivals_out,
+    gas_ref, arrivals_ref, sems,
 ):
     comps, size_x, size_y, _ = base_ref.shape
     first_lane = lane_ids(size_y) == 0
@@ -619,17 +623,6 @@
     place = jnp.full((1, LANES), lax.axis_index("gy"))
     lower, upper = place != 0, place != lax.axis_size("gy") - 1
     rows = slice(count, count + size_y)
-    face = jnp.where(odd_z, z1_ref[rows], z2_ref[rows])
-    corner = edge_ref[0:size_y]
-    for c in range(comps):
-        for x in range(size_x):
-            total = base_ref[c, x]
-            far = turned(face, -(PACK * c + x))
-            if x == 0:
-                total = total + x_ref[c * size_y : (c + 1) * size_y]
-                far = far + turned(corner, -(PACK * c + size_x))
-            gas_ref[c, x] = total + jnp.where(first_lane, far, 0.0)
-
     slots = arrivals_ref.shape[2]
     for i in range(arrivals_ref.shape[1]):
 
@@ -644,6 +637,22 @@
         z1, z2 = rows_of(z1_ref), rows_of(z2_ref)
         arrivals_ref[4, i] = jnp.where(odd_z, z1, z2)
         arrivals_ref[5, i] = jnp.where(odd_z, z2, z1)
+    copies = [pltpu.make_async_copy(arrivals_ref, arrivals_out, sems.at[comps])]
+    copies[0].start()
+    face = jnp.where(odd_z, z1_ref[rows], z2_ref[rows])
+    corner = edge_ref[0:size_y]
+    for c in range(comps):
+        for x in range(size_x):
+            total = base_ref[c, x]
+            far = turned(face, -(PACK * c + x))
+            if x == 0:
+                total = total + x_ref[c * size_y : (c + 1) * size_y]
+                far = far + turned(corner, -(PACK * c + size_x))
+            gas_ref[c, x] = total + jnp.where(first_lane, far, 0.0)
+        copies.append(pltpu.make_async_copy(gas_ref.at[c], gas_out.at[c], sems.at[c]))
+        copies[-1].start()
+    for copy in copies:
+        copy.wait()
 
 
 def per_device(gas_field, velocity, fraction, response, cell_index, brick_index, crossing):
@@ -752,7 +761,12 @@
     got_mx = got_x if both else moved_along(leaving[1], "gx", -1)
     gas_next, arrivals = call(
         functools.partial(finish_kernel, count), [gas_field.shape, (6, 7, slots, LANES)],
-        base, y1, y2, got_x, got_mx, z1, z2, got_xz,
+        base, y1, y2, got_x, got_mx, z1, z2, got_xz, hbm_outs=(0, 1),
+        scratch=(
+            pltpu.VMEM(gas_field.shape, jnp.float32),
+            pltpu.VMEM((6, 7, slots, LANES), jnp.float32),
+            pltpu.SemaphoreType.DMA((comps + 1,)),
+        ),
     )
     return gas_next, jnp.transpose(velocity_next, (1, 0, 2)), jnp.transpose(arrivals, (0, 2, 1, 3))
 

time: 29.8 us -> 29.6 us (level)
  starting transfers between devices: 12.8 us -> 13.2 us
    ppermute x2, starting transfers between devices: 0.88 us -> 1.58 us  [moved_diagonally(): return lax.ppermute(block, ('gx', 'gz'), route)]
    ppermute x3, waiting for transfers between devices: 0.74 us -> 0.36 us  [moved_along(): lax.ppermute(block, axis, [(i, (i + distance) % count) for i in range(cou...]
  transfers between devices with their start and end apart: 11 -> 11, of which waited for: 2 -> 2; matrix products, arithmetic and copies ran while one was open for 0% -> 0% of each run, Pallas kernels for 30% -> 28%
where the time goes in v8:
time: 29.6 us; the launch traced here: 29.4 us
  Pallas kernels  13.7 us (46%)
  starting transfers between devices  13.2 us (45%)
  waiting for transfers between devices  1.74 us (6%)
  between operations  0.77 us (3%)
    pallas_call x12, Pallas kernels, call(): pl.pallas_call(body, out_shape=[o if isinstance(o, jax.ShapeDtypeStruct)...  13.7 us
    ppermute x3, starting transfers between devices, moved_along(): lax.ppermute(block, axis, [(i, (i + distance) % count) for i in range(cou...  5.57 us
    ppermute x2, starting transfers between devices, swapped_y(): return (lax.ppermute(blocks[0], 'gy', first), middle)  4.76 us
    ppermute x2, starting transfers between devices, moved_diagonally(): return lax.ppermute(block, ('gx', 'gz'), route)  1.58 us
    ppermute x1, waiting for transfers between devices, swapped_z(): lax.ppermute(blocks[1], 'gz', second)  1.36 us
    ppermute x1, starting transfers between devices, swapped_z(): lax.ppermute(blocks[1], 'gz', second)  1.17 us
  transfers between devices with their start and end apart: 11, of which 2 were waited for; matrix products, arithmetic and copies ran while one was open for 0% of the time, Pallas kernels for 28%

profile of v8, /device:TPU:0, one launch (start us, length us, event | category | flops | bytes accessed | tf_op | source)
XLA Modules:
  0.0 29.4 jit_solution(4116107534950279515)
XLA Ops:
  0.6 1.2 %shard_map.94 = (f32[3,18,24,128]{3,2,1,0:T(8,128)S(1)}, f32[16,128]{1,0:T(8,128)S(1)}, f32[48,128]{1,0:T(8,128)S(1)}, f32[3,64,128]{2,1,0:T(8,128)S(1)}, f32[3,...) custom-call(f32[3,16,16,128]{3,2,1,0:T(8,128)} %gas_ref.1, ...), custom_call_target="tpu_custom_call" | custom-call | tf_op jit(solution)/shard_map/pallas_call | solution.py:68
  1.9 3.0 %collective-permute-start.1 = (f32[48,128]{1,0:T(8,128)S(1)}, f32[48,128]{1,0:T(8,128)S(1)}, u32[]{:S(2)}, u32[]{:S(2)}) collective-permute-start(f32[48,128]{1,0:T(8,128)S(1)} %get-tuple-element.51), channel_id=1, source_target_pairs={{0,16},{16,0},{1,17},{17,1},{2,18},{18,2},{3,19},{19,3},{4,20},{20... | collective-permute-start | bytes 73736 | tf_op jit(solution)/shard_map/ppermute | solution.py:37
  4.9 0.6 %collective-permute-start.2 = (f32[16,128]{1,0:T(8,128)S(1)}, f32[16,128]{1,0:T(8,128)S(1)}, u32[]{:S(2)}, u32[]{:S(2)}) collective-permute-start(f32[16,128]{1,0:T(8,128)S(1)} %get-tuple-element.50), channel_id=1, source_target_pairs={{0,28},{4,16},{8,20},{12,24},{16,12},{20,0},{24,4},{28,8},{1,29},{... | collective-permute-start | bytes 24584 | tf_op jit(solution)/shard_map/ppermute | solution.py:62
  5.5 1.1 %collective-permute-start = (f32[16,128]{1,0:T(8,128)S(1)}, f32[16,128]{1,0:T(8,128)S(1)}, u32[]{:S(2)}, u32[]{:S(2)}) collective-permute-start(f32[16,128]{1,0:T(8,128)S(1)} %get-tuple-element.50), channel_id=1, source_target_pairs={{0,12},{4,0},{8,4},{12,8},{1,13},{5,1},{9,5},{13,9},{2,14},{6,2},{... | collective-permute-start | bytes 24584 | tf_op jit(solution)/shard_map/ppermute | solution.py:37
  6.6 2.0 %shard_map.95 = (f32[6528,128]{1,0:T(8,128)S(1)}, f32[2176,128]{1,0:T(8,128)S(1)}, f32[1152,128]{1,0:T(8,128)S(1)}, f32[8,128]{1,0:T(8,128)S(1)}, s32[146]{0:T(256)S(1)}) custom-call(f32[3,18,24,128]{3,2,1,0:T(8,128)S(1)} %get-tuple-element.40.grid_ref.grid_in_ref, f32[3,64,128]{2,1,0:T(8,128)S(1)} %get-tuple-element.41.velocity_ref, ...), custom_call_target="tpu_custom_call" | custom-call | flops 12288000 | bytes 3072000 | tf_op jit(solution)/shard_map/pallas_call | solution.py:68
  8.7 0.0 collective-permute-done.2.edge_ref
  8.7 0.0 collective-permute-done.face_ref
  8.7 0.0 collective-permute-done.1.from_x_ref
  8.7 0.1 shard_map.97
  8.8 0.0 collective-permute-start.4
  8.8 3.1 %collective-permute-start.3 = (f32[56,128]{1,0:T(8,128)S(1)}, f32[56,128]{1,0:T(8,128)S(1)}, u32[]{:S(2)}, u32[]{:S(2)}) collective-permute-start(f32[56,128]{1,0:T(8,128)S(1)} %shard_map.97), channel_id=1, source_target_pairs={{0,1},{1,0},{2,3},{3,2},{4,5},{5,4},{6,7},{7,6},{8,9},{9,8},{10,11... | collective-permute-start | bytes 86024 | tf_op jit(solution)/shard_map/ppermute | solution.py:56
  11.9 2.2 %shard_map.96 = (f32[576,128]{1,0:T(8,128)S(1)}, bf16[72,96,128]{2,1,0:T(8,128)(2,1)S(1)}, bf16[72,256,128]{2,1,0:T(8,128)(2,1)S(1)}, f32[3,18,24,128]{3,2,1,0:T...) custom-call(s32[146]{0:T(256)S(1)} %get-tuple-element.46.list_in.list_, ...), custom_call_target="tpu_custom_call", output_to_operand_aliasing={{3}: (3, {}), {4}: (4, {})} | custom-call | flops 16384000 | bytes 4096000 | tf_op jit(solution)/shard_map/pallas_call | solution.py:68
  14.2 0.0 collective-permute-done.4.second_ref
  14.2 0.0 collective-permute-done.3.first_ref
  14.2 3.0 %shard_map.98 = (f32[3,18,24,128]{3,2,1,0:T(8,128)S(1)}, f32[6528,128]{1,0:T(8,128)S(1)}, f32[576,128]{1,0:T(8,128)S(1)}, f32[2176,128]{1,0:T(8,128)S(1)}, f32[336,128]{1,0:T(8,128)S(1)}) custom-call(s32[146]{0:T(256)S(1)} %get-tuple-element.46.list_in.list_ref, ...), custom_call_target="tpu_custom_call", output_to_operand_aliasing={{0}: (4, {}), {1}: (5, {}), {2}: (9, {}), {3}: (10, {})} | custom-call | flops 8192000 | bytes 2048000 | tf_op jit(solution)/shard_map/pallas_call | solution.py:68
  17.2 0.2 shard_map.100
  17.4 0.1 collective-permute-start.6
  17.5 1.6 %collective-permute-start.5 = (f32[128,128]{1,0:T(8,128)S(1)}, f32[128,128]{1,0:T(8,128)S(1)}, u32[]{:S(2)}, u32[]{:S(2)}) collective-permute-start(f32[128,128]{1,0:T(8,128)S(1)} %get-tuple-element.78), channel_id=1, source_target_pairs={{0,1},{1,0},{2,3},{3,2},{4,5},{5,4},{6,7},{7,6},{8,9},{9,8},{10,11... | collective-permute-start | bytes 196616 | tf_op jit(solution)/shard_map/ppermute | solution.py:56
  19.1 2.4 %shard_map.99.deposit_ref = f32[2176,128]{1,0:T(8,128)S(1)} custom-call(s32[146]{0:T(256)S(1)} %get-tuple-element.46.list_in.list_ref, s32[64]{0:T(128)S(1)} %get-tuple-element.45.brick_ref.brick_in, bf16[72,96,128]{2,1,0:T(8,128)(2,1)S(1)} %get-tuple-element.59.push_ref, ...), custom_call_target="tpu_custom_call", output_to_operand_aliasing={{}: (4, {})} | custom-call | flops 16384000 | bytes 4096000 | tf_op jit(solution)/shard_map/pallas_call | solution.py:68
  21.5 0.4 %shard_map.101 = (f32[3,17,24,128]{3,2,1,0:T(8,128)S(1)}, f32[24,128]{1,0:T(8,128)S(1)}) custom-call(f32[2176,128]{1,0:T(8,128)S(1)} %shard_map.99.deposit_ref, f32[480,128]{1,0:T(8,128)S(1)} %get-tuple-element.63.top_tiles_ref), custom_call_target="tpu_custom_call" | custom-call | flops 4096000 | bytes 1024000 | tf_op jit(solution)/shard_map/pallas_call | solution.py:68
  21.9 0.2 shard_map.103
  22.1 0.0 collective-permute-done.6.y2_ref.second_ref
  22.1 0.0 collective-permute-done.5.y1_ref.first_ref
  22.2 1.0 %collective-permute-start.10 = (f32[80,128]{1,0:T(8,128)S(1)}, f32[80,128]{1,0:T(8,128)S(1)}, u32[]{:S(2)}, u32[]{:S(2)}) collective-permute-start(f32[80,128]{1,0:T(8,128)S(1)} %get-tuple-element.73), channel_id=1, source_target_pairs={{0,20},{4,24},{8,28},{12,16},{16,4},{20,8},{24,12},{28,0},{1,21},{... | collective-permute-start | bytes 122888 | tf_op jit(solution)/shard_map/ppermute | solution.py:62
  23.2 1.4 %collective-permute-start.7 = (f32[160,128]{1,0:T(8,128)S(1)}, f32[160,128]{1,0:T(8,128)S(1)}, u32[]{:S(2)}, u32[]{:S(2)}) collective-permute-start(f32[160,128]{1,0:T(8,128)S(1)} %get-tuple-element.71), channel_id=1, source_target_pairs={{0,16},{16,0},{1,17},{17,1},{2,18},{18,2},{3,19},{19,3},{4,20},{20... | collective-permute-start | bytes 245768 | tf_op jit(solution)/shard_map/ppermute | solution.py:37
  24.6 1.2 %collective-permute-start.9 = (f32[72,128]{1,0:T(8,128)S(1)}, f32[72,128]{1,0:T(8,128)S(1)}, u32[]{:S(2)}, u32[]{:S(2)}) collective-permute-start(f32[72,128]{1,0:T(8,128)S(1)} %get-tuple-element.79), channel_id=1, source_target_pairs={{0,12},{4,8},{8,4},{12,0},{1,13},{5,9},{9,5},{13,1},{2,14},{6,10},... | collective-permute-start | bytes 110600 | tf_op jit(solution)/shard_map/ppermute | solution.py:44
  25.8 0.0 collective-permute-start.8
  25.8 1.0 %shard_map.102 = (f32[3,16,16,128]{3,2,1,0:T(8,128)S(1)}, f32[3,64,128]{2,1,0:T(8,128)}) custom-call(f32[3,18,24,128]{3,2,1,0:T(8,128)S(1)} %get-tuple-element.58.grid_ref, f32[3,17,24,128]{3,2,1,0:T(8,128)S(1)} %get-tuple-element.64.deposit_ref, f32[128,128]{1,0:T(8,128)S(1)} %get-tuple-element.54.top_in_ref.top_ref, ...), custom_call_target="tpu_custom_call" | custom-call | flops 4096000 | bytes 1024000 | tf_op jit(solution)/shard_map/pallas_call | solution.py:68
  26.8 1.4 %collective-permute-done.9.z2_ref = f32[72,128]{1,0:T(8,128)S(1)} collective-permute-done((f32[72,128]{1,0:T(8,128)S(1)}, f32[72,128]{1,0:T(8,128)S(1)}, u32[]{:S(2)}, u32[]{:S(2)}) %collective-permute-start.9) | collective-permute-done | bytes 36896 | tf_op jit(solution)/shard_map/ppermute | solution.py:44
  28.1 0.0 collective-permute-done.8.z1_ref
  28.1 0.0 collective-permute-done.10.edge_ref
  28.1 0.4 %collective-permute-done.7.x_ref.minus_x_ref = f32[160,128]{1,0:T(8,128)S(1)} collective-permute-done((f32[160,128]{1,0:T(8,128)S(1)}, f32[160,128]{1,0:T(8,128)S(1)}, u32[]{:S(2)}, u32[]{:S(2)}) %collective-permute-start.7) | collective-permute-done | bytes 81952 | tf_op jit(solution)/shard_map/ppermute | solution.py:37
  28.5 0.9 %shard_map.105 = (f32[3,16,16,128]{3,2,1,0:T(8,128)}, f32[6,7,8,128]{3,2,1,0:T(8,128)}) custom-call(f32[3,16,16,128]{3,2,1,0:T(8,128)S(1)} %get-tuple-element.67.base_ref, f32[128,128]{1,0:T(8,128)S(1)} %collective-permute-done.5.y1_ref.first_ref, f32[128,128]{1,0:T(8,128)S(1)} %collective-permute-done.6.y2_ref.second_ref, ...), custom_call_target="tpu_custom_call" | custom-call | tf_op jit(solution)/shard_map/pallas_call | solution.py:68
  (3 shorter events, 0.0 us)
Async XLA Ops:
  1.9 6.8 %collective-permute-start.1 = (f32[48,128]{1,0:T(8,128)S(1)}, f32[48,128]{1,0:T(8,128)S(1)}, u32[]{:S(2)}, u32[]{:S(2)}) collective-permute-start(f32[48,128]{1,0:T(8,128)S(1)} %get-tuple-element.51), channel_id=1, source_target_pairs={{0,16},{16,0},{1,17},{17,1},{2,18},{18,2},{3,19},{19,3},{4,20},{20... | collective-permute-start | bytes 73736 | tf_op jit(solution)/shard_map/ppermute | solution.py:37
  4.9 3.7 %collective-permute-start.2 = (f32[16,128]{1,0:T(8,128)S(1)}, f32[16,128]{1,0:T(8,128)S(1)}, u32[]{:S(2)}, u32[]{:S(2)}) collective-permute-start(f32[16,128]{1,0:T(8,128)S(1)} %get-tuple-element.50), channel_id=1, source_target_pairs={{0,28},{4,16},{8,20},{12,24},{16,12},{20,0},{24,4},{28,8},{1,29},{... | collective-permute-start | bytes 24584 | tf_op jit(solution)/shard_map/ppermute | solution.py:62
  5.5 3.2 %collective-permute-start = (f32[16,128]{1,0:T(8,128)S(1)}, f32[16,128]{1,0:T(8,128)S(1)}, u32[]{:S(2)}, u32[]{:S(2)}) collective-permute-start(f32[16,128]{1,0:T(8,128)S(1)} %get-tuple-element.50), channel_id=1, source_target_pairs={{0,12},{4,0},{8,4},{12,8},{1,13},{5,1},{9,5},{13,9},{2,14},{6,2},{... | collective-permute-start | bytes 24584 | tf_op jit(solution)/shard_map/ppermute | solution.py:37
  8.8 5.4 %collective-permute-start.4 = (f32[56,128]{1,0:T(8,128)S(1)}, f32[56,128]{1,0:T(8,128)S(1)}, u32[]{:S(2)}, u32[]{:S(2)}) collective-permute-start(f32[56,128]{1,0:T(8,128)S(1)} %shard_map.97), channel_id=1, source_target_pairs={{0,4},{3,7},{1,2},{2,1},{4,0},{7,3},{5,6},{6,5},{8,12},{11,15},{9,... | collective-permute-start | bytes 86024 | tf_op jit(solution)/shard_map/ppermute | solution.py:55
  8.8 5.4 %collective-permute-start.3 = (f32[56,128]{1,0:T(8,128)S(1)}, f32[56,128]{1,0:T(8,128)S(1)}, u32[]{:S(2)}, u32[]{:S(2)}) collective-permute-start(f32[56,128]{1,0:T(8,128)S(1)} %shard_map.97), channel_id=1, source_target_pairs={{0,1},{1,0},{2,3},{3,2},{4,5},{5,4},{6,7},{7,6},{8,9},{9,8},{10,11... | collective-permute-start | bytes 86024 | tf_op jit(solution)/shard_map/ppermute | solution.py:56
  17.4 4.8 %collective-permute-start.6 = (f32[128,128]{1,0:T(8,128)S(1)}, f32[128,128]{1,0:T(8,128)S(1)}, u32[]{:S(2)}, u32[]{:S(2)}) collective-permute-start(f32[128,128]{1,0:T(8,128)S(1)} %get-tuple-element.77), channel_id=1, source_target_pairs={{0,4},{3,7},{1,2},{2,1},{4,0},{7,3},{5,6},{6,5},{8,12},{11,15},{9,... | collective-permute-start | bytes 196616 | tf_op jit(solution)/shard_map/ppermute | solution.py:55
  17.5 4.7 %collective-permute-start.5 = (f32[128,128]{1,0:T(8,128)S(1)}, f32[128,128]{1,0:T(8,128)S(1)}, u32[]{:S(2)}, u32[]{:S(2)}) collective-permute-start(f32[128,128]{1,0:T(8,128)S(1)} %get-tuple-element.78), channel_id=1, source_target_pairs={{0,1},{1,0},{2,3},{3,2},{4,5},{5,4},{6,7},{7,6},{8,9},{9,8},{10,11... | collective-permute-start | bytes 196616 | tf_op jit(solution)/shard_map/ppermute | solution.py:56
  22.2 5.9 %collective-permute-start.10 = (f32[80,128]{1,0:T(8,128)S(1)}, f32[80,128]{1,0:T(8,128)S(1)}, u32[]{:S(2)}, u32[]{:S(2)}) collective-permute-start(f32[80,128]{1,0:T(8,128)S(1)} %get-tuple-element.73), channel_id=1, source_target_pairs={{0,20},{4,24},{8,28},{12,16},{16,4},{20,8},{24,12},{28,0},{1,21},{... | collective-permute-start | bytes 122888 | tf_op jit(solution)/shard_map/ppermute | solution.py:62
  23.2 5.3 %collective-permute-start.7 = (f32[160,128]{1,0:T(8,128)S(1)}, f32[160,128]{1,0:T(8,128)S(1)}, u32[]{:S(2)}, u32[]{:S(2)}) collective-permute-start(f32[160,128]{1,0:T(8,128)S(1)} %get-tuple-element.71), channel_id=1, source_target_pairs={{0,16},{16,0},{1,17},{17,1},{2,18},{18,2},{3,19},{19,3},{4,20},{20... | collective-permute-start | bytes 245768 | tf_op jit(solution)/shard_map/ppermute | solution.py:37
  24.6 3.5 %collective-permute-start.9 = (f32[72,128]{1,0:T(8,128)S(1)}, f32[72,128]{1,0:T(8,128)S(1)}, u32[]{:S(2)}, u32[]{:S(2)}) collective-permute-start(f32[72,128]{1,0:T(8,128)S(1)} %get-tuple-element.79), channel_id=1, source_target_pairs={{0,12},{4,8},{8,4},{12,0},{1,13},{5,9},{9,5},{13,1},{2,14},{6,10},... | collective-permute-start | bytes 110600 | tf_op jit(solution)/shard_map/ppermute | solution.py:44
  25.8 2.3 %collective-permute-start.8 = (f32[72,128]{1,0:T(8,128)S(1)}, f32[72,128]{1,0:T(8,128)S(1)}, u32[]{:S(2)}, u32[]{:S(2)}) collective-permute-start(f32[72,128]{1,0:T(8,128)S(1)} %get-tuple-element.80), channel_id=1, source_target_pairs={{0,4},{4,0},{8,12},{12,8},{1,5},{5,1},{9,13},{13,9},{2,6},{6,2},{1... | collective-permute-start | bytes 110600 | tf_op jit(solution)/shard_map/ppermute | solution.py:44

commit v9 on v8

--- a/solution.py
+++ b/solution.py
@@ -214,14 +214,15 @@
     table_ref[nblocks * TABLE_ROWS :] = jnp.where(row % TABLE_ROWS == RESPONSE, 1.0, 0.0)
 
 
-def y_lines_kernel(grid_ref, face_ref, from_x_ref, edge_ref, ready_ref, out_ref):
+def y_lines_kernel(grid_ref, face_ref, from_x_ref, edge_ref, ready_ref, first_ref, second_ref):
     comps, size_x = grid_ref.shape[0], grid_ref.shape[1] - 2
     size_y = face_ref.shape[0]
-    for c in range(comps):
-        out_ref[c * size_x : (c + 1) * size_x] = grid_ref[c, 1 : size_x + 1, 0]
-        out_ref[comps * size_x + c : comps * size_x + c + 1] = from_x_ref[c * size_y : c * size_y + 1]
-    line = jnp.where(lane_ids(8) % PACK == size_x, turned(edge_ref[0:8], size_x), face_ref[0:8])
-    out_ref[comps * size_x + comps : comps * size_x + comps + 1] = line[0:1]
+    for out_ref in (first_ref, second_ref):
+        for c in range(comps):
+            out_ref[c * size_x : (c + 1) * size_x] = grid_ref[c, 1 : size_x + 1, 0]
+            out_ref[comps * size_x + c : comps * size_x + c + 1] = from_x_ref[c * size_y : c * size_y + 1]
+        line = jnp.where(lane_ids(8) % PACK == size_x, turned(edge_ref[0:8], size_x), face_ref[0:8])
+        out_ref[comps * size_x + comps : comps * size_x + comps + 1] = line[0:1]
 
 
 def halo_xz_kernel(grid_in_ref, lines_in_ref, face_ref, from_x_ref, edge_ref, grid_ref, lines_ref, top_ref, turned_ref):
@@ -326,20 +327,25 @@
             mine = seen[i * height : (i + 1) * height, i * LANES : (i + 1) * LANES]
             tile, push = stepped(mine, weight_z, rows)
             tiles.append(tile)
-            unused = jnp.zeros((LANES - comps * SPREAD, LANES), jnp.float32)
-            spread = jnp.concatenate([main] * comps + [unused] + [rest] * comps + [unused], axis=0)
-            fresh.append((push.astype(jnp.bfloat16), spread.astype(jnp.bfloat16)))
+            fresh.append((push.astype(jnp.bfloat16), jnp.concatenate([main, rest], axis=0).astype(jnp.bfloat16)))
         return tiles, fresh
 
-    def shared(push, spread):
-        shares = lax.dot_general(push, spread, (((1,), (1,)), ((), ())), preferred_element_type=jnp.float32)
+    def shared(one, two):
+        gap = jnp.zeros((LANES - 2 * SPREAD, LANES), jnp.bfloat16)
+        shares = lax.dot_general(
+            jnp.concatenate([one[0], two[0]], axis=0), jnp.concatenate([one[1], gap, two[1], gap], axis=0),
+            (((1,), (1,)), ((), ())), preferred_element_type=jnp.float32,
+        )
         height = comps * REACH_Z
-        total = shares[:height, :LANES] + shares[:height, LANES:] + shares[height:, :LANES]
-        result = jnp.zeros((REACH_Z, LANES), jnp.float32)
-        for c in range(comps):
-            inside = (lanes >= c * SPREAD) & (lanes < (c + 1) * SPREAD)
-            result = jnp.where(inside, total[c * REACH_Z : (c + 1) * REACH_Z], result)
-        return result
+        results = []
+        for i in (0, 1):
+            mine = shares[2 * i * height : 2 * (i + 1) * height, i * LANES : (i + 1) * LANES]
+            mine = mine[:height] + mine[height:]
+            first, second, third = (mine[c * REACH_Z : (c + 1) * REACH_Z] for c in range(comps))
+            across = turned(jnp.where(lanes < SPREAD, second, third), SPREAD)
+            far = jnp.where(lanes < 2 * SPREAD, second, turned(third, 2 * SPREAD)) + across
+            results.append(jnp.where(lanes < SPREAD, first + turned(first, -SPREAD), far))
+        return results
 
     def add(deposit_ref, at, shares):
         spots = []
@@ -362,7 +368,10 @@
             state_ref[pl.ds(pl.multiple_of(STATE * k, STATE), STATE)] = tile
 
     def deposits_of(kept):
-        return [shared(push, spread) for push, spread in kept]
+        results = []
+        for u in range(0, UNROLL, 2):
+            results.extend(shared(kept[u], kept[u + 1]))
+        return results
 
     return loaded, group_of, keep, deposits_of, add
 
@@ -461,7 +470,7 @@
     return total
 
 
-def send_y_kernel(push, diffuse, leaving_ref, grid_ref, deposit_ref, y_ref, tiles_ref, lines_ref):
+def send_y_kernel(push, diffuse, leaving_ref, grid_ref, deposit_ref, y1_ref, y2_ref, tiles_ref, lines_ref):
     comps, size_x, size_y, size_z = grid_ref.shape[0], grid_ref.shape[1] - 2, grid_ref.shape[2] - 8, grid_ref.shape[3]
     count_x, count_y = size_x // BX, size_y // BY
     rows_z = size_z + 8
@@ -471,8 +480,8 @@
         at = (p * count_y + count_y - 1) * rows_z
         tiles_ref[p * height : (p + 1) * height] = jnp.transpose(deposit_ref[at : at + size_z])[:height]
     first = jnp.full((rows, LANES), odd("gy")) == 0
-    y_ref[0, 0:rows] = jnp.where(first, leaving_ref[2], leaving_ref[3])
-    y_ref[1, 0:rows] = jnp.where(first, leaving_ref[3], leaving_ref[2])
+    y1_ref[0:rows] = jnp.where(first, leaving_ref[2], leaving_ref[3])
+    y2_ref[0:rows] = jnp.where(first, leaving_ref[3], leaving_ref[2])
     lines_ref[...] = jnp.zeros_like(lines_ref)
     for c in range(comps):
         for p in range(count_x):
@@ -486,8 +495,8 @@
         spot = slice(c * ROWS_Y, (c + 1) * ROWS_Y)
         beside = jnp.concatenate([grid_ref[c, 1 : size_x + 1, size_y - 1], jnp.zeros((8, LANES), jnp.float32)], axis=0)
         line = push * lines_ref[spot] + diffuse * beside
-        y_ref[0, rows + c * ROWS_Y : rows + (c + 1) * ROWS_Y] = line
-        y_ref[1, rows + c * ROWS_Y : rows + (c + 1) * ROWS_Y] = line
+        for y_ref in (y1_ref, y2_ref):
+            y_ref[rows + c * ROWS_Y : rows + (c + 1) * ROWS_Y] = line
         for a in range(REACH_X):
             place = PACK * c + a
             value = turned(wrapped, place - c * SPREAD - a * REACH_Y - BY)
@@ -496,8 +505,9 @@
     for p in range(1, count_x):
         corner = corner + turned(packed[p : p + 1], p * BX)
     at = rows + size_x + 1
-    y_ref[0, at : at + 1] = push * corner
-    y_ref[1, at : at + 1] = push * corner
+    for y_ref in (y1_ref, y2_ref):
+        y_ref[at : at + 1] = push * corner
+    y1_ref[y2_ref.shape[0] :] = jnp.zeros((8, LANES), jnp.float32)
 
 
 def merge_kernel(deposit_ref, top_tiles_ref, plane_ref, face_ref, tiles_ref, turned_ref):
@@ -692,8 +702,10 @@
         smem=(5,), smem_outs=(4,), cycles=3000,
     )
     line_rows = -(-(comps * size_x + comps + 1) // 8) * 8
-    (y_lines,) = call(y_lines_kernel, [(line_rows, LANES)], grid, from_z, from_x, from_xz, ready)
-    y1, y2 = swapped_y((y_lines, y_lines))
+    y_lines = call(
+        y_lines_kernel, [(line_rows + 8, LANES), (line_rows, LANES)], grid, from_z, from_x, from_xz, ready
+    )
+    y1, y2 = swapped_y(y_lines)
     square = pltpu.VMEM((LANES, LANES), jnp.float32)
     scalars = (pltpu.SMEM(blocks.shape, jnp.int32), pltpu.SMEM(brick_index.shape, jnp.int32))
     dims = (comps, size_x // BX, size_y // BY, size_z // BZ, rows_z)
@@ -701,7 +713,7 @@
     count = 7 * slots
 
     def parts(many):
-        return [(many, 2 * comps * REACH_Z, LANES), (many, 2 * LANES, LANES)]
+        return [(many, 2 * comps * REACH_Z, LANES), (many, 2 * SPREAD, LANES)]
 
     state, push_parts, spread_parts, grid, lines, top = call(
         functools.partial(gather_kernel, dims),
@@ -726,12 +738,16 @@
     )
     leaving = leaving.reshape(6, count, LANES)
     height = comps * SPREAD
-    to_y, top_tiles = call(
+    to_y1, to_y2, top_tiles = call(
         functools.partial(send_y_kernel, push, diffuse),
-        [(2, count + comps * ROWS_Y, LANES), ((size_x // BX) * height, LANES)],
+        [
+            (count + comps * ROWS_Y + 8, LANES),
+            (count + comps * ROWS_Y, LANES),
+            ((size_x // BX) * height, LANES),
+        ],
         leaving, grid, deposit, cycles=300, scratch=(pltpu.VMEM((comps * ROWS_Y, LANES), jnp.float32),),
     )
-    y1, y2 = swapped_y((to_y[0], to_y[1]))
+    y1, y2 = swapped_y((to_y1, to_y2))
     (deposit,) = call(
         functools.partial(deposit_kernel, dims), [deposit_shape], blocks, brick_index, push_parts, spread_parts, deposit,
         smem=(0, 1), aliases={4: 0}, cycles=4000,

time: 29.6 us -> 29.9 us (1.010)
  waiting for transfers between devices: 1.74 us -> 2.09 us
  Pallas kernels: 13.7 us -> 14 us
  starting transfers between devices: 13.2 us -> 12.9 us
    ppermute x1, starting transfers between devices: 1.17 us -> 0.39 us  [swapped_z(): lax.ppermute(blocks[1], 'gz', second)]
    ppermute x2, starting transfers between devices: 1.58 us -> 2.29 us  [moved_diagonally(): return lax.ppermute(block, ('gx', 'gz'), route)]
    ppermute x1, starting transfers between devices: 0.01 us -> 0.64 us  [swapped_z(): lax.ppermute(blocks[0], 'gz', first)]
    ppermute x3, starting transfers between devices: 5.57 us -> 5.05 us  [moved_along(): lax.ppermute(block, axis, [(i, (i + distance) % count) for i in range(cou...]
  transfers between devices with their start and end apart: 11 -> 11, of which waited for: 2 -> 3; matrix products, arithmetic and copies ran while one was open for 0% -> 0% of each run, Pallas kernels for 28% -> 29%
where the time goes in v9:
time: 29.9 us; the launch traced here: 29.7 us
  Pallas kernels  14 us (47%)
  starting transfers between devices  12.9 us (43%)
  waiting for transfers between devices  2.09 us (7%)
  between operations  0.73 us (2%)
    pallas_call x12, Pallas kernels, call(): pl.pallas_call(body, out_shape=[o if isinstance(o, jax.ShapeDtypeStruct)...  14 us
    ppermute x3, starting transfers between devices, moved_along(): lax.ppermute(block, axis, [(i, (i + distance) % count) for i in range(cou...  5.05 us
    ppermute x2, starting transfers between devices, swapped_y(): return (lax.ppermute(blocks[0], 'gy', first), middle)  4.57 us
    ppermute x2, starting transfers between devices, moved_diagonally(): return lax.ppermute(block, ('gx', 'gz'), route)  2.29 us
    ppermute x1, waiting for transfers between devices, swapped_z(): lax.ppermute(blocks[1], 'gz', second)  1.5 us
    ppermute x1, starting transfers between devices, swapped_z(): lax.ppermute(blocks[0], 'gz', first)  0.64 us
  transfers between devices with their start and end apart: 11, of which 3 were waited for; matrix products, arithmetic and copies ran while one was open for 0% of the time, Pallas kernels for 29%

profile of v9, /device:TPU:0, one launch (start us, length us, event | category | flops | bytes accessed | tf_op | source)
XLA Modules:
  0.0 29.7 jit_solution(1446513688069209860)
XLA Ops:
  0.6 1.2 %shard_map.94 = (f32[3,18,24,128]{3,2,1,0:T(8,128)S(1)}, f32[16,128]{1,0:T(8,128)S(1)}, f32[48,128]{1,0:T(8,128)S(1)}, f32[3,64,128]{2,1,0:T(8,128)S(1)}, f32[3,...) custom-call(f32[3,16,16,128]{3,2,1,0:T(8,128)} %gas_ref.1, ...), custom_call_target="tpu_custom_call" | custom-call | tf_op jit(solution)/shard_map/pallas_call | solution.py:68
  1.9 3.0 %collective-permute-start.1 = (f32[48,128]{1,0:T(8,128)S(1)}, f32[48,128]{1,0:T(8,128)S(1)}, u32[]{:S(2)}, u32[]{:S(2)}) collective-permute-start(f32[48,128]{1,0:T(8,128)S(1)} %get-tuple-element.54), channel_id=1, source_target_pairs={{0,16},{16,0},{1,17},{17,1},{2,18},{18,2},{3,19},{19,3},{4,20},{20... | collective-permute-start | bytes 73736 | tf_op jit(solution)/shard_map/ppermute | solution.py:37
  4.9 0.6 %collective-permute-start.2 = (f32[16,128]{1,0:T(8,128)S(1)}, f32[16,128]{1,0:T(8,128)S(1)}, u32[]{:S(2)}, u32[]{:S(2)}) collective-permute-start(f32[16,128]{1,0:T(8,128)S(1)} %get-tuple-element.53), channel_id=1, source_target_pairs={{0,28},{4,16},{8,20},{12,24},{16,12},{20,0},{24,4},{28,8},{1,29},{... | collective-permute-start | bytes 24584 | tf_op jit(solution)/shard_map/ppermute | solution.py:62
  5.5 1.1 %collective-permute-start = (f32[16,128]{1,0:T(8,128)S(1)}, f32[16,128]{1,0:T(8,128)S(1)}, u32[]{:S(2)}, u32[]{:S(2)}) collective-permute-start(f32[16,128]{1,0:T(8,128)S(1)} %get-tuple-element.53), channel_id=1, source_target_pairs={{0,12},{4,0},{8,4},{12,8},{1,13},{5,1},{9,5},{13,9},{2,14},{6,2},{... | collective-permute-start | bytes 24584 | tf_op jit(solution)/shard_map/ppermute | solution.py:37
  6.6 2.0 %shard_map.95 = (f32[6528,128]{1,0:T(8,128)S(1)}, f32[2176,128]{1,0:T(8,128)S(1)}, f32[1152,128]{1,0:T(8,128)S(1)}, f32[8,128]{1,0:T(8,128)S(1)}, s32[146]{0:T(256)S(1)}) custom-call(f32[3,18,24,128]{3,2,1,0:T(8,128)S(1)} %get-tuple-element.43.grid_ref.grid_in_ref, f32[3,64,128]{2,1,0:T(8,128)S(1)} %get-tuple-element.44.velocity_ref, ...), custom_call_target="tpu_custom_call" | custom-call | flops 12288000 | bytes 3072000 | tf_op jit(solution)/shard_map/pallas_call | solution.py:68
  8.7 0.0 collective-permute-done.2.edge_ref
  8.7 0.0 collective-permute-done.face_ref
  8.7 0.0 collective-permute-done.1.from_x_ref
  8.7 0.1 shard_map.97
  8.8 1.6 %collective-permute-start.3 = (f32[64,128]{1,0:T(8,128)S(1)}, f32[64,128]{1,0:T(8,128)S(1)}, u32[]{:S(2)}, u32[]{:S(2)}) collective-permute-start(f32[64,128]{1,0:T(8,128)S(1)} %get-tuple-element.59), channel_id=1, source_target_pairs={{0,1},{1,0},{2,3},{3,2},{4,5},{5,4},{6,7},{7,6},{8,9},{9,8},{10,11... | collective-permute-start | bytes 98312 | tf_op jit(solution)/shard_map/ppermute | solution.py:56
  10.4 0.0 collective-permute-start.4
  10.4 2.2 %shard_map.96 = (f32[576,128]{1,0:T(8,128)S(1)}, bf16[72,96,128]{2,1,0:T(8,128)(2,1)S(1)}, bf16[72,80,128]{2,1,0:T(8,128)(2,1)S(1)}, f32[3,18,24,128]{3,2,1,0:T(...) custom-call(s32[146]{0:T(256)S(1)} %get-tuple-element.49.list_in.list_r, ...), custom_call_target="tpu_custom_call", output_to_operand_aliasing={{3}: (3, {}), {4}: (4, {})} | custom-call | flops 16384000 | bytes 4096000 | tf_op jit(solution)/shard_map/pallas_call | solution.py:68
  12.6 0.0 collective-permute-done.4.second_ref
  12.6 0.1 collective-permute-done.3.first_ref
  12.7 2.9 %shard_map.98 = (f32[3,18,24,128]{3,2,1,0:T(8,128)S(1)}, f32[6528,128]{1,0:T(8,128)S(1)}, f32[576,128]{1,0:T(8,128)S(1)}, f32[2176,128]{1,0:T(8,128)S(1)}, f32[336,128]{1,0:T(8,128)S(1)}) custom-call(s32[146]{0:T(256)S(1)} %get-tuple-element.49.list_in.list_ref, ...), custom_call_target="tpu_custom_call", output_to_operand_aliasing={{0}: (4, {}), {1}: (5, {}), {2}: (9, {}), {3}: (10, {})} | custom-call | flops 8192000 | bytes 2048000 | tf_op jit(solution)/shard_map/pallas_call | solution.py:68
  15.6 0.2 shard_map.100
  15.8 3.0 %collective-permute-start.5 = (f32[136,128]{1,0:T(8,128)S(1)}, f32[136,128]{1,0:T(8,128)S(1)}, u32[]{:S(2)}, u32[]{:S(2)}) collective-permute-start(f32[136,128]{1,0:T(8,128)S(1)} %get-tuple-element.70), channel_id=1, source_target_pairs={{0,1},{1,0},{2,3},{3,2},{4,5},{5,4},{6,7},{7,6},{8,9},{9,8},{10,11... | collective-permute-start | bytes 208904 | tf_op jit(solution)/shard_map/ppermute | solution.py:56
  18.8 0.0 collective-permute-start.6
  18.8 2.8 %shard_map.99.deposit_ref = f32[2176,128]{1,0:T(8,128)S(1)} custom-call(s32[146]{0:T(256)S(1)} %get-tuple-element.49.list_in.list_ref, s32[64]{0:T(128)S(1)} %get-tuple-element.48.brick_ref.brick_in, bf16[72,96,128]{2,1,0:T(8,128)(2,1)S(1)} %get-tuple-element.64.push_ref, ...), custom_call_target="tpu_custom_call", output_to_operand_aliasing={{}: (4, {})} | custom-call | flops 16384000 | bytes 4096000 | tf_op jit(solution)/shard_map/pallas_call | solution.py:68
  21.6 0.4 %shard_map.101 = (f32[3,17,24,128]{3,2,1,0:T(8,128)S(1)}, f32[24,128]{1,0:T(8,128)S(1)}) custom-call(f32[2176,128]{1,0:T(8,128)S(1)} %shard_map.99.deposit_ref, f32[480,128]{1,0:T(8,128)S(1)} %get-tuple-element.68.top_tiles_ref), custom_call_target="tpu_custom_call" | custom-call | flops 4096000 | bytes 1024000 | tf_op jit(solution)/shard_map/pallas_call | solution.py:68
  22.0 0.2 shard_map.103
  22.2 0.0 collective-permute-done.6.y2_ref.second_ref
  22.2 0.0 collective-permute-done.5.y1_ref.first_ref
  22.3 1.7 %collective-permute-start.10 = (f32[80,128]{1,0:T(8,128)S(1)}, f32[80,128]{1,0:T(8,128)S(1)}, u32[]{:S(2)}, u32[]{:S(2)}) collective-permute-start(f32[80,128]{1,0:T(8,128)S(1)} %get-tuple-element.79), channel_id=1, source_target_pairs={{0,20},{4,24},{8,28},{12,16},{16,4},{20,8},{24,12},{28,0},{1,21},{... | collective-permute-start | bytes 122888 | tf_op jit(solution)/shard_map/ppermute | solution.py:62
  24.0 0.9 %collective-permute-start.7 = (f32[160,128]{1,0:T(8,128)S(1)}, f32[160,128]{1,0:T(8,128)S(1)}, u32[]{:S(2)}, u32[]{:S(2)}) collective-permute-start(f32[160,128]{1,0:T(8,128)S(1)} %get-tuple-element.77), channel_id=1, source_target_pairs={{0,16},{16,0},{1,17},{17,1},{2,18},{18,2},{3,19},{19,3},{4,20},{20... | collective-permute-start | bytes 245768 | tf_op jit(solution)/shard_map/ppermute | solution.py:37
  24.9 0.4 %collective-permute-start.9 = (f32[72,128]{1,0:T(8,128)S(1)}, f32[72,128]{1,0:T(8,128)S(1)}, u32[]{:S(2)}, u32[]{:S(2)}) collective-permute-start(f32[72,128]{1,0:T(8,128)S(1)} %get-tuple-element.83), channel_id=1, source_target_pairs={{0,12},{4,8},{8,4},{12,0},{1,13},{5,9},{9,5},{13,1},{2,14},{6,10},... | collective-permute-start | bytes 110600 | tf_op jit(solution)/shard_map/ppermute | solution.py:44
  25.3 0.6 %collective-permute-start.8 = (f32[72,128]{1,0:T(8,128)S(1)}, f32[72,128]{1,0:T(8,128)S(1)}, u32[]{:S(2)}, u32[]{:S(2)}) collective-permute-start(f32[72,128]{1,0:T(8,128)S(1)} %get-tuple-element.84), channel_id=1, source_target_pairs={{0,4},{4,0},{8,12},{12,8},{1,5},{5,1},{9,13},{13,9},{2,6},{6,2},{1... | collective-permute-start | bytes 110600 | tf_op jit(solution)/shard_map/ppermute | solution.py:44
  25.9 1.0 %shard_map.102 = (f32[3,16,16,128]{3,2,1,0:T(8,128)S(1)}, f32[3,64,128]{2,1,0:T(8,128)}) custom-call(f32[3,18,24,128]{3,2,1,0:T(8,128)S(1)} %get-tuple-element.63.grid_ref, f32[3,17,24,128]{3,2,1,0:T(8,128)S(1)} %get-tuple-element.69.deposit_ref, f32[128,128]{1,0:T(8,128)S(1)} %get-tuple-element.57.top_in_ref.top_ref, ...), custom_call_target="tpu_custom_call" | custom-call | flops 4096000 | bytes 1024000 | tf_op jit(solution)/shard_map/pallas_call | solution.py:68
  26.9 1.5 %collective-permute-done.9.z2_ref = f32[72,128]{1,0:T(8,128)S(1)} collective-permute-done((f32[72,128]{1,0:T(8,128)S(1)}, f32[72,128]{1,0:T(8,128)S(1)}, u32[]{:S(2)}, u32[]{:S(2)}) %collective-permute-start.9) | collective-permute-done | bytes 36896 | tf_op jit(solution)/shard_map/ppermute | solution.py:44
  28.4 0.0 collective-permute-done.8.z1_ref
  28.4 0.0 collective-permute-done.10.edge_ref
  28.4 0.5 %collective-permute-done.7.x_ref.minus_x_ref = f32[160,128]{1,0:T(8,128)S(1)} collective-permute-done((f32[160,128]{1,0:T(8,128)S(1)}, f32[160,128]{1,0:T(8,128)S(1)}, u32[]{:S(2)}, u32[]{:S(2)}) %collective-permute-start.7) | collective-permute-done | bytes 81952 | tf_op jit(solution)/shard_map/ppermute | solution.py:37
  28.8 0.9 %shard_map.105 = (f32[3,16,16,128]{3,2,1,0:T(8,128)}, f32[6,7,8,128]{3,2,1,0:T(8,128)}) custom-call(f32[3,16,16,128]{3,2,1,0:T(8,128)S(1)} %get-tuple-element.73.base_ref, f32[136,128]{1,0:T(8,128)S(1)} %collective-permute-done.5.y1_ref.first_ref, f32[128,128]{1,0:T(8,128)S(1)} %collective-permute-done.6.y2_ref.second_ref, ...), custom_call_target="tpu_custom_call" | custom-call | tf_op jit(solution)/shard_map/pallas_call | solution.py:68
  (2 shorter events, 0.0 us)
Async XLA Ops:
  1.9 6.8 %collective-permute-start.1 = (f32[48,128]{1,0:T(8,128)S(1)}, f32[48,128]{1,0:T(8,128)S(1)}, u32[]{:S(2)}, u32[]{:S(2)}) collective-permute-start(f32[48,128]{1,0:T(8,128)S(1)} %get-tuple-element.54), channel_id=1, source_target_pairs={{0,16},{16,0},{1,17},{17,1},{2,18},{18,2},{3,19},{19,3},{4,20},{20... | collective-permute-start | bytes 73736 | tf_op jit(solution)/shard_map/ppermute | solution.py:37
  4.9 3.7 %collective-permute-start.2 = (f32[16,128]{1,0:T(8,128)S(1)}, f32[16,128]{1,0:T(8,128)S(1)}, u32[]{:S(2)}, u32[]{:S(2)}) collective-permute-start(f32[16,128]{1,0:T(8,128)S(1)} %get-tuple-element.53), channel_id=1, source_target_pairs={{0,28},{4,16},{8,20},{12,24},{16,12},{20,0},{24,4},{28,8},{1,29},{... | collective-permute-start | bytes 24584 | tf_op jit(solution)/shard_map/ppermute | solution.py:62
  5.5 3.2 %collective-permute-start = (f32[16,128]{1,0:T(8,128)S(1)}, f32[16,128]{1,0:T(8,128)S(1)}, u32[]{:S(2)}, u32[]{:S(2)}) collective-permute-start(f32[16,128]{1,0:T(8,128)S(1)} %get-tuple-element.53), channel_id=1, source_target_pairs={{0,12},{4,0},{8,4},{12,8},{1,13},{5,1},{9,5},{13,9},{2,14},{6,2},{... | collective-permute-start | bytes 24584 | tf_op jit(solution)/shard_map/ppermute | solution.py:37
  8.8 3.9 %collective-permute-start.3 = (f32[64,128]{1,0:T(8,128)S(1)}, f32[64,128]{1,0:T(8,128)S(1)}, u32[]{:S(2)}, u32[]{:S(2)}) collective-permute-start(f32[64,128]{1,0:T(8,128)S(1)} %get-tuple-element.59), channel_id=1, source_target_pairs={{0,1},{1,0},{2,3},{3,2},{4,5},{5,4},{6,7},{7,6},{8,9},{9,8},{10,11... | collective-permute-start | bytes 98312 | tf_op jit(solution)/shard_map/ppermute | solution.py:56
  10.4 2.2 %collective-permute-start.4 = (f32[56,128]{1,0:T(8,128)S(1)}, f32[56,128]{1,0:T(8,128)S(1)}, u32[]{:S(2)}, u32[]{:S(2)}) collective-permute-start(f32[56,128]{1,0:T(8,128)S(1)} %get-tuple-element.60), channel_id=1, source_target_pairs={{0,4},{3,7},{1,2},{2,1},{4,0},{7,3},{5,6},{6,5},{8,12},{11,15},{9,... | collective-permute-start | bytes 86024 | tf_op jit(solution)/shard_map/ppermute | solution.py:55
  15.8 6.4 %collective-permute-start.5 = (f32[136,128]{1,0:T(8,128)S(1)}, f32[136,128]{1,0:T(8,128)S(1)}, u32[]{:S(2)}, u32[]{:S(2)}) collective-permute-start(f32[136,128]{1,0:T(8,128)S(1)} %get-tuple-element.70), channel_id=1, source_target_pairs={{0,1},{1,0},{2,3},{3,2},{4,5},{5,4},{6,7},{7,6},{8,9},{9,8},{10,11... | collective-permute-start | bytes 208904 | tf_op jit(solution)/shard_map/ppermute | solution.py:56
  18.8 3.5 %collective-permute-start.6 = (f32[128,128]{1,0:T(8,128)S(1)}, f32[128,128]{1,0:T(8,128)S(1)}, u32[]{:S(2)}, u32[]{:S(2)}) collective-permute-start(f32[128,128]{1,0:T(8,128)S(1)} %get-tuple-element.71), channel_id=1, source_target_pairs={{0,4},{3,7},{1,2},{2,1},{4,0},{7,3},{5,6},{6,5},{8,12},{11,15},{9,... | collective-permute-start | bytes 196616 | tf_op jit(solution)/shard_map/ppermute | solution.py:55
  22.3 6.1 %collective-permute-start.10 = (f32[80,128]{1,0:T(8,128)S(1)}, f32[80,128]{1,0:T(8,128)S(1)}, u32[]{:S(2)}, u32[]{:S(2)}) collective-permute-start(f32[80,128]{1,0:T(8,128)S(1)} %get-tuple-element.79), channel_id=1, source_target_pairs={{0,20},{4,24},{8,28},{12,16},{16,4},{20,8},{24,12},{28,0},{1,21},{... | collective-permute-start | bytes 122888 | tf_op jit(solution)/shard_map/ppermute | solution.py:62
  24.0 4.9 %collective-permute-start.7 = (f32[160,128]{1,0:T(8,128)S(1)}, f32[160,128]{1,0:T(8,128)S(1)}, u32[]{:S(2)}, u32[]{:S(2)}) collective-permute-start(f32[160,128]{1,0:T(8,128)S(1)} %get-tuple-element.77), channel_id=1, source_target_pairs={{0,16},{16,0},{1,17},{17,1},{2,18},{18,2},{3,19},{19,3},{4,20},{20... | collective-permute-start | bytes 245768 | tf_op jit(solution)/shard_map/ppermute | solution.py:37
  24.9 3.5 %collective-permute-start.9 = (f32[72,128]{1,0:T(8,128)S(1)}, f32[72,128]{1,0:T(8,128)S(1)}, u32[]{:S(2)}, u32[]{:S(2)}) collective-permute-start(f32[72,128]{1,0:T(8,128)S(1)} %get-tuple-element.83), channel_id=1, source_target_pairs={{0,12},{4,8},{8,4},{12,0},{1,13},{5,9},{9,5},{13,1},{2,14},{6,10},... | collective-permute-start | bytes 110600 | tf_op jit(solution)/shard_map/ppermute | solution.py:44
  25.3 3.1 %collective-permute-start.8 = (f32[72,128]{1,0:T(8,128)S(1)}, f32[72,128]{1,0:T(8,128)S(1)}, u32[]{:S(2)}, u32[]{:S(2)}) collective-permute-start(f32[72,128]{1,0:T(8,128)S(1)} %get-tuple-element.84), channel_id=1, source_target_pairs={{0,4},{4,0},{8,12},{12,8},{1,5},{5,1},{9,13},{13,9},{2,6},{6,2},{1... | collective-permute-start | bytes 110600 | tf_op jit(solution)/shard_map/ppermute | solution.py:44

commit v10 on v8

--- a/solution.py
+++ b/solution.py
@@ -214,7 +214,15 @@
     table_ref[nblocks * TABLE_ROWS :] = jnp.where(row % TABLE_ROWS == RESPONSE, 1.0, 0.0)
 
 
-def y_lines_kernel(grid_ref, face_ref, from_x_ref, edge_ref, ready_ref, out_ref):
+def upper_faces(faces_ref):
+    nx, nz = lax.axis_size("gx"), lax.axis_size("gz")
+    i, k = lax.axis_index("gx"), lax.axis_index("gz")
+    above = lax.rem(k + 1, nz)
+    return faces_ref.at[i * nz + above], faces_ref.at[lax.rem(i + 1, nx) * nz + above]
+
+
+def y_lines_kernel(grid_ref, faces_ref, from_x_ref, ready_ref, out_ref):
+    face_ref, edge_ref = upper_faces(faces_ref)
     comps, size_x = grid_ref.shape[0], grid_ref.shape[1] - 2
     size_y = face_ref.shape[0]
     for c in range(comps):
@@ -380,10 +388,11 @@
 
 
 def gather_kernel(
-    dims, list_in, brick_in, table_ref, grid_in_ref, lines_in_ref, face_ref, from_x_ref, edge_ref,
+    dims, list_in, brick_in, table_ref, grid_in_ref, lines_in_ref, faces_ref, from_x_ref,
     state_ref, push_ref, spread_ref, grid_ref, lines_ref, top_ref, list_ref, brick_ref, turned_ref, sems,
 ):
     copies = fetched(sems, (list_in, list_ref), (brick_in, brick_ref))
+    face_ref, edge_ref = upper_faces(faces_ref)
     halo_xz_kernel(grid_in_ref, lines_in_ref, face_ref, from_x_ref, edge_ref, grid_ref, lines_ref, top_ref, turned_ref)
     for copy in copies:
         copy.wait()
@@ -676,9 +685,8 @@
         + [jax.ShapeDtypeStruct(array.shape, array.dtype) for array in inputs[1:]],
         *inputs, hbm=range(7), scratch=(pltpu.SemaphoreType.DMA((7,)),), limit=40,
     )
-    from_z = moved_along(face, "gz", -1)
     from_x = moved_along(plane, "gx", -1)
-    from_xz = moved_diagonally(face, -1)
+    faces = lax.all_gather(face, ("gx", "gz"))
     lines, deposit, table, ready, blocks = call(
         prepare_kernel,
         [
@@ -692,7 +700,7 @@
         smem=(5,), smem_outs=(4,), cycles=3000,
     )
     line_rows = -(-(comps * size_x + comps + 1) // 8) * 8
-    (y_lines,) = call(y_lines_kernel, [(line_rows, LANES)], grid, from_z, from_x, from_xz, ready)
+    (y_lines,) = call(y_lines_kernel, [(line_rows, LANES)], grid, faces, from_x, ready)
     y1, y2 = swapped_y((y_lines, y_lines))
     square = pltpu.VMEM((LANES, LANES), jnp.float32)
     scalars = (pltpu.SMEM(blocks.shape, jnp.int32), pltpu.SMEM(brick_index.shape, jnp.int32))
@@ -708,7 +716,7 @@
         [(STATE * spare, LANES)]
         + [jax.ShapeDtypeStruct(shape, jnp.bfloat16) for shape in parts(nblocks + UNROLL)]
         + [grid_shape, lines_shape, (LANES, LANES)],
-        blocks, brick_index, table, grid, lines, from_z, from_x, from_xz,
+        blocks, brick_index, table, grid, lines, faces, from_x,
         aliases={3: 3, 4: 4}, cycles=4000, scratch=(*scalars, square, pltpu.SemaphoreType.DMA((2,))),
     )
     grid, lines, state, deposit, leaving = call(

time: 29.6 us -> 36.9 us (1.25)
  blocking collectives: 0 us -> 9.21 us
  starting transfers between devices: 13.2 us -> 11.3 us
  Pallas kernels: 13.7 us -> 14.1 us
    all_gather x0 -> x1, blocking collectives: none -> 9.21 us  [per_device(): faces = lax.all_gather(face, ('gx', 'gz'))]
    ppermute x3 -> x2, starting transfers between devices: 5.57 us -> 3.65 us  [moved_along(): lax.ppermute(block, axis, [(i, (i + distance) % count) for i in range(cou...]
    ppermute x2 -> x1, starting transfers between devices: 1.58 us -> 0.06 us  [moved_diagonally(): return lax.ppermute(block, ('gx', 'gz'), route)]
    ppermute x1, starting transfers between devices: 1.17 us -> 2.3 us  [swapped_z(): lax.ppermute(blocks[1], 'gz', second)]
    ppermute x1, waiting for transfers between devices: 1.36 us -> 0.66 us  [swapped_z(): lax.ppermute(blocks[1], 'gz', second)]
    ppermute x3 -> x2, waiting for transfers between devices: 0.36 us -> 0.91 us  [moved_along(): lax.ppermute(block, axis, [(i, (i + distance) % count) for i in range(cou...]
    pallas_call x12, Pallas kernels: 13.7 us -> 14.1 us  [call(): pl.pallas_call(body, out_shape=[o if isinstance(o, jax.ShapeDtypeStruct)...]
  transfers between devices with their start and end apart: 11 -> 9, of which waited for: 2 -> 2; matrix products, arithmetic and copies ran while one was open for 0% -> 0% of each run, Pallas kernels for 28% -> 25%
where the time goes in v10:
time: 36.9 us; the launch traced here: 37 us
  Pallas kernels  14.1 us (38%)
  starting transfers between devices  11.3 us (31%)
  blocking collectives  9.21 us (25%)
  waiting for transfers between devices  1.59 us (4%)
  between operations  0.74 us (2%)
    pallas_call x12, Pallas kernels, call(): pl.pallas_call(body, out_shape=[o if isinstance(o, jax.ShapeDtypeStruct)...  14.1 us
    all_gather x1, blocking collectives, per_device(): faces = lax.all_gather(face, ('gx', 'gz'))  9.21 us
    ppermute x2, starting transfers between devices, swapped_y(): return (lax.ppermute(blocks[0], 'gy', first), middle)  4.86 us
    ppermute x2, starting transfers between devices, moved_along(): lax.ppermute(block, axis, [(i, (i + distance) % count) for i in range(cou...  3.65 us
    ppermute x1, starting transfers between devices, swapped_z(): lax.ppermute(blocks[1], 'gz', second)  2.3 us
    ppermute x2, waiting for transfers between devices, moved_along(): lax.ppermute(block, axis, [(i, (i + distance) % count) for i in range(cou...  0.91 us
  transfers between devices with their start and end apart: 9, of which 2 were waited for; matrix products, arithmetic and copies ran while one was open for 0% of the time, Pallas kernels for 25%

profile of v10, /device:TPU:0, one launch (start us, length us, event | category | flops | bytes accessed | tf_op | source)
XLA Modules:
  0.0 37.0 jit_solution(10959357874783405035)
XLA Ops:
  0.6 1.2 %shard_map.94 = (f32[3,18,24,128]{3,2,1,0:T(8,128)S(1)}, f32[16,128]{1,0:T(8,128)S(1)}, f32[48,128]{1,0:T(8,128)S(1)}, f32[3,64,128]{2,1,0:T(8,128)S(1)}, f32[3,...) custom-call(f32[3,16,16,128]{3,2,1,0:T(8,128)} %gas_ref.1, ...), custom_call_target="tpu_custom_call" | custom-call | tf_op jit(solution)/shard_map/pallas_call | solution.py:68
  1.9 3.0 %collective-permute-start = (f32[48,128]{1,0:T(8,128)S(1)}, f32[48,128]{1,0:T(8,128)S(1)}, u32[]{:S(2)}, u32[]{:S(2)}) collective-permute-start(f32[48,128]{1,0:T(8,128)S(1)} %get-tuple-element.51), channel_id=1, source_target_pairs={{0,16},{16,0},{1,17},{17,1},{2,18},{18,2},{3,19},{19,3},{4,20},{20... | collective-permute-start | bytes 73736 | tf_op jit(solution)/shard_map/ppermute | solution.py:37
  4.9 2.0 %shard_map.95 = (f32[6528,128]{1,0:T(8,128)S(1)}, f32[2176,128]{1,0:T(8,128)S(1)}, f32[1152,128]{1,0:T(8,128)S(1)}, f32[8,128]{1,0:T(8,128)S(1)}, s32[146]{0:T(256)S(1)}) custom-call(f32[3,18,24,128]{3,2,1,0:T(8,128)S(1)} %get-tuple-element.40.grid_ref.grid_in_ref, f32[3,64,128]{2,1,0:T(8,128)S(1)} %get-tuple-element.41.velocity_ref, ...), custom_call_target="tpu_custom_call" | custom-call | flops 12288000 | bytes 3072000 | tf_op jit(solution)/shard_map/pallas_call | solution.py:68
  6.9 9.2 %all-gather = f32[128,128]{1,0:T(8,128)S(1)} all-gather(f32[16,128]{1,0:T(8,128)S(1)} %get-tuple-element.50), channel_id=2, replica_groups=mesh['gx'=2,'gz'=4,'gy'=4] {'gx','gz'}, dimensions={0}, use_global_device_ids=true | all-gather | bytes 73728 | tf_op jit(solution)/shard_map/all_gather | solution.py:689
  16.2 0.0 collective-permute-done.from_x_ref
  16.2 0.1 shard_map.97
  16.2 0.3 collective-permute-start.2
  16.6 2.8 %collective-permute-start.1 = (f32[56,128]{1,0:T(8,128)S(1)}, f32[56,128]{1,0:T(8,128)S(1)}, u32[]{:S(2)}, u32[]{:S(2)}) collective-permute-start(f32[56,128]{1,0:T(8,128)S(1)} %shard_map.97), channel_id=1, source_target_pairs={{0,1},{1,0},{2,3},{3,2},{4,5},{5,4},{6,7},{7,6},{8,9},{9,8},{10,11... | collective-permute-start | bytes 86024 | tf_op jit(solution)/shard_map/ppermute | solution.py:56
  19.4 2.8 %shard_map.96 = (f32[576,128]{1,0:T(8,128)S(1)}, bf16[72,96,128]{2,1,0:T(8,128)(2,1)S(1)}, bf16[72,256,128]{2,1,0:T(8,128)(2,1)S(1)}, f32[3,18,24,128]{3,2,1,0:T...) custom-call(s32[146]{0:T(256)S(1)} %get-tuple-element.46.list_in.list_, ...), custom_call_target="tpu_custom_call", output_to_operand_aliasing={{3}: (3, {}), {4}: (4, {})} | custom-call | flops 16384000 | bytes 4096000 | tf_op jit(solution)/shard_map/pallas_call | solution.py:68
  22.2 0.0 collective-permute-done.2.second_ref
  22.2 0.0 collective-permute-done.1.first_ref
  22.2 2.6 %shard_map.98 = (f32[3,18,24,128]{3,2,1,0:T(8,128)S(1)}, f32[6528,128]{1,0:T(8,128)S(1)}, f32[576,128]{1,0:T(8,128)S(1)}, f32[2176,128]{1,0:T(8,128)S(1)}, f32[336,128]{1,0:T(8,128)S(1)}) custom-call(s32[146]{0:T(256)S(1)} %get-tuple-element.46.list_in.list_ref, ...), custom_call_target="tpu_custom_call", output_to_operand_aliasing={{0}: (4, {}), {1}: (5, {}), {2}: (9, {}), {3}: (10, {})} | custom-call | flops 8192000 | bytes 2048000 | tf_op jit(solution)/shard_map/pallas_call | solution.py:68
  24.8 0.2 shard_map.100
  25.0 0.1 collective-permute-start.4
  25.1 2.0 %collective-permute-start.3 = (f32[128,128]{1,0:T(8,128)S(1)}, f32[128,128]{1,0:T(8,128)S(1)}, u32[]{:S(2)}, u32[]{:S(2)}) collective-permute-start(f32[128,128]{1,0:T(8,128)S(1)} %get-tuple-element.78), channel_id=1, source_target_pairs={{0,1},{1,0},{2,3},{3,2},{4,5},{5,4},{6,7},{7,6},{8,9},{9,8},{10,11... | collective-permute-start | bytes 196616 | tf_op jit(solution)/shard_map/ppermute | solution.py:56
  27.1 2.8 %shard_map.99.deposit_ref = f32[2176,128]{1,0:T(8,128)S(1)} custom-call(s32[146]{0:T(256)S(1)} %get-tuple-element.46.list_in.list_ref, s32[64]{0:T(128)S(1)} %get-tuple-element.45.brick_ref.brick_in, bf16[72,96,128]{2,1,0:T(8,128)(2,1)S(1)} %get-tuple-element.59.push_ref, ...), custom_call_target="tpu_custom_call", output_to_operand_aliasing={{}: (4, {})} | custom-call | flops 16384000 | bytes 4096000 | tf_op jit(solution)/shard_map/pallas_call | solution.py:68
  29.9 0.4 %shard_map.101 = (f32[3,17,24,128]{3,2,1,0:T(8,128)S(1)}, f32[24,128]{1,0:T(8,128)S(1)}) custom-call(f32[2176,128]{1,0:T(8,128)S(1)} %shard_map.99.deposit_ref, f32[480,128]{1,0:T(8,128)S(1)} %get-tuple-element.63.top_tiles_ref), custom_call_target="tpu_custom_call" | custom-call | flops 4096000 | bytes 1024000 | tf_op jit(solution)/shard_map/pallas_call | solution.py:68
  30.3 0.2 shard_map.103
  30.5 0.0 collective-permute-done.4.y2_ref.second_ref
  30.5 0.0 collective-permute-done.3.y1_ref.first_ref
  30.5 0.1 collective-permute-start.8
  30.6 0.6 %collective-permute-start.5 = (f32[160,128]{1,0:T(8,128)S(1)}, f32[160,128]{1,0:T(8,128)S(1)}, u32[]{:S(2)}, u32[]{:S(2)}) collective-permute-start(f32[160,128]{1,0:T(8,128)S(1)} %get-tuple-element.71), channel_id=1, source_target_pairs={{0,16},{16,0},{1,17},{17,1},{2,18},{18,2},{3,19},{19,3},{4,20},{20... | collective-permute-start | bytes 245768 | tf_op jit(solution)/shard_map/ppermute | solution.py:37
  31.2 2.3 %collective-permute-start.7 = (f32[72,128]{1,0:T(8,128)S(1)}, f32[72,128]{1,0:T(8,128)S(1)}, u32[]{:S(2)}, u32[]{:S(2)}) collective-permute-start(f32[72,128]{1,0:T(8,128)S(1)} %get-tuple-element.79), channel_id=1, source_target_pairs={{0,12},{4,8},{8,4},{12,0},{1,13},{5,9},{9,5},{13,1},{2,14},{6,10},... | collective-permute-start | bytes 110600 | tf_op jit(solution)/shard_map/ppermute | solution.py:44
  33.5 0.0 collective-permute-start.6
  33.5 1.0 %shard_map.102 = (f32[3,16,16,128]{3,2,1,0:T(8,128)S(1)}, f32[3,64,128]{2,1,0:T(8,128)}) custom-call(f32[3,18,24,128]{3,2,1,0:T(8,128)S(1)} %get-tuple-element.58.grid_ref, f32[3,17,24,128]{3,2,1,0:T(8,128)S(1)} %get-tuple-element.64.deposit_ref, f32[128,128]{1,0:T(8,128)S(1)} %get-tuple-element.54.top_in_ref.top_ref, ...), custom_call_target="tpu_custom_call" | custom-call | flops 4096000 | bytes 1024000 | tf_op jit(solution)/shard_map/pallas_call | solution.py:68
  34.5 0.7 %collective-permute-done.7.z2_ref = f32[72,128]{1,0:T(8,128)S(1)} collective-permute-done((f32[72,128]{1,0:T(8,128)S(1)}, f32[72,128]{1,0:T(8,128)S(1)}, u32[]{:S(2)}, u32[]{:S(2)}) %collective-permute-start.7) | collective-permute-done | bytes 36896 | tf_op jit(solution)/shard_map/ppermute | solution.py:44
  35.2 0.0 collective-permute-done.6.z1_ref
  35.2 0.0 collective-permute-done.8.edge_ref
  35.2 0.9 %collective-permute-done.5.x_ref.minus_x_ref = f32[160,128]{1,0:T(8,128)S(1)} collective-permute-done((f32[160,128]{1,0:T(8,128)S(1)}, f32[160,128]{1,0:T(8,128)S(1)}, u32[]{:S(2)}, u32[]{:S(2)}) %collective-permute-start.5) | collective-permute-done | bytes 81952 | tf_op jit(solution)/shard_map/ppermute | solution.py:37
  36.1 0.9 %shard_map.105 = (f32[3,16,16,128]{3,2,1,0:T(8,128)}, f32[6,7,8,128]{3,2,1,0:T(8,128)}) custom-call(f32[3,16,16,128]{3,2,1,0:T(8,128)S(1)} %get-tuple-element.67.base_ref, f32[128,128]{1,0:T(8,128)S(1)} %collective-permute-done.3.y1_ref.first_ref, f32[128,128]{1,0:T(8,128)S(1)} %collective-permute-done.4.y2_ref.second_ref, ...), custom_call_target="tpu_custom_call" | custom-call | tf_op jit(solution)/shard_map/pallas_call | solution.py:68
  (3 shorter events, 0.0 us)
Async XLA Ops:
  1.9 14.3 %collective-permute-start = (f32[48,128]{1,0:T(8,128)S(1)}, f32[48,128]{1,0:T(8,128)S(1)}, u32[]{:S(2)}, u32[]{:S(2)}) collective-permute-start(f32[48,128]{1,0:T(8,128)S(1)} %get-tuple-element.51), channel_id=1, source_target_pairs={{0,16},{16,0},{1,17},{17,1},{2,18},{18,2},{3,19},{19,3},{4,20},{20... | collective-permute-start | bytes 73736 | tf_op jit(solution)/shard_map/ppermute | solution.py:37
  16.2 5.9 %collective-permute-start.2 = (f32[56,128]{1,0:T(8,128)S(1)}, f32[56,128]{1,0:T(8,128)S(1)}, u32[]{:S(2)}, u32[]{:S(2)}) collective-permute-start(f32[56,128]{1,0:T(8,128)S(1)} %shard_map.97), channel_id=1, source_target_pairs={{0,4},{3,7},{1,2},{2,1},{4,0},{7,3},{5,6},{6,5},{8,12},{11,15},{9,... | collective-permute-start | bytes 86024 | tf_op jit(solution)/shard_map/ppermute | solution.py:55
  16.6 5.6 %collective-permute-start.1 = (f32[56,128]{1,0:T(8,128)S(1)}, f32[56,128]{1,0:T(8,128)S(1)}, u32[]{:S(2)}, u32[]{:S(2)}) collective-permute-start(f32[56,128]{1,0:T(8,128)S(1)} %shard_map.97), channel_id=1, source_target_pairs={{0,1},{1,0},{2,3},{3,2},{4,5},{5,4},{6,7},{7,6},{8,9},{9,8},{10,11... | collective-permute-start | bytes 86024 | tf_op jit(solution)/shard_map/ppermute | solution.py:56
  25.0 5.5 %collective-permute-start.4 = (f32[128,128]{1,0:T(8,128)S(1)}, f32[128,128]{1,0:T(8,128)S(1)}, u32[]{:S(2)}, u32[]{:S(2)}) collective-permute-start(f32[128,128]{1,0:T(8,128)S(1)} %get-tuple-element.77), channel_id=1, source_target_pairs={{0,4},{3,7},{1,2},{2,1},{4,0},{7,3},{5,6},{6,5},{8,12},{11,15},{9,... | collective-permute-start | bytes 196616 | tf_op jit(solution)/shard_map/ppermute | solution.py:55
  25.1 5.4 %collective-permute-start.3 = (f32[128,128]{1,0:T(8,128)S(1)}, f32[128,128]{1,0:T(8,128)S(1)}, u32[]{:S(2)}, u32[]{:S(2)}) collective-permute-start(f32[128,128]{1,0:T(8,128)S(1)} %get-tuple-element.78), channel_id=1, source_target_pairs={{0,1},{1,0},{2,3},{3,2},{4,5},{5,4},{6,7},{7,6},{8,9},{9,8},{10,11... | collective-permute-start | bytes 196616 | tf_op jit(solution)/shard_map/ppermute | solution.py:56
  30.5 4.6 %collective-permute-start.8 = (f32[80,128]{1,0:T(8,128)S(1)}, f32[80,128]{1,0:T(8,128)S(1)}, u32[]{:S(2)}, u32[]{:S(2)}) collective-permute-start(f32[80,128]{1,0:T(8,128)S(1)} %get-tuple-element.73), channel_id=1, source_target_pairs={{0,20},{4,24},{8,28},{12,16},{16,4},{20,8},{24,12},{28,0},{1,21},{... | collective-permute-start | bytes 122888 | tf_op jit(solution)/shard_map/ppermute | solution.py:62
  30.6 5.5 %collective-permute-start.5 = (f32[160,128]{1,0:T(8,128)S(1)}, f32[160,128]{1,0:T(8,128)S(1)}, u32[]{:S(2)}, u32[]{:S(2)}) collective-permute-start(f32[160,128]{1,0:T(8,128)S(1)} %get-tuple-element.71), channel_id=1, source_target_pairs={{0,16},{16,0},{1,17},{17,1},{2,18},{18,2},{3,19},{19,3},{4,20},{20... | collective-permute-start | bytes 245768 | tf_op jit(solution)/shard_map/ppermute | solution.py:37
  31.2 3.9 %collective-permute-start.7 = (f32[72,128]{1,0:T(8,128)S(1)}, f32[72,128]{1,0:T(8,128)S(1)}, u32[]{:S(2)}, u32[]{:S(2)}) collective-permute-start(f32[72,128]{1,0:T(8,128)S(1)} %get-tuple-element.79), channel_id=1, source_target_pairs={{0,12},{4,8},{8,4},{12,0},{1,13},{5,9},{9,5},{13,1},{2,14},{6,10},... | collective-permute-start | bytes 110600 | tf_op jit(solution)/shard_map/ppermute | solution.py:44
  33.5 1.6 %collective-permute-start.6 = (f32[72,128]{1,0:T(8,128)S(1)}, f32[72,128]{1,0:T(8,128)S(1)}, u32[]{:S(2)}, u32[]{:S(2)}) collective-permute-start(f32[72,128]{1,0:T(8,128)S(1)} %get-tuple-element.80), channel_id=1, source_target_pairs={{0,4},{4,0},{8,12},{12,8},{1,5},{5,1},{9,13},{13,9},{2,6},{6,2},{1... | collective-permute-start | bytes 110600 | tf_op jit(solution)/shard_map/ppermute | solution.py:44

commit v11 on v8

--- a/solution.py
+++ b/solution.py
@@ -22,6 +22,7 @@
 SPREAD = REACH_X * REACH_Y
 REACH_Z = 2 * BZ
 UNROLL = 8
+WIDE = 16
 
 WEIGHT, ALONG_Y, IN_Y, ALONG_Z, IN_Z, RESPONSE, MOVING, OFFSET = 0, 5, 6, 7, 8, 9, 10, 13
 TABLE_ROWS = 16
@@ -100,7 +101,7 @@
 ):
     comps, size_x, size_y, _ = gas_ref.shape
     pairs = [
-        (gas_ref, grid_ref.at[:, 1 : size_x + 1, 0:size_y]),
+        *((gas_ref.at[c], grid_ref.at[c, 1 : size_x + 1, 0:size_y]) for c in range(comps)),
         (velocity_in, velocity_ref), (fraction_in, fraction_ref), (response_in, response_ref),
         (cell_in, cell_ref), (brick_in, brick_ref), (crossing_in, crossing_ref),
     ]
@@ -113,16 +114,16 @@
         grid_ref[c, size_x + 1] = zeros
         for x in range(size_x):
             grid_ref[c, x + 1, size_y:] = zeros[size_y:]
-    copies[0].wait()
     lane = lane_ids(size_y)
     face = jnp.zeros((size_y, LANES), jnp.float32)
     for c in range(comps):
+        copies[c].wait()
         plane_ref[c * size_y : (c + 1) * size_y] = grid_ref[c, 1, 0:size_y]
         for x in range(size_x):
             place = PACK * c + x
             face = jnp.where(lane == place, turned(grid_ref[c, x + 1, 0:size_y], place), face)
     face_ref[...] = face
-    for copy in copies[1:]:
+    for copy in copies[comps:]:
         copy.wait()
 
 
@@ -167,7 +168,7 @@
     count_x, count_y, count_z = size_x // BX, size_y // BY, size_z // BZ
     rows_z = size_z + 8
 
-    room = nblocks + UNROLL
+    room = nblocks + WIDE
 
     def visit(k, counts):
         late = jnp.where(lax.rem(lax.div(brick_ref[k], count_z), count_y) == count_y - 1, 1, 0)
@@ -176,7 +177,7 @@
 
     early, late = lax.fori_loop(0, nblocks, visit, (jnp.int32(0), jnp.int32(0)), unroll=8)
     for base, count in ((0, early), (room, late)):
-        for u in range(UNROLL):
+        for u in range(WIDE):
             list_ref[base + count + u] = nblocks
     list_ref[2 * room] = early
     list_ref[2 * room + 1] = late
@@ -351,7 +352,7 @@
 
     def group_of(taken):
         tiles, fresh = [], []
-        for u in range(0, UNROLL, 2):
+        for u in range(0, len(taken), 2):
             both, kept = gathered(taken[u], taken[u + 1])
             tiles.extend(both)
             fresh.extend(kept)
@@ -367,9 +368,23 @@
     return loaded, group_of, keep, deposits_of, add
 
 
-def groups_in(list_ref, late):
+def groups_in(list_ref, late, many=UNROLL):
     room = (list_ref.shape[0] - 2) // 2
-    return late * room, (list_ref[2 * room + late] + UNROLL - 1) // UNROLL
+    return late * room, (list_ref[2 * room + late] + many - 1) // many
+
+
+def leave(crossing_ref, state_ref, leaving_ref, faces):
+    slots = crossing_ref.shape[1]
+    rows = leaving_ref.shape[0] // (len(faces) * slots)
+    for i, face in enumerate(faces):
+        tiles = []
+        for slot in range(slots):
+            block = crossing_ref[face, slot]
+            spot = pl.ds(pl.multiple_of(jnp.maximum(block, 0) * STATE, STATE), STATE)
+            live = jnp.full((STATE, LANES), block, jnp.int32) >= 0
+            tiles.append(jnp.where(live, state_ref[spot], 0.0))
+        for slot, tile in enumerate(tiles):
+            leaving_ref[pl.ds(i * rows * slots + slot, rows, stride=slots)] = tile[:rows]
 
 
 def fetched(sems, *pairs):
@@ -399,19 +414,26 @@
             push_ref[group * UNROLL + i] = push
             spread_ref[group * UNROLL + i] = spread
 
-
-def deposit_kernel(dims, list_ref, brick_ref, push_ref, spread_ref, deposit_in_ref, deposit_ref):
+    for i in range(UNROLL):
+        push_ref[groups * UNROLL + i] = jnp.zeros(push_ref.shape[1:], push_ref.dtype)
+        spread_ref[groups * UNROLL + i] = jnp.zeros(spread_ref.shape[1:], spread_ref.dtype)
+
+
+def deposit_kernel(
+    dims, list_ref, brick_ref, crossing_ref, push_ref, spread_ref, state_ref, deposit_in_ref, deposit_ref, leaving_ref
+):
     _, _, _, deposits_of, add = block_steps(dims, list_ref, brick_ref)
-    base, groups = groups_in(list_ref, 0)
+    base, groups = groups_in(list_ref, 0, WIDE)
+    leave(crossing_ref, state_ref, leaving_ref, (0, 1, 4, 5))
 
     @pl.loop(0, groups)
     def _(group):
-        mine = [group * UNROLL + i for i in range(UNROLL)]
-        add(deposit_ref, base + group * UNROLL, deposits_of([(push_ref[i], spread_ref[i]) for i in mine]))
+        mine = [group * WIDE + i for i in range(WIDE)]
+        add(deposit_ref, base + group * WIDE, deposits_of([(push_ref[i], spread_ref[i]) for i in mine]))
 
 
 def late_kernel(
-    dims, slots, list_in, brick_in, crossing_in, table_ref, grid_in_ref, lines_in_ref, top_in_ref, first_ref, second_ref,
+    dims, list_in, brick_in, crossing_in, table_ref, grid_in_ref, lines_in_ref, top_in_ref, first_ref, second_ref,
     state_in_ref, deposit_in_ref,
     grid_ref, lines_ref, state_ref, deposit_ref, leaving_ref,
     push_ref, spread_ref, list_ref, brick_ref, crossing_ref, turned_ref, sems,
@@ -440,16 +462,7 @@
             push_ref[i] = push
             spread_ref[i] = spread
 
-    rows = leaving_ref.shape[0] // (6 * slots)
-    for face in range(6):
-        tiles = []
-        for slot in range(slots):
-            block = crossing_ref[face, slot]
-            spot = pl.ds(pl.multiple_of(jnp.maximum(block, 0) * STATE, STATE), STATE)
-            live = jnp.full((STATE, LANES), block, jnp.int32) >= 0
-            tiles.append(jnp.where(live, state_ref[spot], 0.0))
-        for slot, tile in enumerate(tiles):
-            leaving_ref[pl.ds(face * rows * slots + slot, rows, stride=slots)] = tile[:rows]
+    leave(crossing_ref, state_ref, leaving_ref, (2, 3))
 
 
 def top_rows(deposit_ref, q, count_x, count_y, rows_z, size_z):
@@ -471,8 +484,8 @@
         at = (p * count_y + count_y - 1) * rows_z
         tiles_ref[p * height : (p + 1) * height] = jnp.transpose(deposit_ref[at : at + size_z])[:height]
     first = jnp.full((rows, LANES), odd("gy")) == 0
-    y_ref[0, 0:rows] = jnp.where(first, leaving_ref[2], leaving_ref[3])
-    y_ref[1, 0:rows] = jnp.where(first, leaving_ref[3], leaving_ref[2])
+    y_ref[0, 0:rows] = jnp.where(first, leaving_ref[0], leaving_ref[1])
+    y_ref[1, 0:rows] = jnp.where(first, leaving_ref[1], leaving_ref[0])
     lines_ref[...] = jnp.zeros_like(lines_ref)
     for c in range(comps):
         for p in range(count_x):
@@ -486,8 +499,9 @@
         spot = slice(c * ROWS_Y, (c + 1) * ROWS_Y)
         beside = jnp.concatenate([grid_ref[c, 1 : size_x + 1, size_y - 1], jnp.zeros((8, LANES), jnp.float32)], axis=0)
         line = push * lines_ref[spot] + diffuse * beside
-        y_ref[0, rows + c * ROWS_Y : rows + (c + 1) * ROWS_Y] = line
-        y_ref[1, rows + c * ROWS_Y : rows + (c + 1) * ROWS_Y] = line
+        at = rows + c * (size_x + 1)
+        y_ref[0, at : at + size_x + 1] = line[: size_x + 1]
+        y_ref[1, at : at + size_x + 1] = line[: size_x + 1]
         for a in range(REACH_X):
             place = PACK * c + a
             value = turned(wrapped, place - c * SPREAD - a * REACH_Y - BY)
@@ -495,7 +509,7 @@
     corner = packed[0:1]
     for p in range(1, count_x):
         corner = corner + turned(packed[p : p + 1], p * BX)
-    at = rows + size_x + 1
+    at = rows + comps * (size_x + 1)
     y_ref[0, at : at + 1] = push * corner
     y_ref[1, at : at + 1] = push * corner
 
@@ -572,7 +586,7 @@
     lane, sub = lane_ids(size_y), row_ids(size_y)
     top = top_ref[0:size_y]
     for c in range(comps):
-        at = count + c * ROWS_Y
+        at = count + c * (size_x + 1)
         lines = below(y1_ref, y2_ref, slice(at, at + size_x))
         for x in range(size_x):
             here = grid_ref[c, x + 1, 0:size_y]
@@ -596,20 +610,20 @@
     edge = comps * size_y
     x_ref[0:edge] = x_in_ref[...]
     for c in range(comps):
-        at = count + c * ROWS_Y + size_x
+        at = count + c * (size_x + 1) + size_x
         spot = slice(c * size_y, c * size_y + 1)
         x_ref[spot] = x_in_ref[spot] + below(first_ref, second_ref, slice(at, at + 1))
     x_ref[edge : edge + count] = leaving_ref[0]
     if x_ref.shape[0] > edge + count:
         x_ref[edge + count : edge + 2 * count] = leaving_ref[1]
-    at = count + size_x + 1
+    at = count + comps * (size_x + 1)
     edge_ref[size_y:] = jnp.zeros((edge_ref.shape[0] - size_y, LANES), jnp.float32)
     edge_ref[0:size_y] = z_in_ref[...]
     edge_ref[0:1] = z_in_ref[0:1] + below(first_ref, second_ref, slice(at, at + 1))
     up = odd("gz")
-    z_ref[up, 0:count] = leaving_ref[4]
+    z_ref[up, 0:count] = leaving_ref[2]
     z_ref[up, count : count + size_y] = edge_ref[0:size_y]
-    z_ref[1 - up, 0:count] = leaving_ref[5]
+    z_ref[1 - up, 0:count] = leaving_ref[3]
     z_ref[1 - up, count : count + size_y] = jnp.zeros((size_y, LANES), jnp.float32)
 
 
@@ -674,7 +688,7 @@
         begin_kernel,
         [grid_shape, (size_y, LANES), (comps * size_y, LANES)]
         + [jax.ShapeDtypeStruct(array.shape, array.dtype) for array in inputs[1:]],
-        *inputs, hbm=range(7), scratch=(pltpu.SemaphoreType.DMA((7,)),), limit=40,
+        *inputs, hbm=range(7), scratch=(pltpu.SemaphoreType.DMA((comps + 6,)),),
     )
     from_z = moved_along(face, "gz", -1)
     from_x = moved_along(plane, "gx", -1)
@@ -686,7 +700,7 @@
             deposit_shape,
             (TABLE_ROWS * spare, LANES),
             (8, LANES),
-            jax.ShapeDtypeStruct((2 * (nblocks + UNROLL) + 2,), jnp.int32),
+            jax.ShapeDtypeStruct((2 * (nblocks + WIDE) + 2,), jnp.int32),
         ],
         grid, velocity, fraction, response, cell_index, brick_index,
         smem=(5,), smem_outs=(4,), cycles=3000,
@@ -706,14 +720,14 @@
     state, push_parts, spread_parts, grid, lines, top = call(
         functools.partial(gather_kernel, dims),
         [(STATE * spare, LANES)]
-        + [jax.ShapeDtypeStruct(shape, jnp.bfloat16) for shape in parts(nblocks + UNROLL)]
+        + [jax.ShapeDtypeStruct(shape, jnp.bfloat16) for shape in parts(nblocks + 2 * UNROLL)]
         + [grid_shape, lines_shape, (LANES, LANES)],
         blocks, brick_index, table, grid, lines, from_z, from_x, from_xz,
         aliases={3: 3, 4: 4}, cycles=4000, scratch=(*scalars, square, pltpu.SemaphoreType.DMA((2,))),
     )
     grid, lines, state, deposit, leaving = call(
-        functools.partial(late_kernel, dims, slots),
-        [grid_shape, lines_shape, (STATE * spare, LANES), deposit_shape, (6 * count, LANES)],
+        functools.partial(late_kernel, dims),
+        [grid_shape, lines_shape, (STATE * spare, LANES), deposit_shape, (2 * count, LANES)],
         blocks, brick_index, crossing, table, grid, lines, top, y1, y2, state, deposit,
         aliases={4: 0, 5: 1, 9: 2, 10: 3}, cycles=2000,
         scratch=[
@@ -724,18 +738,20 @@
             pltpu.SemaphoreType.DMA((3,)),
         ],
     )
-    leaving = leaving.reshape(6, count, LANES)
+    leaving = leaving.reshape(2, count, LANES)
     height = comps * SPREAD
     to_y, top_tiles = call(
         functools.partial(send_y_kernel, push, diffuse),
-        [(2, count + comps * ROWS_Y, LANES), ((size_x // BX) * height, LANES)],
+        [(2, count + line_rows, LANES), ((size_x // BX) * height, LANES)],
         leaving, grid, deposit, cycles=300, scratch=(pltpu.VMEM((comps * ROWS_Y, LANES), jnp.float32),),
     )
     y1, y2 = swapped_y((to_y[0], to_y[1]))
-    (deposit,) = call(
-        functools.partial(deposit_kernel, dims), [deposit_shape], blocks, brick_index, push_parts, spread_parts, deposit,
-        smem=(0, 1), aliases={4: 0}, cycles=4000,
-    )
+    deposit, leaving = call(
+        functools.partial(deposit_kernel, dims), [deposit_shape, (4 * count, LANES)],
+        blocks, brick_index, crossing, push_parts, spread_parts, state, deposit,
+        smem=(0, 1, 2), aliases={6: 0}, cycles=4000,
+    )
+    leaving = leaving.reshape(4, count, LANES)
     deposit, over = call(
         merge_kernel, [(comps, size_x + 1, ROWS_Y, LANES), (ROWS_Y, LANES)], deposit, top_tiles,
         cycles=1000, scratch=(pltpu.VMEM(((size_x // BX) * (size_y // BY) * height, LANES), jnp.float32), square),

time: 29.6 us -> 29.3 us (0.990); the launches traced: 29.4 us -> 29.4 us
  starting transfers between devices: 13.2 us -> 12.5 us
  waiting for transfers between devices: 1.74 us -> 2.42 us
    ppermute x3, starting transfers between devices: 5.57 us -> 4.6 us  [moved_along(): lax.ppermute(block, axis, [(i, (i + distance) % count) for i in range(cou...]
    ppermute x3, waiting for transfers between devices: 0.36 us -> 1.3 us  [moved_along(): lax.ppermute(block, axis, [(i, (i + distance) % count) for i in range(cou...]
    ppermute x1, waiting for transfers between devices: 1.36 us -> 1.06 us  [swapped_z(): lax.ppermute(blocks[1], 'gz', second)]
where the time goes in v11:
time: 29.3 us; the launch traced here: 29.4 us
  Pallas kernels  13.7 us (47%)
  starting transfers between devices  12.5 us (43%)
  waiting for transfers between devices  2.42 us (8%)
  between operations  0.75 us (3%)
    pallas_call x12, Pallas kernels, call(): pl.pallas_call(body, out_shape=[o if isinstance(o, jax.ShapeDtypeStruct)...  13.7 us
    ppermute x2, starting transfers between devices, swapped_y(): return (lax.ppermute(blocks[0], 'gy', first), middle)  4.66 us
    ppermute x3, starting transfers between devices, moved_along(): lax.ppermute(block, axis, [(i, (i + distance) % count) for i in range(cou...  4.6 us
    ppermute x2, starting transfers between devices, moved_diagonally(): return lax.ppermute(block, ('gx', 'gz'), route)  1.79 us
    ppermute x1, starting transfers between devices, swapped_z(): lax.ppermute(blocks[1], 'gz', second)  1.33 us
    ppermute x3, waiting for transfers between devices, moved_along(): lax.ppermute(block, axis, [(i, (i + distance) % count) for i in range(cou...  1.3 us
    ppermute x1, waiting for transfers between devices, swapped_z(): lax.ppermute(blocks[1], 'gz', second)  1.06 us
  transfers between devices with their start and end apart: 11, of which 2 were waited for; matrix products, arithmetic and copies ran while one was open for 0% of the time, Pallas kernels for 28%

profile of v11, /device:TPU:0, one launch (start us, length us, event | category | flops | bytes accessed | tf_op | source)
XLA Modules:
  0.0 29.4 jit_solution(2370697450080388922)
XLA Ops:
  0.6 1.3 %shard_map.94 = (f32[3,18,24,128]{3,2,1,0:T(8,128)S(1)}, f32[16,128]{1,0:T(8,128)S(1)}, f32[48,128]{1,0:T(8,128)S(1)}, f32[3,64,128]{2,1,0:T(8,128)S(1)}, f32[3,...) custom-call(f32[3,16,16,128]{3,2,1,0:T(8,128)} %gas_ref.1, ...), custom_call_target="tpu_custom_call" | custom-call | tf_op jit(solution)/shard_map/pallas_call | solution.py:69
  1.9 3.0 %collective-permute-start.1 = (f32[48,128]{1,0:T(8,128)S(1)}, f32[48,128]{1,0:T(8,128)S(1)}, u32[]{:S(2)}, u32[]{:S(2)}) collective-permute-start(f32[48,128]{1,0:T(8,128)S(1)} %get-tuple-element.53), channel_id=1, source_target_pairs={{0,16},{16,0},{1,17},{17,1},{2,18},{18,2},{3,19},{19,3},{4,20},{20... | collective-permute-start | bytes 73736 | tf_op jit(solution)/shard_map/ppermute | solution.py:38
  5.0 0.6 %collective-permute-start.2 = (f32[16,128]{1,0:T(8,128)S(1)}, f32[16,128]{1,0:T(8,128)S(1)}, u32[]{:S(2)}, u32[]{:S(2)}) collective-permute-start(f32[16,128]{1,0:T(8,128)S(1)} %get-tuple-element.52), channel_id=1, source_target_pairs={{0,28},{4,16},{8,20},{12,24},{16,12},{20,0},{24,4},{28,8},{1,29},{... | collective-permute-start | bytes 24584 | tf_op jit(solution)/shard_map/ppermute | solution.py:63
  5.6 1.1 %collective-permute-start = (f32[16,128]{1,0:T(8,128)S(1)}, f32[16,128]{1,0:T(8,128)S(1)}, u32[]{:S(2)}, u32[]{:S(2)}) collective-permute-start(f32[16,128]{1,0:T(8,128)S(1)} %get-tuple-element.52), channel_id=1, source_target_pairs={{0,12},{4,0},{8,4},{12,8},{1,13},{5,1},{9,5},{13,9},{2,14},{6,2},{... | collective-permute-start | bytes 24584 | tf_op jit(solution)/shard_map/ppermute | solution.py:38
  6.7 2.3 %shard_map.95 = (f32[6528,128]{1,0:T(8,128)S(1)}, f32[2176,128]{1,0:T(8,128)S(1)}, f32[1152,128]{1,0:T(8,128)S(1)}, f32[8,128]{1,0:T(8,128)S(1)}, s32[162]{0:T(256)S(1)}) custom-call(f32[3,18,24,128]{3,2,1,0:T(8,128)S(1)} %get-tuple-element.42.grid_ref.grid_in_ref, f32[3,64,128]{2,1,0:T(8,128)S(1)} %get-tuple-element.43.velocity_ref, ...), custom_call_target="tpu_custom_call" | custom-call | flops 12288000 | bytes 3072000 | tf_op jit(solution)/shard_map/pallas_call | solution.py:69
  9.0 0.0 collective-permute-done.2.edge_ref
  9.0 0.0 collective-permute-done.face_ref
  9.0 0.0 collective-permute-done.1.from_x_ref
  9.0 0.1 shard_map.97
  9.1 0.0 collective-permute-start.4
  9.1 3.1 %collective-permute-start.3 = (f32[56,128]{1,0:T(8,128)S(1)}, f32[56,128]{1,0:T(8,128)S(1)}, u32[]{:S(2)}, u32[]{:S(2)}) collective-permute-start(f32[56,128]{1,0:T(8,128)S(1)} %shard_map.97), channel_id=1, source_target_pairs={{0,1},{1,0},{2,3},{3,2},{4,5},{5,4},{6,7},{7,6},{8,9},{9,8},{10,11... | collective-permute-start | bytes 86024 | tf_op jit(solution)/shard_map/ppermute | solution.py:57
  12.2 2.3 %shard_map.96 = (f32[576,128]{1,0:T(8,128)S(1)}, bf16[80,96,128]{2,1,0:T(8,128)(2,1)S(1)}, bf16[80,256,128]{2,1,0:T(8,128)(2,1)S(1)}, f32[3,18,24,128]{3,2,1,0:T...) custom-call(s32[162]{0:T(256)S(1)} %get-tuple-element.48.list_in.list_, ...), custom_call_target="tpu_custom_call", output_to_operand_aliasing={{3}: (3, {}), {4}: (4, {})} | custom-call | flops 16384000 | bytes 4096000 | tf_op jit(solution)/shard_map/pallas_call | solution.py:69
  14.6 0.0 collective-permute-done.4.second_ref
  14.6 0.0 collective-permute-done.3.first_ref
  14.6 2.9 %shard_map.98 = (f32[3,18,24,128]{3,2,1,0:T(8,128)S(1)}, f32[6528,128]{1,0:T(8,128)S(1)}, f32[576,128]{1,0:T(8,128)S(1)}, f32[2176,128]{1,0:T(8,128)S(1)}, f32[112,128]{1,0:T(8,128)S(1)}) custom-call(s32[162]{0:T(256)S(1)} %get-tuple-element.48.list_in.list_ref, ...), custom_call_target="tpu_custom_call", output_to_operand_aliasing={{0}: (4, {}), {1}: (5, {}), {2}: (9, {}), {3}: (10, {})} | custom-call | flops 8192000 | bytes 2048000 | tf_op jit(solution)/shard_map/pallas_call | solution.py:69
  17.5 0.2 shard_map.100
  17.7 0.1 collective-permute-start.6
  17.8 1.5 %collective-permute-start.5 = (f32[112,128]{1,0:T(8,128)S(1)}, f32[112,128]{1,0:T(8,128)S(1)}, u32[]{:S(2)}, u32[]{:S(2)}) collective-permute-start(f32[112,128]{1,0:T(8,128)S(1)} %get-tuple-element.82), channel_id=1, source_target_pairs={{0,1},{1,0},{2,3},{3,2},{4,5},{5,4},{6,7},{7,6},{8,9},{9,8},{10,11... | collective-permute-start | bytes 172040 | tf_op jit(solution)/shard_map/ppermute | solution.py:57
  19.3 2.1 %shard_map.99 = (f32[2176,128]{1,0:T(8,128)S(1)}, f32[224,128]{1,0:T(8,128)S(1)}) custom-call(s32[162]{0:T(256)S(1)} %get-tuple-element.48.list_in.list_ref, s32[64]{0:T(128)S(1)} %get-tuple-element.47.brick_ref.brick_in, s32[6,8]{1,0:T(8,128)S(1)} %get-tuple-element.49.crossing_in.crossing_ref, ...), custom_call_target="tpu_custom_call", output_to_operand_aliasing={{0}: (6, {})} | custom-call | flops 16384000 | bytes 4096000 | tf_op jit(solution)/shard_map/pallas_call | solution.py:69
  21.4 0.4 %shard_map.101 = (f32[3,17,24,128]{3,2,1,0:T(8,128)S(1)}, f32[24,128]{1,0:T(8,128)S(1)}) custom-call(f32[2176,128]{1,0:T(8,128)S(1)} %get-tuple-element.65.deposit_ref, f32[480,128]{1,0:T(8,128)S(1)} %get-tuple-element.67.top_tiles_ref), custom_call_target="tpu_custom_call" | custom-call | flops 4096000 | bytes 1024000 | tf_op jit(solution)/shard_map/pallas_call | solution.py:69
  21.9 0.2 shard_map.103
  22.1 0.0 collective-permute-done.6.y2_ref.second_ref
  22.1 0.0 collective-permute-done.5.y1_ref.first_ref
  22.1 1.2 %collective-permute-start.10 = (f32[80,128]{1,0:T(8,128)S(1)}, f32[80,128]{1,0:T(8,128)S(1)}, u32[]{:S(2)}, u32[]{:S(2)}) collective-permute-start(f32[80,128]{1,0:T(8,128)S(1)} %get-tuple-element.77), channel_id=1, source_target_pairs={{0,20},{4,24},{8,28},{12,16},{16,4},{20,8},{24,12},{28,0},{1,21},{... | collective-permute-start | bytes 122888 | tf_op jit(solution)/shard_map/ppermute | solution.py:63
  23.3 0.4 %collective-permute-start.7 = (f32[160,128]{1,0:T(8,128)S(1)}, f32[160,128]{1,0:T(8,128)S(1)}, u32[]{:S(2)}, u32[]{:S(2)}) collective-permute-start(f32[160,128]{1,0:T(8,128)S(1)} %get-tuple-element.75), channel_id=1, source_target_pairs={{0,16},{16,0},{1,17},{17,1},{2,18},{18,2},{3,19},{19,3},{4,20},{20... | collective-permute-start | bytes 245768 | tf_op jit(solution)/shard_map/ppermute | solution.py:38
  23.8 1.3 %collective-permute-start.9 = (f32[72,128]{1,0:T(8,128)S(1)}, f32[72,128]{1,0:T(8,128)S(1)}, u32[]{:S(2)}, u32[]{:S(2)}) collective-permute-start(f32[72,128]{1,0:T(8,128)S(1)} %get-tuple-element.83), channel_id=1, source_target_pairs={{0,12},{4,8},{8,4},{12,0},{1,13},{5,9},{9,5},{13,1},{2,14},{6,10},... | collective-permute-start | bytes 110600 | tf_op jit(solution)/shard_map/ppermute | solution.py:45
  25.1 0.0 collective-permute-start.8
  25.1 1.0 %shard_map.102 = (f32[3,16,16,128]{3,2,1,0:T(8,128)S(1)}, f32[3,64,128]{2,1,0:T(8,128)}) custom-call(f32[3,18,24,128]{3,2,1,0:T(8,128)S(1)} %get-tuple-element.60.grid_ref, f32[3,17,24,128]{3,2,1,0:T(8,128)S(1)} %get-tuple-element.68.deposit_ref, f32[128,128]{1,0:T(8,128)S(1)} %get-tuple-element.56.top_in_ref.top_ref, ...), custom_call_target="tpu_custom_call" | custom-call | flops 4096000 | bytes 1024000 | tf_op jit(solution)/shard_map/pallas_call | solution.py:69
  26.1 1.1 %collective-permute-done.9.z2_ref = f32[72,128]{1,0:T(8,128)S(1)} collective-permute-done((f32[72,128]{1,0:T(8,128)S(1)}, f32[72,128]{1,0:T(8,128)S(1)}, u32[]{:S(2)}, u32[]{:S(2)}) %collective-permute-start.9) | collective-permute-done | bytes 36896 | tf_op jit(solution)/shard_map/ppermute | solution.py:45
  27.2 0.0 collective-permute-done.8.z1_ref
  27.2 0.0 collective-permute-done.10.edge_ref
  27.2 1.3 %collective-permute-done.7.x_ref.minus_x_ref = f32[160,128]{1,0:T(8,128)S(1)} collective-permute-done((f32[160,128]{1,0:T(8,128)S(1)}, f32[160,128]{1,0:T(8,128)S(1)}, u32[]{:S(2)}, u32[]{:S(2)}) %collective-permute-start.7) | collective-permute-done | bytes 81952 | tf_op jit(solution)/shard_map/ppermute | solution.py:38
  28.5 0.9 %shard_map.105 = (f32[3,16,16,128]{3,2,1,0:T(8,128)}, f32[6,7,8,128]{3,2,1,0:T(8,128)}) custom-call(f32[3,16,16,128]{3,2,1,0:T(8,128)S(1)} %get-tuple-element.70.base_ref, f32[112,128]{1,0:T(8,128)S(1)} %collective-permute-done.5.y1_ref.first_ref, f32[112,128]{1,0:T(8,128)S(1)} %collective-permute-done.6.y2_ref.second_ref, ...), custom_call_target="tpu_custom_call" | custom-call | tf_op jit(solution)/shard_map/pallas_call | solution.py:69
  (3 shorter events, 0.0 us)
Async XLA Ops:
  1.9 7.1 %collective-permute-start.1 = (f32[48,128]{1,0:T(8,128)S(1)}, f32[48,128]{1,0:T(8,128)S(1)}, u32[]{:S(2)}, u32[]{:S(2)}) collective-permute-start(f32[48,128]{1,0:T(8,128)S(1)} %get-tuple-element.53), channel_id=1, source_target_pairs={{0,16},{16,0},{1,17},{17,1},{2,18},{18,2},{3,19},{19,3},{4,20},{20... | collective-permute-start | bytes 73736 | tf_op jit(solution)/shard_map/ppermute | solution.py:38
  5.0 4.0 %collective-permute-start.2 = (f32[16,128]{1,0:T(8,128)S(1)}, f32[16,128]{1,0:T(8,128)S(1)}, u32[]{:S(2)}, u32[]{:S(2)}) collective-permute-start(f32[16,128]{1,0:T(8,128)S(1)} %get-tuple-element.52), channel_id=1, source_target_pairs={{0,28},{4,16},{8,20},{12,24},{16,12},{20,0},{24,4},{28,8},{1,29},{... | collective-permute-start | bytes 24584 | tf_op jit(solution)/shard_map/ppermute | solution.py:63
  5.6 3.4 %collective-permute-start = (f32[16,128]{1,0:T(8,128)S(1)}, f32[16,128]{1,0:T(8,128)S(1)}, u32[]{:S(2)}, u32[]{:S(2)}) collective-permute-start(f32[16,128]{1,0:T(8,128)S(1)} %get-tuple-element.52), channel_id=1, source_target_pairs={{0,12},{4,0},{8,4},{12,8},{1,13},{5,1},{9,5},{13,9},{2,14},{6,2},{... | collective-permute-start | bytes 24584 | tf_op jit(solution)/shard_map/ppermute | solution.py:38
  9.1 5.5 %collective-permute-start.4 = (f32[56,128]{1,0:T(8,128)S(1)}, f32[56,128]{1,0:T(8,128)S(1)}, u32[]{:S(2)}, u32[]{:S(2)}) collective-permute-start(f32[56,128]{1,0:T(8,128)S(1)} %shard_map.97), channel_id=1, source_target_pairs={{0,4},{3,7},{1,2},{2,1},{4,0},{7,3},{5,6},{6,5},{8,12},{11,15},{9,... | collective-permute-start | bytes 86024 | tf_op jit(solution)/shard_map/ppermute | solution.py:56
  9.1 5.5 %collective-permute-start.3 = (f32[56,128]{1,0:T(8,128)S(1)}, f32[56,128]{1,0:T(8,128)S(1)}, u32[]{:S(2)}, u32[]{:S(2)}) collective-permute-start(f32[56,128]{1,0:T(8,128)S(1)} %shard_map.97), channel_id=1, source_target_pairs={{0,1},{1,0},{2,3},{3,2},{4,5},{5,4},{6,7},{7,6},{8,9},{9,8},{10,11... | collective-permute-start | bytes 86024 | tf_op jit(solution)/shard_map/ppermute | solution.py:57
  17.7 4.4 %collective-permute-start.6 = (f32[112,128]{1,0:T(8,128)S(1)}, f32[112,128]{1,0:T(8,128)S(1)}, u32[]{:S(2)}, u32[]{:S(2)}) collective-permute-start(f32[112,128]{1,0:T(8,128)S(1)} %get-tuple-element.81), channel_id=1, source_target_pairs={{0,4},{3,7},{1,2},{2,1},{4,0},{7,3},{5,6},{6,5},{8,12},{11,15},{9,... | collective-permute-start | bytes 172040 | tf_op jit(solution)/shard_map/ppermute | solution.py:56
  17.8 4.3 %collective-permute-start.5 = (f32[112,128]{1,0:T(8,128)S(1)}, f32[112,128]{1,0:T(8,128)S(1)}, u32[]{:S(2)}, u32[]{:S(2)}) collective-permute-start(f32[112,128]{1,0:T(8,128)S(1)} %get-tuple-element.82), channel_id=1, source_target_pairs={{0,1},{1,0},{2,3},{3,2},{4,5},{5,4},{6,7},{7,6},{8,9},{9,8},{10,11... | collective-permute-start | bytes 172040 | tf_op jit(solution)/shard_map/ppermute | solution.py:57
  22.1 5.0 %collective-permute-start.10 = (f32[80,128]{1,0:T(8,128)S(1)}, f32[80,128]{1,0:T(8,128)S(1)}, u32[]{:S(2)}, u32[]{:S(2)}) collective-permute-start(f32[80,128]{1,0:T(8,128)S(1)} %get-tuple-element.77), channel_id=1, source_target_pairs={{0,20},{4,24},{8,28},{12,16},{16,4},{20,8},{24,12},{28,0},{1,21},{... | collective-permute-start | bytes 122888 | tf_op jit(solution)/shard_map/ppermute | solution.py:63
  23.3 5.1 %collective-permute-start.7 = (f32[160,128]{1,0:T(8,128)S(1)}, f32[160,128]{1,0:T(8,128)S(1)}, u32[]{:S(2)}, u32[]{:S(2)}) collective-permute-start(f32[160,128]{1,0:T(8,128)S(1)} %get-tuple-element.75), channel_id=1, source_target_pairs={{0,16},{16,0},{1,17},{17,1},{2,18},{18,2},{3,19},{19,3},{4,20},{20... | collective-permute-start | bytes 245768 | tf_op jit(solution)/shard_map/ppermute | solution.py:38
  23.8 3.4 %collective-permute-start.9 = (f32[72,128]{1,0:T(8,128)S(1)}, f32[72,128]{1,0:T(8,128)S(1)}, u32[]{:S(2)}, u32[]{:S(2)}) collective-permute-start(f32[72,128]{1,0:T(8,128)S(1)} %get-tuple-element.83), channel_id=1, source_target_pairs={{0,12},{4,8},{8,4},{12,0},{1,13},{5,9},{9,5},{13,1},{2,14},{6,10},... | collective-permute-start | bytes 110600 | tf_op jit(solution)/shard_map/ppermute | solution.py:45
  25.1 2.1 %collective-permute-start.8 = (f32[72,128]{1,0:T(8,128)S(1)}, f32[72,128]{1,0:T(8,128)S(1)}, u32[]{:S(2)}, u32[]{:S(2)}) collective-permute-start(f32[72,128]{1,0:T(8,128)S(1)} %get-tuple-element.84), channel_id=1, source_target_pairs={{0,4},{4,0},{8,12},{12,8},{1,5},{5,1},{9,13},{13,9},{2,6},{6,2},{1... | collective-permute-start | bytes 110600 | tf_op jit(solution)/shard_map/ppermute | solution.py:45

commit v12 on v11

--- a/solution.py
+++ b/solution.py
@@ -101,7 +101,7 @@
 ):
     comps, size_x, size_y, _ = gas_ref.shape
     pairs = [
-        *((gas_ref.at[c], grid_ref.at[c, 1 : size_x + 1, 0:size_y]) for c in range(comps)),
+        (gas_ref, grid_ref.at[:, 1 : size_x + 1, 0:size_y]),
         (velocity_in, velocity_ref), (fraction_in, fraction_ref), (response_in, response_ref),
         (cell_in, cell_ref), (brick_in, brick_ref), (crossing_in, crossing_ref),
     ]
@@ -114,16 +114,16 @@
         grid_ref[c, size_x + 1] = zeros
         for x in range(size_x):
             grid_ref[c, x + 1, size_y:] = zeros[size_y:]
+    copies[0].wait()
     lane = lane_ids(size_y)
     face = jnp.zeros((size_y, LANES), jnp.float32)
     for c in range(comps):
-        copies[c].wait()
         plane_ref[c * size_y : (c + 1) * size_y] = grid_ref[c, 1, 0:size_y]
         for x in range(size_x):
             place = PACK * c + x
             face = jnp.where(lane == place, turned(grid_ref[c, x + 1, 0:size_y], place), face)
     face_ref[...] = face
-    for copy in copies[comps:]:
+    for copy in copies[1:]:
         copy.wait()
 
 
@@ -168,19 +168,15 @@
     count_x, count_y, count_z = size_x // BX, size_y // BY, size_z // BZ
     rows_z = size_z + 8
 
-    room = nblocks + WIDE
 
     def visit(k, counts):
         late = jnp.where(lax.rem(lax.div(brick_ref[k], count_z), count_y) == count_y - 1, 1, 0)
-        list_ref[jnp.where(late == 1, room + counts[1], counts[0])] = k
+        list_ref[jnp.where(late == 1, nblocks + counts[1], counts[0])] = k
         return counts[0] + 1 - late, counts[1] + late
 
     early, late = lax.fori_loop(0, nblocks, visit, (jnp.int32(0), jnp.int32(0)), unroll=8)
-    for base, count in ((0, early), (room, late)):
-        for u in range(WIDE):
-            list_ref[base + count + u] = nblocks
-    list_ref[2 * room] = early
-    list_ref[2 * room + 1] = late
+    list_ref[2 * nblocks] = early
+    list_ref[2 * nblocks + 1] = late
     ready_ref[...] = jnp.zeros_like(ready_ref)
 
     deposit_ref[...] = jnp.zeros_like(deposit_ref)
@@ -263,7 +259,7 @@
     lay_out_top(turned_ref, lines_ref, count_y - 1, comps, count_x, count_y, size_z)
 
 
-def block_steps(dims, list_ref, brick_ref):
+def block_steps(dims, list_ref, brick_ref, end):
     comps, _, count_y, count_z, rows_z = dims
     nblocks = brick_ref.shape[0]
     sub = row_ids(8)
@@ -275,7 +271,7 @@
         return jnp.where(rows == inside, 1.0 - along, 0.0) + jnp.where(rows == inside + 1.0, along, 0.0)
 
     def place_of(at):
-        k = list_ref[at]
+        k = jnp.where(at < end, list_ref[jnp.minimum(at, 2 * nblocks + 1)], nblocks)
         brick = jnp.where(k < nblocks, brick_ref[jnp.minimum(k, nblocks - 1)], 0)
         brick_x = lax.div(brick, count_y * count_z)
         brick_y = lax.rem(lax.div(brick, count_z), count_y)
@@ -370,7 +366,8 @@
 
 def groups_in(list_ref, late, many=UNROLL):
     room = (list_ref.shape[0] - 2) // 2
-    return late * room, (list_ref[2 * room + late] + many - 1) // many
+    count = list_ref[2 * room + late]
+    return late * room, (count + many - 1) // many, late * room + count
 
 
 def leave(crossing_ref, state_ref, leaving_ref, faces):
@@ -402,8 +399,8 @@
     halo_xz_kernel(grid_in_ref, lines_in_ref, face_ref, from_x_ref, edge_ref, grid_ref, lines_ref, top_ref, turned_ref)
     for copy in copies:
         copy.wait()
-    loaded, group_of, keep, _, _ = block_steps(dims, list_ref, brick_ref)
-    base, groups = groups_in(list_ref, 0)
+    base, groups, end = groups_in(list_ref, 0)
+    loaded, group_of, keep, _, _ = block_steps(dims, list_ref, brick_ref, end)
 
     @pl.loop(0, groups)
     def _(group):
@@ -422,8 +419,8 @@
 def deposit_kernel(
     dims, list_ref, brick_ref, crossing_ref, push_ref, spread_ref, state_ref, deposit_in_ref, deposit_ref, leaving_ref
 ):
-    _, _, _, deposits_of, add = block_steps(dims, list_ref, brick_ref)
-    base, groups = groups_in(list_ref, 0, WIDE)
+    base, groups, end = groups_in(list_ref, 0, WIDE)
+    _, _, _, deposits_of, add = block_steps(dims, list_ref, brick_ref, end)
     leave(crossing_ref, state_ref, leaving_ref, (0, 1, 4, 5))
 
     @pl.loop(0, groups)
@@ -444,8 +441,8 @@
     )
     for copy in copies:
         copy.wait()
-    loaded, group_of, keep, deposits_of, add = block_steps(dims, list_ref, brick_ref)
-    base, groups = groups_in(list_ref, 1)
+    base, groups, end = groups_in(list_ref, 1)
+    loaded, group_of, keep, deposits_of, add = block_steps(dims, list_ref, brick_ref, end)
     push_ref[...] = jnp.zeros_like(push_ref)
     spread_ref[...] = jnp.zeros_like(spread_ref)
 
@@ -688,7 +685,7 @@
         begin_kernel,
         [grid_shape, (size_y, LANES), (comps * size_y, LANES)]
         + [jax.ShapeDtypeStruct(array.shape, array.dtype) for array in inputs[1:]],
-        *inputs, hbm=range(7), scratch=(pltpu.SemaphoreType.DMA((comps + 6,)),),
+        *inputs, hbm=range(7), scratch=(pltpu.SemaphoreType.DMA((7,)),),
     )
     from_z = moved_along(face, "gz", -1)
     from_x = moved_along(plane, "gx", -1)
@@ -700,7 +697,7 @@
             deposit_shape,
             (TABLE_ROWS * spare, LANES),
             (8, LANES),
-            jax.ShapeDtypeStruct((2 * (nblocks + WIDE) + 2,), jnp.int32),
+            jax.ShapeDtypeStruct((2 * nblocks + 2,), jnp.int32),
         ],
         grid, velocity, fraction, response, cell_index, brick_index,
         smem=(5,), smem_outs=(4,), cycles=3000,
@@ -768,7 +765,7 @@
     both = lax.axis_size("gx") == 2
     to_x, to_z, to_xz = call(
         functools.partial(relay_kernel, size_x, size_y, comps, count),
-        [(edge + (2 if both else 1) * count, LANES), (2, count + size_y, LANES), (count + size_y + 8, LANES)],
+        [(edge + (2 if both else 1) * count, LANES), (2, count + size_y, LANES), (count + size_y, LANES)],
         y1, y2, to_x, to_z, leaving,
     )
     got_x = moved_along(to_x, "gx", 1)

time: 29.3 us -> 29.1 us (level)
  waiting for transfers between devices: 2.42 us -> 1.55 us
  starting transfers between devices: 12.5 us -> 13 us
    ppermute x2, starting transfers between devices: 1.79 us -> 0.68 us  [moved_diagonally(): return lax.ppermute(block, ('gx', 'gz'), route)]
    ppermute x1, waiting for transfers between devices: 1.06 us -> 0.19 us  [swapped_z(): lax.ppermute(blocks[1], 'gz', second)]
    ppermute x3, starting transfers between devices: 4.6 us -> 5.24 us  [moved_along(): lax.ppermute(block, axis, [(i, (i + distance) % count) for i in range(cou...]
    ppermute x2, starting transfers between devices: 4.66 us -> 5.21 us  [swapped_y(): return (lax.ppermute(blocks[0], 'gy', first), middle)]
    ppermute x1, starting transfers between devices: 1.33 us -> 1.81 us  [swapped_z(): lax.ppermute(blocks[1], 'gz', second)]
    ppermute x2, waiting for transfers between devices: 0.01 us -> 0.47 us  [moved_diagonally(): return lax.ppermute(block, ('gx', 'gz'), route)]
    ppermute x3, waiting for transfers between devices: 1.3 us -> 0.87 us  [moved_along(): lax.ppermute(block, axis, [(i, (i + distance) % count) for i in range(cou...]
  transfers between devices with their start and end apart: 11 -> 11, of which waited for: 2 -> 3; matrix products, arithmetic and copies ran while one was open for 0% -> 0% of each run, Pallas kernels for 28% -> 30%
where the time goes in v12:
time: 29.1 us
  Pallas kernels  13.8 us (47%)
  starting transfers between devices  13 us (45%)
  waiting for transfers between devices  1.55 us (5%)
  between operations  0.77 us (3%)
    pallas_call x12, Pallas kernels, call(): pl.pallas_call(body, out_shape=[o if isinstance(o, jax.ShapeDtypeStruct)...  13.8 us
    ppermute x3, starting transfers between devices, moved_along(): lax.ppermute(block, axis, [(i, (i + distance) % count) for i in range(cou...  5.24 us
    ppermute x2, starting transfers between devices, swapped_y(): return (lax.ppermute(blocks[0], 'gy', first), middle)  5.21 us
    ppermute x1, starting transfers between devices, swapped_z(): lax.ppermute(blocks[1], 'gz', second)  1.81 us
    ppermute x3, waiting for transfers between devices, moved_along(): lax.ppermute(block, axis, [(i, (i + distance) % count) for i in range(cou...  0.87 us
    ppermute x2, starting transfers between devices, moved_diagonally(): return lax.ppermute(block, ('gx', 'gz'), route)  0.68 us
  transfers between devices with their start and end apart: 11, of which 3 were waited for; matrix products, arithmetic and copies ran while one was open for 0% of the time, Pallas kernels for 30%

profile of v12, /device:TPU:0, one launch (start us, length us, event | category | flops | bytes accessed | tf_op | source)
XLA Modules:
  0.0 29.1 jit_solution(10323178860680364717)
XLA Ops:
  0.6 1.2 %shard_map.94 = (f32[3,18,24,128]{3,2,1,0:T(8,128)S(1)}, f32[16,128]{1,0:T(8,128)S(1)}, f32[48,128]{1,0:T(8,128)S(1)}, f32[3,64,128]{2,1,0:T(8,128)S(1)}, f32[3,...) custom-call(f32[3,16,16,128]{3,2,1,0:T(8,128)} %gas_ref.1, ...), custom_call_target="tpu_custom_call" | custom-call | tf_op jit(solution)/shard_map/pallas_call | solution.py:69
  1.9 3.0 %collective-permute-start.1 = (f32[48,128]{1,0:T(8,128)S(1)}, f32[48,128]{1,0:T(8,128)S(1)}, u32[]{:S(2)}, u32[]{:S(2)}) collective-permute-start(f32[48,128]{1,0:T(8,128)S(1)} %get-tuple-element.53), channel_id=1, source_target_pairs={{0,16},{16,0},{1,17},{17,1},{2,18},{18,2},{3,19},{19,3},{4,20},{20... | collective-permute-start | bytes 73736 | tf_op jit(solution)/shard_map/ppermute | solution.py:38
  4.9 0.6 %collective-permute-start.2 = (f32[16,128]{1,0:T(8,128)S(1)}, f32[16,128]{1,0:T(8,128)S(1)}, u32[]{:S(2)}, u32[]{:S(2)}) collective-permute-start(f32[16,128]{1,0:T(8,128)S(1)} %get-tuple-element.52), channel_id=1, source_target_pairs={{0,28},{4,16},{8,20},{12,24},{16,12},{20,0},{24,4},{28,8},{1,29},{... | collective-permute-start | bytes 24584 | tf_op jit(solution)/shard_map/ppermute | solution.py:63
  5.5 1.1 %collective-permute-start = (f32[16,128]{1,0:T(8,128)S(1)}, f32[16,128]{1,0:T(8,128)S(1)}, u32[]{:S(2)}, u32[]{:S(2)}) collective-permute-start(f32[16,128]{1,0:T(8,128)S(1)} %get-tuple-element.52), channel_id=1, source_target_pairs={{0,12},{4,0},{8,4},{12,8},{1,13},{5,1},{9,5},{13,9},{2,14},{6,2},{... | collective-permute-start | bytes 24584 | tf_op jit(solution)/shard_map/ppermute | solution.py:38
  6.6 2.0 %shard_map.95 = (f32[6528,128]{1,0:T(8,128)S(1)}, f32[2176,128]{1,0:T(8,128)S(1)}, f32[1152,128]{1,0:T(8,128)S(1)}, f32[8,128]{1,0:T(8,128)S(1)}, s32[130]{0:T(256)S(1)}) custom-call(f32[3,18,24,128]{3,2,1,0:T(8,128)S(1)} %get-tuple-element.42.grid_ref.grid_in_ref, f32[3,64,128]{2,1,0:T(8,128)S(1)} %get-tuple-element.43.velocity_ref, ...), custom_call_target="tpu_custom_call" | custom-call | flops 12288000 | bytes 3072000 | tf_op jit(solution)/shard_map/pallas_call | solution.py:69
  8.7 0.0 collective-permute-done.2.edge_ref
  8.7 0.0 collective-permute-done.face_ref
  8.7 0.0 collective-permute-done.1.from_x_ref
  8.7 0.1 shard_map.97
  8.8 0.0 collective-permute-start.4
  8.8 3.1 %collective-permute-start.3 = (f32[56,128]{1,0:T(8,128)S(1)}, f32[56,128]{1,0:T(8,128)S(1)}, u32[]{:S(2)}, u32[]{:S(2)}) collective-permute-start(f32[56,128]{1,0:T(8,128)S(1)} %shard_map.97), channel_id=1, source_target_pairs={{0,1},{1,0},{2,3},{3,2},{4,5},{5,4},{6,7},{7,6},{8,9},{9,8},{10,11... | collective-permute-start | bytes 86024 | tf_op jit(solution)/shard_map/ppermute | solution.py:57
  11.9 2.6 %shard_map.96 = (f32[576,128]{1,0:T(8,128)S(1)}, bf16[80,96,128]{2,1,0:T(8,128)(2,1)S(1)}, bf16[80,256,128]{2,1,0:T(8,128)(2,1)S(1)}, f32[3,18,24,128]{3,2,1,0:T...) custom-call(s32[130]{0:T(256)S(1)} %get-tuple-element.48.list_in.list_, ...), custom_call_target="tpu_custom_call", output_to_operand_aliasing={{3}: (3, {}), {4}: (4, {})} | custom-call | flops 16384000 | bytes 4096000 | tf_op jit(solution)/shard_map/pallas_call | solution.py:69
  14.6 0.0 collective-permute-done.4.second_ref
  14.6 0.0 collective-permute-done.3.first_ref
  14.6 2.5 %shard_map.98 = (f32[3,18,24,128]{3,2,1,0:T(8,128)S(1)}, f32[6528,128]{1,0:T(8,128)S(1)}, f32[576,128]{1,0:T(8,128)S(1)}, f32[2176,128]{1,0:T(8,128)S(1)}, f32[112,128]{1,0:T(8,128)S(1)}) custom-call(s32[130]{0:T(256)S(1)} %get-tuple-element.48.list_in.list_ref, ...), custom_call_target="tpu_custom_call", output_to_operand_aliasing={{0}: (4, {}), {1}: (5, {}), {2}: (9, {}), {3}: (10, {})} | custom-call | flops 8192000 | bytes 2048000 | tf_op jit(solution)/shard_map/pallas_call | solution.py:69
  17.1 0.2 shard_map.100
  17.3 0.1 collective-permute-start.6
  17.4 2.1 %collective-permute-start.5 = (f32[112,128]{1,0:T(8,128)S(1)}, f32[112,128]{1,0:T(8,128)S(1)}, u32[]{:S(2)}, u32[]{:S(2)}) collective-permute-start(f32[112,128]{1,0:T(8,128)S(1)} %get-tuple-element.82), channel_id=1, source_target_pairs={{0,1},{1,0},{2,3},{3,2},{4,5},{5,4},{6,7},{7,6},{8,9},{9,8},{10,11... | collective-permute-start | bytes 172040 | tf_op jit(solution)/shard_map/ppermute | solution.py:57
  19.5 2.6 %shard_map.99 = (f32[2176,128]{1,0:T(8,128)S(1)}, f32[224,128]{1,0:T(8,128)S(1)}) custom-call(s32[130]{0:T(256)S(1)} %get-tuple-element.48.list_in.list_ref, s32[64]{0:T(128)S(1)} %get-tuple-element.47.brick_ref.brick_in, s32[6,8]{1,0:T(8,128)S(1)} %get-tuple-element.49.crossing_in.crossing_ref, ...), custom_call_target="tpu_custom_call", output_to_operand_aliasing={{0}: (6, {})} | custom-call | flops 16384000 | bytes 4096000 | tf_op jit(solution)/shard_map/pallas_call | solution.py:69
  22.1 0.4 %shard_map.101 = (f32[3,17,24,128]{3,2,1,0:T(8,128)S(1)}, f32[24,128]{1,0:T(8,128)S(1)}) custom-call(f32[2176,128]{1,0:T(8,128)S(1)} %get-tuple-element.65.deposit_ref, f32[480,128]{1,0:T(8,128)S(1)} %get-tuple-element.67.top_tiles_ref), custom_call_target="tpu_custom_call" | custom-call | flops 4096000 | bytes 1024000 | tf_op jit(solution)/shard_map/pallas_call | solution.py:69
  22.5 0.2 shard_map.103
  22.7 0.0 collective-permute-done.6.y2_ref.second_ref
  22.7 0.0 collective-permute-done.5.y1_ref.first_ref
  22.7 0.1 collective-permute-start.10
  22.8 1.1 %collective-permute-start.7 = (f32[160,128]{1,0:T(8,128)S(1)}, f32[160,128]{1,0:T(8,128)S(1)}, u32[]{:S(2)}, u32[]{:S(2)}) collective-permute-start(f32[160,128]{1,0:T(8,128)S(1)} %get-tuple-element.75), channel_id=1, source_target_pairs={{0,16},{16,0},{1,17},{17,1},{2,18},{18,2},{3,19},{19,3},{4,20},{20... | collective-permute-start | bytes 245768 | tf_op jit(solution)/shard_map/ppermute | solution.py:38
  23.9 1.8 %collective-permute-start.9 = (f32[72,128]{1,0:T(8,128)S(1)}, f32[72,128]{1,0:T(8,128)S(1)}, u32[]{:S(2)}, u32[]{:S(2)}) collective-permute-start(f32[72,128]{1,0:T(8,128)S(1)} %get-tuple-element.83), channel_id=1, source_target_pairs={{0,12},{4,8},{8,4},{12,0},{1,13},{5,9},{9,5},{13,1},{2,14},{6,10},... | collective-permute-start | bytes 110600 | tf_op jit(solution)/shard_map/ppermute | solution.py:45
  25.7 0.0 collective-permute-start.8
  25.7 1.0 %shard_map.102 = (f32[3,16,16,128]{3,2,1,0:T(8,128)S(1)}, f32[3,64,128]{2,1,0:T(8,128)}) custom-call(f32[3,18,24,128]{3,2,1,0:T(8,128)S(1)} %get-tuple-element.60.grid_ref, f32[3,17,24,128]{3,2,1,0:T(8,128)S(1)} %get-tuple-element.68.deposit_ref, f32[128,128]{1,0:T(8,128)S(1)} %get-tuple-element.56.top_in_ref.top_ref, ...), custom_call_target="tpu_custom_call" | custom-call | flops 4096000 | bytes 1024000 | tf_op jit(solution)/shard_map/pallas_call | solution.py:69
  26.7 0.5 %collective-permute-done.10.edge_ref = f32[72,128]{1,0:T(8,128)S(1)} collective-permute-done((f32[72,128]{1,0:T(8,128)S(1)}, f32[72,128]{1,0:T(8,128)S(1)}, u32[]{:S(2)}, u32[]{:S(2)}) %collective-permute-start.10) | collective-permute-done | bytes 36896 | tf_op jit(solution)/shard_map/ppermute | solution.py:63
  27.2 0.2 collective-permute-done.9.z2_ref
  27.4 0.0 collective-permute-done.8.z1_ref
  27.4 0.9 %collective-permute-done.7.x_ref.minus_x_ref = f32[160,128]{1,0:T(8,128)S(1)} collective-permute-done((f32[160,128]{1,0:T(8,128)S(1)}, f32[160,128]{1,0:T(8,128)S(1)}, u32[]{:S(2)}, u32[]{:S(2)}) %collective-permute-start.7) | collective-permute-done | bytes 81952 | tf_op jit(solution)/shard_map/ppermute | solution.py:38
  28.2 0.9 %shard_map.105 = (f32[3,16,16,128]{3,2,1,0:T(8,128)}, f32[6,7,8,128]{3,2,1,0:T(8,128)}) custom-call(f32[3,16,16,128]{3,2,1,0:T(8,128)S(1)} %get-tuple-element.70.base_ref, f32[112,128]{1,0:T(8,128)S(1)} %collective-permute-done.5.y1_ref.first_ref, f32[112,128]{1,0:T(8,128)S(1)} %collective-permute-done.6.y2_ref.second_ref, ...), custom_call_target="tpu_custom_call" | custom-call | tf_op jit(solution)/shard_map/pallas_call | solution.py:69
  (3 shorter events, 0.0 us)
Async XLA Ops:
  1.9 6.8 %collective-permute-start.1 = (f32[48,128]{1,0:T(8,128)S(1)}, f32[48,128]{1,0:T(8,128)S(1)}, u32[]{:S(2)}, u32[]{:S(2)}) collective-permute-start(f32[48,128]{1,0:T(8,128)S(1)} %get-tuple-element.53), channel_id=1, source_target_pairs={{0,16},{16,0},{1,17},{17,1},{2,18},{18,2},{3,19},{19,3},{4,20},{20... | collective-permute-start | bytes 73736 | tf_op jit(solution)/shard_map/ppermute | solution.py:38
  4.9 3.7 %collective-permute-start.2 = (f32[16,128]{1,0:T(8,128)S(1)}, f32[16,128]{1,0:T(8,128)S(1)}, u32[]{:S(2)}, u32[]{:S(2)}) collective-permute-start(f32[16,128]{1,0:T(8,128)S(1)} %get-tuple-element.52), channel_id=1, source_target_pairs={{0,28},{4,16},{8,20},{12,24},{16,12},{20,0},{24,4},{28,8},{1,29},{... | collective-permute-start | bytes 24584 | tf_op jit(solution)/shard_map/ppermute | solution.py:63
  5.5 3.2 %collective-permute-start = (f32[16,128]{1,0:T(8,128)S(1)}, f32[16,128]{1,0:T(8,128)S(1)}, u32[]{:S(2)}, u32[]{:S(2)}) collective-permute-start(f32[16,128]{1,0:T(8,128)S(1)} %get-tuple-element.52), channel_id=1, source_target_pairs={{0,12},{4,0},{8,4},{12,8},{1,13},{5,1},{9,5},{13,9},{2,14},{6,2},{... | collective-permute-start | bytes 24584 | tf_op jit(solution)/shard_map/ppermute | solution.py:38
  8.8 5.8 %collective-permute-start.4 = (f32[56,128]{1,0:T(8,128)S(1)}, f32[56,128]{1,0:T(8,128)S(1)}, u32[]{:S(2)}, u32[]{:S(2)}) collective-permute-start(f32[56,128]{1,0:T(8,128)S(1)} %shard_map.97), channel_id=1, source_target_pairs={{0,4},{3,7},{1,2},{2,1},{4,0},{7,3},{5,6},{6,5},{8,12},{11,15},{9,... | collective-permute-start | bytes 86024 | tf_op jit(solution)/shard_map/ppermute | solution.py:56
  8.8 5.8 %collective-permute-start.3 = (f32[56,128]{1,0:T(8,128)S(1)}, f32[56,128]{1,0:T(8,128)S(1)}, u32[]{:S(2)}, u32[]{:S(2)}) collective-permute-start(f32[56,128]{1,0:T(8,128)S(1)} %shard_map.97), channel_id=1, source_target_pairs={{0,1},{1,0},{2,3},{3,2},{4,5},{5,4},{6,7},{7,6},{8,9},{9,8},{10,11... | collective-permute-start | bytes 86024 | tf_op jit(solution)/shard_map/ppermute | solution.py:57
  17.3 5.4 %collective-permute-start.6 = (f32[112,128]{1,0:T(8,128)S(1)}, f32[112,128]{1,0:T(8,128)S(1)}, u32[]{:S(2)}, u32[]{:S(2)}) collective-permute-start(f32[112,128]{1,0:T(8,128)S(1)} %get-tuple-element.81), channel_id=1, source_target_pairs={{0,4},{3,7},{1,2},{2,1},{4,0},{7,3},{5,6},{6,5},{8,12},{11,15},{9,... | collective-permute-start | bytes 172040 | tf_op jit(solution)/shard_map/ppermute | solution.py:56
  17.4 5.3 %collective-permute-start.5 = (f32[112,128]{1,0:T(8,128)S(1)}, f32[112,128]{1,0:T(8,128)S(1)}, u32[]{:S(2)}, u32[]{:S(2)}) collective-permute-start(f32[112,128]{1,0:T(8,128)S(1)} %get-tuple-element.82), channel_id=1, source_target_pairs={{0,1},{1,0},{2,3},{3,2},{4,5},{5,4},{6,7},{7,6},{8,9},{9,8},{10,11... | collective-permute-start | bytes 172040 | tf_op jit(solution)/shard_map/ppermute | solution.py:57
  22.7 4.4 %collective-permute-start.10 = (f32[72,128]{1,0:T(8,128)S(1)}, f32[72,128]{1,0:T(8,128)S(1)}, u32[]{:S(2)}, u32[]{:S(2)}) collective-permute-start(f32[72,128]{1,0:T(8,128)S(1)} %get-tuple-element.77), channel_id=1, source_target_pairs={{0,20},{4,24},{8,28},{12,16},{16,4},{20,8},{24,12},{28,0},{1,21},{... | collective-permute-start | bytes 110600 | tf_op jit(solution)/shard_map/ppermute | solution.py:63
  22.8 5.4 %collective-permute-start.7 = (f32[160,128]{1,0:T(8,128)S(1)}, f32[160,128]{1,0:T(8,128)S(1)}, u32[]{:S(2)}, u32[]{:S(2)}) collective-permute-start(f32[160,128]{1,0:T(8,128)S(1)} %get-tuple-element.75), channel_id=1, source_target_pairs={{0,16},{16,0},{1,17},{17,1},{2,18},{18,2},{3,19},{19,3},{4,20},{20... | collective-permute-start | bytes 245768 | tf_op jit(solution)/shard_map/ppermute | solution.py:38
  23.9 3.4 %collective-permute-start.9 = (f32[72,128]{1,0:T(8,128)S(1)}, f32[72,128]{1,0:T(8,128)S(1)}, u32[]{:S(2)}, u32[]{:S(2)}) collective-permute-start(f32[72,128]{1,0:T(8,128)S(1)} %get-tuple-element.83), channel_id=1, source_target_pairs={{0,12},{4,8},{8,4},{12,0},{1,13},{5,9},{9,5},{13,1},{2,14},{6,10},... | collective-permute-start | bytes 110600 | tf_op jit(solution)/shard_map/ppermute | solution.py:45
  25.7 1.6 %collective-permute-start.8 = (f32[72,128]{1,0:T(8,128)S(1)}, f32[72,128]{1,0:T(8,128)S(1)}, u32[]{:S(2)}, u32[]{:S(2)}) collective-permute-start(f32[72,128]{1,0:T(8,128)S(1)} %get-tuple-element.84), channel_id=1, source_target_pairs={{0,4},{4,0},{8,12},{12,8},{1,5},{5,1},{9,13},{13,9},{2,6},{6,2},{1... | collective-permute-start | bytes 110600 | tf_op jit(solution)/shard_map/ppermute | solution.py:45

commit v13 on v12

--- a/solution.py
+++ b/solution.py
@@ -471,7 +471,7 @@
     return total
 
 
-def send_y_kernel(push, diffuse, leaving_ref, grid_ref, deposit_ref, y_ref, tiles_ref, lines_ref):
+def send_y_kernel(push, diffuse, leaving_ref, grid_ref, deposit_ref, y1_ref, y2_ref, tiles_ref, lines_ref):
     comps, size_x, size_y, size_z = grid_ref.shape[0], grid_ref.shape[1] - 2, grid_ref.shape[2] - 8, grid_ref.shape[3]
     count_x, count_y = size_x // BX, size_y // BY
     rows_z = size_z + 8
@@ -481,8 +481,8 @@
         at = (p * count_y + count_y - 1) * rows_z
         tiles_ref[p * height : (p + 1) * height] = jnp.transpose(deposit_ref[at : at + size_z])[:height]
     first = jnp.full((rows, LANES), odd("gy")) == 0
-    y_ref[0, 0:rows] = jnp.where(first, leaving_ref[0], leaving_ref[1])
-    y_ref[1, 0:rows] = jnp.where(first, leaving_ref[1], leaving_ref[0])
+    y1_ref[0:rows] = jnp.where(first, leaving_ref[0], leaving_ref[1])
+    y2_ref[0:rows] = jnp.where(first, leaving_ref[1], leaving_ref[0])
     lines_ref[...] = jnp.zeros_like(lines_ref)
     for c in range(comps):
         for p in range(count_x):
@@ -497,8 +497,8 @@
         beside = jnp.concatenate([grid_ref[c, 1 : size_x + 1, size_y - 1], jnp.zeros((8, LANES), jnp.float32)], axis=0)
         line = push * lines_ref[spot] + diffuse * beside
         at = rows + c * (size_x + 1)
-        y_ref[0, at : at + size_x + 1] = line[: size_x + 1]
-        y_ref[1, at : at + size_x + 1] = line[: size_x + 1]
+        y1_ref[at : at + size_x + 1] = line[: size_x + 1]
+        y2_ref[at : at + size_x + 1] = line[: size_x + 1]
         for a in range(REACH_X):
             place = PACK * c + a
             value = turned(wrapped, place - c * SPREAD - a * REACH_Y - BY)
@@ -507,8 +507,8 @@
     for p in range(1, count_x):
         corner = corner + turned(packed[p : p + 1], p * BX)
     at = rows + comps * (size_x + 1)
-    y_ref[0, at : at + 1] = push * corner
-    y_ref[1, at : at + 1] = push * corner
+    y1_ref[at : at + 1] = push * corner
+    y2_ref[at : at + 1] = push * corner
 
 
 def merge_kernel(deposit_ref, top_tiles_ref, plane_ref, face_ref, tiles_ref, turned_ref):
@@ -603,7 +603,7 @@
     return jnp.where(jnp.full((1, LANES), lax.axis_index("gy")) != 0, got, 0.0)
 
 
-def relay_kernel(size_x, size_y, comps, count, first_ref, second_ref, x_in_ref, z_in_ref, leaving_ref, x_ref, z_ref, edge_ref):
+def relay_kernel(size_x, size_y, comps, count, first_ref, second_ref, x_in_ref, z_in_ref, leaving_ref, x_ref, z1_ref, z2_ref, edge_ref):
     edge = comps * size_y
     x_ref[0:edge] = x_in_ref[...]
     for c in range(comps):
@@ -617,11 +617,12 @@
     edge_ref[size_y:] = jnp.zeros((edge_ref.shape[0] - size_y, LANES), jnp.float32)
     edge_ref[0:size_y] = z_in_ref[...]
     edge_ref[0:1] = z_in_ref[0:1] + below(first_ref, second_ref, slice(at, at + 1))
-    up = odd("gz")
-    z_ref[up, 0:count] = leaving_ref[2]
-    z_ref[up, count : count + size_y] = edge_ref[0:size_y]
-    z_ref[1 - up, 0:count] = leaving_ref[3]
-    z_ref[1 - up, count : count + size_y] = jnp.zeros((size_y, LANES), jnp.float32)
+    first = jnp.full((1, LANES), odd("gz")) == 0
+    plus = jnp.concatenate([leaving_ref[2], edge_ref[0:size_y]], axis=0)
+    minus = jnp.concatenate([leaving_ref[3], jnp.zeros((size_y, LANES), jnp.float32)], axis=0)
+    z1_ref[...] = jnp.where(first, plus, minus)
+    z2_ref[0 : count + size_y] = jnp.where(first, minus, plus)
+    z2_ref[count + size_y :] = jnp.zeros((z2_ref.shape[0] - count - size_y, LANES), jnp.float32)
 
 
 def finish_kernel(
@@ -737,12 +738,12 @@
     )
     leaving = leaving.reshape(2, count, LANES)
     height = comps * SPREAD
-    to_y, top_tiles = call(
+    to_y1, to_y2, top_tiles = call(
         functools.partial(send_y_kernel, push, diffuse),
-        [(2, count + line_rows, LANES), ((size_x // BX) * height, LANES)],
+        [(count + line_rows, LANES), (count + line_rows, LANES), ((size_x // BX) * height, LANES)],
         leaving, grid, deposit, cycles=300, scratch=(pltpu.VMEM((comps * ROWS_Y, LANES), jnp.float32),),
     )
-    y1, y2 = swapped_y((to_y[0], to_y[1]))
+    y1, y2 = swapped_y((to_y1, to_y2))
     deposit, leaving = call(
         functools.partial(deposit_kernel, dims), [deposit_shape, (4 * count, LANES)],
         blocks, brick_index, crossing, push_parts, spread_parts, state, deposit,
@@ -763,13 +764,13 @@
     )
     edge = comps * size_y
     both = lax.axis_size("gx") == 2
-    to_x, to_z, to_xz = call(
+    to_x, to_z1, to_z2, to_xz = call(
         functools.partial(relay_kernel, size_x, size_y, comps, count),
-        [(edge + (2 if both else 1) * count, LANES), (2, count + size_y, LANES), (count + size_y, LANES)],
+        [(edge + (2 if both else 1) * count, LANES), *[(count + size_y + 8 * more, LANES) for more in range(3)]],
         y1, y2, to_x, to_z, leaving,
     )
     got_x = moved_along(to_x, "gx", 1)
-    z1, z2 = swapped_z((to_z[0], to_z[1]))
+    z1, z2 = swapped_z((to_z1, to_z2))
     got_xz = moved_diagonally(to_xz, 1)
     got_mx = got_x if both else moved_along(leaving[1], "gx", -1)
     gas_next, arrivals = call(

time: 29.1 us -> 29.2 us (level)
  waiting for transfers between devices: 1.55 us -> 1.89 us
    ppermute x1, waiting for transfers between devices: 0.19 us -> 1.39 us  [swapped_z(): lax.ppermute(blocks[1], 'gz', second)]
    ppermute x3, waiting for transfers between devices: 0.87 us -> 0.01 us  [moved_along(): lax.ppermute(block, axis, [(i, (i + distance) % count) for i in range(cou...]
    ppermute x3, starting transfers between devices: 5.24 us -> 5.74 us  [moved_along(): lax.ppermute(block, axis, [(i, (i + distance) % count) for i in range(cou...]
    ppermute x1, starting transfers between devices: 1.81 us -> 1.35 us  [swapped_z(): lax.ppermute(blocks[1], 'gz', second)]
    ppermute x2, starting transfers between devices: 5.21 us -> 4.84 us  [swapped_y(): return (lax.ppermute(blocks[0], 'gy', first), middle)]
where the time goes in v13:
time: 29.2 us; the launch traced here: 29.3 us
  Pallas kernels  13.8 us (47%)
  starting transfers between devices  12.9 us (44%)
  waiting for transfers between devices  1.89 us (6%)
  between operations  0.75 us (3%)
    pallas_call x12, Pallas kernels, call(): pl.pallas_call(body, out_shape=[o if isinstance(o, jax.ShapeDtypeStruct)...  13.8 us
    ppermute x3, starting transfers between devices, moved_along(): lax.ppermute(block, axis, [(i, (i + distance) % count) for i in range(cou...  5.74 us
    ppermute x2, starting transfers between devices, swapped_y(): return (lax.ppermute(blocks[0], 'gy', first), middle)  4.84 us
    ppermute x1, waiting for transfers between devices, swapped_z(): lax.ppermute(blocks[1], 'gz', second)  1.39 us
    ppermute x1, starting transfers between devices, swapped_z(): lax.ppermute(blocks[1], 'gz', second)  1.35 us
    ppermute x2, starting transfers between devices, moved_diagonally(): return lax.ppermute(block, ('gx', 'gz'), route)  0.93 us
  transfers between devices with their start and end apart: 11, of which 3 were waited for; matrix products, arithmetic and copies ran while one was open for 0% of the time, Pallas kernels for 30%

profile of v13, /device:TPU:0, one launch (start us, length us, event | category | flops | bytes accessed | tf_op | source)
XLA Modules:
  0.0 29.3 jit_solution(10827535547581391834)
XLA Ops:
  0.6 1.2 %shard_map.94 = (f32[3,18,24,128]{3,2,1,0:T(8,128)S(1)}, f32[16,128]{1,0:T(8,128)S(1)}, f32[48,128]{1,0:T(8,128)S(1)}, f32[3,64,128]{2,1,0:T(8,128)S(1)}, f32[3,...) custom-call(f32[3,16,16,128]{3,2,1,0:T(8,128)} %gas_ref.1, ...), custom_call_target="tpu_custom_call" | custom-call | tf_op jit(solution)/shard_map/pallas_call | solution.py:69
  1.9 3.0 %collective-permute-start.1 = (f32[48,128]{1,0:T(8,128)S(1)}, f32[48,128]{1,0:T(8,128)S(1)}, u32[]{:S(2)}, u32[]{:S(2)}) collective-permute-start(f32[48,128]{1,0:T(8,128)S(1)} %get-tuple-element.55), channel_id=1, source_target_pairs={{0,16},{16,0},{1,17},{17,1},{2,18},{18,2},{3,19},{19,3},{4,20},{20... | collective-permute-start | bytes 73736 | tf_op jit(solution)/shard_map/ppermute | solution.py:38
  4.9 0.6 %collective-permute-start.2 = (f32[16,128]{1,0:T(8,128)S(1)}, f32[16,128]{1,0:T(8,128)S(1)}, u32[]{:S(2)}, u32[]{:S(2)}) collective-permute-start(f32[16,128]{1,0:T(8,128)S(1)} %get-tuple-element.54), channel_id=1, source_target_pairs={{0,28},{4,16},{8,20},{12,24},{16,12},{20,0},{24,4},{28,8},{1,29},{... | collective-permute-start | bytes 24584 | tf_op jit(solution)/shard_map/ppermute | solution.py:63
  5.5 1.1 %collective-permute-start = (f32[16,128]{1,0:T(8,128)S(1)}, f32[16,128]{1,0:T(8,128)S(1)}, u32[]{:S(2)}, u32[]{:S(2)}) collective-permute-start(f32[16,128]{1,0:T(8,128)S(1)} %get-tuple-element.54), channel_id=1, source_target_pairs={{0,12},{4,0},{8,4},{12,8},{1,13},{5,1},{9,5},{13,9},{2,14},{6,2},{... | collective-permute-start | bytes 24584 | tf_op jit(solution)/shard_map/ppermute | solution.py:38
  6.6 2.0 %shard_map.95 = (f32[6528,128]{1,0:T(8,128)S(1)}, f32[2176,128]{1,0:T(8,128)S(1)}, f32[1152,128]{1,0:T(8,128)S(1)}, f32[8,128]{1,0:T(8,128)S(1)}, s32[130]{0:T(256)S(1)}) custom-call(f32[3,18,24,128]{3,2,1,0:T(8,128)S(1)} %get-tuple-element.44.grid_ref.grid_in_ref, f32[3,64,128]{2,1,0:T(8,128)S(1)} %get-tuple-element.45.velocity_ref, ...), custom_call_target="tpu_custom_call" | custom-call | flops 12288000 | bytes 3072000 | tf_op jit(solution)/shard_map/pallas_call | solution.py:69
  8.7 0.0 collective-permute-done.2.edge_ref
  8.7 0.0 collective-permute-done.face_ref
  8.7 0.0 collective-permute-done.1.from_x_ref
  8.7 0.1 shard_map.97
  8.8 0.0 collective-permute-start.4
  8.8 3.1 %collective-permute-start.3 = (f32[56,128]{1,0:T(8,128)S(1)}, f32[56,128]{1,0:T(8,128)S(1)}, u32[]{:S(2)}, u32[]{:S(2)}) collective-permute-start(f32[56,128]{1,0:T(8,128)S(1)} %shard_map.97), channel_id=1, source_target_pairs={{0,1},{1,0},{2,3},{3,2},{4,5},{5,4},{6,7},{7,6},{8,9},{9,8},{10,11... | collective-permute-start | bytes 86024 | tf_op jit(solution)/shard_map/ppermute | solution.py:57
  11.9 2.6 %shard_map.96 = (f32[576,128]{1,0:T(8,128)S(1)}, bf16[80,96,128]{2,1,0:T(8,128)(2,1)S(1)}, bf16[80,256,128]{2,1,0:T(8,128)(2,1)S(1)}, f32[3,18,24,128]{3,2,1,0:T...) custom-call(s32[130]{0:T(256)S(1)} %get-tuple-element.50.list_in.list_, ...), custom_call_target="tpu_custom_call", output_to_operand_aliasing={{3}: (3, {}), {4}: (4, {})} | custom-call | flops 16384000 | bytes 4096000 | tf_op jit(solution)/shard_map/pallas_call | solution.py:69
  14.6 0.0 collective-permute-done.4.second_ref
  14.6 0.0 collective-permute-done.3.first_ref
  14.6 2.5 %shard_map.98 = (f32[3,18,24,128]{3,2,1,0:T(8,128)S(1)}, f32[6528,128]{1,0:T(8,128)S(1)}, f32[576,128]{1,0:T(8,128)S(1)}, f32[2176,128]{1,0:T(8,128)S(1)}, f32[112,128]{1,0:T(8,128)S(1)}) custom-call(s32[130]{0:T(256)S(1)} %get-tuple-element.50.list_in.list_ref, ...), custom_call_target="tpu_custom_call", output_to_operand_aliasing={{0}: (4, {}), {1}: (5, {}), {2}: (9, {}), {3}: (10, {})} | custom-call | flops 8192000 | bytes 2048000 | tf_op jit(solution)/shard_map/pallas_call | solution.py:69
  17.1 0.2 shard_map.100
  17.3 1.7 %collective-permute-start.5 = (f32[112,128]{1,0:T(8,128)S(1)}, f32[112,128]{1,0:T(8,128)S(1)}, u32[]{:S(2)}, u32[]{:S(2)}) collective-permute-start(f32[112,128]{1,0:T(8,128)S(1)} %get-tuple-element.71), channel_id=1, source_target_pairs={{0,1},{1,0},{2,3},{3,2},{4,5},{5,4},{6,7},{7,6},{8,9},{9,8},{10,11... | collective-permute-start | bytes 172040 | tf_op jit(solution)/shard_map/ppermute | solution.py:57
  19.0 0.0 collective-permute-start.6
  19.0 2.6 %shard_map.99 = (f32[2176,128]{1,0:T(8,128)S(1)}, f32[224,128]{1,0:T(8,128)S(1)}) custom-call(s32[130]{0:T(256)S(1)} %get-tuple-element.50.list_in.list_ref, s32[64]{0:T(128)S(1)} %get-tuple-element.49.brick_ref.brick_in, s32[6,8]{1,0:T(8,128)S(1)} %get-tuple-element.51.crossing_in.crossing_ref, ...), custom_call_target="tpu_custom_call", output_to_operand_aliasing={{0}: (6, {})} | custom-call | flops 16384000 | bytes 4096000 | tf_op jit(solution)/shard_map/pallas_call | solution.py:69
  21.6 0.4 %shard_map.101 = (f32[3,17,24,128]{3,2,1,0:T(8,128)S(1)}, f32[24,128]{1,0:T(8,128)S(1)}) custom-call(f32[2176,128]{1,0:T(8,128)S(1)} %get-tuple-element.67.deposit_ref, f32[480,128]{1,0:T(8,128)S(1)} %get-tuple-element.69.top_tiles_ref), custom_call_target="tpu_custom_call" | custom-call | flops 4096000 | bytes 1024000 | tf_op jit(solution)/shard_map/pallas_call | solution.py:69
  22.0 0.2 shard_map.103
  22.2 0.0 collective-permute-done.5.y1_ref.first_ref
  22.2 0.0 collective-permute-done.6.y2_ref.second_ref
  22.3 1.6 %collective-permute-start.7 = (f32[160,128]{1,0:T(8,128)S(1)}, f32[160,128]{1,0:T(8,128)S(1)}, u32[]{:S(2)}, u32[]{:S(2)}) collective-permute-start(f32[160,128]{1,0:T(8,128)S(1)} %get-tuple-element.78), channel_id=1, source_target_pairs={{0,16},{16,0},{1,17},{17,1},{2,18},{18,2},{3,19},{19,3},{4,20},{20... | collective-permute-start | bytes 245768 | tf_op jit(solution)/shard_map/ppermute | solution.py:38
  23.9 0.3 %collective-permute-start.10 = (f32[88,128]{1,0:T(8,128)S(1)}, f32[88,128]{1,0:T(8,128)S(1)}, u32[]{:S(2)}, u32[]{:S(2)}) collective-permute-start(f32[88,128]{1,0:T(8,128)S(1)} %get-tuple-element.81), channel_id=1, source_target_pairs={{0,20},{4,24},{8,28},{12,16},{16,4},{20,8},{24,12},{28,0},{1,21},{... | collective-permute-start | bytes 135176 | tf_op jit(solution)/shard_map/ppermute | solution.py:63
  24.2 1.4 %collective-permute-start.9 = (f32[80,128]{1,0:T(8,128)S(1)}, f32[80,128]{1,0:T(8,128)S(1)}, u32[]{:S(2)}, u32[]{:S(2)}) collective-permute-start(f32[80,128]{1,0:T(8,128)S(1)} %get-tuple-element.80), channel_id=1, source_target_pairs={{0,12},{4,8},{8,4},{12,0},{1,13},{5,9},{9,5},{13,1},{2,14},{6,10},... | collective-permute-start | bytes 122888 | tf_op jit(solution)/shard_map/ppermute | solution.py:45
  25.6 0.0 collective-permute-start.8
  25.6 1.0 %shard_map.102 = (f32[3,16,16,128]{3,2,1,0:T(8,128)S(1)}, f32[3,64,128]{2,1,0:T(8,128)}) custom-call(f32[3,18,24,128]{3,2,1,0:T(8,128)S(1)} %get-tuple-element.62.grid_ref, f32[3,17,24,128]{3,2,1,0:T(8,128)S(1)} %get-tuple-element.70.deposit_ref, f32[128,128]{1,0:T(8,128)S(1)} %get-tuple-element.58.top_in_ref.top_ref, ...), custom_call_target="tpu_custom_call" | custom-call | flops 4096000 | bytes 1024000 | tf_op jit(solution)/shard_map/pallas_call | solution.py:69
  26.5 0.2 collective-permute-done.8.z1_ref
  26.8 1.4 %collective-permute-done.9.z2_ref = f32[80,128]{1,0:T(8,128)S(1)} collective-permute-done((f32[80,128]{1,0:T(8,128)S(1)}, f32[80,128]{1,0:T(8,128)S(1)}, u32[]{:S(2)}, u32[]{:S(2)}) %collective-permute-start.9) | collective-permute-done | bytes 40992 | tf_op jit(solution)/shard_map/ppermute | solution.py:45
  28.2 0.2 collective-permute-done.10.edge_ref
  28.4 0.0 collective-permute-done.7.x_ref.minus_x_ref
  28.4 0.9 %shard_map.105 = (f32[3,16,16,128]{3,2,1,0:T(8,128)}, f32[6,7,8,128]{3,2,1,0:T(8,128)}) custom-call(f32[3,16,16,128]{3,2,1,0:T(8,128)S(1)} %get-tuple-element.73.base_ref, f32[112,128]{1,0:T(8,128)S(1)} %collective-permute-done.5.y1_ref.first_ref, f32[112,128]{1,0:T(8,128)S(1)} %collective-permute-done.6.y2_ref.second_ref, ...), custom_call_target="tpu_custom_call" | custom-call | tf_op jit(solution)/shard_map/pallas_call | solution.py:69
  (1 shorter events, 0.0 us)
Async XLA Ops:
  1.9 6.8 %collective-permute-start.1 = (f32[48,128]{1,0:T(8,128)S(1)}, f32[48,128]{1,0:T(8,128)S(1)}, u32[]{:S(2)}, u32[]{:S(2)}) collective-permute-start(f32[48,128]{1,0:T(8,128)S(1)} %get-tuple-element.55), channel_id=1, source_target_pairs={{0,16},{16,0},{1,17},{17,1},{2,18},{18,2},{3,19},{19,3},{4,20},{20... | collective-permute-start | bytes 73736 | tf_op jit(solution)/shard_map/ppermute | solution.py:38
  4.9 3.7 %collective-permute-start.2 = (f32[16,128]{1,0:T(8,128)S(1)}, f32[16,128]{1,0:T(8,128)S(1)}, u32[]{:S(2)}, u32[]{:S(2)}) collective-permute-start(f32[16,128]{1,0:T(8,128)S(1)} %get-tuple-element.54), channel_id=1, source_target_pairs={{0,28},{4,16},{8,20},{12,24},{16,12},{20,0},{24,4},{28,8},{1,29},{... | collective-permute-start | bytes 24584 | tf_op jit(solution)/shard_map/ppermute | solution.py:63
  5.5 3.2 %collective-permute-start = (f32[16,128]{1,0:T(8,128)S(1)}, f32[16,128]{1,0:T(8,128)S(1)}, u32[]{:S(2)}, u32[]{:S(2)}) collective-permute-start(f32[16,128]{1,0:T(8,128)S(1)} %get-tuple-element.54), channel_id=1, source_target_pairs={{0,12},{4,0},{8,4},{12,8},{1,13},{5,1},{9,5},{13,9},{2,14},{6,2},{... | collective-permute-start | bytes 24584 | tf_op jit(solution)/shard_map/ppermute | solution.py:38
  8.8 5.8 %collective-permute-start.4 = (f32[56,128]{1,0:T(8,128)S(1)}, f32[56,128]{1,0:T(8,128)S(1)}, u32[]{:S(2)}, u32[]{:S(2)}) collective-permute-start(f32[56,128]{1,0:T(8,128)S(1)} %shard_map.97), channel_id=1, source_target_pairs={{0,4},{3,7},{1,2},{2,1},{4,0},{7,3},{5,6},{6,5},{8,12},{11,15},{9,... | collective-permute-start | bytes 86024 | tf_op jit(solution)/shard_map/ppermute | solution.py:56
  8.8 5.8 %collective-permute-start.3 = (f32[56,128]{1,0:T(8,128)S(1)}, f32[56,128]{1,0:T(8,128)S(1)}, u32[]{:S(2)}, u32[]{:S(2)}) collective-permute-start(f32[56,128]{1,0:T(8,128)S(1)} %shard_map.97), channel_id=1, source_target_pairs={{0,1},{1,0},{2,3},{3,2},{4,5},{5,4},{6,7},{7,6},{8,9},{9,8},{10,11... | collective-permute-start | bytes 86024 | tf_op jit(solution)/shard_map/ppermute | solution.py:57
  17.3 4.9 %collective-permute-start.5 = (f32[112,128]{1,0:T(8,128)S(1)}, f32[112,128]{1,0:T(8,128)S(1)}, u32[]{:S(2)}, u32[]{:S(2)}) collective-permute-start(f32[112,128]{1,0:T(8,128)S(1)} %get-tuple-element.71), channel_id=1, source_target_pairs={{0,1},{1,0},{2,3},{3,2},{4,5},{5,4},{6,7},{7,6},{8,9},{9,8},{10,11... | collective-permute-start | bytes 172040 | tf_op jit(solution)/shard_map/ppermute | solution.py:57
  19.0 3.2 %collective-permute-start.6 = (f32[112,128]{1,0:T(8,128)S(1)}, f32[112,128]{1,0:T(8,128)S(1)}, u32[]{:S(2)}, u32[]{:S(2)}) collective-permute-start(f32[112,128]{1,0:T(8,128)S(1)} %get-tuple-element.72), channel_id=1, source_target_pairs={{0,4},{3,7},{1,2},{2,1},{4,0},{7,3},{5,6},{6,5},{8,12},{11,15},{9,... | collective-permute-start | bytes 172040 | tf_op jit(solution)/shard_map/ppermute | solution.py:56
  22.3 6.1 %collective-permute-start.7 = (f32[160,128]{1,0:T(8,128)S(1)}, f32[160,128]{1,0:T(8,128)S(1)}, u32[]{:S(2)}, u32[]{:S(2)}) collective-permute-start(f32[160,128]{1,0:T(8,128)S(1)} %get-tuple-element.78), channel_id=1, source_target_pairs={{0,16},{16,0},{1,17},{17,1},{2,18},{18,2},{3,19},{19,3},{4,20},{20... | collective-permute-start | bytes 245768 | tf_op jit(solution)/shard_map/ppermute | solution.py:38
  23.9 4.5 %collective-permute-start.10 = (f32[88,128]{1,0:T(8,128)S(1)}, f32[88,128]{1,0:T(8,128)S(1)}, u32[]{:S(2)}, u32[]{:S(2)}) collective-permute-start(f32[88,128]{1,0:T(8,128)S(1)} %get-tuple-element.81), channel_id=1, source_target_pairs={{0,20},{4,24},{8,28},{12,16},{16,4},{20,8},{24,12},{28,0},{1,21},{... | collective-permute-start | bytes 135176 | tf_op jit(solution)/shard_map/ppermute | solution.py:63
  24.2 4.0 %collective-permute-start.9 = (f32[80,128]{1,0:T(8,128)S(1)}, f32[80,128]{1,0:T(8,128)S(1)}, u32[]{:S(2)}, u32[]{:S(2)}) collective-permute-start(f32[80,128]{1,0:T(8,128)S(1)} %get-tuple-element.80), channel_id=1, source_target_pairs={{0,12},{4,8},{8,4},{12,0},{1,13},{5,9},{9,5},{13,1},{2,14},{6,10},... | collective-permute-start | bytes 122888 | tf_op jit(solution)/shard_map/ppermute | solution.py:45
  25.6 1.2 %collective-permute-start.8 = (f32[72,128]{1,0:T(8,128)S(1)}, f32[72,128]{1,0:T(8,128)S(1)}, u32[]{:S(2)}, u32[]{:S(2)}) collective-permute-start(f32[72,128]{1,0:T(8,128)S(1)} %get-tuple-element.79), channel_id=1, source_target_pairs={{0,4},{4,0},{8,12},{12,8},{1,5},{5,1},{9,13},{13,9},{2,6},{6,2},{1... | collective-permute-start | bytes 110600 | tf_op jit(solution)/shard_map/ppermute | solution.py:45

commit v14 on v13

--- a/solution.py
+++ b/solution.py
@@ -399,21 +399,17 @@
     halo_xz_kernel(grid_in_ref, lines_in_ref, face_ref, from_x_ref, edge_ref, grid_ref, lines_ref, top_ref, turned_ref)
     for copy in copies:
         copy.wait()
-    base, groups, end = groups_in(list_ref, 0)
+    base, groups, end = groups_in(list_ref, 0, WIDE)
     loaded, group_of, keep, _, _ = block_steps(dims, list_ref, brick_ref, end)
 
     @pl.loop(0, groups)
     def _(group):
-        taken = [loaded(base + group * UNROLL + u, lines_ref, table_ref) for u in range(UNROLL)]
+        taken = [loaded(base + group * WIDE + u, lines_ref, table_ref) for u in range(WIDE)]
         tiles, fresh = group_of(taken)
         keep(state_ref, taken, tiles)
         for i, (push, spread) in enumerate(fresh):
-            push_ref[group * UNROLL + i] = push
-            spread_ref[group * UNROLL + i] = spread
-
-    for i in range(UNROLL):
-        push_ref[groups * UNROLL + i] = jnp.zeros(push_ref.shape[1:], push_ref.dtype)
-        spread_ref[groups * UNROLL + i] = jnp.zeros(spread_ref.shape[1:], spread_ref.dtype)
+            push_ref[group * WIDE + i] = push
+            spread_ref[group * WIDE + i] = spread
 
 
 def deposit_kernel(
@@ -718,7 +714,7 @@
     state, push_parts, spread_parts, grid, lines, top = call(
         functools.partial(gather_kernel, dims),
         [(STATE * spare, LANES)]
-        + [jax.ShapeDtypeStruct(shape, jnp.bfloat16) for shape in parts(nblocks + 2 * UNROLL)]
+        + [jax.ShapeDtypeStruct(shape, jnp.bfloat16) for shape in parts(-(-nblocks // WIDE) * WIDE)]
         + [grid_shape, lines_shape, (LANES, LANES)],
         blocks, brick_index, table, grid, lines, from_z, from_x, from_xz,
         aliases={3: 3, 4: 4}, cycles=4000, scratch=(*scalars, square, pltpu.SemaphoreType.DMA((2,))),

time: 29.2 us -> 29.4 us (level)
  Pallas kernels: 13.8 us -> 12.6 us
  starting transfers between devices: 12.9 us -> 13.6 us
  waiting for transfers between devices: 1.89 us -> 2.38 us
    pallas_call x12, Pallas kernels: 13.8 us -> 12.6 us  [call(): pl.pallas_call(body, out_shape=[o if isinstance(o, jax.ShapeDtypeStruct)...]
    ppermute x2, waiting for transfers between devices: 0.25 us -> 1.16 us  [moved_diagonally(): return lax.ppermute(block, ('gx', 'gz'), route)]
    ppermute x3, starting transfers between devices: 5.74 us -> 6.64 us  [moved_along(): lax.ppermute(block, axis, [(i, (i + distance) % count) for i in range(cou...]
    ppermute x1, waiting for transfers between devices: 1.39 us -> 0.97 us  [swapped_z(): lax.ppermute(blocks[1], 'gz', second)]
    ppermute x2, starting transfers between devices: 0.93 us -> 0.6 us  [moved_diagonally(): return lax.ppermute(block, ('gx', 'gz'), route)]
    ppermute x2, starting transfers between devices: 4.84 us -> 5.13 us  [swapped_y(): return (lax.ppermute(blocks[0], 'gy', first), middle)]
  transfers between devices with their start and end apart: 11 -> 11, of which waited for: 3 -> 3; matrix products, arithmetic and copies ran while one was open for 0% -> 0% of each run, Pallas kernels for 30% -> 26%
where the time goes in v14:
time: 29.4 us; the launch traced here: 29.3 us
  starting transfers between devices  13.6 us (46%)
  Pallas kernels  12.6 us (43%)
  waiting for transfers between devices  2.38 us (8%)
  between operations  0.75 us (3%)
    pallas_call x12, Pallas kernels, call(): pl.pallas_call(body, out_shape=[o if isinstance(o, jax.ShapeDtypeStruct)...  12.6 us
    ppermute x3, starting transfers between devices, moved_along(): lax.ppermute(block, axis, [(i, (i + distance) % count) for i in range(cou...  6.64 us
    ppermute x2, starting transfers between devices, swapped_y(): return (lax.ppermute(blocks[0], 'gy', first), middle)  5.13 us
    ppermute x1, starting transfers between devices, swapped_z(): lax.ppermute(blocks[1], 'gz', second)  1.24 us
    ppermute x2, waiting for transfers between devices, moved_diagonally(): return lax.ppermute(block, ('gx', 'gz'), route)  1.16 us
    ppermute x1, waiting for transfers between devices, swapped_z(): lax.ppermute(blocks[1], 'gz', second)  0.97 us
    ppermute x2, starting transfers between devices, moved_diagonally(): return lax.ppermute(block, ('gx', 'gz'), route)  0.6 us
  transfers between devices with their start and end apart: 11, of which 3 were waited for; matrix products, arithmetic and copies ran while one was open for 0% of the time, Pallas kernels for 26%

profile of v14, /device:TPU:0, one launch (start us, length us, event | category | flops | bytes accessed | tf_op | source)
XLA Modules:
  0.0 29.3 jit_solution(1023997974022545867)
XLA Ops:
  0.6 1.2 %shard_map.94 = (f32[3,18,24,128]{3,2,1,0:T(8,128)S(1)}, f32[16,128]{1,0:T(8,128)S(1)}, f32[48,128]{1,0:T(8,128)S(1)}, f32[3,64,128]{2,1,0:T(8,128)S(1)}, f32[3,...) custom-call(f32[3,16,16,128]{3,2,1,0:T(8,128)} %gas_ref.1, ...), custom_call_target="tpu_custom_call" | custom-call | tf_op jit(solution)/shard_map/pallas_call | solution.py:69
  1.9 3.0 %collective-permute-start.1 = (f32[48,128]{1,0:T(8,128)S(1)}, f32[48,128]{1,0:T(8,128)S(1)}, u32[]{:S(2)}, u32[]{:S(2)}) collective-permute-start(f32[48,128]{1,0:T(8,128)S(1)} %get-tuple-element.55), channel_id=1, source_target_pairs={{0,16},{16,0},{1,17},{17,1},{2,18},{18,2},{3,19},{19,3},{4,20},{20... | collective-permute-start | bytes 73736 | tf_op jit(solution)/shard_map/ppermute | solution.py:38
  4.9 0.6 %collective-permute-start.2 = (f32[16,128]{1,0:T(8,128)S(1)}, f32[16,128]{1,0:T(8,128)S(1)}, u32[]{:S(2)}, u32[]{:S(2)}) collective-permute-start(f32[16,128]{1,0:T(8,128)S(1)} %get-tuple-element.54), channel_id=1, source_target_pairs={{0,28},{4,16},{8,20},{12,24},{16,12},{20,0},{24,4},{28,8},{1,29},{... | collective-permute-start | bytes 24584 | tf_op jit(solution)/shard_map/ppermute | solution.py:63
  5.5 1.1 %collective-permute-start = (f32[16,128]{1,0:T(8,128)S(1)}, f32[16,128]{1,0:T(8,128)S(1)}, u32[]{:S(2)}, u32[]{:S(2)}) collective-permute-start(f32[16,128]{1,0:T(8,128)S(1)} %get-tuple-element.54), channel_id=1, source_target_pairs={{0,12},{4,0},{8,4},{12,8},{1,13},{5,1},{9,5},{13,9},{2,14},{6,2},{... | collective-permute-start | bytes 24584 | tf_op jit(solution)/shard_map/ppermute | solution.py:38
  6.6 2.0 %shard_map.95 = (f32[6528,128]{1,0:T(8,128)S(1)}, f32[2176,128]{1,0:T(8,128)S(1)}, f32[1152,128]{1,0:T(8,128)S(1)}, f32[8,128]{1,0:T(8,128)S(1)}, s32[130]{0:T(256)S(1)}) custom-call(f32[3,18,24,128]{3,2,1,0:T(8,128)S(1)} %get-tuple-element.44.grid_ref.grid_in_ref, f32[3,64,128]{2,1,0:T(8,128)S(1)} %get-tuple-element.45.velocity_ref, ...), custom_call_target="tpu_custom_call" | custom-call | flops 12288000 | bytes 3072000 | tf_op jit(solution)/shard_map/pallas_call | solution.py:69
  8.7 0.0 collective-permute-done.2.edge_ref
  8.7 0.0 collective-permute-done.face_ref
  8.7 0.0 collective-permute-done.1.from_x_ref
  8.7 0.1 shard_map.97
  8.8 0.0 collective-permute-start.4
  8.8 3.1 %collective-permute-start.3 = (f32[56,128]{1,0:T(8,128)S(1)}, f32[56,128]{1,0:T(8,128)S(1)}, u32[]{:S(2)}, u32[]{:S(2)}) collective-permute-start(f32[56,128]{1,0:T(8,128)S(1)} %shard_map.97), channel_id=1, source_target_pairs={{0,1},{1,0},{2,3},{3,2},{4,5},{5,4},{6,7},{7,6},{8,9},{9,8},{10,11... | collective-permute-start | bytes 86024 | tf_op jit(solution)/shard_map/ppermute | solution.py:57
  11.9 1.9 %shard_map.96 = (f32[576,128]{1,0:T(8,128)S(1)}, bf16[64,96,128]{2,1,0:T(8,128)(2,1)S(1)}, bf16[64,256,128]{2,1,0:T(8,128)(2,1)S(1)}, f32[3,18,24,128]{3,2,1,0:T...) custom-call(s32[130]{0:T(256)S(1)} %get-tuple-element.50.list_in.list_, ...), custom_call_target="tpu_custom_call", output_to_operand_aliasing={{3}: (3, {}), {4}: (4, {})} | custom-call | flops 16384000 | bytes 4096000 | tf_op jit(solution)/shard_map/pallas_call | solution.py:69
  13.8 0.0 collective-permute-done.4.second_ref
  13.9 0.0 collective-permute-done.3.first_ref
  13.9 2.5 %shard_map.98 = (f32[3,18,24,128]{3,2,1,0:T(8,128)S(1)}, f32[6528,128]{1,0:T(8,128)S(1)}, f32[576,128]{1,0:T(8,128)S(1)}, f32[2176,128]{1,0:T(8,128)S(1)}, f32[112,128]{1,0:T(8,128)S(1)}) custom-call(s32[130]{0:T(256)S(1)} %get-tuple-element.50.list_in.list_ref, ...), custom_call_target="tpu_custom_call", output_to_operand_aliasing={{0}: (4, {}), {1}: (5, {}), {2}: (9, {}), {3}: (10, {})} | custom-call | flops 8192000 | bytes 2048000 | tf_op jit(solution)/shard_map/pallas_call | solution.py:69
  16.4 0.2 shard_map.100
  16.6 2.0 %collective-permute-start.5 = (f32[112,128]{1,0:T(8,128)S(1)}, f32[112,128]{1,0:T(8,128)S(1)}, u32[]{:S(2)}, u32[]{:S(2)}) collective-permute-start(f32[112,128]{1,0:T(8,128)S(1)} %get-tuple-element.71), channel_id=1, source_target_pairs={{0,1},{1,0},{2,3},{3,2},{4,5},{5,4},{6,7},{7,6},{8,9},{9,8},{10,11... | collective-permute-start | bytes 172040 | tf_op jit(solution)/shard_map/ppermute | solution.py:57
  18.6 0.0 collective-permute-start.6
  18.6 2.1 %shard_map.99 = (f32[2176,128]{1,0:T(8,128)S(1)}, f32[224,128]{1,0:T(8,128)S(1)}) custom-call(s32[130]{0:T(256)S(1)} %get-tuple-element.50.list_in.list_ref, s32[64]{0:T(128)S(1)} %get-tuple-element.49.brick_ref.brick_in, s32[6,8]{1,0:T(8,128)S(1)} %get-tuple-element.51.crossing_in.crossing_ref, ...), custom_call_target="tpu_custom_call", output_to_operand_aliasing={{0}: (6, {})} | custom-call | flops 16384000 | bytes 4096000 | tf_op jit(solution)/shard_map/pallas_call | solution.py:69
  20.7 0.4 %shard_map.101 = (f32[3,17,24,128]{3,2,1,0:T(8,128)S(1)}, f32[24,128]{1,0:T(8,128)S(1)}) custom-call(f32[2176,128]{1,0:T(8,128)S(1)} %get-tuple-element.67.deposit_ref, f32[480,128]{1,0:T(8,128)S(1)} %get-tuple-element.69.top_tiles_ref), custom_call_target="tpu_custom_call" | custom-call | flops 4096000 | bytes 1024000 | tf_op jit(solution)/shard_map/pallas_call | solution.py:69
  21.1 0.2 shard_map.103
  21.3 0.0 collective-permute-done.5.y1_ref.first_ref
  21.3 0.0 collective-permute-done.6.y2_ref.second_ref
  21.4 2.5 %collective-permute-start.7 = (f32[160,128]{1,0:T(8,128)S(1)}, f32[160,128]{1,0:T(8,128)S(1)}, u32[]{:S(2)}, u32[]{:S(2)}) collective-permute-start(f32[160,128]{1,0:T(8,128)S(1)} %get-tuple-element.78), channel_id=1, source_target_pairs={{0,16},{16,0},{1,17},{17,1},{2,18},{18,2},{3,19},{19,3},{4,20},{20... | collective-permute-start | bytes 245768 | tf_op jit(solution)/shard_map/ppermute | solution.py:38
  23.9 0.0 collective-permute-start.10
  23.9 1.2 %collective-permute-start.9 = (f32[80,128]{1,0:T(8,128)S(1)}, f32[80,128]{1,0:T(8,128)S(1)}, u32[]{:S(2)}, u32[]{:S(2)}) collective-permute-start(f32[80,128]{1,0:T(8,128)S(1)} %get-tuple-element.80), channel_id=1, source_target_pairs={{0,12},{4,8},{8,4},{12,0},{1,13},{5,9},{9,5},{13,1},{2,14},{6,10},... | collective-permute-start | bytes 122888 | tf_op jit(solution)/shard_map/ppermute | solution.py:45
  25.1 0.0 collective-permute-start.8
  25.1 1.0 %shard_map.102 = (f32[3,16,16,128]{3,2,1,0:T(8,128)S(1)}, f32[3,64,128]{2,1,0:T(8,128)}) custom-call(f32[3,18,24,128]{3,2,1,0:T(8,128)S(1)} %get-tuple-element.62.grid_ref, f32[3,17,24,128]{3,2,1,0:T(8,128)S(1)} %get-tuple-element.70.deposit_ref, f32[128,128]{1,0:T(8,128)S(1)} %get-tuple-element.58.top_in_ref.top_ref, ...), custom_call_target="tpu_custom_call" | custom-call | flops 4096000 | bytes 1024000 | tf_op jit(solution)/shard_map/pallas_call | solution.py:69
  26.1 0.2 collective-permute-done.8.z1_ref
  26.3 1.0 %collective-permute-done.9.z2_ref = f32[80,128]{1,0:T(8,128)S(1)} collective-permute-done((f32[80,128]{1,0:T(8,128)S(1)}, f32[80,128]{1,0:T(8,128)S(1)}, u32[]{:S(2)}, u32[]{:S(2)}) %collective-permute-start.9) | collective-permute-done | bytes 40992 | tf_op jit(solution)/shard_map/ppermute | solution.py:45
  27.3 1.2 %collective-permute-done.10.edge_ref = f32[88,128]{1,0:T(8,128)S(1)} collective-permute-done((f32[88,128]{1,0:T(8,128)S(1)}, f32[88,128]{1,0:T(8,128)S(1)}, u32[]{:S(2)}, u32[]{:S(2)}) %collective-permute-start.10) | collective-permute-done | bytes 45088 | tf_op jit(solution)/shard_map/ppermute | solution.py:63
  28.4 0.0 collective-permute-done.7.x_ref.minus_x_ref
  28.4 0.9 %shard_map.105 = (f32[3,16,16,128]{3,2,1,0:T(8,128)}, f32[6,7,8,128]{3,2,1,0:T(8,128)}) custom-call(f32[3,16,16,128]{3,2,1,0:T(8,128)S(1)} %get-tuple-element.73.base_ref, f32[112,128]{1,0:T(8,128)S(1)} %collective-permute-done.5.y1_ref.first_ref, f32[112,128]{1,0:T(8,128)S(1)} %collective-permute-done.6.y2_ref.second_ref, ...), custom_call_target="tpu_custom_call" | custom-call | tf_op jit(solution)/shard_map/pallas_call | solution.py:69
  (1 shorter events, 0.0 us)
Async XLA Ops:
  1.9 6.8 %collective-permute-start.1 = (f32[48,128]{1,0:T(8,128)S(1)}, f32[48,128]{1,0:T(8,128)S(1)}, u32[]{:S(2)}, u32[]{:S(2)}) collective-permute-start(f32[48,128]{1,0:T(8,128)S(1)} %get-tuple-element.55), channel_id=1, source_target_pairs={{0,16},{16,0},{1,17},{17,1},{2,18},{18,2},{3,19},{19,3},{4,20},{20... | collective-permute-start | bytes 73736 | tf_op jit(solution)/shard_map/ppermute | solution.py:38
  4.9 3.7 %collective-permute-start.2 = (f32[16,128]{1,0:T(8,128)S(1)}, f32[16,128]{1,0:T(8,128)S(1)}, u32[]{:S(2)}, u32[]{:S(2)}) collective-permute-start(f32[16,128]{1,0:T(8,128)S(1)} %get-tuple-element.54), channel_id=1, source_target_pairs={{0,28},{4,16},{8,20},{12,24},{16,12},{20,0},{24,4},{28,8},{1,29},{... | collective-permute-start | bytes 24584 | tf_op jit(solution)/shard_map/ppermute | solution.py:63
  5.5 3.2 %collective-permute-start = (f32[16,128]{1,0:T(8,128)S(1)}, f32[16,128]{1,0:T(8,128)S(1)}, u32[]{:S(2)}, u32[]{:S(2)}) collective-permute-start(f32[16,128]{1,0:T(8,128)S(1)} %get-tuple-element.54), channel_id=1, source_target_pairs={{0,12},{4,0},{8,4},{12,8},{1,13},{5,1},{9,5},{13,9},{2,14},{6,2},{... | collective-permute-start | bytes 24584 | tf_op jit(solution)/shard_map/ppermute | solution.py:38
  8.8 5.1 %collective-permute-start.4 = (f32[56,128]{1,0:T(8,128)S(1)}, f32[56,128]{1,0:T(8,128)S(1)}, u32[]{:S(2)}, u32[]{:S(2)}) collective-permute-start(f32[56,128]{1,0:T(8,128)S(1)} %shard_map.97), channel_id=1, source_target_pairs={{0,4},{3,7},{1,2},{2,1},{4,0},{7,3},{5,6},{6,5},{8,12},{11,15},{9,... | collective-permute-start | bytes 86024 | tf_op jit(solution)/shard_map/ppermute | solution.py:56
  8.8 5.1 %collective-permute-start.3 = (f32[56,128]{1,0:T(8,128)S(1)}, f32[56,128]{1,0:T(8,128)S(1)}, u32[]{:S(2)}, u32[]{:S(2)}) collective-permute-start(f32[56,128]{1,0:T(8,128)S(1)} %shard_map.97), channel_id=1, source_target_pairs={{0,1},{1,0},{2,3},{3,2},{4,5},{5,4},{6,7},{7,6},{8,9},{9,8},{10,11... | collective-permute-start | bytes 86024 | tf_op jit(solution)/shard_map/ppermute | solution.py:57
  16.6 4.8 %collective-permute-start.5 = (f32[112,128]{1,0:T(8,128)S(1)}, f32[112,128]{1,0:T(8,128)S(1)}, u32[]{:S(2)}, u32[]{:S(2)}) collective-permute-start(f32[112,128]{1,0:T(8,128)S(1)} %get-tuple-element.71), channel_id=1, source_target_pairs={{0,1},{1,0},{2,3},{3,2},{4,5},{5,4},{6,7},{7,6},{8,9},{9,8},{10,11... | collective-permute-start | bytes 172040 | tf_op jit(solution)/shard_map/ppermute | solution.py:57
  18.6 2.8 %collective-permute-start.6 = (f32[112,128]{1,0:T(8,128)S(1)}, f32[112,128]{1,0:T(8,128)S(1)}, u32[]{:S(2)}, u32[]{:S(2)}) collective-permute-start(f32[112,128]{1,0:T(8,128)S(1)} %get-tuple-element.72), channel_id=1, source_target_pairs={{0,4},{3,7},{1,2},{2,1},{4,0},{7,3},{5,6},{6,5},{8,12},{11,15},{9,... | collective-permute-start | bytes 172040 | tf_op jit(solution)/shard_map/ppermute | solution.py:56
  21.4 7.1 %collective-permute-start.7 = (f32[160,128]{1,0:T(8,128)S(1)}, f32[160,128]{1,0:T(8,128)S(1)}, u32[]{:S(2)}, u32[]{:S(2)}) collective-permute-start(f32[160,128]{1,0:T(8,128)S(1)} %get-tuple-element.78), channel_id=1, source_target_pairs={{0,16},{16,0},{1,17},{17,1},{2,18},{18,2},{3,19},{19,3},{4,20},{20... | collective-permute-start | bytes 245768 | tf_op jit(solution)/shard_map/ppermute | solution.py:38
  23.9 4.6 %collective-permute-start.10 = (f32[88,128]{1,0:T(8,128)S(1)}, f32[88,128]{1,0:T(8,128)S(1)}, u32[]{:S(2)}, u32[]{:S(2)}) collective-permute-start(f32[88,128]{1,0:T(8,128)S(1)} %get-tuple-element.81), channel_id=1, source_target_pairs={{0,20},{4,24},{8,28},{12,16},{16,4},{20,8},{24,12},{28,0},{1,21},{... | collective-permute-start | bytes 135176 | tf_op jit(solution)/shard_map/ppermute | solution.py:63
  23.9 3.4 %collective-permute-start.9 = (f32[80,128]{1,0:T(8,128)S(1)}, f32[80,128]{1,0:T(8,128)S(1)}, u32[]{:S(2)}, u32[]{:S(2)}) collective-permute-start(f32[80,128]{1,0:T(8,128)S(1)} %get-tuple-element.80), channel_id=1, source_target_pairs={{0,12},{4,8},{8,4},{12,0},{1,13},{5,9},{9,5},{13,1},{2,14},{6,10},... | collective-permute-start | bytes 122888 | tf_op jit(solution)/shard_map/ppermute | solution.py:45
  25.1 1.2 %collective-permute-start.8 = (f32[72,128]{1,0:T(8,128)S(1)}, f32[72,128]{1,0:T(8,128)S(1)}, u32[]{:S(2)}, u32[]{:S(2)}) collective-permute-start(f32[72,128]{1,0:T(8,128)S(1)} %get-tuple-element.79), channel_id=1, source_target_pairs={{0,4},{4,0},{8,12},{12,8},{1,5},{5,1},{9,13},{13,9},{2,6},{6,2},{1... | collective-permute-start | bytes 110600 | tf_op jit(solution)/shard_map/ppermute | solution.py:45

commit v15 on v14

--- a/solution.py
+++ b/solution.py
@@ -372,7 +372,7 @@
 
 def leave(crossing_ref, state_ref, leaving_ref, faces):
     slots = crossing_ref.shape[1]
-    rows = leaving_ref.shape[0] // (len(faces) * slots)
+    rows = (leaving_ref.shape[0] - 8) // (len(faces) * slots)
     for i, face in enumerate(faces):
         tiles = []
         for slot in range(slots):
@@ -471,14 +471,14 @@
     comps, size_x, size_y, size_z = grid_ref.shape[0], grid_ref.shape[1] - 2, grid_ref.shape[2] - 8, grid_ref.shape[3]
     count_x, count_y = size_x // BX, size_y // BY
     rows_z = size_z + 8
-    rows = leaving_ref.shape[1]
+    rows = (leaving_ref.shape[0] - 8) // 2
     height = comps * SPREAD
     for p in range(count_x):
         at = (p * count_y + count_y - 1) * rows_z
         tiles_ref[p * height : (p + 1) * height] = jnp.transpose(deposit_ref[at : at + size_z])[:height]
     first = jnp.full((rows, LANES), odd("gy")) == 0
-    y1_ref[0:rows] = jnp.where(first, leaving_ref[0], leaving_ref[1])
-    y2_ref[0:rows] = jnp.where(first, leaving_ref[1], leaving_ref[0])
+    y1_ref[0:rows] = jnp.where(first, leaving_ref[0:rows], leaving_ref[rows : 2 * rows])
+    y2_ref[0:rows] = jnp.where(first, leaving_ref[rows : 2 * rows], leaving_ref[0:rows])
     lines_ref[...] = jnp.zeros_like(lines_ref)
     for c in range(comps):
         for p in range(count_x):
@@ -606,16 +606,16 @@
         at = count + c * (size_x + 1) + size_x
         spot = slice(c * size_y, c * size_y + 1)
         x_ref[spot] = x_in_ref[spot] + below(first_ref, second_ref, slice(at, at + 1))
-    x_ref[edge : edge + count] = leaving_ref[0]
+    x_ref[edge : edge + count] = leaving_ref[0:count]
     if x_ref.shape[0] > edge + count:
-        x_ref[edge + count : edge + 2 * count] = leaving_ref[1]
+        x_ref[edge + count : edge + 2 * count] = leaving_ref[count : 2 * count]
     at = count + comps * (size_x + 1)
     edge_ref[size_y:] = jnp.zeros((edge_ref.shape[0] - size_y, LANES), jnp.float32)
     edge_ref[0:size_y] = z_in_ref[...]
     edge_ref[0:1] = z_in_ref[0:1] + below(first_ref, second_ref, slice(at, at + 1))
     first = jnp.full((1, LANES), odd("gz")) == 0
-    plus = jnp.concatenate([leaving_ref[2], edge_ref[0:size_y]], axis=0)
-    minus = jnp.concatenate([leaving_ref[3], jnp.zeros((size_y, LANES), jnp.float32)], axis=0)
+    plus = jnp.concatenate([leaving_ref[2 * count : 3 * count], edge_ref[0:size_y]], axis=0)
+    minus = jnp.concatenate([leaving_ref[3 * count : 4 * count], jnp.zeros((size_y, LANES), jnp.float32)], axis=0)
     z1_ref[...] = jnp.where(first, plus, minus)
     z2_ref[0 : count + size_y] = jnp.where(first, minus, plus)
     z2_ref[count + size_y :] = jnp.zeros((z2_ref.shape[0] - count - size_y, LANES), jnp.float32)
@@ -699,7 +699,7 @@
         grid, velocity, fraction, response, cell_index, brick_index,
         smem=(5,), smem_outs=(4,), cycles=3000,
     )
-    line_rows = -(-(comps * size_x + comps + 1) // 8) * 8
+    line_rows = -(-(comps * size_x + comps + 1) // 8) * 8 + 8
     (y_lines,) = call(y_lines_kernel, [(line_rows, LANES)], grid, from_z, from_x, from_xz, ready)
     y1, y2 = swapped_y((y_lines, y_lines))
     square = pltpu.VMEM((LANES, LANES), jnp.float32)
@@ -721,7 +721,7 @@
     )
     grid, lines, state, deposit, leaving = call(
         functools.partial(late_kernel, dims),
-        [grid_shape, lines_shape, (STATE * spare, LANES), deposit_shape, (2 * count, LANES)],
+        [grid_shape, lines_shape, (STATE * spare, LANES), deposit_shape, (2 * count + 8, LANES)],
         blocks, brick_index, crossing, table, grid, lines, top, y1, y2, state, deposit,
         aliases={4: 0, 5: 1, 9: 2, 10: 3}, cycles=2000,
         scratch=[
@@ -732,20 +732,18 @@
             pltpu.SemaphoreType.DMA((3,)),
         ],
     )
-    leaving = leaving.reshape(2, count, LANES)
     height = comps * SPREAD
     to_y1, to_y2, top_tiles = call(
         functools.partial(send_y_kernel, push, diffuse),
-        [(count + line_rows, LANES), (count + line_rows, LANES), ((size_x // BX) * height, LANES)],
+        [(count + line_rows, LANES), (count + line_rows, LANES), ((size_x // BX) * height + 8 * REACH_Y, LANES)],
         leaving, grid, deposit, cycles=300, scratch=(pltpu.VMEM((comps * ROWS_Y, LANES), jnp.float32),),
     )
     y1, y2 = swapped_y((to_y1, to_y2))
     deposit, leaving = call(
-        functools.partial(deposit_kernel, dims), [deposit_shape, (4 * count, LANES)],
+        functools.partial(deposit_kernel, dims), [deposit_shape, (4 * count + 8, LANES)],
         blocks, brick_index, crossing, push_parts, spread_parts, state, deposit,
         smem=(0, 1, 2), aliases={6: 0}, cycles=4000,
     )
-    leaving = leaving.reshape(4, count, LANES)
     deposit, over = call(
         merge_kernel, [(comps, size_x + 1, ROWS_Y, LANES), (ROWS_Y, LANES)], deposit, top_tiles,
         cycles=1000, scratch=(pltpu.VMEM(((size_x // BX) * (size_y // BY) * height, LANES), jnp.float32), square),
@@ -768,7 +766,7 @@
     got_x = moved_along(to_x, "gx", 1)
     z1, z2 = swapped_z((to_z1, to_z2))
     got_xz = moved_diagonally(to_xz, 1)
-    got_mx = got_x if both else moved_along(leaving[1], "gx", -1)
+    got_mx = got_x if both else moved_along(leaving[count : 2 * count], "gx", -1)
     gas_next, arrivals = call(
         functools.partial(finish_kernel, count), [gas_field.shape, (6, 7, slots, LANES)],
         base, y1, y2, got_x, got_mx, z1, z2, got_xz, hbm_outs=(0, 1),

time: 29.4 us -> 29.2 us (level)
  Pallas kernels: 12.6 us -> 13 us
  starting transfers between devices: 13.6 us -> 13.3 us
    pallas_call x12, Pallas kernels: 12.6 us -> 13 us  [call(): pl.pallas_call(body, out_shape=[o if isinstance(o, jax.ShapeDtypeStruct)...]
    ppermute x2, waiting for transfers between devices: 1.16 us -> 0.74 us  [moved_diagonally(): return lax.ppermute(block, ('gx', 'gz'), route)]
    ppermute x2, starting transfers between devices: 5.13 us -> 4.76 us  [swapped_y(): return (lax.ppermute(blocks[0], 'gy', first), middle)]
    ppermute x1, waiting for transfers between devices: 0.97 us -> 1.3 us  [swapped_z(): lax.ppermute(blocks[1], 'gz', second)]
where the time goes in v15:
time: 29.2 us; the launch traced here: 29.3 us
  starting transfers between devices  13.3 us (46%)
  Pallas kernels  13 us (45%)
  waiting for transfers between devices  2.28 us (8%)
  between operations  0.75 us (3%)
    pallas_call x12, Pallas kernels, call(): pl.pallas_call(body, out_shape=[o if isinstance(o, jax.ShapeDtypeStruct)...  13 us
    ppermute x3, starting transfers between devices, moved_along(): lax.ppermute(block, axis, [(i, (i + distance) % count) for i in range(cou...  6.65 us
    ppermute x2, starting transfers between devices, swapped_y(): return (lax.ppermute(blocks[0], 'gy', first), middle)  4.76 us
    ppermute x1, waiting for transfers between devices, swapped_z(): lax.ppermute(blocks[1], 'gz', second)  1.3 us
    ppermute x1, starting transfers between devices, swapped_z(): lax.ppermute(blocks[1], 'gz', second)  1.24 us
    ppermute x2, waiting for transfers between devices, moved_diagonally(): return lax.ppermute(block, ('gx', 'gz'), route)  0.74 us
    ppermute x2, starting transfers between devices, moved_diagonally(): return lax.ppermute(block, ('gx', 'gz'), route)  0.6 us
  transfers between devices with their start and end apart: 11, of which 3 were waited for; matrix products, arithmetic and copies ran while one was open for 0% of the time, Pallas kernels for 26%

profile of v15, /device:TPU:0, one launch (start us, length us, event | category | flops | bytes accessed | tf_op | source)
XLA Modules:
  0.0 29.3 jit_solution(13414553721635828877)
XLA Ops:
  0.6 1.2 %shard_map.94 = (f32[3,18,24,128]{3,2,1,0:T(8,128)S(1)}, f32[16,128]{1,0:T(8,128)S(1)}, f32[48,128]{1,0:T(8,128)S(1)}, f32[3,64,128]{2,1,0:T(8,128)S(1)}, f32[3,...) custom-call(f32[3,16,16,128]{3,2,1,0:T(8,128)} %gas_ref.1, ...), custom_call_target="tpu_custom_call" | custom-call | tf_op jit(solution)/shard_map/pallas_call | solution.py:69
  1.9 3.0 %collective-permute-start.1 = (f32[48,128]{1,0:T(8,128)S(1)}, f32[48,128]{1,0:T(8,128)S(1)}, u32[]{:S(2)}, u32[]{:S(2)}) collective-permute-start(f32[48,128]{1,0:T(8,128)S(1)} %get-tuple-element.55), channel_id=1, source_target_pairs={{0,16},{16,0},{1,17},{17,1},{2,18},{18,2},{3,19},{19,3},{4,20},{20... | collective-permute-start | bytes 73736 | tf_op jit(solution)/shard_map/ppermute | solution.py:38
  4.9 0.6 %collective-permute-start.2 = (f32[16,128]{1,0:T(8,128)S(1)}, f32[16,128]{1,0:T(8,128)S(1)}, u32[]{:S(2)}, u32[]{:S(2)}) collective-permute-start(f32[16,128]{1,0:T(8,128)S(1)} %get-tuple-element.54), channel_id=1, source_target_pairs={{0,28},{4,16},{8,20},{12,24},{16,12},{20,0},{24,4},{28,8},{1,29},{... | collective-permute-start | bytes 24584 | tf_op jit(solution)/shard_map/ppermute | solution.py:63
  5.5 1.1 %collective-permute-start = (f32[16,128]{1,0:T(8,128)S(1)}, f32[16,128]{1,0:T(8,128)S(1)}, u32[]{:S(2)}, u32[]{:S(2)}) collective-permute-start(f32[16,128]{1,0:T(8,128)S(1)} %get-tuple-element.54), channel_id=1, source_target_pairs={{0,12},{4,0},{8,4},{12,8},{1,13},{5,1},{9,5},{13,9},{2,14},{6,2},{... | collective-permute-start | bytes 24584 | tf_op jit(solution)/shard_map/ppermute | solution.py:38
  6.6 2.0 %shard_map.95 = (f32[6528,128]{1,0:T(8,128)S(1)}, f32[2176,128]{1,0:T(8,128)S(1)}, f32[1152,128]{1,0:T(8,128)S(1)}, f32[8,128]{1,0:T(8,128)S(1)}, s32[130]{0:T(256)S(1)}) custom-call(f32[3,18,24,128]{3,2,1,0:T(8,128)S(1)} %get-tuple-element.44.grid_ref.grid_in_ref, f32[3,64,128]{2,1,0:T(8,128)S(1)} %get-tuple-element.45.velocity_ref, ...), custom_call_target="tpu_custom_call" | custom-call | flops 12288000 | bytes 3072000 | tf_op jit(solution)/shard_map/pallas_call | solution.py:69
  8.7 0.0 collective-permute-done.2.edge_ref
  8.7 0.0 collective-permute-done.face_ref
  8.7 0.0 collective-permute-done.1.from_x_ref
  8.7 0.1 shard_map.97
  8.8 0.0 collective-permute-start.4
  8.8 3.1 %collective-permute-start.3 = (f32[64,128]{1,0:T(8,128)S(1)}, f32[64,128]{1,0:T(8,128)S(1)}, u32[]{:S(2)}, u32[]{:S(2)}) collective-permute-start(f32[64,128]{1,0:T(8,128)S(1)} %shard_map.97), channel_id=1, source_target_pairs={{0,1},{1,0},{2,3},{3,2},{4,5},{5,4},{6,7},{7,6},{8,9},{9,8},{10,11... | collective-permute-start | bytes 98312 | tf_op jit(solution)/shard_map/ppermute | solution.py:57
  11.9 1.9 %shard_map.96 = (f32[576,128]{1,0:T(8,128)S(1)}, bf16[64,96,128]{2,1,0:T(8,128)(2,1)S(1)}, bf16[64,256,128]{2,1,0:T(8,128)(2,1)S(1)}, f32[3,18,24,128]{3,2,1,0:T...) custom-call(s32[130]{0:T(256)S(1)} %get-tuple-element.50.list_in.list_, ...), custom_call_target="tpu_custom_call", output_to_operand_aliasing={{3}: (3, {}), {4}: (4, {})} | custom-call | flops 16384000 | bytes 4096000 | tf_op jit(solution)/shard_map/pallas_call | solution.py:69
  13.8 0.0 collective-permute-done.4.second_ref
  13.9 0.0 collective-permute-done.3.first_ref
  13.9 2.9 %shard_map.98 = (f32[3,18,24,128]{3,2,1,0:T(8,128)S(1)}, f32[6528,128]{1,0:T(8,128)S(1)}, f32[576,128]{1,0:T(8,128)S(1)}, f32[2176,128]{1,0:T(8,128)S(1)}, f32[120,128]{1,0:T(8,128)S(1)}) custom-call(s32[130]{0:T(256)S(1)} %get-tuple-element.50.list_in.list_ref, ...), custom_call_target="tpu_custom_call", output_to_operand_aliasing={{0}: (4, {}), {1}: (5, {}), {2}: (9, {}), {3}: (10, {})} | custom-call | flops 8192000 | bytes 2048000 | tf_op jit(solution)/shard_map/pallas_call | solution.py:69
  16.8 0.2 shard_map.100
  17.0 1.6 %collective-permute-start.5 = (f32[120,128]{1,0:T(8,128)S(1)}, f32[120,128]{1,0:T(8,128)S(1)}, u32[]{:S(2)}, u32[]{:S(2)}) collective-permute-start(f32[120,128]{1,0:T(8,128)S(1)} %get-tuple-element.71), channel_id=1, source_target_pairs={{0,1},{1,0},{2,3},{3,2},{4,5},{5,4},{6,7},{7,6},{8,9},{9,8},{10,11... | collective-permute-start | bytes 184328 | tf_op jit(solution)/shard_map/ppermute | solution.py:57
  18.6 0.0 collective-permute-start.6
  18.6 2.2 %shard_map.99 = (f32[2176,128]{1,0:T(8,128)S(1)}, f32[232,128]{1,0:T(8,128)S(1)}) custom-call(s32[130]{0:T(256)S(1)} %get-tuple-element.50.list_in.list_ref, s32[64]{0:T(128)S(1)} %get-tuple-element.49.brick_ref.brick_in, s32[6,8]{1,0:T(8,128)S(1)} %get-tuple-element.51.crossing_in.crossing_ref, ...), custom_call_target="tpu_custom_call", output_to_operand_aliasing={{0}: (6, {})} | custom-call | flops 16384000 | bytes 4096000 | tf_op jit(solution)/shard_map/pallas_call | solution.py:69
  20.8 0.4 %shard_map.101 = (f32[3,17,24,128]{3,2,1,0:T(8,128)S(1)}, f32[24,128]{1,0:T(8,128)S(1)}) custom-call(f32[2176,128]{1,0:T(8,128)S(1)} %get-tuple-element.67.deposit_ref, f32[544,128]{1,0:T(8,128)S(1)} %get-tuple-element.69.top_tiles_ref), custom_call_target="tpu_custom_call" | custom-call | flops 4096000 | bytes 1024000 | tf_op jit(solution)/shard_map/pallas_call | solution.py:69
  21.2 0.2 shard_map.103
  21.4 0.0 collective-permute-done.5.y1_ref.first_ref
  21.4 0.0 collective-permute-done.6.y2_ref.second_ref
  21.4 2.5 %collective-permute-start.7 = (f32[160,128]{1,0:T(8,128)S(1)}, f32[160,128]{1,0:T(8,128)S(1)}, u32[]{:S(2)}, u32[]{:S(2)}) collective-permute-start(f32[160,128]{1,0:T(8,128)S(1)} %get-tuple-element.78), channel_id=1, source_target_pairs={{0,16},{16,0},{1,17},{17,1},{2,18},{18,2},{3,19},{19,3},{4,20},{20... | collective-permute-start | bytes 245768 | tf_op jit(solution)/shard_map/ppermute | solution.py:38
  23.9 0.0 collective-permute-start.10
  23.9 1.2 %collective-permute-start.9 = (f32[80,128]{1,0:T(8,128)S(1)}, f32[80,128]{1,0:T(8,128)S(1)}, u32[]{:S(2)}, u32[]{:S(2)}) collective-permute-start(f32[80,128]{1,0:T(8,128)S(1)} %get-tuple-element.80), channel_id=1, source_target_pairs={{0,12},{4,8},{8,4},{12,0},{1,13},{5,9},{9,5},{13,1},{2,14},{6,10},... | collective-permute-start | bytes 122888 | tf_op jit(solution)/shard_map/ppermute | solution.py:45
  25.2 0.0 collective-permute-start.8
  25.2 1.0 %shard_map.102 = (f32[3,16,16,128]{3,2,1,0:T(8,128)S(1)}, f32[3,64,128]{2,1,0:T(8,128)}) custom-call(f32[3,18,24,128]{3,2,1,0:T(8,128)S(1)} %get-tuple-element.62.grid_ref, f32[3,17,24,128]{3,2,1,0:T(8,128)S(1)} %get-tuple-element.70.deposit_ref, f32[128,128]{1,0:T(8,128)S(1)} %get-tuple-element.58.top_in_ref.top_ref, ...), custom_call_target="tpu_custom_call" | custom-call | flops 4096000 | bytes 1024000 | tf_op jit(solution)/shard_map/pallas_call | solution.py:69
  26.2 0.2 collective-permute-done.8.z1_ref
  26.4 1.3 %collective-permute-done.9.z2_ref = f32[80,128]{1,0:T(8,128)S(1)} collective-permute-done((f32[80,128]{1,0:T(8,128)S(1)}, f32[80,128]{1,0:T(8,128)S(1)}, u32[]{:S(2)}, u32[]{:S(2)}) %collective-permute-start.9) | collective-permute-done | bytes 40992 | tf_op jit(solution)/shard_map/ppermute | solution.py:45
  27.7 0.7 %collective-permute-done.10.edge_ref = f32[88,128]{1,0:T(8,128)S(1)} collective-permute-done((f32[88,128]{1,0:T(8,128)S(1)}, f32[88,128]{1,0:T(8,128)S(1)}, u32[]{:S(2)}, u32[]{:S(2)}) %collective-permute-start.10) | collective-permute-done | bytes 45088 | tf_op jit(solution)/shard_map/ppermute | solution.py:63
  28.4 0.0 collective-permute-done.7.x_ref.minus_x_ref
  28.4 0.9 %shard_map.105 = (f32[3,16,16,128]{3,2,1,0:T(8,128)}, f32[6,7,8,128]{3,2,1,0:T(8,128)}) custom-call(f32[3,16,16,128]{3,2,1,0:T(8,128)S(1)} %get-tuple-element.73.base_ref, f32[120,128]{1,0:T(8,128)S(1)} %collective-permute-done.5.y1_ref.first_ref, f32[120,128]{1,0:T(8,128)S(1)} %collective-permute-done.6.y2_ref.second_ref, ...), custom_call_target="tpu_custom_call" | custom-call | tf_op jit(solution)/shard_map/pallas_call | solution.py:69
  (1 shorter events, 0.0 us)
Async XLA Ops:
  1.9 6.8 %collective-permute-start.1 = (f32[48,128]{1,0:T(8,128)S(1)}, f32[48,128]{1,0:T(8,128)S(1)}, u32[]{:S(2)}, u32[]{:S(2)}) collective-permute-start(f32[48,128]{1,0:T(8,128)S(1)} %get-tuple-element.55), channel_id=1, source_target_pairs={{0,16},{16,0},{1,17},{17,1},{2,18},{18,2},{3,19},{19,3},{4,20},{20... | collective-permute-start | bytes 73736 | tf_op jit(solution)/shard_map/ppermute | solution.py:38
  4.9 3.7 %collective-permute-start.2 = (f32[16,128]{1,0:T(8,128)S(1)}, f32[16,128]{1,0:T(8,128)S(1)}, u32[]{:S(2)}, u32[]{:S(2)}) collective-permute-start(f32[16,128]{1,0:T(8,128)S(1)} %get-tuple-element.54), channel_id=1, source_target_pairs={{0,28},{4,16},{8,20},{12,24},{16,12},{20,0},{24,4},{28,8},{1,29},{... | collective-permute-start | bytes 24584 | tf_op jit(solution)/shard_map/ppermute | solution.py:63
  5.5 3.2 %collective-permute-start = (f32[16,128]{1,0:T(8,128)S(1)}, f32[16,128]{1,0:T(8,128)S(1)}, u32[]{:S(2)}, u32[]{:S(2)}) collective-permute-start(f32[16,128]{1,0:T(8,128)S(1)} %get-tuple-element.54), channel_id=1, source_target_pairs={{0,12},{4,0},{8,4},{12,8},{1,13},{5,1},{9,5},{13,9},{2,14},{6,2},{... | collective-permute-start | bytes 24584 | tf_op jit(solution)/shard_map/ppermute | solution.py:38
  8.8 5.1 %collective-permute-start.4 = (f32[64,128]{1,0:T(8,128)S(1)}, f32[64,128]{1,0:T(8,128)S(1)}, u32[]{:S(2)}, u32[]{:S(2)}) collective-permute-start(f32[64,128]{1,0:T(8,128)S(1)} %shard_map.97), channel_id=1, source_target_pairs={{0,4},{3,7},{1,2},{2,1},{4,0},{7,3},{5,6},{6,5},{8,12},{11,15},{9,... | collective-permute-start | bytes 98312 | tf_op jit(solution)/shard_map/ppermute | solution.py:56
  8.8 5.1 %collective-permute-start.3 = (f32[64,128]{1,0:T(8,128)S(1)}, f32[64,128]{1,0:T(8,128)S(1)}, u32[]{:S(2)}, u32[]{:S(2)}) collective-permute-start(f32[64,128]{1,0:T(8,128)S(1)} %shard_map.97), channel_id=1, source_target_pairs={{0,1},{1,0},{2,3},{3,2},{4,5},{5,4},{6,7},{7,6},{8,9},{9,8},{10,11... | collective-permute-start | bytes 98312 | tf_op jit(solution)/shard_map/ppermute | solution.py:57
  17.0 4.4 %collective-permute-start.5 = (f32[120,128]{1,0:T(8,128)S(1)}, f32[120,128]{1,0:T(8,128)S(1)}, u32[]{:S(2)}, u32[]{:S(2)}) collective-permute-start(f32[120,128]{1,0:T(8,128)S(1)} %get-tuple-element.71), channel_id=1, source_target_pairs={{0,1},{1,0},{2,3},{3,2},{4,5},{5,4},{6,7},{7,6},{8,9},{9,8},{10,11... | collective-permute-start | bytes 184328 | tf_op jit(solution)/shard_map/ppermute | solution.py:57
  18.6 2.8 %collective-permute-start.6 = (f32[120,128]{1,0:T(8,128)S(1)}, f32[120,128]{1,0:T(8,128)S(1)}, u32[]{:S(2)}, u32[]{:S(2)}) collective-permute-start(f32[120,128]{1,0:T(8,128)S(1)} %get-tuple-element.72), channel_id=1, source_target_pairs={{0,4},{3,7},{1,2},{2,1},{4,0},{7,3},{5,6},{6,5},{8,12},{11,15},{9,... | collective-permute-start | bytes 184328 | tf_op jit(solution)/shard_map/ppermute | solution.py:56
  21.4 7.0 %collective-permute-start.7 = (f32[160,128]{1,0:T(8,128)S(1)}, f32[160,128]{1,0:T(8,128)S(1)}, u32[]{:S(2)}, u32[]{:S(2)}) collective-permute-start(f32[160,128]{1,0:T(8,128)S(1)} %get-tuple-element.78), channel_id=1, source_target_pairs={{0,16},{16,0},{1,17},{17,1},{2,18},{18,2},{3,19},{19,3},{4,20},{20... | collective-permute-start | bytes 245768 | tf_op jit(solution)/shard_map/ppermute | solution.py:38
  23.9 4.5 %collective-permute-start.10 = (f32[88,128]{1,0:T(8,128)S(1)}, f32[88,128]{1,0:T(8,128)S(1)}, u32[]{:S(2)}, u32[]{:S(2)}) collective-permute-start(f32[88,128]{1,0:T(8,128)S(1)} %get-tuple-element.81), channel_id=1, source_target_pairs={{0,20},{4,24},{8,28},{12,16},{16,4},{20,8},{24,12},{28,0},{1,21},{... | collective-permute-start | bytes 135176 | tf_op jit(solution)/shard_map/ppermute | solution.py:63
  23.9 3.8 %collective-permute-start.9 = (f32[80,128]{1,0:T(8,128)S(1)}, f32[80,128]{1,0:T(8,128)S(1)}, u32[]{:S(2)}, u32[]{:S(2)}) collective-permute-start(f32[80,128]{1,0:T(8,128)S(1)} %get-tuple-element.80), channel_id=1, source_target_pairs={{0,12},{4,8},{8,4},{12,0},{1,13},{5,9},{9,5},{13,1},{2,14},{6,10},... | collective-permute-start | bytes 122888 | tf_op jit(solution)/shard_map/ppermute | solution.py:45
  25.2 1.2 %collective-permute-start.8 = (f32[72,128]{1,0:T(8,128)S(1)}, f32[72,128]{1,0:T(8,128)S(1)}, u32[]{:S(2)}, u32[]{:S(2)}) collective-permute-start(f32[72,128]{1,0:T(8,128)S(1)} %get-tuple-element.79), channel_id=1, source_target_pairs={{0,4},{4,0},{8,12},{12,8},{1,5},{5,1},{9,13},{13,9},{2,6},{6,2},{1... | collective-permute-start | bytes 110600 | tf_op jit(solution)/shard_map/ppermute | solution.py:45

commit v16 on v15

--- a/solution.py
+++ b/solution.py
@@ -413,7 +413,8 @@
 
 
 def deposit_kernel(
-    dims, list_ref, brick_ref, crossing_ref, push_ref, spread_ref, state_ref, deposit_in_ref, deposit_ref, leaving_ref
+    dims, push, diffuse, list_ref, brick_ref, crossing_ref, push_ref, spread_ref, state_ref, deposit_in_ref, top_tiles_ref,
+    grid_ref, deposit_ref, leaving_ref, plane_ref, x_ref, z_ref, face_ref, tiles_ref, turned_ref,
 ):
     base, groups, end = groups_in(list_ref, 0, WIDE)
     _, _, _, deposits_of, add = block_steps(dims, list_ref, brick_ref, end)
@@ -424,12 +425,16 @@
         mine = [group * WIDE + i for i in range(WIDE)]
         add(deposit_ref, base + group * WIDE, deposits_of([(push_ref[i], spread_ref[i]) for i in mine]))
 
+    merge(deposit_ref, top_tiles_ref, plane_ref, face_ref, tiles_ref, turned_ref)
+    send_xz(push, diffuse, grid_ref, plane_ref, face_ref, x_ref, z_ref)
+
 
 def late_kernel(
-    dims, list_in, brick_in, crossing_in, table_ref, grid_in_ref, lines_in_ref, top_in_ref, first_ref, second_ref,
+    dims, push, diffuse, list_in, brick_in, crossing_in, table_ref, grid_in_ref, lines_in_ref, top_in_ref,
+    first_ref, second_ref,
     state_in_ref, deposit_in_ref,
-    grid_ref, lines_ref, state_ref, deposit_ref, leaving_ref,
-    push_ref, spread_ref, list_ref, brick_ref, crossing_ref, turned_ref, sems,
+    grid_ref, lines_ref, state_ref, deposit_ref, y1_ref, y2_ref, tiles_ref,
+    push_ref, spread_ref, list_ref, brick_ref, crossing_ref, turned_ref, leaving_ref, y_lines_ref, sems,
 ):
     copies = fetched(sems, (list_in, list_ref), (brick_in, brick_ref), (crossing_in, crossing_ref))
     halo_y_kernel(
@@ -451,11 +456,12 @@
         tiles, fresh = group_of(taken)
         add(deposit_ref, before, shares)
         keep(state_ref, taken, tiles)
-        for i, (push, spread) in enumerate(fresh):
-            push_ref[i] = push
+        for i, (kept, spread) in enumerate(fresh):
+            push_ref[i] = kept
             spread_ref[i] = spread
 
     leave(crossing_ref, state_ref, leaving_ref, (2, 3))
+    send_y(push, diffuse, leaving_ref, grid_ref, deposit_ref, y1_ref, y2_ref, tiles_ref, y_lines_ref)
 
 
 def top_rows(deposit_ref, q, count_x, count_y, rows_z, size_z):
@@ -467,7 +473,7 @@
     return total
 
 
-def send_y_kernel(push, diffuse, leaving_ref, grid_ref, deposit_ref, y1_ref, y2_ref, tiles_ref, lines_ref):
+def send_y(push, diffuse, leaving_ref, grid_ref, deposit_ref, y1_ref, y2_ref, tiles_ref, lines_ref):
     comps, size_x, size_y, size_z = grid_ref.shape[0], grid_ref.shape[1] - 2, grid_ref.shape[2] - 8, grid_ref.shape[3]
     count_x, count_y = size_x // BX, size_y // BY
     rows_z = size_z + 8
@@ -507,7 +513,7 @@
     y2_ref[at : at + 1] = push * corner
 
 
-def merge_kernel(deposit_ref, top_tiles_ref, plane_ref, face_ref, tiles_ref, turned_ref):
+def merge(deposit_ref, top_tiles_ref, plane_ref, face_ref, tiles_ref, turned_ref):
     comps, planes = plane_ref.shape[:2]
     count_x, size_z = (planes - 1) // BX, plane_ref.shape[3]
     rows_z = size_z + 8
@@ -560,7 +566,7 @@
     face_ref[...] = jnp.transpose(turned_ref[...])[: face_ref.shape[0]]
 
 
-def send_xz_kernel(push, diffuse, grid_ref, deposit_ref, face_ref, x_ref, z_ref):
+def send_xz(push, diffuse, grid_ref, deposit_ref, face_ref, x_ref, z_ref):
     comps, size_x = grid_ref.shape[0], grid_ref.shape[1] - 2
     size_y = z_ref.shape[0]
     lane = lane_ids(size_y)
@@ -719,9 +725,18 @@
         blocks, brick_index, table, grid, lines, from_z, from_x, from_xz,
         aliases={3: 3, 4: 4}, cycles=4000, scratch=(*scalars, square, pltpu.SemaphoreType.DMA((2,))),
     )
-    grid, lines, state, deposit, leaving = call(
-        functools.partial(late_kernel, dims),
-        [grid_shape, lines_shape, (STATE * spare, LANES), deposit_shape, (2 * count + 8, LANES)],
+    height = comps * SPREAD
+    grid, lines, state, deposit, to_y1, to_y2, top_tiles = call(
+        functools.partial(late_kernel, dims, push, diffuse),
+        [
+            grid_shape,
+            lines_shape,
+            (STATE * spare, LANES),
+            deposit_shape,
+            (count + line_rows, LANES),
+            (count + line_rows, LANES),
+            ((size_x // BX) * height + 8 * REACH_Y, LANES),
+        ],
         blocks, brick_index, crossing, table, grid, lines, top, y1, y2, state, deposit,
         aliases={4: 0, 5: 1, 9: 2, 10: 3}, cycles=2000,
         scratch=[
@@ -729,28 +744,28 @@
             *scalars,
             pltpu.SMEM(crossing.shape, jnp.int32),
             square,
+            pltpu.VMEM((2 * count + 8, LANES), jnp.float32),
+            pltpu.VMEM((comps * ROWS_Y, LANES), jnp.float32),
             pltpu.SemaphoreType.DMA((3,)),
         ],
     )
-    height = comps * SPREAD
-    to_y1, to_y2, top_tiles = call(
-        functools.partial(send_y_kernel, push, diffuse),
-        [(count + line_rows, LANES), (count + line_rows, LANES), ((size_x // BX) * height + 8 * REACH_Y, LANES)],
-        leaving, grid, deposit, cycles=300, scratch=(pltpu.VMEM((comps * ROWS_Y, LANES), jnp.float32),),
-    )
     y1, y2 = swapped_y((to_y1, to_y2))
-    deposit, leaving = call(
-        functools.partial(deposit_kernel, dims), [deposit_shape, (4 * count + 8, LANES)],
-        blocks, brick_index, crossing, push_parts, spread_parts, state, deposit,
-        smem=(0, 1, 2), aliases={6: 0}, cycles=4000,
-    )
-    deposit, over = call(
-        merge_kernel, [(comps, size_x + 1, ROWS_Y, LANES), (ROWS_Y, LANES)], deposit, top_tiles,
-        cycles=1000, scratch=(pltpu.VMEM(((size_x // BX) * (size_y // BY) * height, LANES), jnp.float32), square),
-    )
-    to_x, to_z = call(
-        functools.partial(send_xz_kernel, push, diffuse), [(comps * size_y, LANES), (size_y, LANES)],
-        grid, deposit, over, cycles=500,
+    _, leaving, deposit, to_x, to_z = call(
+        functools.partial(deposit_kernel, dims, push, diffuse),
+        [
+            deposit_shape,
+            (4 * count + 8, LANES),
+            (comps, size_x + 1, ROWS_Y, LANES),
+            (comps * size_y, LANES),
+            (size_y, LANES),
+        ],
+        blocks, brick_index, crossing, push_parts, spread_parts, state, deposit, top_tiles, grid,
+        smem=(0, 1, 2), aliases={6: 0}, cycles=5000,
+        scratch=(
+            pltpu.VMEM((ROWS_Y, LANES), jnp.float32),
+            pltpu.VMEM(((size_x // BX) * (size_y // BY) * height, LANES), jnp.float32),
+            square,
+        ),
     )
     base, velocity_next = call(
         functools.partial(base_kernel, push, diffuse, count), [gas_field.shape, (comps, nblocks, LANES)],

time: 29.2 us -> 28.6 us (0.979); the launches traced: 29.3 us -> 28.2 us
  waiting for transfers between devices: 2.28 us -> 1.71 us
  starting transfers between devices: 13.3 us -> 12.8 us
    ppermute x3, starting transfers between devices: 6.65 us -> 5.72 us  [moved_along(): lax.ppermute(block, axis, [(i, (i + distance) % count) for i in range(cou...]
    ppermute x2, starting transfers between devices: 0.6 us -> 0.95 us  [moved_diagonally(): return lax.ppermute(block, ('gx', 'gz'), route)]
    ppermute x1, waiting for transfers between devices: 1.3 us -> 0.95 us  [swapped_z(): lax.ppermute(blocks[1], 'gz', second)]
    pallas_call x12 -> x9, Pallas kernels: 13 us -> 12.9 us  [call(): pl.pallas_call(body, out_shape=[o if isinstance(o, jax.ShapeDtypeStruct)...]
  transfers between devices with their start and end apart: 11 -> 11, of which waited for: 3 -> 3; matrix products, arithmetic and copies ran while one was open for 0% -> 0% of each run, Pallas kernels for 26% -> 27%
where the time goes in v16:
time: 28.6 us; the launch traced here: 28.2 us
  Pallas kernels  12.9 us (45%)
  starting transfers between devices  12.8 us (45%)
  waiting for transfers between devices  1.71 us (6%)
  between operations  0.75 us (3%)
    pallas_call x9, Pallas kernels, call(): pl.pallas_call(body, out_shape=[o if isinstance(o, jax.ShapeDtypeStruct)...  12.9 us
    ppermute x3, starting transfers between devices, moved_along(): lax.ppermute(block, axis, [(i, (i + distance) % count) for i in range(cou...  5.72 us
    ppermute x2, starting transfers between devices, swapped_y(): return (lax.ppermute(blocks[0], 'gy', first), middle)  4.78 us
    ppermute x1, starting transfers between devices, swapped_z(): lax.ppermute(blocks[1], 'gz', second)  1.35 us
    ppermute x1, waiting for transfers between devices, swapped_z(): lax.ppermute(blocks[1], 'gz', second)  0.95 us
    ppermute x2, starting transfers between devices, moved_diagonally(): return lax.ppermute(block, ('gx', 'gz'), route)  0.95 us
  transfers between devices with their start and end apart: 11, of which 3 were waited for; matrix products, arithmetic and copies ran while one was open for 0% of the time, Pallas kernels for 27%

profile of v16, /device:TPU:0, one launch (start us, length us, event | category | flops | bytes accessed | tf_op | source)
XLA Modules:
  0.0 28.2 jit_solution(7027870321418265753)
XLA Ops:
  0.6 1.2 %shard_map.94 = (f32[3,18,24,128]{3,2,1,0:T(8,128)S(1)}, f32[16,128]{1,0:T(8,128)S(1)}, f32[48,128]{1,0:T(8,128)S(1)}, f32[3,64,128]{2,1,0:T(8,128)S(1)}, f32[3,...) custom-call(f32[3,16,16,128]{3,2,1,0:T(8,128)} %gas_ref.1, ...), custom_call_target="tpu_custom_call" | custom-call | tf_op jit(solution)/shard_map/pallas_call | solution.py:69
  1.9 3.0 %collective-permute-start.1 = (f32[48,128]{1,0:T(8,128)S(1)}, f32[48,128]{1,0:T(8,128)S(1)}, u32[]{:S(2)}, u32[]{:S(2)}) collective-permute-start(f32[48,128]{1,0:T(8,128)S(1)} %get-tuple-element.52), channel_id=1, source_target_pairs={{0,16},{16,0},{1,17},{17,1},{2,18},{18,2},{3,19},{19,3},{4,20},{20... | collective-permute-start | bytes 73736 | tf_op jit(solution)/shard_map/ppermute | solution.py:38
  4.9 0.6 %collective-permute-start.2 = (f32[16,128]{1,0:T(8,128)S(1)}, f32[16,128]{1,0:T(8,128)S(1)}, u32[]{:S(2)}, u32[]{:S(2)}) collective-permute-start(f32[16,128]{1,0:T(8,128)S(1)} %get-tuple-element.51), channel_id=1, source_target_pairs={{0,28},{4,16},{8,20},{12,24},{16,12},{20,0},{24,4},{28,8},{1,29},{... | collective-permute-start | bytes 24584 | tf_op jit(solution)/shard_map/ppermute | solution.py:63
  5.5 1.1 %collective-permute-start = (f32[16,128]{1,0:T(8,128)S(1)}, f32[16,128]{1,0:T(8,128)S(1)}, u32[]{:S(2)}, u32[]{:S(2)}) collective-permute-start(f32[16,128]{1,0:T(8,128)S(1)} %get-tuple-element.51), channel_id=1, source_target_pairs={{0,12},{4,0},{8,4},{12,8},{1,13},{5,1},{9,5},{13,9},{2,14},{6,2},{... | collective-permute-start | bytes 24584 | tf_op jit(solution)/shard_map/ppermute | solution.py:38
  6.6 2.0 %shard_map.95 = (f32[6528,128]{1,0:T(8,128)S(1)}, f32[2176,128]{1,0:T(8,128)S(1)}, f32[1152,128]{1,0:T(8,128)S(1)}, f32[8,128]{1,0:T(8,128)S(1)}, s32[130]{0:T(256)S(1)}) custom-call(f32[3,18,24,128]{3,2,1,0:T(8,128)S(1)} %get-tuple-element.41.grid_ref.grid_in_ref, f32[3,64,128]{2,1,0:T(8,128)S(1)} %get-tuple-element.42.velocity_ref, ...), custom_call_target="tpu_custom_call" | custom-call | flops 12288000 | bytes 3072000 | tf_op jit(solution)/shard_map/pallas_call | solution.py:69
  8.7 0.0 collective-permute-done.2.edge_ref
  8.7 0.0 collective-permute-done.face_ref
  8.7 0.0 collective-permute-done.1.from_x_ref
  8.7 0.1 shard_map.97
  8.8 0.0 collective-permute-start.4
  8.8 3.1 %collective-permute-start.3 = (f32[64,128]{1,0:T(8,128)S(1)}, f32[64,128]{1,0:T(8,128)S(1)}, u32[]{:S(2)}, u32[]{:S(2)}) collective-permute-start(f32[64,128]{1,0:T(8,128)S(1)} %shard_map.97), channel_id=1, source_target_pairs={{0,1},{1,0},{2,3},{3,2},{4,5},{5,4},{6,7},{7,6},{8,9},{9,8},{10,11... | collective-permute-start | bytes 98312 | tf_op jit(solution)/shard_map/ppermute | solution.py:57
  11.9 1.9 %shard_map.96 = (f32[576,128]{1,0:T(8,128)S(1)}, bf16[64,96,128]{2,1,0:T(8,128)(2,1)S(1)}, bf16[64,256,128]{2,1,0:T(8,128)(2,1)S(1)}, f32[3,18,24,128]{3,2,1,0:T...) custom-call(s32[130]{0:T(256)S(1)} %get-tuple-element.47.list_in.list_, ...), custom_call_target="tpu_custom_call", output_to_operand_aliasing={{3}: (3, {}), {4}: (4, {})} | custom-call | flops 16384000 | bytes 4096000 | tf_op jit(solution)/shard_map/pallas_call | solution.py:69
  13.8 0.0 collective-permute-done.4.second_ref
  13.9 0.0 collective-permute-done.3.first_ref
  13.9 3.0 %shard_map.98 = (f32[3,18,24,128]{3,2,1,0:T(8,128)S(1)}, f32[6528,128]{1,0:T(8,128)S(1)}, f32[576,128]{1,0:T(8,128)S(1)}, f32[2176,128]{1,0:T(8,128)S(1)}, f32[1...) custom-call(s32[130]{0:T(256)S(1)} %get-tuple-element.47.list_in.lis, ...), custom_call_target="tpu_custom_call", output_to_operand_aliasing={{0}: (4, {}), {1}: (5, {}), {2}: (9, {}), {3}: (10, {})} | custom-call | flops 8192000 | bytes 2048000 | tf_op jit(solution)/shard_map/pallas_call | solution.py:69
  16.9 1.6 %collective-permute-start.5 = (f32[120,128]{1,0:T(8,128)S(1)}, f32[120,128]{1,0:T(8,128)S(1)}, u32[]{:S(2)}, u32[]{:S(2)}) collective-permute-start(f32[120,128]{1,0:T(8,128)S(1)} %get-tuple-element.66), channel_id=1, source_target_pairs={{0,1},{1,0},{2,3},{3,2},{4,5},{5,4},{6,7},{7,6},{8,9},{9,8},{10,11... | collective-permute-start | bytes 184328 | tf_op jit(solution)/shard_map/ppermute | solution.py:57
  18.5 0.0 collective-permute-start.6
  18.5 2.7 %shard_map.99 = (f32[2176,128]{1,0:T(8,128)S(1)}, f32[232,128]{1,0:T(8,128)S(1)}, f32[3,17,24,128]{3,2,1,0:T(8,128)S(1)}, f32[48,128]{1,0:T(8,128)S(1)}, f32[16,128]{1,0:T(8,128)S(1)}) custom-call(s32[130]{0:T(256)S(1)} %get-tuple-element.47.list_in.list_ref, s32[64]{0:T(128)S(1)} %get-tuple-element.46.brick_ref.brick_in, ...), custom_call_target="tpu_custom_call", output_to_operand_aliasing={{0}: (6, {})} | custom-call | flops 20480000 | bytes 5120000 | tf_op jit(solution)/shard_map/pallas_call | solution.py:69
  21.3 0.0 collective-permute-done.5.y1_ref.first_ref
  21.3 0.0 collective-permute-done.6.y2_ref.second_ref
  21.3 1.6 %collective-permute-start.7 = (f32[160,128]{1,0:T(8,128)S(1)}, f32[160,128]{1,0:T(8,128)S(1)}, u32[]{:S(2)}, u32[]{:S(2)}) collective-permute-start(f32[160,128]{1,0:T(8,128)S(1)} %get-tuple-element.72), channel_id=1, source_target_pairs={{0,16},{16,0},{1,17},{17,1},{2,18},{18,2},{3,19},{19,3},{4,20},{20... | collective-permute-start | bytes 245768 | tf_op jit(solution)/shard_map/ppermute | solution.py:38
  22.9 0.4 %collective-permute-start.10 = (f32[88,128]{1,0:T(8,128)S(1)}, f32[88,128]{1,0:T(8,128)S(1)}, u32[]{:S(2)}, u32[]{:S(2)}) collective-permute-start(f32[88,128]{1,0:T(8,128)S(1)} %get-tuple-element.75), channel_id=1, source_target_pairs={{0,20},{4,24},{8,28},{12,16},{16,4},{20,8},{24,12},{28,0},{1,21},{... | collective-permute-start | bytes 135176 | tf_op jit(solution)/shard_map/ppermute | solution.py:63
  23.3 1.4 %collective-permute-start.9 = (f32[80,128]{1,0:T(8,128)S(1)}, f32[80,128]{1,0:T(8,128)S(1)}, u32[]{:S(2)}, u32[]{:S(2)}) collective-permute-start(f32[80,128]{1,0:T(8,128)S(1)} %get-tuple-element.74), channel_id=1, source_target_pairs={{0,12},{4,8},{8,4},{12,0},{1,13},{5,9},{9,5},{13,1},{2,14},{6,10},... | collective-permute-start | bytes 122888 | tf_op jit(solution)/shard_map/ppermute | solution.py:45
  24.6 0.0 collective-permute-start.8
  24.6 1.0 %shard_map.100 = (f32[3,16,16,128]{3,2,1,0:T(8,128)S(1)}, f32[3,64,128]{2,1,0:T(8,128)}) custom-call(f32[3,18,24,128]{3,2,1,0:T(8,128)S(1)} %get-tuple-element.59.grid_ref, f32[3,17,24,128]{3,2,1,0:T(8,128)S(1)} %get-tuple-element.65.deposit_ref, f32[128,128]{1,0:T(8,128)S(1)} %get-tuple-element.55.top_in_ref.top_ref, ...), custom_call_target="tpu_custom_call" | custom-call | flops 4096000 | bytes 1024000 | tf_op jit(solution)/shard_map/pallas_call | solution.py:69
  25.6 0.2 collective-permute-done.8.z1_ref
  25.8 0.9 %collective-permute-done.9.z2_ref = f32[80,128]{1,0:T(8,128)S(1)} collective-permute-done((f32[80,128]{1,0:T(8,128)S(1)}, f32[80,128]{1,0:T(8,128)S(1)}, u32[]{:S(2)}, u32[]{:S(2)}) %collective-permute-start.9) | collective-permute-done | bytes 40992 | tf_op jit(solution)/shard_map/ppermute | solution.py:45
  26.8 0.5 %collective-permute-done.10.edge_ref = f32[88,128]{1,0:T(8,128)S(1)} collective-permute-done((f32[88,128]{1,0:T(8,128)S(1)}, f32[88,128]{1,0:T(8,128)S(1)}, u32[]{:S(2)}, u32[]{:S(2)}) %collective-permute-start.10) | collective-permute-done | bytes 45088 | tf_op jit(solution)/shard_map/ppermute | solution.py:63
  27.3 0.0 collective-permute-done.7.x_ref.minus_x_ref
  27.3 0.9 %shard_map.102 = (f32[3,16,16,128]{3,2,1,0:T(8,128)}, f32[6,7,8,128]{3,2,1,0:T(8,128)}) custom-call(f32[3,16,16,128]{3,2,1,0:T(8,128)S(1)} %get-tuple-element.68.base_ref, f32[120,128]{1,0:T(8,128)S(1)} %collective-permute-done.5.y1_ref.first_ref, f32[120,128]{1,0:T(8,128)S(1)} %collective-permute-done.6.y2_ref.second_ref, ...), custom_call_target="tpu_custom_call" | custom-call | tf_op jit(solution)/shard_map/pallas_call | solution.py:69
  (1 shorter events, 0.0 us)
Async XLA Ops:
  1.9 6.8 %collective-permute-start.1 = (f32[48,128]{1,0:T(8,128)S(1)}, f32[48,128]{1,0:T(8,128)S(1)}, u32[]{:S(2)}, u32[]{:S(2)}) collective-permute-start(f32[48,128]{1,0:T(8,128)S(1)} %get-tuple-element.52), channel_id=1, source_target_pairs={{0,16},{16,0},{1,17},{17,1},{2,18},{18,2},{3,19},{19,3},{4,20},{20... | collective-permute-start | bytes 73736 | tf_op jit(solution)/shard_map/ppermute | solution.py:38
  4.9 3.7 %collective-permute-start.2 = (f32[16,128]{1,0:T(8,128)S(1)}, f32[16,128]{1,0:T(8,128)S(1)}, u32[]{:S(2)}, u32[]{:S(2)}) collective-permute-start(f32[16,128]{1,0:T(8,128)S(1)} %get-tuple-element.51), channel_id=1, source_target_pairs={{0,28},{4,16},{8,20},{12,24},{16,12},{20,0},{24,4},{28,8},{1,29},{... | collective-permute-start | bytes 24584 | tf_op jit(solution)/shard_map/ppermute | solution.py:63
  5.5 3.2 %collective-permute-start = (f32[16,128]{1,0:T(8,128)S(1)}, f32[16,128]{1,0:T(8,128)S(1)}, u32[]{:S(2)}, u32[]{:S(2)}) collective-permute-start(f32[16,128]{1,0:T(8,128)S(1)} %get-tuple-element.51), channel_id=1, source_target_pairs={{0,12},{4,0},{8,4},{12,8},{1,13},{5,1},{9,5},{13,9},{2,14},{6,2},{... | collective-permute-start | bytes 24584 | tf_op jit(solution)/shard_map/ppermute | solution.py:38
  8.8 5.1 %collective-permute-start.4 = (f32[64,128]{1,0:T(8,128)S(1)}, f32[64,128]{1,0:T(8,128)S(1)}, u32[]{:S(2)}, u32[]{:S(2)}) collective-permute-start(f32[64,128]{1,0:T(8,128)S(1)} %shard_map.97), channel_id=1, source_target_pairs={{0,4},{3,7},{1,2},{2,1},{4,0},{7,3},{5,6},{6,5},{8,12},{11,15},{9,... | collective-permute-start | bytes 98312 | tf_op jit(solution)/shard_map/ppermute | solution.py:56
  8.8 5.1 %collective-permute-start.3 = (f32[64,128]{1,0:T(8,128)S(1)}, f32[64,128]{1,0:T(8,128)S(1)}, u32[]{:S(2)}, u32[]{:S(2)}) collective-permute-start(f32[64,128]{1,0:T(8,128)S(1)} %shard_map.97), channel_id=1, source_target_pairs={{0,1},{1,0},{2,3},{3,2},{4,5},{5,4},{6,7},{7,6},{8,9},{9,8},{10,11... | collective-permute-start | bytes 98312 | tf_op jit(solution)/shard_map/ppermute | solution.py:57
  16.9 4.4 %collective-permute-start.5 = (f32[120,128]{1,0:T(8,128)S(1)}, f32[120,128]{1,0:T(8,128)S(1)}, u32[]{:S(2)}, u32[]{:S(2)}) collective-permute-start(f32[120,128]{1,0:T(8,128)S(1)} %get-tuple-element.66), channel_id=1, source_target_pairs={{0,1},{1,0},{2,3},{3,2},{4,5},{5,4},{6,7},{7,6},{8,9},{9,8},{10,11... | collective-permute-start | bytes 184328 | tf_op jit(solution)/shard_map/ppermute | solution.py:57
  18.5 2.8 %collective-permute-start.6 = (f32[120,128]{1,0:T(8,128)S(1)}, f32[120,128]{1,0:T(8,128)S(1)}, u32[]{:S(2)}, u32[]{:S(2)}) collective-permute-start(f32[120,128]{1,0:T(8,128)S(1)} %get-tuple-element.67), channel_id=1, source_target_pairs={{0,4},{3,7},{1,2},{2,1},{4,0},{7,3},{5,6},{6,5},{8,12},{11,15},{9,... | collective-permute-start | bytes 184328 | tf_op jit(solution)/shard_map/ppermute | solution.py:56
  21.3 5.9 %collective-permute-start.7 = (f32[160,128]{1,0:T(8,128)S(1)}, f32[160,128]{1,0:T(8,128)S(1)}, u32[]{:S(2)}, u32[]{:S(2)}) collective-permute-start(f32[160,128]{1,0:T(8,128)S(1)} %get-tuple-element.72), channel_id=1, source_target_pairs={{0,16},{16,0},{1,17},{17,1},{2,18},{18,2},{3,19},{19,3},{4,20},{20... | collective-permute-start | bytes 245768 | tf_op jit(solution)/shard_map/ppermute | solution.py:38
  22.9 4.4 %collective-permute-start.10 = (f32[88,128]{1,0:T(8,128)S(1)}, f32[88,128]{1,0:T(8,128)S(1)}, u32[]{:S(2)}, u32[]{:S(2)}) collective-permute-start(f32[88,128]{1,0:T(8,128)S(1)} %get-tuple-element.75), channel_id=1, source_target_pairs={{0,20},{4,24},{8,28},{12,16},{16,4},{20,8},{24,12},{28,0},{1,21},{... | collective-permute-start | bytes 135176 | tf_op jit(solution)/shard_map/ppermute | solution.py:63
  23.3 3.5 %collective-permute-start.9 = (f32[80,128]{1,0:T(8,128)S(1)}, f32[80,128]{1,0:T(8,128)S(1)}, u32[]{:S(2)}, u32[]{:S(2)}) collective-permute-start(f32[80,128]{1,0:T(8,128)S(1)} %get-tuple-element.74), channel_id=1, source_target_pairs={{0,12},{4,8},{8,4},{12,0},{1,13},{5,9},{9,5},{13,1},{2,14},{6,10},... | collective-permute-start | bytes 122888 | tf_op jit(solution)/shard_map/ppermute | solution.py:45
  24.6 1.2 %collective-permute-start.8 = (f32[72,128]{1,0:T(8,128)S(1)}, f32[72,128]{1,0:T(8,128)S(1)}, u32[]{:S(2)}, u32[]{:S(2)}) collective-permute-start(f32[72,128]{1,0:T(8,128)S(1)} %get-tuple-element.73), channel_id=1, source_target_pairs={{0,4},{4,0},{8,12},{12,8},{1,5},{5,1},{9,13},{13,9},{2,6},{6,2},{1... | collective-permute-start | bytes 110600 | tf_op jit(solution)/shard_map/ppermute | solution.py:45

commit v17 on v16

--- a/solution.py
+++ b/solution.py
@@ -775,7 +775,7 @@
     both = lax.axis_size("gx") == 2
     to_x, to_z1, to_z2, to_xz = call(
         functools.partial(relay_kernel, size_x, size_y, comps, count),
-        [(edge + (2 if both else 1) * count, LANES), *[(count + size_y + 8 * more, LANES) for more in range(3)]],
+        [(edge + (2 if both else 1) * count, LANES), *[(count + size_y + 8 * more, LANES) for more in (0, 2, 1)]],
         y1, y2, to_x, to_z, leaving,
     )
     got_x = moved_along(to_x, "gx", 1)

time: 28.6 us -> 29.4 us (1.028)
  starting transfers between devices: 12.8 us -> 13.5 us
  Pallas kernels: 12.9 us -> 13.4 us
    ppermute x1, starting transfers between devices: 0.01 us -> 1.38 us  [swapped_z(): lax.ppermute(blocks[0], 'gz', first)]
    ppermute x1, starting transfers between devices: 1.35 us -> 0.31 us  [swapped_z(): lax.ppermute(blocks[1], 'gz', second)]
    ppermute x1, waiting for transfers between devices: 0.95 us -> 0.01 us  [swapped_z(): lax.ppermute(blocks[1], 'gz', second)]
    ppermute x2, waiting for transfers between devices: 0.5 us -> 1.45 us  [moved_diagonally(): return lax.ppermute(block, ('gx', 'gz'), route)]
    pallas_call x9, Pallas kernels: 12.9 us -> 13.4 us  [call(): pl.pallas_call(body, out_shape=[o if isinstance(o, jax.ShapeDtypeStruct)...]
    ppermute x2, starting transfers between devices: 4.78 us -> 5.19 us  [swapped_y(): return (lax.ppermute(blocks[0], 'gy', first), middle)]
    ppermute x3, starting transfers between devices: 5.72 us -> 5.32 us  [moved_along(): lax.ppermute(block, axis, [(i, (i + distance) % count) for i in range(cou...]
    ppermute x2, starting transfers between devices: 0.95 us -> 1.24 us  [moved_diagonally(): return lax.ppermute(block, ('gx', 'gz'), route)]
  transfers between devices with their start and end apart: 11 -> 11, of which waited for: 3 -> 1; matrix products, arithmetic and copies ran while one was open for 0% -> 0% of each run, Pallas kernels for 27% -> 29%
where the time goes in v17:
time: 29.4 us; the launch traced here: 29.1 us
  starting transfers between devices  13.5 us (46%)
  Pallas kernels  13.4 us (46%)
  waiting for transfers between devices  1.47 us (5%)
  between operations  0.75 us (3%)
    pallas_call x9, Pallas kernels, call(): pl.pallas_call(body, out_shape=[o if isinstance(o, jax.ShapeDtypeStruct)...  13.4 us
    ppermute x3, starting transfers between devices, moved_along(): lax.ppermute(block, axis, [(i, (i + distance) % count) for i in range(cou...  5.32 us
    ppermute x2, starting transfers between devices, swapped_y(): return (lax.ppermute(blocks[0], 'gy', first), middle)  5.19 us
    ppermute x2, waiting for transfers between devices, moved_diagonally(): return lax.ppermute(block, ('gx', 'gz'), route)  1.45 us
    ppermute x1, starting transfers between devices, swapped_z(): lax.ppermute(blocks[0], 'gz', first)  1.38 us
    ppermute x2, starting transfers between devices, moved_diagonally(): return lax.ppermute(block, ('gx', 'gz'), route)  1.24 us
  transfers between devices with their start and end apart: 11, of which 1 were waited for; matrix products, arithmetic and copies ran while one was open for 0% of the time, Pallas kernels for 29%

profile of v17, /device:TPU:0, one launch (start us, length us, event | category | flops | bytes accessed | tf_op | source)
XLA Modules:
  0.0 29.1 jit_solution(10839158826659828764)
XLA Ops:
  0.6 1.2 %shard_map.94 = (f32[3,18,24,128]{3,2,1,0:T(8,128)S(1)}, f32[16,128]{1,0:T(8,128)S(1)}, f32[48,128]{1,0:T(8,128)S(1)}, f32[3,64,128]{2,1,0:T(8,128)S(1)}, f32[3,...) custom-call(f32[3,16,16,128]{3,2,1,0:T(8,128)} %gas_ref.1, ...), custom_call_target="tpu_custom_call" | custom-call | tf_op jit(solution)/shard_map/pallas_call | solution.py:69
  1.9 3.0 %collective-permute-start.1 = (f32[48,128]{1,0:T(8,128)S(1)}, f32[48,128]{1,0:T(8,128)S(1)}, u32[]{:S(2)}, u32[]{:S(2)}) collective-permute-start(f32[48,128]{1,0:T(8,128)S(1)} %get-tuple-element.52), channel_id=1, source_target_pairs={{0,16},{16,0},{1,17},{17,1},{2,18},{18,2},{3,19},{19,3},{4,20},{20... | collective-permute-start | bytes 73736 | tf_op jit(solution)/shard_map/ppermute | solution.py:38
  4.9 0.6 %collective-permute-start.2 = (f32[16,128]{1,0:T(8,128)S(1)}, f32[16,128]{1,0:T(8,128)S(1)}, u32[]{:S(2)}, u32[]{:S(2)}) collective-permute-start(f32[16,128]{1,0:T(8,128)S(1)} %get-tuple-element.51), channel_id=1, source_target_pairs={{0,28},{4,16},{8,20},{12,24},{16,12},{20,0},{24,4},{28,8},{1,29},{... | collective-permute-start | bytes 24584 | tf_op jit(solution)/shard_map/ppermute | solution.py:63
  5.5 1.1 %collective-permute-start = (f32[16,128]{1,0:T(8,128)S(1)}, f32[16,128]{1,0:T(8,128)S(1)}, u32[]{:S(2)}, u32[]{:S(2)}) collective-permute-start(f32[16,128]{1,0:T(8,128)S(1)} %get-tuple-element.51), channel_id=1, source_target_pairs={{0,12},{4,0},{8,4},{12,8},{1,13},{5,1},{9,5},{13,9},{2,14},{6,2},{... | collective-permute-start | bytes 24584 | tf_op jit(solution)/shard_map/ppermute | solution.py:38
  6.6 2.0 %shard_map.95 = (f32[6528,128]{1,0:T(8,128)S(1)}, f32[2176,128]{1,0:T(8,128)S(1)}, f32[1152,128]{1,0:T(8,128)S(1)}, f32[8,128]{1,0:T(8,128)S(1)}, s32[130]{0:T(256)S(1)}) custom-call(f32[3,18,24,128]{3,2,1,0:T(8,128)S(1)} %get-tuple-element.41.grid_ref.grid_in_ref, f32[3,64,128]{2,1,0:T(8,128)S(1)} %get-tuple-element.42.velocity_ref, ...), custom_call_target="tpu_custom_call" | custom-call | flops 12288000 | bytes 3072000 | tf_op jit(solution)/shard_map/pallas_call | solution.py:69
  8.7 0.0 collective-permute-done.2.edge_ref
  8.7 0.0 collective-permute-done.face_ref
  8.7 0.0 collective-permute-done.1.from_x_ref
  8.7 0.1 shard_map.97
  8.8 0.0 collective-permute-start.4
  8.8 3.1 %collective-permute-start.3 = (f32[64,128]{1,0:T(8,128)S(1)}, f32[64,128]{1,0:T(8,128)S(1)}, u32[]{:S(2)}, u32[]{:S(2)}) collective-permute-start(f32[64,128]{1,0:T(8,128)S(1)} %shard_map.97), channel_id=1, source_target_pairs={{0,1},{1,0},{2,3},{3,2},{4,5},{5,4},{6,7},{7,6},{8,9},{9,8},{10,11... | collective-permute-start | bytes 98312 | tf_op jit(solution)/shard_map/ppermute | solution.py:57
  11.9 2.3 %shard_map.96 = (f32[576,128]{1,0:T(8,128)S(1)}, bf16[64,96,128]{2,1,0:T(8,128)(2,1)S(1)}, bf16[64,256,128]{2,1,0:T(8,128)(2,1)S(1)}, f32[3,18,24,128]{3,2,1,0:T...) custom-call(s32[130]{0:T(256)S(1)} %get-tuple-element.47.list_in.list_, ...), custom_call_target="tpu_custom_call", output_to_operand_aliasing={{3}: (3, {}), {4}: (4, {})} | custom-call | flops 16384000 | bytes 4096000 | tf_op jit(solution)/shard_map/pallas_call | solution.py:69
  14.3 0.0 collective-permute-done.4.second_ref
  14.3 0.0 collective-permute-done.3.first_ref
  14.3 2.6 %shard_map.98 = (f32[3,18,24,128]{3,2,1,0:T(8,128)S(1)}, f32[6528,128]{1,0:T(8,128)S(1)}, f32[576,128]{1,0:T(8,128)S(1)}, f32[2176,128]{1,0:T(8,128)S(1)}, f32[1...) custom-call(s32[130]{0:T(256)S(1)} %get-tuple-element.47.list_in.lis, ...), custom_call_target="tpu_custom_call", output_to_operand_aliasing={{0}: (4, {}), {1}: (5, {}), {2}: (9, {}), {3}: (10, {})} | custom-call | flops 8192000 | bytes 2048000 | tf_op jit(solution)/shard_map/pallas_call | solution.py:69
  16.9 2.0 %collective-permute-start.5 = (f32[120,128]{1,0:T(8,128)S(1)}, f32[120,128]{1,0:T(8,128)S(1)}, u32[]{:S(2)}, u32[]{:S(2)}) collective-permute-start(f32[120,128]{1,0:T(8,128)S(1)} %get-tuple-element.66), channel_id=1, source_target_pairs={{0,1},{1,0},{2,3},{3,2},{4,5},{5,4},{6,7},{7,6},{8,9},{9,8},{10,11... | collective-permute-start | bytes 184328 | tf_op jit(solution)/shard_map/ppermute | solution.py:57
  19.0 0.0 collective-permute-start.6
  19.0 3.2 %shard_map.99 = (f32[2176,128]{1,0:T(8,128)S(1)}, f32[232,128]{1,0:T(8,128)S(1)}, f32[3,17,24,128]{3,2,1,0:T(8,128)S(1)}, f32[48,128]{1,0:T(8,128)S(1)}, f32[16,128]{1,0:T(8,128)S(1)}) custom-call(s32[130]{0:T(256)S(1)} %get-tuple-element.47.list_in.list_ref, s32[64]{0:T(128)S(1)} %get-tuple-element.46.brick_ref.brick_in, ...), custom_call_target="tpu_custom_call", output_to_operand_aliasing={{0}: (6, {})} | custom-call | flops 20480000 | bytes 5120000 | tf_op jit(solution)/shard_map/pallas_call | solution.py:69
  22.2 0.0 collective-permute-done.5.y1_ref.first_ref
  22.2 0.0 collective-permute-done.6.y2_ref.second_ref
  22.2 1.2 %collective-permute-start.7 = (f32[160,128]{1,0:T(8,128)S(1)}, f32[160,128]{1,0:T(8,128)S(1)}, u32[]{:S(2)}, u32[]{:S(2)}) collective-permute-start(f32[160,128]{1,0:T(8,128)S(1)} %get-tuple-element.72), channel_id=1, source_target_pairs={{0,16},{16,0},{1,17},{17,1},{2,18},{18,2},{3,19},{19,3},{4,20},{20... | collective-permute-start | bytes 245768 | tf_op jit(solution)/shard_map/ppermute | solution.py:38
  23.4 0.3 %collective-permute-start.9 = (f32[88,128]{1,0:T(8,128)S(1)}, f32[88,128]{1,0:T(8,128)S(1)}, u32[]{:S(2)}, u32[]{:S(2)}) collective-permute-start(f32[88,128]{1,0:T(8,128)S(1)} %get-tuple-element.74), channel_id=1, source_target_pairs={{0,12},{4,8},{8,4},{12,0},{1,13},{5,9},{9,5},{13,1},{2,14},{6,10},... | collective-permute-start | bytes 135176 | tf_op jit(solution)/shard_map/ppermute | solution.py:45
  23.7 0.6 %collective-permute-start.10 = (f32[80,128]{1,0:T(8,128)S(1)}, f32[80,128]{1,0:T(8,128)S(1)}, u32[]{:S(2)}, u32[]{:S(2)}) collective-permute-start(f32[80,128]{1,0:T(8,128)S(1)} %get-tuple-element.75), channel_id=1, source_target_pairs={{0,20},{4,24},{8,28},{12,16},{16,4},{20,8},{24,12},{28,0},{1,21},{... | collective-permute-start | bytes 122888 | tf_op jit(solution)/shard_map/ppermute | solution.py:63
  24.4 1.4 %collective-permute-start.8 = (f32[72,128]{1,0:T(8,128)S(1)}, f32[72,128]{1,0:T(8,128)S(1)}, u32[]{:S(2)}, u32[]{:S(2)}) collective-permute-start(f32[72,128]{1,0:T(8,128)S(1)} %get-tuple-element.73), channel_id=1, source_target_pairs={{0,4},{4,0},{8,12},{12,8},{1,5},{5,1},{9,13},{13,9},{2,6},{6,2},{1... | collective-permute-start | bytes 110600 | tf_op jit(solution)/shard_map/ppermute | solution.py:45
  25.7 1.0 %shard_map.100 = (f32[3,16,16,128]{3,2,1,0:T(8,128)S(1)}, f32[3,64,128]{2,1,0:T(8,128)}) custom-call(f32[3,18,24,128]{3,2,1,0:T(8,128)S(1)} %get-tuple-element.59.grid_ref, f32[3,17,24,128]{3,2,1,0:T(8,128)S(1)} %get-tuple-element.65.deposit_ref, f32[128,128]{1,0:T(8,128)S(1)} %get-tuple-element.55.top_in_ref.top_ref, ...), custom_call_target="tpu_custom_call" | custom-call | flops 4096000 | bytes 1024000 | tf_op jit(solution)/shard_map/pallas_call | solution.py:69
  26.7 0.0 collective-permute-done.8.z1_ref
  26.7 1.4 %collective-permute-done.10.edge_ref = f32[80,128]{1,0:T(8,128)S(1)} collective-permute-done((f32[80,128]{1,0:T(8,128)S(1)}, f32[80,128]{1,0:T(8,128)S(1)}, u32[]{:S(2)}, u32[]{:S(2)}) %collective-permute-start.10) | collective-permute-done | bytes 40992 | tf_op jit(solution)/shard_map/ppermute | solution.py:63
  28.2 0.0 collective-permute-done.9.z2_ref
  28.2 0.0 collective-permute-done.7.x_ref.minus_x_ref
  28.2 0.9 %shard_map.102 = (f32[3,16,16,128]{3,2,1,0:T(8,128)}, f32[6,7,8,128]{3,2,1,0:T(8,128)}) custom-call(f32[3,16,16,128]{3,2,1,0:T(8,128)S(1)} %get-tuple-element.68.base_ref, f32[120,128]{1,0:T(8,128)S(1)} %collective-permute-done.5.y1_ref.first_ref, f32[120,128]{1,0:T(8,128)S(1)} %collective-permute-done.6.y2_ref.second_ref, ...), custom_call_target="tpu_custom_call" | custom-call | tf_op jit(solution)/shard_map/pallas_call | solution.py:69
  (1 shorter events, 0.0 us)
Async XLA Ops:
  1.9 6.8 %collective-permute-start.1 = (f32[48,128]{1,0:T(8,128)S(1)}, f32[48,128]{1,0:T(8,128)S(1)}, u32[]{:S(2)}, u32[]{:S(2)}) collective-permute-start(f32[48,128]{1,0:T(8,128)S(1)} %get-tuple-element.52), channel_id=1, source_target_pairs={{0,16},{16,0},{1,17},{17,1},{2,18},{18,2},{3,19},{19,3},{4,20},{20... | collective-permute-start | bytes 73736 | tf_op jit(solution)/shard_map/ppermute | solution.py:38
  4.9 3.7 %collective-permute-start.2 = (f32[16,128]{1,0:T(8,128)S(1)}, f32[16,128]{1,0:T(8,128)S(1)}, u32[]{:S(2)}, u32[]{:S(2)}) collective-permute-start(f32[16,128]{1,0:T(8,128)S(1)} %get-tuple-element.51), channel_id=1, source_target_pairs={{0,28},{4,16},{8,20},{12,24},{16,12},{20,0},{24,4},{28,8},{1,29},{... | collective-permute-start | bytes 24584 | tf_op jit(solution)/shard_map/ppermute | solution.py:63
  5.5 3.2 %collective-permute-start = (f32[16,128]{1,0:T(8,128)S(1)}, f32[16,128]{1,0:T(8,128)S(1)}, u32[]{:S(2)}, u32[]{:S(2)}) collective-permute-start(f32[16,128]{1,0:T(8,128)S(1)} %get-tuple-element.51), channel_id=1, source_target_pairs={{0,12},{4,0},{8,4},{12,8},{1,13},{5,1},{9,5},{13,9},{2,14},{6,2},{... | collective-permute-start | bytes 24584 | tf_op jit(solution)/shard_map/ppermute | solution.py:38
  8.8 5.5 %collective-permute-start.4 = (f32[64,128]{1,0:T(8,128)S(1)}, f32[64,128]{1,0:T(8,128)S(1)}, u32[]{:S(2)}, u32[]{:S(2)}) collective-permute-start(f32[64,128]{1,0:T(8,128)S(1)} %shard_map.97), channel_id=1, source_target_pairs={{0,4},{3,7},{1,2},{2,1},{4,0},{7,3},{5,6},{6,5},{8,12},{11,15},{9,... | collective-permute-start | bytes 98312 | tf_op jit(solution)/shard_map/ppermute | solution.py:56
  8.8 5.5 %collective-permute-start.3 = (f32[64,128]{1,0:T(8,128)S(1)}, f32[64,128]{1,0:T(8,128)S(1)}, u32[]{:S(2)}, u32[]{:S(2)}) collective-permute-start(f32[64,128]{1,0:T(8,128)S(1)} %shard_map.97), channel_id=1, source_target_pairs={{0,1},{1,0},{2,3},{3,2},{4,5},{5,4},{6,7},{7,6},{8,9},{9,8},{10,11... | collective-permute-start | bytes 98312 | tf_op jit(solution)/shard_map/ppermute | solution.py:57
  16.9 5.3 %collective-permute-start.5 = (f32[120,128]{1,0:T(8,128)S(1)}, f32[120,128]{1,0:T(8,128)S(1)}, u32[]{:S(2)}, u32[]{:S(2)}) collective-permute-start(f32[120,128]{1,0:T(8,128)S(1)} %get-tuple-element.66), channel_id=1, source_target_pairs={{0,1},{1,0},{2,3},{3,2},{4,5},{5,4},{6,7},{7,6},{8,9},{9,8},{10,11... | collective-permute-start | bytes 184328 | tf_op jit(solution)/shard_map/ppermute | solution.py:57
  19.0 3.2 %collective-permute-start.6 = (f32[120,128]{1,0:T(8,128)S(1)}, f32[120,128]{1,0:T(8,128)S(1)}, u32[]{:S(2)}, u32[]{:S(2)}) collective-permute-start(f32[120,128]{1,0:T(8,128)S(1)} %get-tuple-element.67), channel_id=1, source_target_pairs={{0,4},{3,7},{1,2},{2,1},{4,0},{7,3},{5,6},{6,5},{8,12},{11,15},{9,... | collective-permute-start | bytes 184328 | tf_op jit(solution)/shard_map/ppermute | solution.py:56
  22.2 5.9 %collective-permute-start.7 = (f32[160,128]{1,0:T(8,128)S(1)}, f32[160,128]{1,0:T(8,128)S(1)}, u32[]{:S(2)}, u32[]{:S(2)}) collective-permute-start(f32[160,128]{1,0:T(8,128)S(1)} %get-tuple-element.72), channel_id=1, source_target_pairs={{0,16},{16,0},{1,17},{17,1},{2,18},{18,2},{3,19},{19,3},{4,20},{20... | collective-permute-start | bytes 245768 | tf_op jit(solution)/shard_map/ppermute | solution.py:38
  23.4 4.8 %collective-permute-start.9 = (f32[88,128]{1,0:T(8,128)S(1)}, f32[88,128]{1,0:T(8,128)S(1)}, u32[]{:S(2)}, u32[]{:S(2)}) collective-permute-start(f32[88,128]{1,0:T(8,128)S(1)} %get-tuple-element.74), channel_id=1, source_target_pairs={{0,12},{4,8},{8,4},{12,0},{1,13},{5,9},{9,5},{13,1},{2,14},{6,10},... | collective-permute-start | bytes 135176 | tf_op jit(solution)/shard_map/ppermute | solution.py:45
  23.7 4.4 %collective-permute-start.10 = (f32[80,128]{1,0:T(8,128)S(1)}, f32[80,128]{1,0:T(8,128)S(1)}, u32[]{:S(2)}, u32[]{:S(2)}) collective-permute-start(f32[80,128]{1,0:T(8,128)S(1)} %get-tuple-element.75), channel_id=1, source_target_pairs={{0,20},{4,24},{8,28},{12,16},{16,4},{20,8},{24,12},{28,0},{1,21},{... | collective-permute-start | bytes 122888 | tf_op jit(solution)/shard_map/ppermute | solution.py:63
  24.4 2.4 %collective-permute-start.8 = (f32[72,128]{1,0:T(8,128)S(1)}, f32[72,128]{1,0:T(8,128)S(1)}, u32[]{:S(2)}, u32[]{:S(2)}) collective-permute-start(f32[72,128]{1,0:T(8,128)S(1)} %get-tuple-element.73), channel_id=1, source_target_pairs={{0,4},{4,0},{8,12},{12,8},{1,5},{5,1},{9,13},{13,9},{2,6},{6,2},{1... | collective-permute-start | bytes 110600 | tf_op jit(solution)/shard_map/ppermute | solution.py:45

commit v18 on v16

--- a/solution.py
+++ b/solution.py
@@ -22,7 +22,7 @@
 SPREAD = REACH_X * REACH_Y
 REACH_Z = 2 * BZ
 UNROLL = 8
-WIDE = 16
+WIDE = 20
 
 WEIGHT, ALONG_Y, IN_Y, ALONG_Z, IN_Z, RESPONSE, MOVING, OFFSET = 0, 5, 6, 7, 8, 9, 10, 13
 TABLE_ROWS = 16

time: 28.6 us -> 28.6 us (level)
  Pallas kernels: 12.9 us -> 13.4 us
  starting transfers between devices: 12.8 us -> 12.5 us
    pallas_call x9, Pallas kernels: 12.9 us -> 13.4 us  [call(): pl.pallas_call(body, out_shape=[o if isinstance(o, jax.ShapeDtypeStruct)...]
    ppermute x2, starting transfers between devices: 4.78 us -> 4.48 us  [swapped_y(): return (lax.ppermute(blocks[0], 'gy', first), middle)]
  transfers between devices with their start and end apart: 11 -> 11, of which waited for: 3 -> 3; matrix products, arithmetic and copies ran while one was open for 0% -> 0% of each run, Pallas kernels for 27% -> 29%
where the time goes in v18:
time: 28.6 us; the launch traced here: 28.4 us
  Pallas kernels  13.4 us (47%)
  starting transfers between devices  12.5 us (44%)
  waiting for transfers between devices  1.71 us (6%)
  between operations  0.75 us (3%)
    pallas_call x9, Pallas kernels, call(): pl.pallas_call(body, out_shape=[o if isinstance(o, jax.ShapeDtypeStruct)...  13.4 us
    ppermute x3, starting transfers between devices, moved_along(): lax.ppermute(block, axis, [(i, (i + distance) % count) for i in range(cou...  5.72 us
    ppermute x2, starting transfers between devices, swapped_y(): return (lax.ppermute(blocks[0], 'gy', first), middle)  4.48 us
    ppermute x1, starting transfers between devices, swapped_z(): lax.ppermute(blocks[1], 'gz', second)  1.35 us
    ppermute x1, waiting for transfers between devices, swapped_z(): lax.ppermute(blocks[1], 'gz', second)  0.95 us
    ppermute x2, starting transfers between devices, moved_diagonally(): return lax.ppermute(block, ('gx', 'gz'), route)  0.95 us
  transfers between devices with their start and end apart: 11, of which 3 were waited for; matrix products, arithmetic and copies ran while one was open for 0% of the time, Pallas kernels for 29%

profile of v18, /device:TPU:0, one launch (start us, length us, event | category | flops | bytes accessed | tf_op | source)
XLA Modules:
  0.0 28.4 jit_solution(5076738731547475882)
XLA Ops:
  0.6 1.2 %shard_map.94 = (f32[3,18,24,128]{3,2,1,0:T(8,128)S(1)}, f32[16,128]{1,0:T(8,128)S(1)}, f32[48,128]{1,0:T(8,128)S(1)}, f32[3,64,128]{2,1,0:T(8,128)S(1)}, f32[3,...) custom-call(f32[3,16,16,128]{3,2,1,0:T(8,128)} %gas_ref.1, ...), custom_call_target="tpu_custom_call" | custom-call | tf_op jit(solution)/shard_map/pallas_call | solution.py:69
  1.9 3.0 %collective-permute-start.1 = (f32[48,128]{1,0:T(8,128)S(1)}, f32[48,128]{1,0:T(8,128)S(1)}, u32[]{:S(2)}, u32[]{:S(2)}) collective-permute-start(f32[48,128]{1,0:T(8,128)S(1)} %get-tuple-element.52), channel_id=1, source_target_pairs={{0,16},{16,0},{1,17},{17,1},{2,18},{18,2},{3,19},{19,3},{4,20},{20... | collective-permute-start | bytes 73736 | tf_op jit(solution)/shard_map/ppermute | solution.py:38
  4.9 0.6 %collective-permute-start.2 = (f32[16,128]{1,0:T(8,128)S(1)}, f32[16,128]{1,0:T(8,128)S(1)}, u32[]{:S(2)}, u32[]{:S(2)}) collective-permute-start(f32[16,128]{1,0:T(8,128)S(1)} %get-tuple-element.51), channel_id=1, source_target_pairs={{0,28},{4,16},{8,20},{12,24},{16,12},{20,0},{24,4},{28,8},{1,29},{... | collective-permute-start | bytes 24584 | tf_op jit(solution)/shard_map/ppermute | solution.py:63
  5.5 1.1 %collective-permute-start = (f32[16,128]{1,0:T(8,128)S(1)}, f32[16,128]{1,0:T(8,128)S(1)}, u32[]{:S(2)}, u32[]{:S(2)}) collective-permute-start(f32[16,128]{1,0:T(8,128)S(1)} %get-tuple-element.51), channel_id=1, source_target_pairs={{0,12},{4,0},{8,4},{12,8},{1,13},{5,1},{9,5},{13,9},{2,14},{6,2},{... | collective-permute-start | bytes 24584 | tf_op jit(solution)/shard_map/ppermute | solution.py:38
  6.6 2.0 %shard_map.95 = (f32[6528,128]{1,0:T(8,128)S(1)}, f32[2176,128]{1,0:T(8,128)S(1)}, f32[1152,128]{1,0:T(8,128)S(1)}, f32[8,128]{1,0:T(8,128)S(1)}, s32[130]{0:T(256)S(1)}) custom-call(f32[3,18,24,128]{3,2,1,0:T(8,128)S(1)} %get-tuple-element.41.grid_ref.grid_in_ref, f32[3,64,128]{2,1,0:T(8,128)S(1)} %get-tuple-element.42.velocity_ref, ...), custom_call_target="tpu_custom_call" | custom-call | flops 12288000 | bytes 3072000 | tf_op jit(solution)/shard_map/pallas_call | solution.py:69
  8.7 0.0 collective-permute-done.2.edge_ref
  8.7 0.0 collective-permute-done.face_ref
  8.7 0.0 collective-permute-done.1.from_x_ref
  8.7 0.1 shard_map.97
  8.8 0.0 collective-permute-start.4
  8.8 3.1 %collective-permute-start.3 = (f32[64,128]{1,0:T(8,128)S(1)}, f32[64,128]{1,0:T(8,128)S(1)}, u32[]{:S(2)}, u32[]{:S(2)}) collective-permute-start(f32[64,128]{1,0:T(8,128)S(1)} %shard_map.97), channel_id=1, source_target_pairs={{0,1},{1,0},{2,3},{3,2},{4,5},{5,4},{6,7},{7,6},{8,9},{9,8},{10,11... | collective-permute-start | bytes 98312 | tf_op jit(solution)/shard_map/ppermute | solution.py:57
  11.9 2.2 %shard_map.96 = (f32[576,128]{1,0:T(8,128)S(1)}, bf16[80,96,128]{2,1,0:T(8,128)(2,1)S(1)}, bf16[80,256,128]{2,1,0:T(8,128)(2,1)S(1)}, f32[3,18,24,128]{3,2,1,0:T...) custom-call(s32[130]{0:T(256)S(1)} %get-tuple-element.47.list_in.list_, ...), custom_call_target="tpu_custom_call", output_to_operand_aliasing={{3}: (3, {}), {4}: (4, {})} | custom-call | flops 16384000 | bytes 4096000 | tf_op jit(solution)/shard_map/pallas_call | solution.py:69
  14.1 0.0 collective-permute-done.4.second_ref
  14.1 0.0 collective-permute-done.3.first_ref
  14.2 3.0 %shard_map.98 = (f32[3,18,24,128]{3,2,1,0:T(8,128)S(1)}, f32[6528,128]{1,0:T(8,128)S(1)}, f32[576,128]{1,0:T(8,128)S(1)}, f32[2176,128]{1,0:T(8,128)S(1)}, f32[1...) custom-call(s32[130]{0:T(256)S(1)} %get-tuple-element.47.list_in.lis, ...), custom_call_target="tpu_custom_call", output_to_operand_aliasing={{0}: (4, {}), {1}: (5, {}), {2}: (9, {}), {3}: (10, {})} | custom-call | flops 8192000 | bytes 2048000 | tf_op jit(solution)/shard_map/pallas_call | solution.py:69
  17.2 1.3 %collective-permute-start.5 = (f32[120,128]{1,0:T(8,128)S(1)}, f32[120,128]{1,0:T(8,128)S(1)}, u32[]{:S(2)}, u32[]{:S(2)}) collective-permute-start(f32[120,128]{1,0:T(8,128)S(1)} %get-tuple-element.66), channel_id=1, source_target_pairs={{0,1},{1,0},{2,3},{3,2},{4,5},{5,4},{6,7},{7,6},{8,9},{9,8},{10,11... | collective-permute-start | bytes 184328 | tf_op jit(solution)/shard_map/ppermute | solution.py:57
  18.5 0.0 collective-permute-start.6
  18.5 3.0 %shard_map.99 = (f32[2176,128]{1,0:T(8,128)S(1)}, f32[232,128]{1,0:T(8,128)S(1)}, f32[3,17,24,128]{3,2,1,0:T(8,128)S(1)}, f32[48,128]{1,0:T(8,128)S(1)}, f32[16,128]{1,0:T(8,128)S(1)}) custom-call(s32[130]{0:T(256)S(1)} %get-tuple-element.47.list_in.list_ref, s32[64]{0:T(128)S(1)} %get-tuple-element.46.brick_ref.brick_in, ...), custom_call_target="tpu_custom_call", output_to_operand_aliasing={{0}: (6, {})} | custom-call | flops 20480000 | bytes 5120000 | tf_op jit(solution)/shard_map/pallas_call | solution.py:69
  21.5 0.0 collective-permute-done.5.y1_ref.first_ref
  21.5 0.0 collective-permute-done.6.y2_ref.second_ref
  21.6 1.6 %collective-permute-start.7 = (f32[160,128]{1,0:T(8,128)S(1)}, f32[160,128]{1,0:T(8,128)S(1)}, u32[]{:S(2)}, u32[]{:S(2)}) collective-permute-start(f32[160,128]{1,0:T(8,128)S(1)} %get-tuple-element.72), channel_id=1, source_target_pairs={{0,16},{16,0},{1,17},{17,1},{2,18},{18,2},{3,19},{19,3},{4,20},{20... | collective-permute-start | bytes 245768 | tf_op jit(solution)/shard_map/ppermute | solution.py:38
  23.1 0.4 %collective-permute-start.10 = (f32[88,128]{1,0:T(8,128)S(1)}, f32[88,128]{1,0:T(8,128)S(1)}, u32[]{:S(2)}, u32[]{:S(2)}) collective-permute-start(f32[88,128]{1,0:T(8,128)S(1)} %get-tuple-element.75), channel_id=1, source_target_pairs={{0,20},{4,24},{8,28},{12,16},{16,4},{20,8},{24,12},{28,0},{1,21},{... | collective-permute-start | bytes 135176 | tf_op jit(solution)/shard_map/ppermute | solution.py:63
  23.5 1.4 %collective-permute-start.9 = (f32[80,128]{1,0:T(8,128)S(1)}, f32[80,128]{1,0:T(8,128)S(1)}, u32[]{:S(2)}, u32[]{:S(2)}) collective-permute-start(f32[80,128]{1,0:T(8,128)S(1)} %get-tuple-element.74), channel_id=1, source_target_pairs={{0,12},{4,8},{8,4},{12,0},{1,13},{5,9},{9,5},{13,1},{2,14},{6,10},... | collective-permute-start | bytes 122888 | tf_op jit(solution)/shard_map/ppermute | solution.py:45
  24.8 0.0 collective-permute-start.8
  24.9 1.0 %shard_map.100 = (f32[3,16,16,128]{3,2,1,0:T(8,128)S(1)}, f32[3,64,128]{2,1,0:T(8,128)}) custom-call(f32[3,18,24,128]{3,2,1,0:T(8,128)S(1)} %get-tuple-element.59.grid_ref, f32[3,17,24,128]{3,2,1,0:T(8,128)S(1)} %get-tuple-element.65.deposit_ref, f32[128,128]{1,0:T(8,128)S(1)} %get-tuple-element.55.top_in_ref.top_ref, ...), custom_call_target="tpu_custom_call" | custom-call | flops 4096000 | bytes 1024000 | tf_op jit(solution)/shard_map/pallas_call | solution.py:69
  25.8 0.2 collective-permute-done.8.z1_ref
  26.1 0.9 %collective-permute-done.9.z2_ref = f32[80,128]{1,0:T(8,128)S(1)} collective-permute-done((f32[80,128]{1,0:T(8,128)S(1)}, f32[80,128]{1,0:T(8,128)S(1)}, u32[]{:S(2)}, u32[]{:S(2)}) %collective-permute-start.9) | collective-permute-done | bytes 40992 | tf_op jit(solution)/shard_map/ppermute | solution.py:45
  27.0 0.5 %collective-permute-done.10.edge_ref = f32[88,128]{1,0:T(8,128)S(1)} collective-permute-done((f32[88,128]{1,0:T(8,128)S(1)}, f32[88,128]{1,0:T(8,128)S(1)}, u32[]{:S(2)}, u32[]{:S(2)}) %collective-permute-start.10) | collective-permute-done | bytes 45088 | tf_op jit(solution)/shard_map/ppermute | solution.py:63
  27.5 0.0 collective-permute-done.7.x_ref.minus_x_ref
  27.5 0.9 %shard_map.102 = (f32[3,16,16,128]{3,2,1,0:T(8,128)}, f32[6,7,8,128]{3,2,1,0:T(8,128)}) custom-call(f32[3,16,16,128]{3,2,1,0:T(8,128)S(1)} %get-tuple-element.68.base_ref, f32[120,128]{1,0:T(8,128)S(1)} %collective-permute-done.5.y1_ref.first_ref, f32[120,128]{1,0:T(8,128)S(1)} %collective-permute-done.6.y2_ref.second_ref, ...), custom_call_target="tpu_custom_call" | custom-call | tf_op jit(solution)/shard_map/pallas_call | solution.py:69
  (1 shorter events, 0.0 us)
Async XLA Ops:
  1.9 6.8 %collective-permute-start.1 = (f32[48,128]{1,0:T(8,128)S(1)}, f32[48,128]{1,0:T(8,128)S(1)}, u32[]{:S(2)}, u32[]{:S(2)}) collective-permute-start(f32[48,128]{1,0:T(8,128)S(1)} %get-tuple-element.52), channel_id=1, source_target_pairs={{0,16},{16,0},{1,17},{17,1},{2,18},{18,2},{3,19},{19,3},{4,20},{20... | collective-permute-start | bytes 73736 | tf_op jit(solution)/shard_map/ppermute | solution.py:38
  4.9 3.7 %collective-permute-start.2 = (f32[16,128]{1,0:T(8,128)S(1)}, f32[16,128]{1,0:T(8,128)S(1)}, u32[]{:S(2)}, u32[]{:S(2)}) collective-permute-start(f32[16,128]{1,0:T(8,128)S(1)} %get-tuple-element.51), channel_id=1, source_target_pairs={{0,28},{4,16},{8,20},{12,24},{16,12},{20,0},{24,4},{28,8},{1,29},{... | collective-permute-start | bytes 24584 | tf_op jit(solution)/shard_map/ppermute | solution.py:63
  5.5 3.2 %collective-permute-start = (f32[16,128]{1,0:T(8,128)S(1)}, f32[16,128]{1,0:T(8,128)S(1)}, u32[]{:S(2)}, u32[]{:S(2)}) collective-permute-start(f32[16,128]{1,0:T(8,128)S(1)} %get-tuple-element.51), channel_id=1, source_target_pairs={{0,12},{4,0},{8,4},{12,8},{1,13},{5,1},{9,5},{13,9},{2,14},{6,2},{... | collective-permute-start | bytes 24584 | tf_op jit(solution)/shard_map/ppermute | solution.py:38
  8.8 5.4 %collective-permute-start.4 = (f32[64,128]{1,0:T(8,128)S(1)}, f32[64,128]{1,0:T(8,128)S(1)}, u32[]{:S(2)}, u32[]{:S(2)}) collective-permute-start(f32[64,128]{1,0:T(8,128)S(1)} %shard_map.97), channel_id=1, source_target_pairs={{0,4},{3,7},{1,2},{2,1},{4,0},{7,3},{5,6},{6,5},{8,12},{11,15},{9,... | collective-permute-start | bytes 98312 | tf_op jit(solution)/shard_map/ppermute | solution.py:56
  8.8 5.3 %collective-permute-start.3 = (f32[64,128]{1,0:T(8,128)S(1)}, f32[64,128]{1,0:T(8,128)S(1)}, u32[]{:S(2)}, u32[]{:S(2)}) collective-permute-start(f32[64,128]{1,0:T(8,128)S(1)} %shard_map.97), channel_id=1, source_target_pairs={{0,1},{1,0},{2,3},{3,2},{4,5},{5,4},{6,7},{7,6},{8,9},{9,8},{10,11... | collective-permute-start | bytes 98312 | tf_op jit(solution)/shard_map/ppermute | solution.py:57
  17.2 4.3 %collective-permute-start.5 = (f32[120,128]{1,0:T(8,128)S(1)}, f32[120,128]{1,0:T(8,128)S(1)}, u32[]{:S(2)}, u32[]{:S(2)}) collective-permute-start(f32[120,128]{1,0:T(8,128)S(1)} %get-tuple-element.66), channel_id=1, source_target_pairs={{0,1},{1,0},{2,3},{3,2},{4,5},{5,4},{6,7},{7,6},{8,9},{9,8},{10,11... | collective-permute-start | bytes 184328 | tf_op jit(solution)/shard_map/ppermute | solution.py:57
  18.5 3.0 %collective-permute-start.6 = (f32[120,128]{1,0:T(8,128)S(1)}, f32[120,128]{1,0:T(8,128)S(1)}, u32[]{:S(2)}, u32[]{:S(2)}) collective-permute-start(f32[120,128]{1,0:T(8,128)S(1)} %get-tuple-element.67), channel_id=1, source_target_pairs={{0,4},{3,7},{1,2},{2,1},{4,0},{7,3},{5,6},{6,5},{8,12},{11,15},{9,... | collective-permute-start | bytes 184328 | tf_op jit(solution)/shard_map/ppermute | solution.py:56
  21.6 5.9 %collective-permute-start.7 = (f32[160,128]{1,0:T(8,128)S(1)}, f32[160,128]{1,0:T(8,128)S(1)}, u32[]{:S(2)}, u32[]{:S(2)}) collective-permute-start(f32[160,128]{1,0:T(8,128)S(1)} %get-tuple-element.72), channel_id=1, source_target_pairs={{0,16},{16,0},{1,17},{17,1},{2,18},{18,2},{3,19},{19,3},{4,20},{20... | collective-permute-start | bytes 245768 | tf_op jit(solution)/shard_map/ppermute | solution.py:38
  23.1 4.4 %collective-permute-start.10 = (f32[88,128]{1,0:T(8,128)S(1)}, f32[88,128]{1,0:T(8,128)S(1)}, u32[]{:S(2)}, u32[]{:S(2)}) collective-permute-start(f32[88,128]{1,0:T(8,128)S(1)} %get-tuple-element.75), channel_id=1, source_target_pairs={{0,20},{4,24},{8,28},{12,16},{16,4},{20,8},{24,12},{28,0},{1,21},{... | collective-permute-start | bytes 135176 | tf_op jit(solution)/shard_map/ppermute | solution.py:63
  23.5 3.5 %collective-permute-start.9 = (f32[80,128]{1,0:T(8,128)S(1)}, f32[80,128]{1,0:T(8,128)S(1)}, u32[]{:S(2)}, u32[]{:S(2)}) collective-permute-start(f32[80,128]{1,0:T(8,128)S(1)} %get-tuple-element.74), channel_id=1, source_target_pairs={{0,12},{4,8},{8,4},{12,0},{1,13},{5,9},{9,5},{13,1},{2,14},{6,10},... | collective-permute-start | bytes 122888 | tf_op jit(solution)/shard_map/ppermute | solution.py:45
  24.8 1.2 %collective-permute-start.8 = (f32[72,128]{1,0:T(8,128)S(1)}, f32[72,128]{1,0:T(8,128)S(1)}, u32[]{:S(2)}, u32[]{:S(2)}) collective-permute-start(f32[72,128]{1,0:T(8,128)S(1)} %get-tuple-element.73), channel_id=1, source_target_pairs={{0,4},{4,0},{8,12},{12,8},{1,5},{5,1},{9,13},{13,9},{2,6},{6,2},{1... | collective-permute-start | bytes 110600 | tf_op jit(solution)/shard_map/ppermute | solution.py:45
